TPU v7x, 32 devices: a whole 2x2x4 slice. The times are simulated.
32 devices in a mesh: runs: 2 (over x), gx: 16 (over z, y, core).
Axes of the slice: x: 2, y: 2, z: 4, core: 2. Of those that a mesh axis runs over, the one named last changes fastest.
Arguments:
- inputs: bfloat16 [1024, 6144], P('runs', 'gx'), parts along dimension 0, may hold values from -6 to 6
- out_grad: bfloat16 [1024, 6144], P('runs', 'gx'), parts along dimension 0, may hold values from -1.5 to 1.5
- w_qkv: bfloat16 [6144, 3, 8192], P(None, None, 'gx'), may hold values from -0.109375 to 0.109375
- w_out: bfloat16 [8192, 6144], P('gx'), may hold values from -0.0625 to 0.0625
- saved_qkv: bfloat16 [1024, 3, 8192], P('runs', None, 'gx'), parts along dimension 0, may hold values from -30 to 30
- positions: int32 [1024], P('runs'), parts along dimension 0, may hold values from 0 to 511, as said below
Outputs:
- input_grad: bfloat16 [1024, 6144], P('runs', 'gx'), parts along dimension 0
- grad_w_qkv: bfloat16 [12288, 3, 8192], P('runs', None, 'gx'), parts along dimension 0
- grad_w_out: bfloat16 [16384, 6144], P(('runs', 'gx')), parts along dimension 0
There are 2 independent parts, one for each index of `runs`. A program takes and returns all parts, laid end to end along the dimension named above; an argument that names none is the same for every part. Nothing has to cross between parts.
Inputs may be any that keep to these rules, and one draw needn't show every extreme that they name: `positions`: each of 0 to 511 appears once.
All inputs are finite; a program needn't handle non-finite values.
Results may differ from a plain program's by a relative error of at most 0.018.
Values may be sent and summed in bfloat16 or wider, within the bound.
No kernel may reach another device: no remote copies, remote signals or barrier semaphores. Data moves between devices by JAX's collectives and lax.ppermute only.
A program may use at most 192 MiB of HBM per device.

v0:
```python
import math

import jax
import jax.numpy as jnp
from jax import lax
from jax.sharding import PartitionSpec as P

HD = 128


def attend_backward(full_grad, w_out, saved_qkv, positions):
    seq_len = saved_qkv.shape[0]
    columns = saved_qkv.shape[2]
    heads_here = columns // HD
    factor = 1.0 / math.sqrt(HD)
    queries = saved_qkv[:, 0].reshape(seq_len, heads_here, HD)
    keys = saved_qkv[:, 1].reshape(seq_len, heads_here, HD)
    values = saved_qkv[:, 2].reshape(seq_len, heads_here, HD)
    scores = jnp.einsum("qhd,khd->hqk", queries, keys, preferred_element_type=jnp.float32) * factor
    visible = positions[None, :] <= positions[:, None]
    scores = jnp.where(visible[None], scores, jnp.float32(-1e30))
    highest = jnp.max(scores, axis=-1, keepdims=True)
    expd = jnp.exp(scores - highest)
    attn = expd / jnp.sum(expd, axis=-1, keepdims=True)
    attn_b = attn.astype(jnp.bfloat16)
    attended = jnp.einsum(
        "hqk,khd->qhd", attn_b, values, preferred_element_type=jnp.float32
    ).astype(jnp.bfloat16)
    grad_out_h = lax.dot_general(
        full_grad, w_out, (((1,), (1,)), ((), ())), preferred_element_type=jnp.float32
    ).astype(jnp.bfloat16)
    grad_w_out = lax.dot_general(
        attended.reshape(seq_len, columns),
        full_grad,
        (((0,), (0,)), ((), ())),
        preferred_element_type=jnp.float32,
    ).astype(jnp.bfloat16)
    grad_heads = grad_out_h.reshape(seq_len, heads_here, HD)
    grad_attn = jnp.einsum("qhd,khd->hqk", grad_heads, values, preferred_element_type=jnp.float32)
    row_dot = jnp.sum(grad_heads.astype(jnp.float32) * attended.astype(jnp.float32), axis=-1).T[
        :, :, None
    ]
    grad_scores = (attn * (grad_attn - row_dot) * factor).astype(jnp.bfloat16)
    grad_q = jnp.einsum(
        "hqk,khd->qhd", grad_scores, keys, preferred_element_type=jnp.float32
    ).astype(jnp.bfloat16)
    grad_k = jnp.einsum(
        "hqk,qhd->khd", grad_scores, queries, preferred_element_type=jnp.float32
    ).astype(jnp.bfloat16)
    grad_v = jnp.einsum(
        "hqk,qhd->khd", attn_b, grad_heads, preferred_element_type=jnp.float32
    ).astype(jnp.bfloat16)
    grad_qkv = jnp.stack([grad_q, grad_k, grad_v], axis=1).reshape(seq_len, 3 * columns)
    return (grad_w_out, grad_qkv)


def on_device(inputs, out_grad, w_qkv, w_out, saved_qkv, positions):
    columns = saved_qkv.shape[2]
    full_in, full_grad = (
        lax.all_gather(inputs, "gx", axis=1, tiled=True),
        lax.all_gather(out_grad, "gx", axis=1, tiled=True),
    )
    grad_w_out, grad_qkv = attend_backward(full_grad, w_out, saved_qkv, positions)
    grad_flat = lax.dot_general(
        full_in, grad_qkv, (((0,), (0,)), ((), ())), preferred_element_type=jnp.float32
    ).astype(jnp.bfloat16)
    grad_w_qkv = grad_flat.reshape(grad_flat.shape[0], 3, columns)
    w_flat = w_qkv.reshape(w_qkv.shape[0], 3 * columns)
    partial_sum = lax.dot_general(
        grad_qkv, w_flat, (((1,), (1,)), ((), ())), preferred_element_type=jnp.float32
    )
    input_grad = lax.psum_scatter(partial_sum, "gx", scatter_dimension=1, tiled=True).astype(
        jnp.bfloat16
    )
    return (input_grad, grad_w_qkv, grad_w_out)


def solution(mesh):
    placed = (
        P("runs", "gx"),
        P("runs", "gx"),
        P(None, None, "gx"),
        P("gx", None),
        P("runs", None, "gx"),
        P("runs"),
    )
    return jax.shard_map(
        on_device,
        mesh=mesh,
        in_specs=placed,
        out_specs=(P("runs", "gx"), P("runs", None, "gx"), P(("runs", "gx"), None)),
        check_vma=False,
    )
```

profile of v0, /device:TPU:0, one launch (start us, length us, event | category | flops | bytes accessed | tf_op | source)
XLA Modules:
  0.0 289.9 jit_solution(7139888527081610768)
XLA Ops:
  7.2 0.7 all-gather.3.cloned.1.call-update
  7.9 0.7 all-gather.5.cloned.1.call-update
  8.7 1.5 fusion.13
  10.6 0.2 copy.44
  10.8 24.7 %copy.31 = bf16[6144,3,512]{0,2,1:T(8,128)(2,1)} copy(bf16[6144,3,512]{2,0,1:T(8,128)(2,1)} %param.8) | data formatting | bytes 37748736 | tf_op args[2]
  35.7 3.7 %fusion.14 = (f32[4,512]{1,0:T(4,128)S(1)}, f32[4,512,512]{1,2,0:T(8,128)}) fusion(pred[512,512]{0,1:T(8,128)(4,1)S(1)} %broadcast_compare_fusion, bf16[512,4,128]{0,2,1:T(8,128)(2,1)S(1)} %bitcast.57, bf16[512,4,128]{0,2,1:T(8,128)(2,1)S(1)} %bitcast.59), kind=kOutput, calls=%fused_computation.27 | convolution fusion | flops 272630272 | bytes 5513216 | tf_op jit(solution)/shard_map/sub | solution.py:23
  39.5 2.8 fusion.5
  42.2 36.3 %all-gather.3.cloned.1.call-done = bf16[512,6144]{1,0:T(8,128)(2,1)} async-done(((bf16[512,384]{1,0:T(8,128)(2,1)}), bf16[512,6144]{1,0:T(8,128)(2,1)}) %all-gather.3.cloned.1.call-update) | async-done | bytes 6291472 | tf_op jit(solution)/shard_map/all_gather | solution.py:61
  78.6 8.2 %convolution_convert_fusion.2 = bf16[512,512]{0,1:T(8,128)(2,1)S(1)} fusion(bf16[512,6144]{1,0:T(8,128)(2,1)} %all-gather.3.cloned.1.call-done, bf16[512,6144]{1,0:T(8,128)(2,1)} %param.9), kind=kOutput, calls=%fused_computation.13 | convolution fusion | flops 3221487616 | bytes 13107200 | tf_op jit(solution)/shard_map/dot_general | solution.py:29
  86.8 0.8 fusion.7
  87.6 1.3 multiply_reduce_fusion
  88.9 0.4 copy-done
  89.3 0.9 multiply_convert_fusion
  90.2 0.5 copy-done.2
  90.7 0.4 fusion.8
  91.1 0.8 fusion.6
  91.9 1.3 pad_maximum_fusion
  93.3 15.3 %fusion.15 = f32[512,6144]{1,0:T(8,128)} fusion(bf16[512,1536]{0,1:T(8,128)(2,1)} %bitcast.61, bf16[6144,1536]{0,1:T(8,128)(2,1)S(1)} %bitcast.51), kind=kOutput, calls=%fused_computation.28 | convolution fusion | flops 9663676416 | bytes 33030144 | tf_op jit(solution)/shard_map/dot_general | solution.py:69
  108.6 36.0 %all-gather.5.cloned.1.call-done = bf16[512,6144]{1,0:T(8,128)(2,1)} async-done(((bf16[512,384]{1,0:T(8,128)(2,1)}), bf16[512,6144]{1,0:T(8,128)(2,1)}) %all-gather.5.cloned.1.call-update) | async-done | bytes 6291472 | tf_op jit(solution)/shard_map/all_gather | solution.py:60
  144.6 16.2 %convolution_convert_fusion = bf16[1536,6144]{1,0:T(8,128)(2,1)} fusion(bf16[512,1536]{0,1:T(8,128)(2,1)S(1)} %bitcast.62, bf16[512,6144]{1,0:T(8,128)(2,1)} %all-gather.5.cloned.1.call-done), kind=kOutput, calls=%fused_computation.1 | convolution fusion | flops 9673113600 | bytes 26738688 | tf_op jit(solution)/shard_map/dot_general | solution.py:64
  160.8 25.4 %copy.32 = bf16[6144,3,512]{2,0,1:T(8,128)(2,1)} copy(bf16[6144,3,512]{0,2,1:T(8,128)(2,1)} %bitcast.52) | data formatting | bytes 37748736
  186.2 8.1 %convolution_convert_fusion.1 = bf16[512,6144]{1,0:T(8,128)(2,1)} fusion(bf16[512,512]{0,1:T(8,128)(2,1)S(1)} %bitcast.63, bf16[512,6144]{1,0:T(8,128)(2,1)} %all-gather.3.cloned.1.call-done), kind=kOutput, calls=%fused_computation.2 | convolution fusion | flops 3224371200 | bytes 13107200 | tf_op jit(solution)/shard_map/dot_general | solution.py:32
  194.3 87.2 %reduce-scatter.2.cloned.1.call-done = f32[512,384]{1,0:T(8,128)} async-done(((f32[512,6144]{1,0:T(8,128)}), f32[512,384]{1,0:T(8,128)}) %reduce-scatter.2.cloned.1.call-update) | async-done | bytes 786448 | tf_op jit(solution)/shard_map/reduce_scatter | solution.py:72
  281.5 1.9 convert_element_type.64
  (28 shorter events, 0.8 us)
Async XLA Ops:
  7.2 71.4 %all-gather.3.cloned.1.call-start = ((), (), s32[]{:S(2)}) async-start(), calls=%async_computation.1 | async-start | bytes 6684672 | tf_op jit(solution)/shard_map/all_gather | solution.py:61
  7.9 136.7 %all-gather.5.cloned.1.call-start = ((), (), s32[]{:S(2)}) async-start(), calls=%async_computation.3 | async-start | bytes 6684672 | tf_op jit(solution)/shard_map/all_gather | solution.py:60
  8.6 272.8 %reduce-scatter.2.cloned.1.call-start = ((), (), s32[]{:S(2)}) async-start(), calls=%async_computation.2 | async-start | bytes 13369344 | tf_op jit(solution)/shard_map/reduce_scatter | solution.py:72
  10.6 25.1 %copy-start.1 = (bf16[512,1,512]{0,2,1:T(8,128)(2,1)}, bf16[512,1,512]{0,2,1:T(8,128)(2,1)S(1)}, u32[]{:S(2)}) copy-start(bf16[512,1,512]{0,2,1:T(8,128)(2,1)S(1)} %copy.42) | copy-start | bytes 1572868
  10.8 24.7 %copy-start.5 = (s32[512]{0:T(512)S(1)}, s32[512]{0:T(512)}, u32[]{:S(2)}) copy-start(s32[512]{0:T(512)} %param.11) | copy-start | bytes 6148
  78.6 14.7 %slice-start = ((s8[18874368]{0:T(1024)(128)(4,1)}), s8[4194304]{0:T(1024)(128)(4,1)S(1)}, s32[]{:S(2)}) async-start(s8[18874368]{0:T(1024)(128)(4,1)} %bitcast.49), calls=%async_computation.4 | async-start | bytes 8388608
  78.6 14.7 %slice-start.1 = ((s8[18874368]{0:T(1024)(128)(4,1)}), s8[4194304]{0:T(1024)(128)(4,1)S(1)}, s32[]{:S(2)}) async-start(s8[18874368]{0:T(1024)(128)(4,1)} %bitcast.49), calls=%async_computation.5 | async-start | bytes 8388608
  78.6 14.7 %slice-start.2 = ((s8[18874368]{0:T(1024)(128)(4,1)}), s8[4194304]{0:T(1024)(128)(4,1)S(1)}, s32[]{:S(2)}) async-start(s8[18874368]{0:T(1024)(128)(4,1)} %bitcast.49), calls=%async_computation.6 | async-start | bytes 8388608
  86.8 2.5 copy-start
  87.6 5.7 %slice-start.3 = ((s8[18874368]{0:T(1024)(128)(4,1)}), s8[4194304]{0:T(1024)(128)(4,1)S(1)}, s32[]{:S(2)}) async-start(s8[18874368]{0:T(1024)(128)(4,1)} %bitcast.49), calls=%async_computation.7 | async-start | bytes 8388608
  89.3 1.4 copy-start.2
  89.3 4.0 %slice-start.4 = ((s8[18874368]{0:T(1024)(128)(4,1)}), s8[2097152]{0:T(1024)(128)(4,1)S(1)}, s32[]{:S(2)}) async-start(s8[18874368]{0:T(1024)(128)(4,1)} %bitcast.49), calls=%async_computation.8 | async-start | bytes 4194304
  108.6 36.1 %copy-start.3 = (bf16[512,3,4,128]{0,3,2,1:T(8,128)(2,1)S(1)}, bf16[512,3,4,128]{0,3,2,1:T(8,128)(2,1)}, u32[]{:S(2)}) copy-start(bf16[512,3,4,128]{0,3,2,1:T(8,128)(2,1)} %pad_maximum_fusion) | copy-start | bytes 4718596
  160.8 25.4 %copy-start.4 = (bf16[4,512,128]{1,2,0:T(8,128)(2,1)S(1)}, bf16[4,512,128]{1,2,0:T(8,128)(2,1)}, u32[]{:S(2)}) copy-start(bf16[4,512,128]{1,2,0:T(8,128)(2,1)} %get-tuple-element.15) | copy-start | bytes 1572868
Sparse Core Ops, SparseCore 0:
  10.2 68.3 all-gather.2
  80.7 63.8 all-gather.4
  148.7 132.7 reduce-scatter.1
where the time goes:
time: 291 us; the launch traced here: 290 us
  waiting for transfers between devices  161 us (55%)
  matrix products  55.7 us (19%)
  local copies, waits for them, and re-layouts  53 us (18%)
  between operations  13.9 us (5%)
  other arithmetic  6.23 us (2%)
    reduce_scatter x1, waiting for transfers between devices, on_device(): lax.psum_scatter(partial_sum, 'gx', scatter_dimension=1, tiled=True)  87.2 us
    unnamed x27, local copies, waits for them, and re-layouts  51.6 us
    all_gather x1, waiting for transfers between devices, on_device(): lax.all_gather(out_grad, 'gx', axis=1, tiled=True)  36.3 us
    all_gather x1, waiting for transfers between devices, on_device(): lax.all_gather(inputs, 'gx', axis=1, tiled=True)  36 us
    dot_general x1, matrix products, on_device(): lax.dot_general(full_in, grad_qkv, (((0,), (0,)), ((), ())), preferred_el...  16.2 us
    dot_general x1, matrix products, on_device(): lax.dot_general(grad_qkv, w_flat, (((1,), (1,)), ((), ())), preferred_ele...  15.3 us
    dot_general x1, matrix products, attend_backward(): lax.dot_general(full_grad, w_out, (((1,), (1,)), ((), ())), preferred_ele...  8.18 us
    dot_general x1, matrix products, attend_backward(): lax.dot_general(attended.reshape(seq_len, columns), full_grad, (((0,), (0...  8.07 us
  transfers between devices with their start and end apart: 3, of which 3 were waited for; matrix products, arithmetic and copies ran while one was open for 39% of the time, Pallas kernels for 0%

commit v1 on v0

v1 whole, which is shorter than its diff:
```python
import functools
import math

import jax
import jax.numpy as jnp
from jax import lax
from jax.experimental import pallas as pl
from jax.experimental.pallas import tpu as pltpu
from jax.sharding import PartitionSpec as P

HD = 128
FACTOR = 1.0 / math.sqrt(HD)
MIB = 1 << 20
NT = (((1,), (1,)), ((), ()))
TN = (((0,), (0,)), ((), ()))


def dot(a, b, dims=(((1,), (0,)), ((), ()))):
    return lax.dot_general(a, b, dims, preferred_element_type=jnp.float32)


def params(mib):
    return pltpu.CompilerParams(vmem_limit_bytes=mib * MIB)


def cost(flops, nbytes, transcendentals=0):
    return pl.CostEstimate(flops=flops, bytes_accessed=nbytes, transcendentals=transcendentals)


def attend_kernel(col_ref, row_ref, qkv_ref, attn_ref, out_ref, out_t_ref):
    scores = dot(qkv_ref[0], qkv_ref[1], NT) * FACTOR
    scores = jnp.where(row_ref[...] <= col_ref[...], scores, -1e30)
    expd = jnp.exp(scores - jnp.max(scores, axis=1, keepdims=True))
    attn = (expd / jnp.sum(expd, axis=1, keepdims=True)).astype(jnp.bfloat16)
    attn_ref[0] = attn
    attended = dot(attn, qkv_ref[2])
    out_ref[...] = attended.astype(jnp.bfloat16)
    out_t_ref[...] = attended.T.astype(jnp.bfloat16)


def attend(positions, qkv):
    _, seq, columns = qkv.shape
    heads = columns // HD
    return pl.pallas_call(
        attend_kernel,
        grid=(heads,),
        in_specs=[
            pl.BlockSpec((seq, 1), lambda h: (0, 0)),
            pl.BlockSpec((1, seq), lambda h: (0, 0)),
            pl.BlockSpec((3, seq, HD), lambda h: (0, 0, h)),
        ],
        out_specs=[
            pl.BlockSpec((1, seq, seq), lambda h: (h, 0, 0)),
            pl.BlockSpec((seq, HD), lambda h: (0, h)),
            pl.BlockSpec((HD, seq), lambda h: (h, 0)),
        ],
        out_shape=[
            jax.ShapeDtypeStruct((heads, seq, seq), jnp.bfloat16),
            jax.ShapeDtypeStruct((seq, columns), jnp.bfloat16),
            jax.ShapeDtypeStruct((columns, seq), jnp.bfloat16),
        ],
        compiler_params=params(24),
        cost_estimate=cost(4 * seq * seq * columns, 5 * MIB, heads * seq * seq),
    )(positions[:, None], positions[None, :], qkv)


def attend_back_kernel(qkv_ref, attn_ref, attended_ref, grad_ref, out_ref):
    grad = grad_ref[...]
    attn = attn_ref[0]
    row_dot = jnp.sum(
        grad.astype(jnp.float32) * attended_ref[...].astype(jnp.float32), axis=1, keepdims=True
    )
    grad_attn = dot(grad, qkv_ref[2], NT)
    grad_scores = (attn.astype(jnp.float32) * (grad_attn - row_dot) * FACTOR).astype(jnp.bfloat16)
    out_ref[0] = dot(grad_scores, qkv_ref[1]).astype(jnp.bfloat16)
    out_ref[1] = dot(grad_scores, qkv_ref[0], TN).astype(jnp.bfloat16)
    out_ref[2] = dot(attn, grad, TN).astype(jnp.bfloat16)


def attend_back(qkv, attn, attended, grad):
    _, seq, columns = qkv.shape
    planes = pl.BlockSpec((3, seq, HD), lambda h: (0, 0, h))
    one = pl.BlockSpec((seq, HD), lambda h: (0, h))
    return pl.pallas_call(
        attend_back_kernel,
        grid=(columns // HD,),
        in_specs=[planes, pl.BlockSpec((1, seq, seq), lambda h: (h, 0, 0)), one, one],
        out_specs=planes,
        out_shape=jax.ShapeDtypeStruct(qkv.shape, jnp.bfloat16),
        compiler_params=params(24),
        cost_estimate=cost(8 * seq * seq * columns, 6 * MIB),
    )(qkv, attn, attended, grad)


def block_refs(refs):
    found = []
    for ref in refs:
        found += [ref] if len(ref.shape) == 2 else [ref.at[i] for i in range(ref.shape[0])]
    return found


def count_blocks(blocks):
    return sum(1 if b.ndim == 2 else b.shape[0] for b in blocks)


def features(index_ref, i, width):
    return pl.ds(pl.multiple_of(index_ref[i] * width, 128), width)


def grad_heads_kernel(index_ref, w_ref, *refs):
    *blocks, out_ref, total = refs
    for i, block in enumerate(block_refs(blocks)):
        width = block.shape[1]
        term = dot(block[...], w_ref[:, features(index_ref, i, width)], NT)
        if i == 0:
            total[...] = term
        else:
            total[...] += term
    out_ref[...] = total[...].astype(jnp.bfloat16)


def grad_heads(index, w_out, blocks):
    columns, width = w_out.shape
    seq = blocks[0].shape[-2]
    vmem = pl.BlockSpec(memory_space=pltpu.VMEM)
    return pl.pallas_call(
        grad_heads_kernel,
        in_specs=[pl.BlockSpec(memory_space=pltpu.SMEM)] + [vmem] * (1 + len(blocks)),
        out_specs=vmem,
        out_shape=jax.ShapeDtypeStruct((seq, columns), jnp.bfloat16),
        scratch_shapes=[pltpu.VMEM((seq, columns), jnp.float32)],
        compiler_params=params(32),
        cost_estimate=cost(2 * seq * columns * width, 13 * MIB),
    )(index, w_out, *blocks)


def weight_out_kernel(index_ref, left_ref, *refs):
    *blocks, out_ref, held, sems = refs
    copies = []
    for i, block in enumerate(block_refs(blocks)):
        width = block.shape[1]
        if i >= 2:
            copies[i - 2].wait()
        held[i % 2] = dot(left_ref[...], block[...]).astype(jnp.bfloat16)
        copy = pltpu.make_async_copy(
            held.at[i % 2], out_ref.at[:, features(index_ref, i, width)], sems.at[i % 2]
        )
        copy.start()
        copies.append(copy)
    for copy in copies[-2:]:
        copy.wait()


def weight_out(index, attended_t, blocks):
    columns, seq = attended_t.shape
    part = blocks[0].shape[-1]
    width = part * count_blocks(blocks)
    vmem = pl.BlockSpec(memory_space=pltpu.VMEM)
    return pl.pallas_call(
        weight_out_kernel,
        in_specs=[pl.BlockSpec(memory_space=pltpu.SMEM)] + [vmem] * (1 + len(blocks)),
        out_specs=pl.BlockSpec(memory_space=pl.ANY),
        out_shape=jax.ShapeDtypeStruct((columns, width), jnp.bfloat16),
        scratch_shapes=[pltpu.VMEM((2, columns, part), jnp.bfloat16), pltpu.SemaphoreType.DMA((2,))],
        compiler_params=params(24),
        cost_estimate=cost(2 * seq * columns * width, 13 * MIB),
    )(index, attended_t, *blocks)


def weight_qkv_kernel(index_ref, grad_ref, *refs):
    *blocks, out_ref, held, sems = refs
    copies = []
    for i, block in enumerate(block_refs(blocks)):
        width = block.shape[1]
        if i >= 2:
            copies[i - 2].wait()
        turned = block[...].T
        for slot in range(3):
            held[i % 2, slot] = dot(turned, grad_ref[slot]).astype(jnp.bfloat16)
        copy = pltpu.make_async_copy(
            held.at[i % 2], out_ref.at[:, features(index_ref, i, width)], sems.at[i % 2]
        )
        copy.start()
        copies.append(copy)
    for copy in copies[-2:]:
        copy.wait()


def weight_qkv(index, grad, blocks):
    _, seq, columns = grad.shape
    part = blocks[0].shape[-1]
    width = part * count_blocks(blocks)
    vmem = pl.BlockSpec(memory_space=pltpu.VMEM)
    return pl.pallas_call(
        weight_qkv_kernel,
        in_specs=[pl.BlockSpec(memory_space=pltpu.SMEM)] + [vmem] * (1 + len(blocks)),
        out_specs=pl.BlockSpec(memory_space=pl.ANY),
        out_shape=jax.ShapeDtypeStruct((3, width, columns), jnp.bfloat16),
        scratch_shapes=[
            pltpu.VMEM((2, 3, part, columns), jnp.bfloat16),
            pltpu.SemaphoreType.DMA((2,)),
        ],
        compiler_params=params(32),
        cost_estimate=cost(6 * seq * columns * width, 26 * MIB),
    )(index, grad, *blocks)


def terms_kernel(index_ref, grad_ref, w_ref, out_ref):
    total = dot(grad_ref[0], w_ref[0], NT)
    total += dot(grad_ref[1], w_ref[1], NT)
    total += dot(grad_ref[2], w_ref[2], NT)
    out_ref[0] = total.astype(jnp.bfloat16)


def terms(index, grad, w, part):
    _, seq, columns = grad.shape
    count = index.shape[0]
    return pl.pallas_call(
        terms_kernel,
        grid_spec=pltpu.PrefetchScalarGridSpec(
            num_scalar_prefetch=1,
            grid=(count,),
            in_specs=[
                pl.BlockSpec((3, seq, columns), lambda i, index: (0, 0, 0)),
                pl.BlockSpec((3, part, columns), lambda i, index: (0, index[i], 0)),
            ],
            out_specs=pl.BlockSpec((1, seq, part), lambda i, index: (i, 0, 0)),
        ),
        out_shape=jax.ShapeDtypeStruct((count, seq, part), jnp.bfloat16),
        compiler_params=params(24),
        cost_estimate=cost(6 * seq * columns * part * count, 2 * MIB * count),
    )(index, grad, w)


def plain(n, inputs, out_grad, w_qkv, w_out, saved_qkv, positions):
    full_in = lax.all_gather(inputs, "gx", axis=1, tiled=True)
    full_grad = lax.all_gather(out_grad, "gx", axis=1, tiled=True)
    qkv = saved_qkv.transpose(1, 0, 2)
    attn, attended, _ = attend(positions, qkv)
    grad_h = dot(full_grad, w_out, NT).astype(jnp.bfloat16)
    grad_w_out = dot(attended, full_grad, TN).astype(jnp.bfloat16)
    grad = attend_back(qkv, attn, attended, grad_h)
    grad_w_qkv = jnp.stack([dot(full_in, grad[k], TN).astype(jnp.bfloat16) for k in range(3)], 1)
    partial = sum(dot(grad[k], w_qkv[:, k], NT) for k in range(3))
    input_grad = lax.psum_scatter(partial, "gx", scatter_dimension=1, tiled=True)
    return input_grad.astype(jnp.bfloat16), grad_w_qkv, grad_w_out


def on_device(n, inputs, out_grad, w_qkv, w_out, saved_qkv, positions):
    part = inputs.shape[1]
    if part % 128:
        return plain(n, inputs, out_grad, w_qkv, w_out, saved_qkv, positions)
    same_core = [list(range(core, n, 2)) for core in range(2)]
    swap = [(i, i ^ 1) for i in range(n)]
    core = lax.axis_index("gx") % 2
    evens = jnp.arange(0, n, 2, dtype=jnp.int32)
    index = jnp.concatenate([evens + core, evens + 1 - core])

    def gathered(x):
        mine = lax.all_gather(x, "gx", axis=0, axis_index_groups=same_core)
        return mine, lax.ppermute(mine, "gx", swap)

    grad_blocks = gathered(out_grad)
    in_blocks = gathered(inputs)
    qkv = saved_qkv.transpose(1, 0, 2)
    w = w_qkv.transpose(1, 0, 2)
    attn, attended, attended_t = attend(positions, qkv)
    grad_h = grad_heads(index, w_out, grad_blocks)
    grad = attend_back(qkv, attn, attended, grad_h)
    theirs = terms(index[n // 2 :], grad, w, part)
    mine = terms(index[: n // 2], grad, w, part)
    both = mine + lax.ppermute(theirs, "gx", swap)
    input_grad = lax.psum_scatter(
        both, "gx", scatter_dimension=0, axis_index_groups=same_core, tiled=False
    )
    grad_w_qkv = weight_qkv(index, grad, in_blocks).transpose(1, 0, 2)
    grad_w_out = weight_out(index, attended_t, grad_blocks)
    return input_grad.astype(jnp.bfloat16), grad_w_qkv, grad_w_out


def solution(mesh):
    placed = (
        P("runs", "gx"),
        P("runs", "gx"),
        P(None, None, "gx"),
        P("gx", None),
        P("runs", None, "gx"),
        P("runs"),
    )
    return jax.shard_map(
        functools.partial(on_device, mesh.shape["gx"]),
        mesh=mesh,
        in_specs=placed,
        out_specs=(P("runs", "gx"), P("runs", None, "gx"), P(("runs", "gx"), None)),
        check_vma=False,
    )
```

time: 291 us -> 219 us (0.75)
  Pallas kernels: 0 us -> 59 us
  matrix products: 55.7 us -> 0 us
  waiting for transfers between devices: 161 us -> 117 us
  local copies, waits for them, and re-layouts: 53 us -> 25.1 us
  other arithmetic: 6.23 us -> 2.56 us
    pallas_call x0 -> x7, Pallas kernels: none -> 59 us  [the longest x2 18.7 us: terms(): pl.pallas_call(terms_kernel, grid_spec=pltpu.PrefetchScalarGridSpec(num_s...]
    dot_general x9 -> x0, matrix products: 52 us -> none  [the longest x1 16.2 us: on_device(): lax.dot_general(full_in, grad_qkv, (((0,), (0,)), ((), ())), preferred_el...]
    reduce_scatter x1, waiting for transfers between devices: 87.2 us -> 47 us  [on_device(): lax.psum_scatter(both, 'gx', scatter_dimension=0, axis_index_groups=same_...]
    unnamed x27 -> x26, local copies, waits for them, and re-layouts: 51.6 us -> 24.2 us
    convert_element_type x2 -> x0, other arithmetic: 4.7 us -> none  [the longest x1 2.78 us: attend_backward(): attn_b = attn.astype(jnp.bfloat16)]
    sub x1 -> x0, matrix products: 3.73 us -> none  [attend_backward(): expd = jnp.exp(scores - highest)]
  transfers between devices with their start and end apart: 3 -> 6, of which waited for: 3 -> 3; matrix products, arithmetic and copies ran while one was open for 39% -> 2% of each run, Pallas kernels for 0% -> 27%
where the time goes in v1:
time: 219 us; the launch traced here: 218 us
  waiting for transfers between devices  117 us (53%)
  Pallas kernels  59 us (27%)
  local copies, waits for them, and re-layouts  25.1 us (11%)
  between operations  13.9 us (6%)
  other arithmetic  2.56 us (1%)
    all_gather x2, waiting for transfers between devices, gathered(): mine = lax.all_gather(x, 'gx', axis=0, axis_index_groups=same_core)  69.5 us
    reduce_scatter x1, waiting for transfers between devices, on_device(): lax.psum_scatter(both, 'gx', scatter_dimension=0, axis_index_groups=same_...  47 us
    unnamed x26, local copies, waits for them, and re-layouts  24.2 us
    pallas_call x2, Pallas kernels, terms(): pl.pallas_call(terms_kernel, grid_spec=pltpu.PrefetchScalarGridSpec(num_s...  18.7 us
    pallas_call x1, Pallas kernels, weight_qkv(): pl.pallas_call(weight_qkv_kernel, in_specs=[pl.BlockSpec(memory_space=plt...  15.9 us
    pallas_call x1, Pallas kernels, weight_out(): pl.pallas_call(weight_out_kernel, in_specs=[pl.BlockSpec(memory_space=plt...  10.5 us
    pallas_call x1, Pallas kernels, grad_heads(): pl.pallas_call(grad_heads_kernel, in_specs=[pl.BlockSpec(memory_space=plt...  5.07 us
    pallas_call x1, Pallas kernels, attend(): pl.pallas_call(attend_kernel, grid=(heads,), in_specs=[pl.BlockSpec((seq,...  4.84 us
  transfers between devices with their start and end apart: 6, of which 3 were waited for; matrix products, arithmetic and copies ran while one was open for 2% of the time, Pallas kernels for 27%

profile of v1, /device:TPU:0, one launch (start us, length us, event | category | flops | bytes accessed | tf_op | source)
XLA Modules:
  0.0 218.4 jit_solution(16759841257758449810)
XLA Ops:
  7.2 0.7 all-gather.5.cloned.1.call-update
  7.9 65.4 %all-gather.5.cloned.1.call-done = bf16[4096,384]{1,0:T(8,128)(2,1)} async-done(((bf16[512,384]{1,0:T(8,128)(2,1)}), bf16[4096,384]{1,0:T(8,128)(2,1)}) %all-gather.5.cloned.1.call-update) | async-done | bytes 3145744 | tf_op jit(solution)/shard_map/all_gather | solution.py:260
  73.4 0.8 copy.9.col_ref
  74.3 1.4 copy-done.7
  75.7 0.7 copy-done.11
  76.4 4.8 %shard_map.85 = (bf16[4,512,512]{2,1,0:T(8,128)(2,1)S(1)}, bf16[512,512]{1,0:T(8,128)(2,1)S(1)}, bf16[512,512]{1,0:T(8,128)(2,1)S(1)}) custom-call(s32[512,1]{1,0:T(8,128)S(1)} %copy.9.col_ref, s32[1,512]{1,0:T(1,128)S(1)} %bitcast.16, bf16[3,512,512]{2,1,0:T(8,128)(2,1)S(1)} %bitcast.13), custom_call_target="tpu_custom_call" | custom-call | flops 536870912 | bytes 5242880 | tf_op jit(solution)/shard_map/pallas_call | solution.py:44
  81.2 0.8 copy-done.9
  82.0 0.1 pad_add_fusion.index_ref
  82.1 2.0 copy-done.2
  84.1 2.8 %copy-done.6 = bf16[512,6144]{1,0:T(8,128)(2,1)S(1)} copy-done((bf16[512,6144]{1,0:T(8,128)(2,1)S(1)}, bf16[512,6144]{1,0:T(8,128)(2,1)}, u32[]{:S(2)}) %copy-start.6) | copy-done | bytes 6291480
  86.9 5.1 %shard_map.86.grad_ref = bf16[512,512]{1,0:T(8,128)(2,1)S(1)} custom-call(s32[16]{0:T(128)S(1)} %pad_add_fusion.index_ref, bf16[512,6144]{1,0:T(8,128)(2,1)S(1)} %copy-done.6, bf16[8,512,384]{2,1,0:T(8,128)(2,1)S(1)} %bitcast.11, bf16[8,512,384]{2,1,0:T(8,128)(2,1)S(1)} %collective-permute-done.refs_1_), custom_call_target="tpu_custom_call" | custom-call | flops 3221225472 | bytes 13631488 | tf_op jit(solution)/shard_map/pallas_call | solution.py:126
  92.0 4.0 %shard_map.87.grad_ref = bf16[3,512,512]{2,1,0:T(8,128)(2,1)S(1)} custom-call(bf16[3,512,512]{2,1,0:T(8,128)(2,1)S(1)} %bitcast.14, bf16[4,512,512]{2,1,0:T(8,128)(2,1)S(1)} %get-tuple-element.6.attn_ref, bf16[512,512]{1,0:T(8,128)(2,1)S(1)} %get-tuple-element.7.attended_ref, bf16[512,512]{1,0:T(8,128)(2,1)S(1)} %shard_map.86.grad_ref), custom_call_target="tpu_custom_call" | custom-call | flops 1073741824 | bytes 6291456 | tf_op jit(solution)/shard_map/pallas_call | solution.py:84
  96.1 6.4 %copy-done = bf16[6144,3,512]{2,0,1:T(8,128)(2,1)S(1)} copy-done((bf16[6144,3,512]{2,0,1:T(8,128)(2,1)S(1)}, bf16[6144,3,512]{2,0,1:T(8,128)(2,1)}, u32[]{:S(2)}) %copy-start) | copy-done | bytes 18874392
  102.4 9.3 %shard_map.89 = bf16[8,512,384]{2,1,0:T(8,128)(2,1)S(1)} custom-call(s32[8]{0:T(128)S(1)} %get-tuple-element.9.index_ref, bf16[3,512,512]{2,1,0:T(8,128)(2,1)S(1)} %shard_map.87.grad_ref, bf16[3,6144,512]{2,1,0:T(8,128)(2,1)S(1)} %bitcast.8), custom_call_target="tpu_custom_call" | custom-call | flops 4831838208 | bytes 16777216 | tf_op jit(solution)/shard_map/pallas_call | solution.py:218
  111.7 0.6 collective-permute-start.1
  112.3 6.4 %copy-done.1 = bf16[6144,3,512]{2,0,1:T(8,128)(2,1)S(1)} copy-done((bf16[6144,3,512]{2,0,1:T(8,128)(2,1)S(1)}, bf16[6144,3,512]{2,0,1:T(8,128)(2,1)}, u32[]{:S(2)}) %copy-start.1) | copy-done | bytes 18874392
  118.7 9.4 %shard_map.88 = bf16[8,512,384]{2,1,0:T(8,128)(2,1)S(1)} custom-call(s32[8]{0:T(128)S(1)} %get-tuple-element.10.index_ref, bf16[3,512,512]{2,1,0:T(8,128)(2,1)S(1)} %shard_map.87.grad_ref, bf16[3,6144,512]{2,1,0:T(8,128)(2,1)S(1)} %bitcast.9), custom_call_target="tpu_custom_call" | custom-call | flops 4831838208 | bytes 16777216 | tf_op jit(solution)/shard_map/pallas_call | solution.py:218
  128.1 2.5 %add.22 = bf16[8,512,384]{2,1,0:T(8,128)(2,1)} add(bf16[8,512,384]{2,1,0:T(8,128)(2,1)S(1)} %shard_map.88, bf16[8,512,384]{2,1,0:T(8,128)(2,1)S(1)} %collective-permute-done.1) | non-fusion elementwise | flops 1572864 | bytes 9437184 | tf_op jit(solution)/shard_map/add | solution.py:272
  130.6 4.1 %all-gather.7.cloned.1.call-done = bf16[4096,384]{1,0:T(8,128)(2,1)} async-done(((bf16[512,384]{1,0:T(8,128)(2,1)}), bf16[4096,384]{1,0:T(8,128)(2,1)}) %all-gather.7.cloned.1.call-update) | async-done | bytes 3145744 | tf_op jit(solution)/shard_map/all_gather | solution.py:260
  134.7 1.9 copy-done.3
  136.6 1.9 copy-done.5
  138.5 10.5 %shard_map.91 = bf16[512,6144]{1,0:T(8,128)(2,1)} custom-call(s32[16]{0:T(128)S(1)} %pad_add_fusion.index_ref, bf16[512,512]{1,0:T(8,128)(2,1)S(1)} %copy-done.10, bf16[8,512,384]{2,1,0:T(8,128)(2,1)S(1)} %bitcast.12, bf16[8,512,384]{2,1,0:T(8,128)(2,1)S(1)} %copy-done.5), custom_call_target="tpu_custom_call" | custom-call | flops 3221225472 | bytes 13631488 | tf_op jit(solution)/shard_map/pallas_call | solution.py:159
  149.0 15.9 %shard_map.90 = bf16[3,6144,512]{2,1,0:T(8,128)(2,1)} custom-call(s32[16]{0:T(128)S(1)} %pad_add_fusion.index_ref, bf16[3,512,512]{2,1,0:T(8,128)(2,1)S(1)} %shard_map.87.grad_ref, bf16[8,512,384]{2,1,0:T(8,128)(2,1)S(1)} %bitcast.18, bf16[8,512,384]{2,1,0:T(8,128)(2,1)S(1)} %collective-permute-done.2.refs_1_), custom_call_target="tpu_custom_call" | custom-call | flops 9663676416 | bytes 27262976 | tf_op jit(solution)/shard_map/pallas_call | solution.py:194
  164.8 47.0 %reduce-scatter.2.cloned.1.call-done = bf16[1,512,384]{2,1,0:T(8,128)(2,1)} async-done(((bf16[8,512,384]{2,1,0:T(8,128)(2,1)}), bf16[1,512,384]{2,1,0:T(8,128)(2,1)}) %reduce-scatter.2.cloned.1.call-update) | async-done | bytes 393232 | tf_op jit(solution)/shard_map/reduce_scatter | solution.py:273
  (28 shorter events, 0.2 us)
Async XLA Ops:
  7.2 66.2 %all-gather.5.cloned.1.call-start = ((), (), s32[]{:S(2)}) async-start(), calls=%async_computation.2 | async-start | bytes 3538944 | tf_op jit(solution)/shard_map/all_gather | solution.py:260
  7.9 126.8 %all-gather.7.cloned.1.call-start = ((), (), s32[]{:S(2)}) async-start(), calls=%async_computation.3 | async-start | bytes 3538944 | tf_op jit(solution)/shard_map/all_gather | solution.py:260
  73.4 8.7 %collective-permute-start = (bf16[8,512,384]{2,1,0:T(8,128)(2,1)}, bf16[8,512,384]{2,1,0:T(8,128)(2,1)S(1)}, u32[]{:S(2)}, u32[]{:S(2)}) collective-permute-start(bf16[8,512,384]{2,1,0:T(8,128)(2,1)} %bitcast.10), channel_id=1, source_target_pairs={{0,1},{1,0},{2,3},{3,2},{4,5},{5,4},{6,7},{7,6},{8,9},{9,8},{10,11... | collective-permute-start | bytes 9437192 | tf_op jit(solution)/shard_map/ppermute | solution.py:261
  73.4 138.4 %reduce-scatter.2.cloned.1.call-start = ((), (), s32[]{:S(2)}) async-start(), calls=%async_computation.1 | async-start | bytes 3538944 | tf_op jit(solution)/shard_map/reduce_scatter | solution.py:273
  74.3 1.4 copy-start.7
  75.7 0.7 copy-start.11
  81.2 0.8 copy-start.9
  82.1 2.0 copy-start.2
  84.1 2.8 %copy-start.6 = (bf16[512,6144]{1,0:T(8,128)(2,1)S(1)}, bf16[512,6144]{1,0:T(8,128)(2,1)}, u32[]{:S(2)}) copy-start(bf16[512,6144]{1,0:T(8,128)(2,1)} %w_ref.1) | copy-start | bytes 18874372
  86.9 5.1 %copy-start.4 = (bf16[8,512,384]{2,1,0:T(8,128)(2,1)}, bf16[8,512,384]{2,1,0:T(8,128)(2,1)S(1)}, u32[]{:S(2)}) copy-start(bf16[8,512,384]{2,1,0:T(8,128)(2,1)S(1)} %collective-permute-done.refs_1_) | copy-start | bytes 9437188
  86.9 5.1 %copy-start.8 = (bf16[512,3,512]{2,0,1:T(8,128)(2,1)S(1)}, bf16[512,3,512]{2,0,1:T(8,128)(2,1)}, u32[]{:S(2)}) copy-start(bf16[512,3,512]{2,0,1:T(8,128)(2,1)} %param.10) | copy-start | bytes 4718596
  96.1 6.4 %copy-start = (bf16[6144,3,512]{2,0,1:T(8,128)(2,1)S(1)}, bf16[6144,3,512]{2,0,1:T(8,128)(2,1)}, u32[]{:S(2)}) copy-start(bf16[6144,3,512]{2,0,1:T(8,128)(2,1)} %param.8) | copy-start | bytes 56623108
  111.7 16.4 %collective-permute-start.1 = (bf16[8,512,384]{2,1,0:T(8,128)(2,1)S(1)}, bf16[8,512,384]{2,1,0:T(8,128)(2,1)S(1)}, u32[]{:S(2)}, u32[]{:S(2)}) collective-permute-start(bf16[8,512,384]{2,1,0:T(8,128)(2,1)S(1)} %shard_map.89), channel_id=1, source_target_pairs={{0,1},{1,0},{2,3},{3,2},{4,5},{5,4},{6,7},{7,6},{8,9},{9,8},{10,11... | collective-permute-start | bytes 9437192 | tf_op jit(solution)/shard_map/ppermute | solution.py:272
  112.3 6.4 %copy-start.1 = (bf16[6144,3,512]{2,0,1:T(8,128)(2,1)S(1)}, bf16[6144,3,512]{2,0,1:T(8,128)(2,1)}, u32[]{:S(2)}) copy-start(bf16[6144,3,512]{2,0,1:T(8,128)(2,1)} %param.8) | copy-start | bytes 56623108
  130.6 4.1 %copy-start.10 = (bf16[512,512]{1,0:T(8,128)(2,1)S(1)}, bf16[512,512]{1,0:T(8,128)(2,1)}, u32[]{:S(2)}) copy-start(bf16[512,512]{1,0:T(8,128)(2,1)} %copy-done.9) | copy-start | bytes 1572868
  134.7 14.3 %collective-permute-start.2 = (bf16[8,512,384]{2,1,0:T(8,128)(2,1)}, bf16[8,512,384]{2,1,0:T(8,128)(2,1)S(1)}, u32[]{:S(2)}, u32[]{:S(2)}) collective-permute-start(bf16[8,512,384]{2,1,0:T(8,128)(2,1)} %bitcast.17), channel_id=1, source_target_pairs={{0,1},{1,0},{2,3},{3,2},{4,5},{5,4},{6,7},{7,6},{8,9},{9,8},{10,11... | collective-permute-start | bytes 9437192 | tf_op jit(solution)/shard_map/ppermute | solution.py:261
  134.7 1.9 copy-start.3
  136.6 1.9 copy-start.5
  138.5 10.5 %copy-start.12 = (bf16[4096,384]{1,0:T(8,128)(2,1)S(1)}, bf16[4096,384]{1,0:T(8,128)(2,1)}, u32[]{:S(2)}) copy-start(bf16[4096,384]{1,0:T(8,128)(2,1)} %all-gather.7.cloned.1.call-done) | copy-start | bytes 9437188
Sparse Core Ops, SparseCore 0:
  10.2 63.1 all-gather.4
  75.5 59.0 all-gather.6
  138.8 72.9 reduce-scatter.1

commit v2 on v1

v2 whole, which is shorter than its diff:
```python
import functools
import math

import jax
import jax.numpy as jnp
from jax import lax
from jax.experimental import pallas as pl
from jax.experimental.pallas import tpu as pltpu
from jax.sharding import PartitionSpec as P

HD = 128
FACTOR = 1.0 / math.sqrt(HD)
MIB = 1 << 20
NT = (((1,), (1,)), ((), ()))
TN = (((0,), (0,)), ((), ()))


def dot(a, b, dims=(((1,), (0,)), ((), ()))):
    return lax.dot_general(a, b, dims, preferred_element_type=jnp.float32)


def params(mib):
    return pltpu.CompilerParams(vmem_limit_bytes=mib * MIB)


def cost(flops, nbytes, transcendentals=0):
    return pl.CostEstimate(flops=flops, bytes_accessed=nbytes, transcendentals=transcendentals)


def attend_kernel(col_ref, row_ref, qkv_ref, attn_ref, out_ref, out_t_ref):
    scores = dot(qkv_ref[0], qkv_ref[1], NT) * FACTOR
    scores = jnp.where(row_ref[...] <= col_ref[...], scores, -1e30)
    expd = jnp.exp(scores - jnp.max(scores, axis=1, keepdims=True))
    attn = (expd / jnp.sum(expd, axis=1, keepdims=True)).astype(jnp.bfloat16)
    attn_ref[0] = attn
    attended = dot(attn, qkv_ref[2])
    out_ref[...] = attended.astype(jnp.bfloat16)
    out_t_ref[...] = attended.T.astype(jnp.bfloat16)


def attend(positions, qkv):
    _, seq, columns = qkv.shape
    heads = columns // HD
    return pl.pallas_call(
        attend_kernel,
        grid=(heads,),
        in_specs=[
            pl.BlockSpec((seq, 1), lambda h: (0, 0)),
            pl.BlockSpec((1, seq), lambda h: (0, 0)),
            pl.BlockSpec((3, seq, HD), lambda h: (0, 0, h)),
        ],
        out_specs=[
            pl.BlockSpec((1, seq, seq), lambda h: (h, 0, 0)),
            pl.BlockSpec((seq, HD), lambda h: (0, h)),
            pl.BlockSpec((HD, seq), lambda h: (h, 0)),
        ],
        out_shape=[
            jax.ShapeDtypeStruct((heads, seq, seq), jnp.bfloat16),
            jax.ShapeDtypeStruct((seq, columns), jnp.bfloat16),
            jax.ShapeDtypeStruct((columns, seq), jnp.bfloat16),
        ],
        compiler_params=params(24),
        cost_estimate=cost(4 * seq * seq * columns, 5 * MIB, heads * seq * seq),
    )(positions[:, None], positions[None, :], qkv)


def attend_back_kernel(qkv_ref, attn_ref, attended_ref, grad_ref, out_ref):
    grad = grad_ref[...]
    attn = attn_ref[0]
    row_dot = jnp.sum(
        grad.astype(jnp.float32) * attended_ref[...].astype(jnp.float32), axis=1, keepdims=True
    )
    grad_attn = dot(grad, qkv_ref[2], NT)
    grad_scores = (attn.astype(jnp.float32) * (grad_attn - row_dot) * FACTOR).astype(jnp.bfloat16)
    out_ref[0] = dot(grad_scores, qkv_ref[1]).astype(jnp.bfloat16)
    out_ref[1] = dot(grad_scores, qkv_ref[0], TN).astype(jnp.bfloat16)
    out_ref[2] = dot(attn, grad, TN).astype(jnp.bfloat16)


def attend_back(qkv, attn, attended, grad):
    _, seq, columns = qkv.shape
    planes = pl.BlockSpec((3, seq, HD), lambda h: (0, 0, h))
    one = pl.BlockSpec((seq, HD), lambda h: (0, h))
    return pl.pallas_call(
        attend_back_kernel,
        grid=(columns // HD,),
        in_specs=[planes, pl.BlockSpec((1, seq, seq), lambda h: (h, 0, 0)), one, one],
        out_specs=planes,
        out_shape=jax.ShapeDtypeStruct(qkv.shape, jnp.bfloat16),
        compiler_params=params(24),
        cost_estimate=cost(8 * seq * seq * columns, 6 * MIB),
    )(qkv, attn, attended, grad)


def features(index_ref, i, width):
    return pl.ds(pl.multiple_of(index_ref[i] * width, 128), width)


def grad_heads_kernel(count, first, last, index_ref, *refs):
    blocks, weights, rest = refs[:count], refs[count : 2 * count], refs[2 * count :]
    total = None if first else rest[0][...]
    for block, weight in zip(blocks, weights):
        term = dot(block[...], weight[...], NT)
        total = term if total is None else total + term
    rest[-1][...] = total.astype(jnp.bfloat16) if last else total


def grad_heads(index, w_out, blocks, total=None, last=False):
    columns = w_out.shape[0]
    seq, part = blocks[0].shape
    count = len(blocks)

    def weight(i):
        return pl.BlockSpec((columns, part), lambda step, index: (0, index[i]))

    block = pl.BlockSpec((seq, part), lambda step, index: (0, 0))
    whole = pl.BlockSpec((seq, columns), lambda step, index: (0, 0))
    first = total is None
    return pl.pallas_call(
        functools.partial(grad_heads_kernel, count, first, last),
        grid_spec=pltpu.PrefetchScalarGridSpec(
            num_scalar_prefetch=1,
            grid=(1,),
            in_specs=[block] * count + [weight(i) for i in range(count)] + [whole] * (not first),
            out_specs=whole,
        ),
        out_shape=jax.ShapeDtypeStruct((seq, columns), jnp.bfloat16 if last else jnp.float32),
        compiler_params=params(40),
        cost_estimate=cost(2 * seq * columns * part * count, MIB * count),
    )(index, *blocks, *[w_out] * count, *([] if first else [total]))


SLOTS = 4


def weight_kernel(count, turn, index_ref, left_ref, *refs):
    blocks, (out_ref, held, sems) = refs[:count], refs[-3:]
    copies = []
    for i, block in enumerate(blocks):
        width = block.shape[1]
        slot = i % SLOTS
        if i >= SLOTS:
            copies[i - SLOTS].wait()
        if turn:
            turned = block[...].T
            for k in range(3):
                held[slot, k] = dot(turned, left_ref[k]).astype(jnp.bfloat16)
        else:
            held[slot] = dot(left_ref[...], block[...]).astype(jnp.bfloat16)
        copy = pltpu.make_async_copy(
            held.at[slot], out_ref.at[:, features(index_ref, i, width)], sems.at[slot]
        )
        copy.start()
        copies.append(copy)
    for copy in copies[-SLOTS:]:
        copy.wait()


def weight_grad(index, left, blocks, shape, into=None):
    turn = left.ndim == 3
    seq, part = blocks[0].shape
    count = len(blocks)
    held = (3, part, left.shape[2]) if turn else (left.shape[0], part)
    vmem = pl.BlockSpec(memory_space=pltpu.VMEM)
    rest = pl.BlockSpec(memory_space=pl.ANY)
    size = math.prod(held)
    return pl.pallas_call(
        functools.partial(weight_kernel, count, turn),
        in_specs=[pl.BlockSpec(memory_space=pltpu.SMEM)]
        + [vmem] * (1 + count)
        + [rest] * (into is not None),
        out_specs=rest,
        out_shape=jax.ShapeDtypeStruct(shape, jnp.bfloat16),
        scratch_shapes=[
            pltpu.VMEM((SLOTS, *held), jnp.bfloat16),
            pltpu.SemaphoreType.DMA((SLOTS,)),
        ],
        input_output_aliases={} if into is None else {2 + count: 0},
        compiler_params=params(40),
        cost_estimate=cost(2 * seq * size * count, 3 * size * count),
    )(index, left, *blocks, *([] if into is None else [into]))


def terms_kernel(index_ref, core_ref, grad_ref, w_ref, theirs_ref, mine_ref):
    total = dot(grad_ref[0], w_ref[0], NT)
    total += dot(grad_ref[1], w_ref[1], NT)
    total += dot(grad_ref[2], w_ref[2], NT)
    total = total.astype(jnp.bfloat16)
    part = total.shape[1] // 2

    @pl.when(core_ref[0] == 0)
    def _():
        mine_ref[0] = total[:, :part]
        theirs_ref[0] = total[:, part:]

    @pl.when(core_ref[0] == 1)
    def _():
        mine_ref[0] = total[:, part:]
        theirs_ref[0] = total[:, :part]


def terms(chips, core, grad, w, part):
    _, seq, columns = grad.shape
    count = chips.shape[0]
    out = pl.BlockSpec((1, seq, part), lambda i, chips, core: (i, 0, 0))
    shape = jax.ShapeDtypeStruct((count, seq, part), jnp.bfloat16)
    return pl.pallas_call(
        terms_kernel,
        grid_spec=pltpu.PrefetchScalarGridSpec(
            num_scalar_prefetch=2,
            grid=(count,),
            in_specs=[
                pl.BlockSpec((3, seq, columns), lambda i, chips, core: (0, 0, 0)),
                pl.BlockSpec((3, 2 * part, columns), lambda i, chips, core: (0, chips[i], 0)),
            ],
            out_specs=[out, out],
        ),
        out_shape=[shape, shape],
        compiler_params=params(48),
        cost_estimate=cost(12 * seq * columns * part * count, 5 * MIB * count),
    )(chips, core, grad, w)


def plain(n, inputs, out_grad, w_qkv, w_out, saved_qkv, positions):
    full_in = lax.all_gather(inputs, "gx", axis=1, tiled=True)
    full_grad = lax.all_gather(out_grad, "gx", axis=1, tiled=True)
    qkv = saved_qkv.transpose(1, 0, 2)
    attn, attended, _ = attend(positions, qkv)
    grad_h = dot(full_grad, w_out, NT).astype(jnp.bfloat16)
    grad_w_out = dot(attended, full_grad, TN).astype(jnp.bfloat16)
    grad = attend_back(qkv, attn, attended, grad_h)
    grad_w_qkv = jnp.stack([dot(full_in, grad[k], TN).astype(jnp.bfloat16) for k in range(3)], 1)
    partial = sum(dot(grad[k], w_qkv[:, k], NT) for k in range(3))
    input_grad = lax.psum_scatter(partial, "gx", scatter_dimension=1, tiled=True)
    return input_grad.astype(jnp.bfloat16), grad_w_qkv, grad_w_out


def ring_order(chips):
    if chips == 8:
        return [0, 2, 4, 6, 7, 5, 3, 1]
    return list(range(chips))


def on_device(n, inputs, out_grad, w_qkv, w_out, saved_qkv, positions):
    seq, part = inputs.shape
    if part % 128 or n != 16:
        return plain(n, inputs, out_grad, w_qkv, w_out, saved_qkv, positions)
    chips, half = n // 2, seq // 2
    far = chips // 2
    order = ring_order(chips)
    after = {order[i]: order[(i + 1) % chips] for i in range(chips)}
    ahead = [(2 * c + k, 2 * after[c] + k) for c in order for k in range(2)]
    back = [(j, i) for i, j in ahead]
    swap = [(i, i ^ 1) for i in range(n)]
    here = [[order[(order.index(i // 2) + k) % chips] for k in range(chips)] for i in range(n)]

    me = lax.axis_index("gx")
    core = me % 2
    chip_at = lax.dynamic_slice(jnp.array(here, jnp.int32), (me, 0), (1, chips))[0]
    core_ref = core.astype(jnp.int32)[None]

    def send(x, perm):
        return lax.ppermute(x, "gx", perm)

    def index_of(offsets):
        at = jnp.stack([chip_at[k % chips] for k in offsets])
        return jnp.concatenate([2 * at + core, 2 * at + 1 - core]).astype(jnp.int32)

    def gathered(x):
        parts = [((0,), [x, send(x, swap)])]
        right = left = x
        for step in range(1, far):
            right, left = send(right, ahead), send(left, back)
            parts.append(((-step, step), [right, left, send(right, swap), send(left, swap)]))
        last = jnp.concatenate([send(right[:half], ahead), send(left[half:], back)])
        parts.append(((far,), [last, send(last, swap)]))
        return parts

    qkv = saved_qkv.transpose(1, 0, 2)
    w = w_qkv.transpose(1, 0, 2)
    grad_parts = gathered(out_grad)
    inputs, _ = lax.optimization_barrier((inputs, grad_parts[far - 1][1][:2]))
    in_parts = gathered(inputs)

    attn, attended, attended_t = attend(positions, qkv)

    def joined(parts):
        offsets = [k for ks, _ in parts for k in ks]
        own = [b for ks, bs in parts for b in bs[: len(ks)]]
        other = [b for ks, bs in parts for b in bs[len(ks) :]]
        return index_of(offsets), own + other

    grad_h = None
    for some in (grad_parts[:2], grad_parts[2:3], grad_parts[3:4], grad_parts[4:]):
        index, blocks = joined(some)
        grad_h = grad_heads(index, w_out, blocks, grad_h, some[-1][0] == (far,))
    grad = attend_back(qkv, attn, attended, grad_h)

    def summed(offsets):
        at = jnp.stack([chip_at[k % chips] for k in offsets]).astype(jnp.int32)
        theirs, mine = terms(at, core_ref, grad, w, part)
        return mine.astype(jnp.float32) + send(theirs, swap).astype(jnp.float32)

    low = summed((far,))[0].astype(jnp.bfloat16)
    right, left = send(low[:half], ahead), send(low[half:], back)
    for step in range(far - 1, 0, -1):
        total = summed((step, -step))
        if step == far - 1:
            right = jnp.pad(right, ((0, half), (0, 0)))
            left = jnp.pad(left, ((half, 0), (0, 0)))
        right = send((total[0] + right.astype(jnp.float32)).astype(jnp.bfloat16), ahead)
        left = send((total[1] + left.astype(jnp.float32)).astype(jnp.bfloat16), back)
    input_grad = summed((0,))[0] + right.astype(jnp.float32) + left.astype(jnp.float32)

    def weight_of(left_side, parts, shape):
        result = None
        for some in (parts[:2], parts[2:3], parts[3:4], parts[4:]):
            index, blocks = joined(some)
            result = weight_grad(index, left_side, blocks, shape, result)
        return result

    grad_w_out = weight_of(attended_t, grad_parts, w_out.shape)
    grad_w_qkv = weight_of(grad, in_parts, w.shape).transpose(1, 0, 2)
    return input_grad.astype(jnp.bfloat16), grad_w_qkv, grad_w_out


def solution(mesh):
    placed = (
        P("runs", "gx"),
        P("runs", "gx"),
        P(None, None, "gx"),
        P("gx", None),
        P("runs", None, "gx"),
        P("runs"),
    )
    return jax.shard_map(
        functools.partial(on_device, mesh.shape["gx"]),
        mesh=mesh,
        in_specs=placed,
        out_specs=(P("runs", "gx"), P("runs", None, "gx"), P(("runs", "gx"), None)),
        check_vma=False,
    )
```

time: 219 us -> 165 us (0.75)
  waiting for transfers between devices: 117 us -> 39.1 us
  starting transfers between devices: 0.68 us -> 29.3 us
  local copies, waits for them, and re-layouts: 25.1 us -> 12.3 us
  between operations: 13.9 us -> 1.72 us
  Pallas kernels: 59 us -> 69.3 us
  other arithmetic: 2.56 us -> 12.8 us
    all_gather x2 -> x0, waiting for transfers between devices: 69.5 us -> none  [gathered(): mine = lax.all_gather(x, 'gx', axis=0, axis_index_groups=same_core)]
    reduce_scatter x1 -> x0, waiting for transfers between devices: 47 us -> none  [on_device(): lax.psum_scatter(both, 'gx', scatter_dimension=0, axis_index_groups=same_...]
    ppermute x3 -> x45, waiting for transfers between devices: 0.01 us -> 39.1 us  [send(): return lax.ppermute(x, 'gx', perm)]
    ppermute x3 -> x45, starting transfers between devices: 0.56 us -> 29.3 us  [send(): return lax.ppermute(x, 'gx', perm)]
    unnamed x26 -> x28, local copies, waits for them, and re-layouts: 24.2 us -> 6.89 us
    another operation x0 -> x3, other arithmetic: none -> 5.8 us  [summed(): at = jnp.stack([chip_at[k % chips] for k in offsets]).astype(jnp.int32)]
    pallas_call x3 -> x12, Pallas kernels: 31.4 us -> 37 us  [the longest x8 28.5 us: weight_grad(): pl.pallas_call(functools.partial(weight_kernel, count, turn), in_specs=[p...]
    pallas_call x2 -> x5, Pallas kernels: 18.7 us -> 23.4 us  [terms(): pl.pallas_call(terms_kernel, grid_spec=pltpu.PrefetchScalarGridSpec(num_s...]
  transfers between devices with their start and end apart: 6 -> 45, of which waited for: 3 -> 12; matrix products, arithmetic and copies ran while one was open for 2% -> 11% of each run, Pallas kernels for 27% -> 42%
where the time goes in v2:
time: 165 us
  Pallas kernels  69.3 us (42%)
  waiting for transfers between devices  39.1 us (24%)
  starting transfers between devices  29.3 us (18%)
  other arithmetic  12.8 us (8%)
  local copies, waits for them, and re-layouts  12.3 us (7%)
  between operations  1.72 us (1%)
    ppermute x45, waiting for transfers between devices, send(): return lax.ppermute(x, 'gx', perm)  39.1 us
    ppermute x45, starting transfers between devices, send(): return lax.ppermute(x, 'gx', perm)  29.3 us
    pallas_call x8, Pallas kernels, weight_grad(): pl.pallas_call(functools.partial(weight_kernel, count, turn), in_specs=[p...  28.5 us
    pallas_call x5, Pallas kernels, terms(): pl.pallas_call(terms_kernel, grid_spec=pltpu.PrefetchScalarGridSpec(num_s...  23.4 us
    pallas_call x4, Pallas kernels, grad_heads(): pl.pallas_call(functools.partial(grad_heads_kernel, count, first, last),...  8.48 us
    unnamed x28, local copies, waits for them, and re-layouts  6.89 us
    another operation x3, other arithmetic, summed(): at = jnp.stack([chip_at[k % chips] for k in offsets]).astype(jnp.int32)  5.8 us
    pallas_call x1, Pallas kernels, attend(): pl.pallas_call(attend_kernel, grid=(heads,), in_specs=[pl.BlockSpec((seq,...  4.86 us
  transfers between devices with their start and end apart: 45, of which 12 were waited for; matrix products, arithmetic and copies ran while one was open for 11% of the time, Pallas kernels for 42%

profile of v2, /device:TPU:0, one launch (start us, length us, event | category | flops | bytes accessed | tf_op | source)
XLA Modules:
  0.0 164.6 jit_solution(9316114790514066903)
XLA Ops:
  0.6 3.1 %collective-permute-start = (bf16[512,384]{1,0:T(8,128)(2,1)}, bf16[512,384]{1,0:T(8,128)(2,1)S(1)}, u32[]{:S(2)}, u32[]{:S(2)}) collective-permute-start(bf16[512,384]{1,0:T(8,128)(2,1)} %refs_0_.4), channel_id=1, source_target_pairs={{0,4},{1,5},{4,8},{5,9},{8,12},{9,13},{12,14},{13,15},{14,10},{15,... | collective-permute-start | bytes 1179656 | tf_op jit(solution)/shard_map/ppermute | solution.py:263
  6.5 6.5 %collective-permute-done.refs_1_ = bf16[512,384]{1,0:T(8,128)(2,1)S(1)} collective-permute-done((bf16[512,384]{1,0:T(8,128)(2,1)}, bf16[512,384]{1,0:T(8,128)(2,1)S(1)}, u32[]{:S(2)}, u32[]{:S(2)}) %collective-permute-start) | collective-permute-done | bytes 393248 | tf_op jit(solution)/shard_map/ppermute | solution.py:263
  24.8 3.0 %collective-permute-done.5.refs_1_ = bf16[512,384]{1,0:T(8,128)(2,1)S(1)} collective-permute-done((bf16[512,384]{1,0:T(8,128)(2,1)S(1)}, bf16[512,384]{1,0:T(8,128)(2,1)S(1)}, u32[]{:S(2)}, u32[]{:S(2)}) %collective-permute-start.5) | collective-permute-done | bytes 393248 | tf_op jit(solution)/shard_map/ppermute | solution.py:263
  43.9 4.9 %shard_map.94 = (bf16[4,512,512]{2,1,0:T(8,128)(2,1)S(1)}, bf16[512,512]{1,0:T(8,128)(2,1)S(1)}, bf16[512,512]{1,0:T(8,128)(2,1)S(1)}) custom-call(s32[512,1]{1,0:T(8,128)S(1)} %copy-done.8, s32[1,512]{1,0:T(1,128)S(1)} %bitcast.63, bf16[3,512,512]{2,1,0:T(8,128)(2,1)S(1)} %bitcast.60), custom_call_target="tpu_custom_call" | custom-call | flops 536870912 | bytes 5242880 | tf_op jit(solution)/shard_map/pallas_call | solution.py:44
  48.8 2.8 %copy-done = bf16[512,6144]{1,0:T(8,128)(2,1)S(1)} copy-done((bf16[512,6144]{1,0:T(8,128)(2,1)S(1)}, bf16[512,6144]{1,0:T(8,128)(2,1)}, u32[]{:S(2)}) %copy-start) | copy-done | bytes 6291480
  58.8 3.5 %shard_map.109.refs_4_ = bf16[512,6144]{1,0:T(8,128)(2,1)} custom-call(s32[6]{0:T(128)S(1)} %pad_add_fusion.3.index_ref, bf16[512,512]{1,0:T(8,128)(2,1)S(1)} %get-tuple-element.30.left_ref, bf16[512,384]{1,0:T(8,128)(2,1)S(1)} %copy-done.2, bf16[512,384]{1,0:T(8,128)(2,1)S(1)} %collective-permute-done.refs_1_, ...), custom_call_target="tpu_custom_call" | custom-call | flops 1207959552 | bytes 3538944 | tf_op jit(solution)/shard_map/pallas_call | solution.py:167
  62.3 2.8 %shard_map.96.refs_8_ = f32[512,512]{1,0:T(8,128)S(1)} custom-call(s32[4]{0:T(128)S(1)} %pad_add_fusion.2.index_ref, bf16[512,384]{1,0:T(8,128)(2,1)S(1)} %collective-permute-done.1.refs_0_, bf16[512,384]{1,0:T(8,128)(2,1)S(1)} %copy-done.4, bf16[512,384]{1,0:T(8,128)(2,1)} %collective-permute-done.11.refs_2_, ...), custom_call_target="tpu_custom_call" | custom-call | flops 805306368 | bytes 4194304 | tf_op jit(solution)/shard_map/pallas_call | solution.py:119
  65.1 3.1 %shard_map.110.refs_4_ = bf16[512,6144]{1,0:T(8,128)(2,1)} custom-call(s32[4]{0:T(128)S(1)} %pad_add_fusion.2.index_ref, bf16[512,512]{1,0:T(8,128)(2,1)S(1)} %get-tuple-element.30.left_ref, bf16[512,384]{1,0:T(8,128)(2,1)S(1)} %collective-permute-done.1.refs_0_, bf16[512,384]{1,0:T(8,128)(2,1)S(1)} %copy-done.4, ...), custom_call_target="tpu_custom_call", output_to_operand_aliasing={{}: (6, {})} | custom-call | flops 805306368 | bytes 2359296 | tf_op jit(solution)/shard_map/pallas_call | solution.py:167
  72.6 2.6 %shard_map.111.refs_2_ = bf16[512,6144]{1,0:T(8,128)(2,1)} custom-call(s32[4]{0:T(128)S(1)} %pad_add_fusion.1.index_ref, bf16[512,512]{1,0:T(8,128)(2,1)S(1)} %get-tuple-element.30.left_ref, bf16[512,384]{1,0:T(8,128)(2,1)S(1)} %collective-permute-done.2.refs_0_, ...), custom_call_target="tpu_custom_call", output_to_operand_aliasing={{}: (6, {})} | custom-call | flops 805306368 | bytes 2359296 | tf_op jit(solution)/shard_map/pallas_call | solution.py:167
  76.6 4.0 %shard_map.99.grad_ref.left_ref = bf16[3,512,512]{2,1,0:T(8,128)(2,1)S(1)} custom-call(bf16[3,512,512]{2,1,0:T(8,128)(2,1)S(1)} %bitcast.61, bf16[4,512,512]{2,1,0:T(8,128)(2,1)S(1)} %get-tuple-element.17.attn_ref, bf16[512,512]{1,0:T(8,128)(2,1)S(1)} %get-tuple-element.18.attended_ref, bf16[512,512]{1,0:T(8,128)(2,1)S(1)} %shard_map.98.grad_ref), custom_call_target="tpu_custom_call" | custom-call | flops 1073741824 | bytes 6291456 | tf_op jit(solution)/shard_map/pallas_call | solution.py:84
  80.6 3.8 %shard_map.104 = (bf16[1,512,384]{2,1,0:T(8,128)(2,1)S(1)}, bf16[1,512,384]{2,1,0:T(8,128)(2,1)S(1)}) custom-call(s32[1]{0:T(128)} %bitcast.5.index_ref, s32[1]{0:T(128)} %bitcast.1.core_ref, bf16[3,512,512]{2,1,0:T(8,128)(2,1)S(1)} %shard_map.99.grad_ref.left_ref, bf16[3,6144,512]{2,1,0:T(8,128)(2,1)} %bitcast.64), custom_call_target="tpu_custom_call" | custom-call | flops 1207959552 | bytes 5242880 | tf_op jit(solution)/shard_map/pallas_call | solution.py:207
  84.5 5.3 %shard_map.103 = (bf16[2,512,384]{2,1,0:T(8,128)(2,1)S(1)}, bf16[2,512,384]{2,1,0:T(8,128)(2,1)S(1)}) custom-call(s32[2]{0:T(128)S(1)} %copy-done.11, s32[1]{0:T(128)} %bitcast.1.core_ref, bf16[3,512,512]{2,1,0:T(8,128)(2,1)S(1)} %shard_map.99.grad_ref.left_ref, bf16[3,6144,512]{2,1,0:T(8,128)(2,1)} %bitcast.65), custom_call_target="tpu_custom_call" | custom-call | flops 2415919104 | bytes 10485760 | tf_op jit(solution)/shard_map/pallas_call | solution.py:207
  90.3 5.3 %shard_map.102 = (bf16[2,512,384]{2,1,0:T(8,128)(2,1)S(1)}, bf16[2,512,384]{2,1,0:T(8,128)(2,1)S(1)}) custom-call(s32[2]{0:T(128)S(1)} %copy-done.12, s32[1]{0:T(128)} %bitcast.1.core_ref, bf16[3,512,512]{2,1,0:T(8,128)(2,1)S(1)} %shard_map.99.grad_ref.left_ref, bf16[3,6144,512]{2,1,0:T(8,128)(2,1)} %bitcast.66), custom_call_target="tpu_custom_call" | custom-call | flops 2415919104 | bytes 10485760 | tf_op jit(solution)/shard_map/pallas_call | solution.py:207
  95.6 3.8 %shard_map.100 = (bf16[1,512,384]{2,1,0:T(8,128)(2,1)S(1)}, bf16[1,512,384]{2,1,0:T(8,128)(2,1)S(1)}) custom-call(s32[1]{0:T(128)} %bitcast.index_ref, s32[1]{0:T(128)} %bitcast.1.core_ref, bf16[3,512,512]{2,1,0:T(8,128)(2,1)S(1)} %shard_map.99.grad_ref.left_ref, bf16[3,6144,512]{2,1,0:T(8,128)(2,1)} %bitcast.67), custom_call_target="tpu_custom_call" | custom-call | flops 1207959552 | bytes 5242880 | tf_op jit(solution)/shard_map/pallas_call | solution.py:207
  103.3 5.3 %shard_map.101 = (bf16[2,512,384]{2,1,0:T(8,128)(2,1)S(1)}, bf16[2,512,384]{2,1,0:T(8,128)(2,1)S(1)}) custom-call(s32[2]{0:T(128)S(1)} %copy-done.10, s32[1]{0:T(128)} %bitcast.1.core_ref, bf16[3,512,512]{2,1,0:T(8,128)(2,1)S(1)} %shard_map.99.grad_ref.left_ref, bf16[3,6144,512]{2,1,0:T(8,128)(2,1)} %bitcast.68), custom_call_target="tpu_custom_call" | custom-call | flops 2415919104 | bytes 10485760 | tf_op jit(solution)/shard_map/pallas_call | solution.py:207
  111.5 6.4 %collective-permute-done.25 = bf16[256,384]{1,0:T(8,128)(2,1)S(1)} collective-permute-done((bf16[256,384]{1,0:T(8,128)(2,1)S(1)}, bf16[256,384]{1,0:T(8,128)(2,1)S(1)}, u32[]{:S(2)}, u32[]{:S(2)}) %collective-permute-start.25) | collective-permute-done | bytes 196640 | tf_op jit(solution)/shard_map/ppermute | solution.py:263
  121.2 5.9 %shard_map.105.refs_4_ = bf16[3,6144,512]{2,1,0:T(8,128)(2,1)} custom-call(s32[6]{0:T(128)S(1)} %pad_add_fusion.3.index_ref, bf16[3,512,512]{2,1,0:T(8,128)(2,1)S(1)} %shard_map.99.grad_ref.left_ref, bf16[512,384]{1,0:T(8,128)(2,1)S(1)} %copy-done.7, bf16[512,384]{1,0:T(8,128)(2,1)S(1)} %collective-permute-done.29.refs_1_, ...), custom_call_target="tpu_custom_call" | custom-call | flops 3623878656 | bytes 10616832 | tf_op jit(solution)/shard_map/pallas_call | solution.py:167
  127.1 2.8 %collective-permute-done.35.refs_1_ = bf16[512,384]{1,0:T(8,128)(2,1)S(1)} collective-permute-done((bf16[512,384]{1,0:T(8,128)(2,1)S(1)}, bf16[512,384]{1,0:T(8,128)(2,1)S(1)}, u32[]{:S(2)}, u32[]{:S(2)}) %collective-permute-start.35) | collective-permute-done | bytes 393248 | tf_op jit(solution)/shard_map/ppermute | solution.py:263
  132.2 6.1 %collective-permute-done.26 = bf16[512,384]{1,0:T(8,128)(2,1)S(1)} collective-permute-done((bf16[512,384]{1,0:T(8,128)(2,1)S(1)}, bf16[512,384]{1,0:T(8,128)(2,1)S(1)}, u32[]{:S(2)}, u32[]{:S(2)}) %collective-permute-start.26) | collective-permute-done | bytes 393248 | tf_op jit(solution)/shard_map/ppermute | solution.py:263
  142.6 3.8 %collective-permute-done.23 = bf16[512,384]{1,0:T(8,128)(2,1)S(1)} collective-permute-done((bf16[512,384]{1,0:T(8,128)(2,1)S(1)}, bf16[512,384]{1,0:T(8,128)(2,1)S(1)}, u32[]{:S(2)}, u32[]{:S(2)}) %collective-permute-start.23) | collective-permute-done | bytes 393248 | tf_op jit(solution)/shard_map/ppermute | solution.py:263
  146.4 2.9 %collective-permute-done.27 = bf16[512,384]{1,0:T(8,128)(2,1)S(1)} collective-permute-done((bf16[512,384]{1,0:T(8,128)(2,1)S(1)}, bf16[512,384]{1,0:T(8,128)(2,1)S(1)}, u32[]{:S(2)}, u32[]{:S(2)}) %collective-permute-start.27) | collective-permute-done | bytes 393248 | tf_op jit(solution)/shard_map/ppermute | solution.py:263
  152.1 4.3 %shard_map.106.refs_4_ = bf16[3,6144,512]{2,1,0:T(8,128)(2,1)} custom-call(s32[4]{0:T(128)S(1)} %pad_add_fusion.2.index_ref, bf16[3,512,512]{2,1,0:T(8,128)(2,1)S(1)} %shard_map.99.grad_ref.left_ref, bf16[512,384]{1,0:T(8,128)(2,1)S(1)} %collective-permute-done.30.refs_0_, ...), custom_call_target="tpu_custom_call", output_to_operand_aliasing={{}: (6, {})} | custom-call | flops 2415919104 | bytes 7077888 | tf_op jit(solution)/shard_map/pallas_call | solution.py:167
  156.3 4.3 %shard_map.107.refs_2_ = bf16[3,6144,512]{2,1,0:T(8,128)(2,1)} custom-call(s32[4]{0:T(128)S(1)} %pad_add_fusion.1.index_ref, bf16[3,512,512]{2,1,0:T(8,128)(2,1)S(1)} %shard_map.99.grad_ref.left_ref, bf16[512,384]{1,0:T(8,128)(2,1)S(1)} %collective-permute-done.31.refs_0_, ...), custom_call_target="tpu_custom_call", output_to_operand_aliasing={{}: (6, {})} | custom-call | flops 2415919104 | bytes 7077888 | tf_op jit(solution)/shard_map/pallas_call | solution.py:167
  160.6 3.0 %shard_map.108 = bf16[3,6144,512]{2,1,0:T(8,128)(2,1)} custom-call(s32[2]{0:T(128)S(1)} %pad_add_fusion.index_ref, bf16[3,512,512]{2,1,0:T(8,128)(2,1)S(1)} %shard_map.99.grad_ref.left_ref, bf16[512,384]{1,0:T(8,128)(2,1)S(1)} %constant_dynamic-update-slice_fusion.2.refs_0_, ...), custom_call_target="tpu_custom_call", output_to_operand_aliasing={{}: (4, {})} | custom-call | flops 1207959552 | bytes 3538944 | tf_op jit(solution)/shard_map/pallas_call | solution.py:167
  (142 shorter events, 63.9 us)
Async XLA Ops:
  0.6 12.3 %collective-permute-start = (bf16[512,384]{1,0:T(8,128)(2,1)}, bf16[512,384]{1,0:T(8,128)(2,1)S(1)}, u32[]{:S(2)}, u32[]{:S(2)}) collective-permute-start(bf16[512,384]{1,0:T(8,128)(2,1)} %refs_0_.4), channel_id=1, source_target_pairs={{0,4},{1,5},{4,8},{5,9},{8,12},{9,13},{12,14},{13,15},{14,10},{15,... | collective-permute-start | bytes 1179656 | tf_op jit(solution)/shard_map/ppermute | solution.py:263
  3.7 14.4 %collective-permute-start.4 = (bf16[512,384]{1,0:T(8,128)(2,1)}, bf16[512,384]{1,0:T(8,128)(2,1)S(1)}, u32[]{:S(2)}, u32[]{:S(2)}) collective-permute-start(bf16[512,384]{1,0:T(8,128)(2,1)} %refs_0_.4), channel_id=1, source_target_pairs={{4,0},{5,1},{8,4},{9,5},{12,8},{13,9},{14,12},{15,13},{10,14},{11,... | collective-permute-start | bytes 1179656 | tf_op jit(solution)/shard_map/ppermute | solution.py:263
  3.7 35.1 %collective-permute-start.13 = (bf16[512,384]{1,0:T(8,128)(2,1)}, bf16[512,384]{1,0:T(8,128)(2,1)S(1)}, u32[]{:S(2)}, u32[]{:S(2)}) collective-permute-start(bf16[512,384]{1,0:T(8,128)(2,1)} %refs_0_.4), channel_id=1, source_target_pairs={{0,1},{1,0},{2,3},{3,2},{4,5},{5,4},{6,7},{7,6},{8,9},{9,8},{10,11... | collective-permute-start | bytes 1179656 | tf_op jit(solution)/shard_map/ppermute | solution.py:263
  30.3 18.5 %collective-permute-start.15 = (bf16[512,384]{1,0:T(8,128)(2,1)S(1)}, bf16[512,384]{1,0:T(8,128)(2,1)S(1)}, u32[]{:S(2)}, u32[]{:S(2)}) collective-permute-start(bf16[512,384]{1,0:T(8,128)(2,1)S(1)} %collective-permute-done.4.refs_2_), channel_id=1, source_target_pairs={{0,1},{1,0},{2,3},{3,2},{4,5},{5,4},{6,7},{7,6},{8,9},{9,8},{10,11... | collective-permute-start | bytes 1179656 | tf_op jit(solution)/shard_map/ppermute | solution.py:263
  32.7 23.1 %collective-permute-start.11 = (bf16[512,384]{1,0:T(8,128)(2,1)S(1)}, bf16[512,384]{1,0:T(8,128)(2,1)}, u32[]{:S(2)}, u32[]{:S(2)}) collective-permute-start(bf16[512,384]{1,0:T(8,128)(2,1)S(1)} %collective-permute-done.1.refs_0_), channel_id=1, source_target_pairs={{0,1},{1,0},{2,3},{3,2},{4,5},{5,4},{6,7},{7,6},{8,9},{9,8},{10,11... | collective-permute-start | bytes 1179656 | tf_op jit(solution)/shard_map/ppermute | solution.py:263
  36.5 19.6 %collective-permute-start.3 = (bf16[256,384]{1,0:T(8,128)(2,1)}, bf16[256,384]{1,0:T(8,128)(2,1)}, u32[]{:S(2)}, u32[]{:S(2)}) collective-permute-start(bf16[256,384]{1,0:T(8,128)(2,1)} %slice.144), channel_id=1, source_target_pairs={{0,4},{1,5},{4,8},{5,9},{8,12},{9,13},{12,14},{13,15},{14,10},{15,... | collective-permute-start | bytes 589832 | tf_op jit(solution)/shard_map/ppermute | solution.py:263
  38.8 17.4 %collective-permute-start.7 = (bf16[256,384]{1,0:T(8,128)(2,1)}, bf16[256,384]{1,0:T(8,128)(2,1)}, u32[]{:S(2)}, u32[]{:S(2)}) collective-permute-start(bf16[256,384]{1,0:T(8,128)(2,1)} %slice.145), channel_id=1, source_target_pairs={{4,0},{5,1},{8,4},{9,5},{12,8},{13,9},{14,12},{15,13},{10,14},{11,... | collective-permute-start | bytes 589832 | tf_op jit(solution)/shard_map/ppermute | solution.py:263
  40.9 17.7 %collective-permute-start.12 = (bf16[512,384]{1,0:T(8,128)(2,1)}, bf16[512,384]{1,0:T(8,128)(2,1)S(1)}, u32[]{:S(2)}, u32[]{:S(2)}) collective-permute-start(bf16[512,384]{1,0:T(8,128)(2,1)} %copy-done.3), channel_id=1, source_target_pairs={{0,1},{1,0},{2,3},{3,2},{4,5},{5,4},{6,7},{7,6},{8,9},{9,8},{10,11... | collective-permute-start | bytes 1179656 | tf_op jit(solution)/shard_map/ppermute | solution.py:263
  54.1 14.6 %collective-permute-start.29 = (bf16[512,384]{1,0:T(8,128)(2,1)S(1)}, bf16[512,384]{1,0:T(8,128)(2,1)S(1)}, u32[]{:S(2)}, u32[]{:S(2)}) collective-permute-start(bf16[512,384]{1,0:T(8,128)(2,1)S(1)} %copy-done.7), channel_id=1, source_target_pairs={{0,4},{1,5},{4,8},{5,9},{8,12},{9,13},{12,14},{13,15},{14,10},{15,... | collective-permute-start | bytes 1179656 | tf_op jit(solution)/shard_map/ppermute | solution.py:263
  55.7 14.5 %collective-permute-start.33 = (bf16[512,384]{1,0:T(8,128)(2,1)S(1)}, bf16[512,384]{1,0:T(8,128)(2,1)S(1)}, u32[]{:S(2)}, u32[]{:S(2)}) collective-permute-start(bf16[512,384]{1,0:T(8,128)(2,1)S(1)} %copy-done.7), channel_id=1, source_target_pairs={{4,0},{5,1},{8,4},{9,5},{12,8},{13,9},{14,12},{15,13},{10,14},{11,... | collective-permute-start | bytes 1179656 | tf_op jit(solution)/shard_map/ppermute | solution.py:263
  56.2 14.5 %collective-permute-start.9 = (bf16[512,384]{1,0:T(8,128)(2,1)S(1)}, bf16[512,384]{1,0:T(8,128)(2,1)S(1)}, u32[]{:S(2)}, u32[]{:S(2)}) collective-permute-start(bf16[512,384]{1,0:T(8,128)(2,1)S(1)} %collective-permute-done.2.refs_0_), channel_id=1, source_target_pairs={{0,1},{1,0},{2,3},{3,2},{4,5},{5,4},{6,7},{7,6},{8,9},{9,8},{10,11... | collective-permute-start | bytes 1179656 | tf_op jit(solution)/shard_map/ppermute | solution.py:263
  58.6 16.6 %collective-permute-start.8 = (bf16[512,384]{1,0:T(8,128)(2,1)S(1)}, bf16[512,384]{1,0:T(8,128)(2,1)S(1)}, u32[]{:S(2)}, u32[]{:S(2)}) collective-permute-start(bf16[512,384]{1,0:T(8,128)(2,1)S(1)} %constant_dynamic-update-slice_fusion.refs_0_), channel_id=1, source_target_pairs={{0,1},{1,0},{2,3},{3,2},{4,5},{5,4},{6,7},{7,6},{8,9},{9,8},{10,11... | collective-permute-start | bytes 1179656 | tf_op jit(solution)/shard_map/ppermute | solution.py:263
  68.2 40.4 %collective-permute-start.42 = (bf16[512,384]{1,0:T(8,128)(2,1)S(1)}, bf16[512,384]{1,0:T(8,128)(2,1)S(1)}, u32[]{:S(2)}, u32[]{:S(2)}) collective-permute-start(bf16[512,384]{1,0:T(8,128)(2,1)S(1)} %copy-done.7), channel_id=1, source_target_pairs={{0,1},{1,0},{2,3},{3,2},{4,5},{5,4},{6,7},{7,6},{8,9},{9,8},{10,11... | collective-permute-start | bytes 1179656 | tf_op jit(solution)/shard_map/ppermute | solution.py:263
  68.7 40.0 %collective-permute-start.30 = (bf16[512,384]{1,0:T(8,128)(2,1)S(1)}, bf16[512,384]{1,0:T(8,128)(2,1)S(1)}, u32[]{:S(2)}, u32[]{:S(2)}) collective-permute-start(bf16[512,384]{1,0:T(8,128)(2,1)S(1)} %collective-permute-done.29.refs_1_), channel_id=1, source_target_pairs={{0,4},{1,5},{4,8},{5,9},{8,12},{9,13},{12,14},{13,15},{14,10},{15,... | collective-permute-start | bytes 1179656 | tf_op jit(solution)/shard_map/ppermute | solution.py:263
  70.3 39.0 %collective-permute-start.34 = (bf16[512,384]{1,0:T(8,128)(2,1)S(1)}, bf16[512,384]{1,0:T(8,128)(2,1)S(1)}, u32[]{:S(2)}, u32[]{:S(2)}) collective-permute-start(bf16[512,384]{1,0:T(8,128)(2,1)S(1)} %collective-permute-done.33.refs_2_), channel_id=1, source_target_pairs={{4,0},{5,1},{8,4},{9,5},{12,8},{13,9},{14,12},{15,13},{10,14},{11,... | collective-permute-start | bytes 1179656 | tf_op jit(solution)/shard_map/ppermute | solution.py:263
  84.4 17.1 %collective-permute-start.20 = (bf16[1,512,384]{2,1,0:T(8,128)(2,1)S(1)}, bf16[1,512,384]{2,1,0:T(8,128)(2,1)S(1)}, u32[]{:S(2)}, u32[]{:S(2)}) collective-permute-start(bf16[1,512,384]{2,1,0:T(8,128)(2,1)S(1)} %get-tuple-element.28), channel_id=1, source_target_pairs={{0,1},{1,0},{2,3},{3,2},{4,5},{5,4},{6,7},{7,6},{8,9},{9,8},{10,11... | collective-permute-start | bytes 1179656 | tf_op jit(solution)/shard_map/ppermute | solution.py:263
  89.8 21.1 %collective-permute-start.19 = (bf16[2,512,384]{2,1,0:T(8,128)(2,1)S(1)}, bf16[2,512,384]{2,1,0:T(8,128)(2,1)S(1)}, u32[]{:S(2)}, u32[]{:S(2)}) collective-permute-start(bf16[2,512,384]{2,1,0:T(8,128)(2,1)S(1)} %get-tuple-element.26), channel_id=1, source_target_pairs={{0,1},{1,0},{2,3},{3,2},{4,5},{5,4},{6,7},{7,6},{8,9},{9,8},{10,11... | collective-permute-start | bytes 2359304 | tf_op jit(solution)/shard_map/ppermute | solution.py:263
  109.2 20.7 %collective-permute-start.18 = (bf16[2,512,384]{2,1,0:T(8,128)(2,1)S(1)}, bf16[2,512,384]{2,1,0:T(8,128)(2,1)S(1)}, u32[]{:S(2)}, u32[]{:S(2)}) collective-permute-start(bf16[2,512,384]{2,1,0:T(8,128)(2,1)S(1)} %get-tuple-element.24), channel_id=1, source_target_pairs={{0,1},{1,0},{2,3},{3,2},{4,5},{5,4},{6,7},{7,6},{8,9},{9,8},{10,11... | collective-permute-start | bytes 2359304 | tf_op jit(solution)/shard_map/ppermute | solution.py:263
  118.4 21.7 %collective-permute-start.17 = (bf16[2,512,384]{2,1,0:T(8,128)(2,1)S(1)}, bf16[2,512,384]{2,1,0:T(8,128)(2,1)S(1)}, u32[]{:S(2)}, u32[]{:S(2)}) collective-permute-start(bf16[2,512,384]{2,1,0:T(8,128)(2,1)S(1)} %get-tuple-element.22), channel_id=1, source_target_pairs={{0,1},{1,0},{2,3},{3,2},{4,5},{5,4},{6,7},{7,6},{8,9},{9,8},{10,11... | collective-permute-start | bytes 2359304 | tf_op jit(solution)/shard_map/ppermute | solution.py:263
  118.5 13.2 %collective-permute-start.22 = (bf16[512,384]{1,0:T(8,128)(2,1)S(1)}, bf16[512,384]{1,0:T(8,128)(2,1)S(1)}, u32[]{:S(2)}, u32[]{:S(2)}) collective-permute-start(bf16[512,384]{1,0:T(8,128)(2,1)S(1)} %get-tuple-element.37), channel_id=1, source_target_pairs={{0,4},{1,5},{4,8},{5,9},{8,12},{9,13},{12,14},{13,15},{14,10},{15,... | collective-permute-start | bytes 1179656 | tf_op jit(solution)/shard_map/ppermute | solution.py:263
  120.8 17.6 %collective-permute-start.26 = (bf16[512,384]{1,0:T(8,128)(2,1)S(1)}, bf16[512,384]{1,0:T(8,128)(2,1)S(1)}, u32[]{:S(2)}, u32[]{:S(2)}) collective-permute-start(bf16[512,384]{1,0:T(8,128)(2,1)S(1)} %get-tuple-element.38), channel_id=1, source_target_pairs={{4,0},{5,1},{8,4},{9,5},{12,8},{13,9},{14,12},{15,13},{10,14},{11,... | collective-permute-start | bytes 1179656 | tf_op jit(solution)/shard_map/ppermute | solution.py:263
  129.9 19.5 %collective-permute-start.40 = (bf16[512,384]{1,0:T(8,128)(2,1)S(1)}, bf16[512,384]{1,0:T(8,128)(2,1)S(1)}, u32[]{:S(2)}, u32[]{:S(2)}) collective-permute-start(bf16[512,384]{1,0:T(8,128)(2,1)S(1)} %collective-permute-done.30.refs_0_), channel_id=1, source_target_pairs={{0,1},{1,0},{2,3},{3,2},{4,5},{5,4},{6,7},{7,6},{8,9},{9,8},{10,11... | collective-permute-start | bytes 1179656 | tf_op jit(solution)/shard_map/ppermute | solution.py:263
  146.4 17.3 %collective-permute-start.16 = (bf16[1,512,384]{2,1,0:T(8,128)(2,1)S(1)}, bf16[1,512,384]{2,1,0:T(8,128)(2,1)S(1)}, u32[]{:S(2)}, u32[]{:S(2)}) collective-permute-start(bf16[1,512,384]{2,1,0:T(8,128)(2,1)S(1)} %get-tuple-element.20), channel_id=1, source_target_pairs={{0,1},{1,0},{2,3},{3,2},{4,5},{5,4},{6,7},{7,6},{8,9},{9,8},{10,11... | collective-permute-start | bytes 1179656 | tf_op jit(solution)/shard_map/ppermute | solution.py:263
  150.0 13.6 %collective-permute-start.24 = (bf16[512,384]{1,0:T(8,128)(2,1)S(1)}, bf16[512,384]{1,0:T(8,128)(2,1)S(1)}, u32[]{:S(2)}, u32[]{:S(2)}) collective-permute-start(bf16[512,384]{1,0:T(8,128)(2,1)S(1)} %get-tuple-element.33), channel_id=1, source_target_pairs={{0,4},{1,5},{4,8},{5,9},{8,12},{9,13},{12,14},{13,15},{14,10},{15,... | collective-permute-start | bytes 1179656 | tf_op jit(solution)/shard_map/ppermute | solution.py:263
  (34 other events, 290.2 us)

commit v3 on v2

v3 whole, which is shorter than its diff:
```python
import functools
import math

import jax
import jax.numpy as jnp
from jax import lax
from jax.experimental import pallas as pl
from jax.experimental.pallas import tpu as pltpu
from jax.sharding import PartitionSpec as P

HD = 128
FACTOR = 1.0 / math.sqrt(HD)
MIB = 1 << 20
NT = (((1,), (1,)), ((), ()))
TN = (((0,), (0,)), ((), ()))


def dot(a, b, dims=(((1,), (0,)), ((), ()))):
    return lax.dot_general(a, b, dims, preferred_element_type=jnp.float32)


def params(mib):
    return pltpu.CompilerParams(vmem_limit_bytes=mib * MIB)


def cost(flops, nbytes, transcendentals=0):
    flops, nbytes = flops // 4096, nbytes // 4096
    return pl.CostEstimate(flops=flops, bytes_accessed=nbytes, transcendentals=transcendentals)


def attend_kernel(col_ref, row_ref, qkv_ref, attn_ref, out_ref, out_t_ref):
    scores = dot(qkv_ref[0], qkv_ref[1], NT) * FACTOR
    scores = jnp.where(row_ref[...] <= col_ref[...], scores, -1e30)
    expd = jnp.exp(scores - jnp.max(scores, axis=1, keepdims=True))
    attn = (expd / jnp.sum(expd, axis=1, keepdims=True)).astype(jnp.bfloat16)
    attn_ref[0] = attn
    attended = dot(attn, qkv_ref[2])
    out_ref[...] = attended.astype(jnp.bfloat16)
    out_t_ref[...] = attended.T.astype(jnp.bfloat16)


def attend(positions, qkv):
    _, seq, columns = qkv.shape
    heads = columns // HD
    return pl.pallas_call(
        attend_kernel,
        grid=(heads,),
        in_specs=[
            pl.BlockSpec((seq, 1), lambda h: (0, 0)),
            pl.BlockSpec((1, seq), lambda h: (0, 0)),
            pl.BlockSpec((3, seq, HD), lambda h: (0, 0, h)),
        ],
        out_specs=[
            pl.BlockSpec((1, seq, seq), lambda h: (h, 0, 0)),
            pl.BlockSpec((seq, HD), lambda h: (0, h)),
            pl.BlockSpec((HD, seq), lambda h: (h, 0)),
        ],
        out_shape=[
            jax.ShapeDtypeStruct((heads, seq, seq), jnp.bfloat16),
            jax.ShapeDtypeStruct((seq, columns), jnp.bfloat16),
            jax.ShapeDtypeStruct((columns, seq), jnp.bfloat16),
        ],
        compiler_params=params(24),
        cost_estimate=cost(4 * seq * seq * columns, 5 * MIB, heads * seq * seq),
    )(positions[:, None], positions[None, :], qkv)


def attend_back_kernel(qkv_ref, attn_ref, attended_ref, grad_ref, out_ref):
    grad = grad_ref[...]
    attn = attn_ref[0]
    row_dot = jnp.sum(
        grad.astype(jnp.float32) * attended_ref[...].astype(jnp.float32), axis=1, keepdims=True
    )
    grad_attn = dot(grad, qkv_ref[2], NT)
    grad_scores = (attn.astype(jnp.float32) * (grad_attn - row_dot) * FACTOR).astype(jnp.bfloat16)
    out_ref[0] = dot(grad_scores, qkv_ref[1]).astype(jnp.bfloat16)
    out_ref[1] = dot(grad_scores, qkv_ref[0], TN).astype(jnp.bfloat16)
    out_ref[2] = dot(attn, grad, TN).astype(jnp.bfloat16)


def attend_back(qkv, attn, attended, grad):
    _, seq, columns = qkv.shape
    planes = pl.BlockSpec((3, seq, HD), lambda h: (0, 0, h))
    one = pl.BlockSpec((seq, HD), lambda h: (0, h))
    return pl.pallas_call(
        attend_back_kernel,
        grid=(columns // HD,),
        in_specs=[planes, pl.BlockSpec((1, seq, seq), lambda h: (h, 0, 0)), one, one],
        out_specs=planes,
        out_shape=jax.ShapeDtypeStruct(qkv.shape, jnp.bfloat16),
        compiler_params=params(24),
        cost_estimate=cost(8 * seq * seq * columns, 6 * MIB),
    )(qkv, attn, attended, grad)


def grad_heads_kernel(count, first, last, plan_ref, *refs):
    blocks, weights, rest = refs[:count], refs[count : 2 * count], refs[2 * count :]
    out_ref, total = rest[-2:]
    for i, (block, weight) in enumerate(zip(blocks, weights)):
        term = dot(block[...], weight[...], NT)
        if i:
            total[...] += term
        else:
            total[...] = term if first else rest[0][...] + term
    out_ref[...] = total[...].astype(jnp.bfloat16) if last else total[...]


def grad_heads(plan, w_out, blocks, total=None, last=False):
    columns = w_out.shape[0]
    seq, part = blocks[0][1].shape
    count = len(blocks)

    def weight(place):
        return pl.BlockSpec((columns, part), lambda step, plan: (0, plan[place]))

    def whole(shape):
        return pl.BlockSpec(shape, lambda step, plan: (0, 0))

    first = total is None
    return pl.pallas_call(
        functools.partial(grad_heads_kernel, count, first, last),
        grid_spec=pltpu.PrefetchScalarGridSpec(
            num_scalar_prefetch=1,
            grid=(1,),
            in_specs=[whole((seq, part))] * count
            + [weight(place) for place, _ in blocks]
            + [whole((seq, columns))] * (not first),
            out_specs=whole((seq, columns)),
            scratch_shapes=[pltpu.VMEM((seq, columns), jnp.float32)],
        ),
        out_shape=jax.ShapeDtypeStruct((seq, columns), jnp.bfloat16 if last else jnp.float32),
        compiler_params=params(40),
        cost_estimate=cost(2 * seq * columns * part * count, MIB * count),
    )(plan, *[block for _, block in blocks], *[w_out] * count, *([] if first else [total]))


SLOTS = 4


def weight_kernel(places, turn, plan_ref, left_ref, *refs):
    out_ref, held, sems = refs[-3:]
    copies = []
    for i, (place, block) in enumerate(zip(places, refs)):
        width = block.shape[1]
        slot = i % SLOTS
        if i >= SLOTS:
            copies[i - SLOTS].wait()
        if turn:
            turned = block[...].T
            for k in range(3):
                held[slot, k] = dot(turned, left_ref[k]).astype(jnp.bfloat16)
        else:
            held[slot] = dot(left_ref[...], block[...]).astype(jnp.bfloat16)
        start = pl.multiple_of(plan_ref[place] * width, 128)
        copy = pltpu.make_async_copy(
            held.at[slot], out_ref.at[:, pl.ds(start, width)], sems.at[slot]
        )
        copy.start()
        copies.append(copy)
    for copy in copies[-SLOTS:]:
        copy.wait()


def weight_grad(plan, left, blocks, shape, into=None):
    turn = left.ndim == 3
    seq, part = blocks[0][1].shape
    count = len(blocks)
    held = (3, part, left.shape[2]) if turn else (left.shape[0], part)
    vmem = pl.BlockSpec(memory_space=pltpu.VMEM)
    rest = pl.BlockSpec(memory_space=pl.ANY)
    size = math.prod(held) * count
    return pl.pallas_call(
        functools.partial(weight_kernel, [place for place, _ in blocks], turn),
        in_specs=[pl.BlockSpec(memory_space=pltpu.SMEM)]
        + [vmem] * (1 + count)
        + [rest] * (into is not None),
        out_specs=rest,
        out_shape=jax.ShapeDtypeStruct(shape, jnp.bfloat16),
        scratch_shapes=[
            pltpu.VMEM((SLOTS, *held), jnp.bfloat16),
            pltpu.SemaphoreType.DMA((SLOTS,)),
        ],
        input_output_aliases={} if into is None else {2 + count: 0},
        compiler_params=params(40),
        cost_estimate=cost(2 * seq * size, 3 * size),
    )(plan, left, *[block for _, block in blocks], *([] if into is None else [into]))


def terms_kernel(plan_ref, grad_ref, w_ref, *out_refs):
    total = dot(grad_ref[0], w_ref[0], NT)
    total += dot(grad_ref[1], w_ref[1], NT)
    total += dot(grad_ref[2], w_ref[2], NT)
    total = total.astype(jnp.bfloat16)
    part = total.shape[1] // 2
    step = pl.program_id(0)
    for i, out_ref in enumerate(out_refs):
        core = plan_ref[0] if i == len(out_refs) - 1 else 1 - plan_ref[0]

        @pl.when((step == i) & (core == 0))
        def _():
            out_ref[0] = total[:, part:]
            out_ref[1] = total[:, :part]

        @pl.when((step == i) & (core == 1))
        def _():
            out_ref[0] = total[:, :part]
            out_ref[1] = total[:, part:]


def terms(plan, place, count, grad, w, part):
    _, seq, columns = grad.shape
    out = pl.BlockSpec((2, seq, part), lambda i, plan: (0, 0, 0))
    shape = jax.ShapeDtypeStruct((2, seq, part), jnp.bfloat16)
    return pl.pallas_call(
        terms_kernel,
        grid_spec=pltpu.PrefetchScalarGridSpec(
            num_scalar_prefetch=1,
            grid=(count,),
            in_specs=[
                pl.BlockSpec((3, seq, columns), lambda i, plan: (0, 0, 0)),
                pl.BlockSpec((3, 2 * part, columns), lambda i, plan: (0, plan[place + i], 0)),
            ],
            out_specs=[out] * count,
        ),
        out_shape=[shape] * count,
        compiler_params=params(48),
        cost_estimate=cost(12 * seq * columns * part * count, 5 * MIB * count),
    )(plan, grad, w)


def plain(n, inputs, out_grad, w_qkv, w_out, saved_qkv, positions):
    full_in = lax.all_gather(inputs, "gx", axis=1, tiled=True)
    full_grad = lax.all_gather(out_grad, "gx", axis=1, tiled=True)
    qkv = saved_qkv.transpose(1, 0, 2)
    attn, attended, _ = attend(positions, qkv)
    grad_h = dot(full_grad, w_out, NT).astype(jnp.bfloat16)
    grad_w_out = dot(attended, full_grad, TN).astype(jnp.bfloat16)
    grad = attend_back(qkv, attn, attended, grad_h)
    grad_w_qkv = jnp.stack([dot(full_in, grad[k], TN).astype(jnp.bfloat16) for k in range(3)], 1)
    partial = sum(dot(grad[k], w_qkv[:, k], NT) for k in range(3))
    input_grad = lax.psum_scatter(partial, "gx", scatter_dimension=1, tiled=True)
    return input_grad.astype(jnp.bfloat16), grad_w_qkv, grad_w_out


def ring_order(chips):
    if chips == 8:
        return [0, 2, 4, 6, 7, 5, 3, 1]
    return list(range(chips))


def plan_of(order, device):
    chips = len(order)
    at = order.index(device // 2)
    core = device % 2

    def chip(offset):
        return order[(at + offset) % chips]

    blocks = [2 * chip(0) + core, 2 * chip(0) + 1 - core]
    for step in range(1, chips // 2):
        behind, ahead = (-step, step) if core == 0 else (step, -step)
        blocks += [2 * chip(behind) + core, 2 * chip(behind) + 1 - core]
        blocks += [2 * chip(ahead) + 1 - core, 2 * chip(ahead) + core]
    blocks += [2 * chip(chips // 2) + core, 2 * chip(chips // 2) + 1 - core]
    summed = [chip(chips // 2)]
    for step in range(chips // 2 - 1, 0, -1):
        ahead = step if core == 0 else -step
        summed += [chip(-ahead), chip(ahead)]
    return [core] + blocks + summed + [chip(0)]


def after(x, *others):
    return lax.optimization_barrier((x, *others))[0]


def together(*arrays):
    return lax.optimization_barrier(arrays)


def f32(x):
    return x.astype(jnp.float32)


def on_device(n, inputs, out_grad, w_qkv, w_out, saved_qkv, positions):
    part = inputs.shape[1]
    if part % 128 or n != 16:
        return plain(n, inputs, out_grad, w_qkv, w_out, saved_qkv, positions)
    order = ring_order(n // 2)
    chips = range(n // 2)
    ring = [(2 * order[i], 2 * order[i - 1]) for i in chips]
    ring = [(j, i) for i, j in ring] + [(i + 1, j + 1) for i, j in ring]
    swap = [(i, i ^ 1) for i in range(n)]
    plans = [plan_of(order, i) for i in range(n)]
    size = len(plans[0])
    plan = lax.dynamic_slice(
        jnp.array(sum(plans, []), jnp.int32), (lax.axis_index("gx") * size,), (size,)
    )

    def send(x):
        return lax.ppermute(x, "gx", ring)

    def swapped(x):
        return lax.ppermute(x, "gx", swap)

    def blocks(step, *arrays):
        first = 1 if step == 0 else 4 * step - 1
        return [(first + i, array) for i, array in enumerate(arrays)]

    def grad_out(index, some, into=None):
        return weight_grad(index, attended_t, some, w_out.shape, into)

    def grad_qkv(index, some, into=None):
        return weight_grad(index, grad, some, w.shape, into)

    qkv = saved_qkv.transpose(1, 0, 2)
    w = w_qkv.transpose(1, 0, 2)

    a1 = send(out_grad)
    other = swapped(out_grad)
    b1 = send(other)
    attn, attended, attended_t = attend(positions, qkv)

    a1 = after(a1, attended)
    a2, a1x = send(a1), swapped(a1)
    g0 = blocks(0, out_grad, other)
    grad_h = grad_heads(after(plan, a1), w_out, g0)

    b1 = after(b1, grad_h)
    b2, b1x = send(b1), swapped(b1)
    out = grad_out(after(plan, b1), g0)

    a2 = after(a2, out)
    a3, a2x = send(a2), swapped(a2)
    g1 = blocks(1, a1, b1, a1x, b1x)
    grad_h = grad_heads(after(plan, a2), w_out, g1, grad_h)

    b2 = after(b2, grad_h)
    b3, b2x = send(b2), swapped(b2)
    out = grad_out(after(plan, b2), g1, out)

    a3 = after(a3, out)
    a4, a3x = send(a3), swapped(a3)
    g2 = blocks(2, a2, b2, a2x, b2x)
    grad_h = grad_heads(after(plan, a3), w_out, g2, grad_h)

    b3 = after(b3, grad_h)
    b3x = swapped(b3)
    inputs = after(inputs, b3)
    other = swapped(inputs)
    i1 = send(inputs)
    out = grad_out(after(plan, b3), g2, out)

    out, other, a3x, b3x, plan = together(out, other, a3x, b3x, plan)
    j1 = send(other)
    f0 = blocks(0, inputs, other)
    g3 = blocks(3, a3, b3, a3x, b3x)
    grad_h = grad_heads(plan, w_out, g3, grad_h)

    grad_h, a4, plan = together(grad_h, a4, plan)
    a4x = swapped(a4)
    out = grad_out(plan, g3, out)

    out, a4x, i1, plan = together(out, a4x, i1, plan)
    i2, i1x = send(i1), swapped(i1)
    g4 = blocks(4, a4, a4x)
    grad_h = grad_heads(plan, w_out, g4, grad_h, last=True)
    grad = attend_back(qkv, attn, attended, grad_h)

    grad, j1, plan = together(grad, j1, plan)
    j2, j1x = send(j1), swapped(j1)
    (t4,) = terms(plan, 17, 1, grad, w, part)

    t4, i2, plan = together(t4, i2, plan)
    theirs = swapped(t4[0])
    i3, i2x = send(i2), swapped(i2)
    out = grad_out(plan, g4, out)

    out, theirs, j2, plan = together(out, theirs, j2, plan)
    m4 = send((f32(t4[1]) + f32(theirs)).astype(jnp.bfloat16))
    j3, j2x = send(j2), swapped(j2)
    theirs, t3 = terms(plan, 18, 2, grad, w, part)

    theirs, t3, m4, i3, plan = together(theirs, t3, m4, i3, plan)
    theirs = swapped(theirs)
    i4, i3x = send(i3), swapped(i3)
    weight = grad_qkv(plan, f0)

    weight, theirs, j3, plan = together(weight, theirs, j3, plan)
    o3 = send((f32(t3[0]) + f32(theirs[0])).astype(jnp.bfloat16))
    theirs2, t2 = terms(plan, 20, 2, grad, w, part)

    theirs2, t2, o3, i4, plan = together(theirs2, t2, o3, i4, plan)
    m3 = send((f32(t3[1]) + f32(theirs[1]) + f32(m4)).astype(jnp.bfloat16))
    theirs = swapped(theirs2)
    j3x = swapped(j3)
    i4x = swapped(i4)
    weight = grad_qkv(plan, blocks(1, i1, j1, i1x, j1x), weight)

    weight, theirs, m3, plan = together(weight, theirs, m3, plan)
    o2 = send((f32(t2[0]) + f32(theirs[0]) + f32(o3)).astype(jnp.bfloat16))
    theirs1, t1 = terms(plan, 22, 2, grad, w, part)

    theirs1, t1, o2, plan = together(theirs1, t1, o2, plan)
    m2 = send((f32(t2[1]) + f32(theirs[1]) + f32(m3)).astype(jnp.bfloat16))
    theirs = swapped(theirs1)
    weight = grad_qkv(plan, blocks(2, i2, j2, i2x, j2x), weight)

    weight, theirs, m2, plan = together(weight, theirs, m2, plan)
    o1 = send((f32(t1[0]) + f32(theirs[0]) + f32(o2)).astype(jnp.bfloat16))
    (t0,) = terms(plan, 24, 1, grad, w, part)
    weight = grad_qkv(plan, blocks(4, i4, i4x), weight)

    weight, t0, o1, plan = together(weight, t0, o1, plan)
    m1 = send((f32(t1[1]) + f32(theirs[1]) + f32(m2)).astype(jnp.bfloat16))
    theirs = swapped((f32(t0[0]) + f32(o1)).astype(jnp.bfloat16))
    weight = grad_qkv(plan, blocks(3, i3, j3, i3x, j3x), weight)

    weight, theirs, m1 = together(weight, theirs, m1)
    input_grad = f32(t0[1]) + f32(m1) + f32(theirs)
    return input_grad.astype(jnp.bfloat16), weight.transpose(1, 0, 2), out


def solution(mesh):
    placed = (
        P("runs", "gx"),
        P("runs", "gx"),
        P(None, None, "gx"),
        P("gx", None),
        P("runs", None, "gx"),
        P("runs"),
    )
    return jax.shard_map(
        functools.partial(on_device, mesh.shape["gx"]),
        mesh=mesh,
        in_specs=placed,
        out_specs=(P("runs", "gx"), P("runs", None, "gx"), P(("runs", "gx"), None)),
        check_vma=False,
    )
```

time: 165 us -> 135 us (0.82)
  waiting for transfers between devices: 39.1 us -> 19.3 us
  other arithmetic: 12.8 us -> 1.97 us
  Pallas kernels: 69.3 us -> 72.7 us
  local copies, waits for them, and re-layouts: 12.3 us -> 9.96 us
    ppermute x45 -> x42, waiting for transfers between devices: 39.1 us -> 19.3 us  [the longest x21 15.2 us: send(): return lax.ppermute(x, 'gx', ring)]
    another operation x3 -> x0, other arithmetic: 5.8 us -> none  [summed(): at = jnp.stack([chip_at[k % chips] for k in offsets]).astype(jnp.int32)]
    sub x3 -> x0, other arithmetic: 2.72 us -> none  [index_of(): return jnp.concatenate([2 * at + core, 2 * at + 1 - core]).astype(jnp.int32)]
    pallas_call x8 -> x10, Pallas kernels: 28.5 us -> 31.1 us  [weight_grad(): pl.pallas_call(functools.partial(weight_kernel, [place for place, _ in bl...]
    add x4 -> x0, other arithmetic: 2.46 us -> none  [the longest x1 1.99 us: index_of(): return jnp.concatenate([2 * at + core, 2 * at + 1 - core]).astype(jnp.int32)]
    slice x6 -> x0, local copies, waits for them, and re-layouts: 2.14 us -> none  [the longest x4 1.43 us: gathered(): last = jnp.concatenate([send(right[:half], ahead), send(left[half:], back)])]
    pallas_call x4 -> x5, Pallas kernels: 8.48 us -> 9.24 us  [grad_heads(): pl.pallas_call(functools.partial(grad_heads_kernel, count, first, last),...]
    unnamed x28 -> x20, local copies, waits for them, and re-layouts: 6.89 us -> 7.63 us
  transfers between devices with their start and end apart: 45 -> 42, of which waited for: 12 -> 13; matrix products, arithmetic and copies ran while one was open for 11% -> 2% of each run, Pallas kernels for 42% -> 54%
where the time goes in v3:
time: 135 us; the launch traced here: 134 us
  Pallas kernels  72.7 us (54%)
  starting transfers between devices  29.4 us (22%)
  waiting for transfers between devices  19.3 us (14%)
  local copies, waits for them, and re-layouts  9.96 us (7%)
  other arithmetic  1.97 us (1%)
    pallas_call x10, Pallas kernels, weight_grad(): pl.pallas_call(functools.partial(weight_kernel, [place for place, _ in bl...  31.1 us
    ppermute x21, starting transfers between devices, send(): return lax.ppermute(x, 'gx', ring)  24.2 us
    pallas_call x5, Pallas kernels, terms(): pl.pallas_call(terms_kernel, grid_spec=pltpu.PrefetchScalarGridSpec(num_s...  23.6 us
    ppermute x21, waiting for transfers between devices, send(): return lax.ppermute(x, 'gx', ring)  15.2 us
    pallas_call x5, Pallas kernels, grad_heads(): pl.pallas_call(functools.partial(grad_heads_kernel, count, first, last),...  9.24 us
    unnamed x20, local copies, waits for them, and re-layouts  7.63 us
    ppermute x21, starting transfers between devices, swapped(): return lax.ppermute(x, 'gx', swap)  5.24 us
    pallas_call x1, Pallas kernels, attend(): pl.pallas_call(attend_kernel, grid=(heads,), in_specs=[pl.BlockSpec((seq,...  4.84 us
  transfers between devices with their start and end apart: 42, of which 13 were waited for; matrix products, arithmetic and copies ran while one was open for 2% of the time, Pallas kernels for 54%

profile of v3, /device:TPU:0, one launch (start us, length us, event | category | flops | bytes accessed | tf_op | source)
XLA Modules:
  0.0 134.4 jit_solution(16898491787171608473)
XLA Ops:
  1.1 2.6 %collective-permute-start.2 = (bf16[512,384]{1,0:T(8,128)(2,1)}, bf16[512,384]{1,0:T(8,128)(2,1)S(1)}, u32[]{:S(2)}, u32[]{:S(2)}) collective-permute-start(bf16[512,384]{1,0:T(8,128)(2,1)} %refs_0_.3), channel_id=1, source_target_pairs={{2,0},{0,4},{4,8},{8,12},{12,14},{14,10},{10,6},{6,2},{1,3},{5,1},... | collective-permute-start | bytes 1179656 | tf_op jit(solution)/shard_map/ppermute | solution.py:300
  10.4 4.8 %shard_map.94 = (bf16[4,512,512]{2,1,0:T(8,128)(2,1)S(1)}, bf16[512,512]{1,0:T(8,128)(2,1)S(1)}, bf16[512,512]{1,0:T(8,128)(2,1)S(1)}) custom-call(s32[512,1]{1,0:T(8,128)S(1)} %copy-done.8, s32[1,512]{1,0:T(1,128)S(1)} %bitcast.41, bf16[3,512,512]{2,1,0:T(8,128)(2,1)S(1)} %bitcast.38), custom_call_target="tpu_custom_call" | custom-call | flops 131072 | bytes 1280 | tf_op jit(solution)/shard_map/pallas_call | solution.py:45
  18.3 2.8 %copy-done = bf16[512,6144]{1,0:T(8,128)(2,1)S(1)} copy-done((bf16[512,6144]{1,0:T(8,128)(2,1)S(1)}, bf16[512,6144]{1,0:T(8,128)(2,1)}, u32[]{:S(2)}) %copy-start) | copy-done | bytes 6291480
  22.1 2.3 %shard_map.95.refs_8_ = f32[512,512]{1,0:T(8,128)S(1)} custom-call(s32[25]{0:T(128)S(1)} %dynamic_slice.3.plan_ref, bf16[512,384]{1,0:T(8,128)(2,1)S(1)} %copy-done.4, bf16[512,384]{1,0:T(8,128)(2,1)} %collective-permute-done.refs_1_, bf16[512,6144]{1,0:T(8,128)(2,1)S(1)} %copy-done, bf16[512,6144]{1,0:T(8,128)(2,1)S(1)} %copy-done), custom_call_target="tpu_custom_call" | custom-call | flops 98304 | bytes 512 | tf_op jit(solution)/shard_map/pallas_call | solution.py:120
  26.6 2.5 %shard_map.96.refs_4_ = bf16[512,6144]{1,0:T(8,128)(2,1)} custom-call(s32[25]{0:T(128)S(1)} %dynamic_slice.3.plan_ref, bf16[512,512]{1,0:T(8,128)(2,1)S(1)} %get-tuple-element.86.left_ref, bf16[512,384]{1,0:T(8,128)(2,1)S(1)} %copy-done.4, bf16[512,384]{1,0:T(8,128)(2,1)} %collective-permute-done.refs_1_), custom_call_target="tpu_custom_call" | custom-call | flops 98304 | bytes 288 | tf_op jit(solution)/shard_map/pallas_call | solution.py:172
  34.4 2.6 %shard_map.98.refs_4_ = bf16[512,6144]{1,0:T(8,128)(2,1)} custom-call(s32[25]{0:T(128)S(1)} %dynamic_slice.3.plan_ref, bf16[512,512]{1,0:T(8,128)(2,1)S(1)} %get-tuple-element.86.left_ref, bf16[512,384]{1,0:T(8,128)(2,1)S(1)} %collective-permute-done.2.refs_0_, bf16[512,384]{1,0:T(8,128)(2,1)S(1)} %collective-permute-done.1.refs_1_, ...), custom_call_target="tpu_custom_call", output_to_operand_aliasing={{}: (6, {})} | custom-call | flops 196608 | bytes 576 | tf_op jit(solution)/shard_map/pallas_call | solution.py:172
  39.0 2.2 %collective-permute-done.7.refs_1_ = bf16[512,384]{1,0:T(8,128)(2,1)S(1)} collective-permute-done((bf16[512,384]{1,0:T(8,128)(2,1)S(1)}, bf16[512,384]{1,0:T(8,128)(2,1)S(1)}, u32[]{:S(2)}, u32[]{:S(2)}) %collective-permute-start.7) | collective-permute-done | bytes 393248 | tf_op jit(solution)/shard_map/ppermute | solution.py:300
  44.8 2.6 %shard_map.100.refs_4_ = bf16[512,6144]{1,0:T(8,128)(2,1)} custom-call(s32[25]{0:T(128)S(1)} %dynamic_slice.3.plan_ref, bf16[512,512]{1,0:T(8,128)(2,1)S(1)} %get-tuple-element.86.left_ref, bf16[512,384]{1,0:T(8,128)(2,1)S(1)} %collective-permute-done.4.refs_0_, bf16[512,384]{1,0:T(8,128)(2,1)S(1)} %collective-permute-done.3.refs_1_, ...), custom_call_target="tpu_custom_call", output_to_operand_aliasing={{}: (6, {})} | custom-call | flops 196608 | bytes 576 | tf_op jit(solution)/shard_map/pallas_call | solution.py:172
  51.1 2.6 %shard_map.102.refs_2_ = bf16[512,6144]{1,0:T(8,128)(2,1)} custom-call(s32[25]{0:T(128)S(1)} %dynamic_slice.3.plan_ref, bf16[512,512]{1,0:T(8,128)(2,1)S(1)} %get-tuple-element.86.left_ref, bf16[512,384]{1,0:T(8,128)(2,1)S(1)} %collective-permute-done.8.refs_0_, bf16[512,384]{1,0:T(8,128)(2,1)S(1)} %collective-permute-done.7.refs_1_, ...), custom_call_target="tpu_custom_call", output_to_operand_aliasing={{}: (6, {})} | custom-call | flops 196608 | bytes 576 | tf_op jit(solution)/shard_map/pallas_call | solution.py:172
  56.6 4.0 %shard_map.104.grad_ref.left_ref = bf16[3,512,512]{2,1,0:T(8,128)(2,1)S(1)} custom-call(bf16[3,512,512]{2,1,0:T(8,128)(2,1)S(1)} %bitcast.39, bf16[4,512,512]{2,1,0:T(8,128)(2,1)S(1)} %get-tuple-element.80.attn_ref, bf16[512,512]{1,0:T(8,128)(2,1)S(1)} %copy-done.6, bf16[512,512]{1,0:T(8,128)(2,1)S(1)} %shard_map.103.grad_ref), custom_call_target="tpu_custom_call" | custom-call | flops 262144 | bytes 1536 | tf_op jit(solution)/shard_map/pallas_call | solution.py:85
  62.2 3.9 %shard_map.105 = bf16[2,512,384]{2,1,0:T(8,128)(2,1)S(1)} custom-call(s32[25]{0:T(128)S(1)} %dynamic_slice.3.plan_ref, bf16[3,512,512]{2,1,0:T(8,128)(2,1)S(1)} %shard_map.104.grad_ref.left_ref, bf16[3,6144,512]{2,1,0:T(8,128)(2,1)} %bitcast.42), custom_call_target="tpu_custom_call" | custom-call | flops 294912 | bytes 1280 | tf_op jit(solution)/shard_map/pallas_call | solution.py:214
  66.7 2.0 %shard_map.106 = bf16[512,6144]{1,0:T(8,128)(2,1)} custom-call(s32[25]{0:T(128)S(1)} %dynamic_slice.3.plan_ref, bf16[512,512]{1,0:T(8,128)(2,1)S(1)} %get-tuple-element.86.left_ref, bf16[512,384]{1,0:T(8,128)(2,1)S(1)} %collective-permute-done.14.refs_0_, bf16[512,384]{1,0:T(8,128)(2,1)S(1)} %collective-permute-done.15.refs_1_, ...), custom_call_target="tpu_custom_call", output_to_operand_aliasing={{}: (4, {})} | custom-call | flops 98304 | bytes 288 | tf_op jit(solution)/shard_map/pallas_call | solution.py:172
  70.1 5.3 %shard_map.107 = (bf16[2,512,384]{2,1,0:T(8,128)(2,1)S(1)}, bf16[2,512,384]{2,1,0:T(8,128)(2,1)S(1)}) custom-call(s32[25]{0:T(128)S(1)} %dynamic_slice.3.plan_ref, bf16[3,512,512]{2,1,0:T(8,128)(2,1)S(1)} %shard_map.104.grad_ref.left_ref, bf16[3,6144,512]{2,1,0:T(8,128)(2,1)} %bitcast.43), custom_call_target="tpu_custom_call" | custom-call | flops 589824 | bytes 2560 | tf_op jit(solution)/shard_map/pallas_call | solution.py:214
  75.4 2.8 %collective-permute-done.21 = bf16[512,384]{1,0:T(8,128)(2,1)S(1)} collective-permute-done((bf16[512,384]{1,0:T(8,128)(2,1)S(1)}, bf16[512,384]{1,0:T(8,128)(2,1)S(1)}, u32[]{:S(2)}, u32[]{:S(2)}) %collective-permute-start.21) | collective-permute-done | bytes 393248 | tf_op jit(solution)/shard_map/ppermute | solution.py:300
  78.7 3.0 %shard_map.108.refs_4_ = bf16[3,6144,512]{2,1,0:T(8,128)(2,1)} custom-call(s32[25]{0:T(128)S(1)} %dynamic_slice.3.plan_ref, bf16[3,512,512]{2,1,0:T(8,128)(2,1)S(1)} %shard_map.104.grad_ref.left_ref, bf16[512,384]{1,0:T(8,128)(2,1)S(1)} %copy-done.7, bf16[512,384]{1,0:T(8,128)(2,1)S(1)} %collective-permute-done.11.refs_1_), custom_call_target="tpu_custom_call" | custom-call | flops 294912 | bytes 864 | tf_op jit(solution)/shard_map/pallas_call | solution.py:172
  82.2 3.8 %collective-permute-done.24.refs_1_ = bf16[512,384]{1,0:T(8,128)(2,1)S(1)} collective-permute-done((bf16[512,384]{1,0:T(8,128)(2,1)S(1)}, bf16[512,384]{1,0:T(8,128)(2,1)S(1)}, u32[]{:S(2)}, u32[]{:S(2)}) %collective-permute-start.24) | collective-permute-done | bytes 393248 | tf_op jit(solution)/shard_map/ppermute | solution.py:300
  86.7 5.3 %shard_map.109 = (bf16[2,512,384]{2,1,0:T(8,128)(2,1)S(1)}, bf16[2,512,384]{2,1,0:T(8,128)(2,1)S(1)}) custom-call(s32[25]{0:T(128)S(1)} %dynamic_slice.3.plan_ref, bf16[3,512,512]{2,1,0:T(8,128)(2,1)S(1)} %shard_map.104.grad_ref.left_ref, bf16[3,6144,512]{2,1,0:T(8,128)(2,1)} %bitcast.44), custom_call_target="tpu_custom_call" | custom-call | flops 589824 | bytes 2560 | tf_op jit(solution)/shard_map/pallas_call | solution.py:214
  92.0 2.5 %collective-permute-done.25 = bf16[512,384]{1,0:T(8,128)(2,1)S(1)} collective-permute-done((bf16[512,384]{1,0:T(8,128)(2,1)S(1)}, bf16[512,384]{1,0:T(8,128)(2,1)S(1)}, u32[]{:S(2)}, u32[]{:S(2)}) %collective-permute-start.25) | collective-permute-done | bytes 393248 | tf_op jit(solution)/shard_map/ppermute | solution.py:300
  97.9 4.2 %shard_map.110.refs_4_ = bf16[3,6144,512]{2,1,0:T(8,128)(2,1)} custom-call(s32[25]{0:T(128)S(1)} %dynamic_slice.3.plan_ref, bf16[3,512,512]{2,1,0:T(8,128)(2,1)S(1)} %shard_map.104.grad_ref.left_ref, bf16[512,384]{1,0:T(8,128)(2,1)S(1)} %collective-permute-done.16.refs_0_, ...), custom_call_target="tpu_custom_call", output_to_operand_aliasing={{}: (6, {})} | custom-call | flops 589824 | bytes 1728 | tf_op jit(solution)/shard_map/pallas_call | solution.py:172
  103.8 5.3 %shard_map.111 = (bf16[2,512,384]{2,1,0:T(8,128)(2,1)S(1)}, bf16[2,512,384]{2,1,0:T(8,128)(2,1)S(1)}) custom-call(s32[25]{0:T(128)S(1)} %dynamic_slice.3.plan_ref, bf16[3,512,512]{2,1,0:T(8,128)(2,1)S(1)} %shard_map.104.grad_ref.left_ref, bf16[3,6144,512]{2,1,0:T(8,128)(2,1)} %bitcast.45), custom_call_target="tpu_custom_call" | custom-call | flops 589824 | bytes 2560 | tf_op jit(solution)/shard_map/pallas_call | solution.py:214
  114.5 4.3 %shard_map.112.refs_2_ = bf16[3,6144,512]{2,1,0:T(8,128)(2,1)} custom-call(s32[25]{0:T(128)S(1)} %dynamic_slice.3.plan_ref, bf16[3,512,512]{2,1,0:T(8,128)(2,1)S(1)} %shard_map.104.grad_ref.left_ref, bf16[512,384]{1,0:T(8,128)(2,1)S(1)} %collective-permute-done.18.refs_0_, ...), custom_call_target="tpu_custom_call", output_to_operand_aliasing={{}: (6, {})} | custom-call | flops 589824 | bytes 1728 | tf_op jit(solution)/shard_map/pallas_call | solution.py:172
  121.0 3.7 %shard_map.114 = bf16[2,512,384]{2,1,0:T(8,128)(2,1)S(1)} custom-call(s32[25]{0:T(128)S(1)} %dynamic_slice.3.plan_ref, bf16[3,512,512]{2,1,0:T(8,128)(2,1)S(1)} %shard_map.104.grad_ref.left_ref, bf16[3,6144,512]{2,1,0:T(8,128)(2,1)} %bitcast.46), custom_call_target="tpu_custom_call" | custom-call | flops 294912 | bytes 1280 | tf_op jit(solution)/shard_map/pallas_call | solution.py:214
  125.2 3.0 %shard_map.113.refs_4_ = bf16[3,6144,512]{2,1,0:T(8,128)(2,1)} custom-call(s32[25]{0:T(128)S(1)} %dynamic_slice.3.plan_ref, bf16[3,512,512]{2,1,0:T(8,128)(2,1)S(1)} %shard_map.104.grad_ref.left_ref, bf16[512,384]{1,0:T(8,128)(2,1)S(1)} %collective-permute-done.26.refs_0_, ...), custom_call_target="tpu_custom_call", output_to_operand_aliasing={{}: (4, {})} | custom-call | flops 294912 | bytes 864 | tf_op jit(solution)/shard_map/pallas_call | solution.py:172
  129.3 4.2 %shard_map.115 = bf16[3,6144,512]{2,1,0:T(8,128)(2,1)} custom-call(s32[25]{0:T(128)S(1)} %dynamic_slice.3.plan_ref, bf16[3,512,512]{2,1,0:T(8,128)(2,1)S(1)} %shard_map.104.grad_ref.left_ref, bf16[512,384]{1,0:T(8,128)(2,1)S(1)} %collective-permute-done.22.refs_0_, ...), custom_call_target="tpu_custom_call", output_to_operand_aliasing={{}: (6, {})} | custom-call | flops 589824 | bytes 1728 | tf_op jit(solution)/shard_map/pallas_call | solution.py:172
  (112 shorter events, 50.8 us)
Async XLA Ops:
  1.1 15.6 %collective-permute-start.2 = (bf16[512,384]{1,0:T(8,128)(2,1)}, bf16[512,384]{1,0:T(8,128)(2,1)S(1)}, u32[]{:S(2)}, u32[]{:S(2)}) collective-permute-start(bf16[512,384]{1,0:T(8,128)(2,1)} %refs_0_.3), channel_id=1, source_target_pairs={{2,0},{0,4},{4,8},{8,12},{12,14},{14,10},{10,6},{6,2},{1,3},{5,1},... | collective-permute-start | bytes 1179656 | tf_op jit(solution)/shard_map/ppermute | solution.py:300
  3.8 20.6 %collective-permute-start.1 = (bf16[512,384]{1,0:T(8,128)(2,1)}, bf16[512,384]{1,0:T(8,128)(2,1)S(1)}, u32[]{:S(2)}, u32[]{:S(2)}) collective-permute-start(bf16[512,384]{1,0:T(8,128)(2,1)} %collective-permute-done.refs_1_), channel_id=1, source_target_pairs={{2,0},{0,4},{4,8},{8,12},{12,14},{14,10},{10,6},{6,2},{1,3},{5,1},... | collective-permute-start | bytes 1179656 | tf_op jit(solution)/shard_map/ppermute | solution.py:300
  16.8 12.3 %collective-permute-start.4 = (bf16[512,384]{1,0:T(8,128)(2,1)S(1)}, bf16[512,384]{1,0:T(8,128)(2,1)S(1)}, u32[]{:S(2)}, u32[]{:S(2)}) collective-permute-start(bf16[512,384]{1,0:T(8,128)(2,1)S(1)} %collective-permute-done.2.refs_0_), channel_id=1, source_target_pairs={{2,0},{0,4},{4,8},{8,12},{12,14},{14,10},{10,6},{6,2},{1,3},{5,1},... | collective-permute-start | bytes 1179656 | tf_op jit(solution)/shard_map/ppermute | solution.py:300
  18.3 12.3 %collective-permute-start.5 = (bf16[512,384]{1,0:T(8,128)(2,1)S(1)}, bf16[512,384]{1,0:T(8,128)(2,1)S(1)}, u32[]{:S(2)}, u32[]{:S(2)}) collective-permute-start(bf16[512,384]{1,0:T(8,128)(2,1)S(1)} %collective-permute-done.2.refs_0_), channel_id=1, source_target_pairs={{0,1},{1,0},{2,3},{3,2},{4,5},{5,4},{6,7},{7,6},{8,9},{9,8},{10,11... | collective-permute-start | bytes 1179656 | tf_op jit(solution)/shard_map/ppermute | solution.py:303
  29.1 7.9 %collective-permute-start.8 = (bf16[512,384]{1,0:T(8,128)(2,1)S(1)}, bf16[512,384]{1,0:T(8,128)(2,1)S(1)}, u32[]{:S(2)}, u32[]{:S(2)}) collective-permute-start(bf16[512,384]{1,0:T(8,128)(2,1)S(1)} %collective-permute-done.4.refs_0_), channel_id=1, source_target_pairs={{2,0},{0,4},{4,8},{8,12},{12,14},{14,10},{10,6},{6,2},{1,3},{5,1},... | collective-permute-start | bytes 1179656 | tf_op jit(solution)/shard_map/ppermute | solution.py:300
  33.2 8.0 %collective-permute-start.7 = (bf16[512,384]{1,0:T(8,128)(2,1)S(1)}, bf16[512,384]{1,0:T(8,128)(2,1)S(1)}, u32[]{:S(2)}, u32[]{:S(2)}) collective-permute-start(bf16[512,384]{1,0:T(8,128)(2,1)S(1)} %collective-permute-done.3.refs_1_), channel_id=1, source_target_pairs={{2,0},{0,4},{4,8},{8,12},{12,14},{14,10},{10,6},{6,2},{1,3},{5,1},... | collective-permute-start | bytes 1179656 | tf_op jit(solution)/shard_map/ppermute | solution.py:300
  37.0 10.4 %collective-permute-start.12 = (bf16[512,384]{1,0:T(8,128)(2,1)S(1)}, bf16[512,384]{1,0:T(8,128)(2,1)S(1)}, u32[]{:S(2)}, u32[]{:S(2)}) collective-permute-start(bf16[512,384]{1,0:T(8,128)(2,1)S(1)} %collective-permute-done.8.refs_0_), channel_id=1, source_target_pairs={{0,1},{1,0},{2,3},{3,2},{4,5},{5,4},{6,7},{7,6},{8,9},{9,8},{10,11... | collective-permute-start | bytes 1179656 | tf_op jit(solution)/shard_map/ppermute | solution.py:303
  43.3 10.4 %collective-permute-start.16 = (bf16[512,384]{1,0:T(8,128)(2,1)S(1)}, bf16[512,384]{1,0:T(8,128)(2,1)S(1)}, u32[]{:S(2)}, u32[]{:S(2)}) collective-permute-start(bf16[512,384]{1,0:T(8,128)(2,1)S(1)} %copy-done.7), channel_id=1, source_target_pairs={{2,0},{0,4},{4,8},{8,12},{12,14},{14,10},{10,6},{6,2},{1,3},{5,1},... | collective-permute-start | bytes 1179656 | tf_op jit(solution)/shard_map/ppermute | solution.py:300
  49.5 11.1 %collective-permute-start.17 = (bf16[512,384]{1,0:T(8,128)(2,1)S(1)}, bf16[512,384]{1,0:T(8,128)(2,1)S(1)}, u32[]{:S(2)}, u32[]{:S(2)}) collective-permute-start(bf16[512,384]{1,0:T(8,128)(2,1)S(1)} %collective-permute-done.11.refs_1_), channel_id=1, source_target_pairs={{2,0},{0,4},{4,8},{8,12},{12,14},{14,10},{10,6},{6,2},{1,3},{5,1},... | collective-permute-start | bytes 1179656 | tf_op jit(solution)/shard_map/ppermute | solution.py:300
  53.7 12.4 %collective-permute-start.18 = (bf16[512,384]{1,0:T(8,128)(2,1)S(1)}, bf16[512,384]{1,0:T(8,128)(2,1)S(1)}, u32[]{:S(2)}, u32[]{:S(2)}) collective-permute-start(bf16[512,384]{1,0:T(8,128)(2,1)S(1)} %collective-permute-done.16.refs_0_), channel_id=1, source_target_pairs={{2,0},{0,4},{4,8},{8,12},{12,14},{14,10},{10,6},{6,2},{1,3},{5,1},... | collective-permute-start | bytes 1179656 | tf_op jit(solution)/shard_map/ppermute | solution.py:300
  60.6 8.2 %collective-permute-start.20 = (bf16[512,384]{1,0:T(8,128)(2,1)S(1)}, bf16[512,384]{1,0:T(8,128)(2,1)S(1)}, u32[]{:S(2)}, u32[]{:S(2)}) collective-permute-start(bf16[512,384]{1,0:T(8,128)(2,1)S(1)} %collective-permute-done.17.refs_1_), channel_id=1, source_target_pairs={{2,0},{0,4},{4,8},{8,12},{12,14},{14,10},{10,6},{6,2},{1,3},{5,1},... | collective-permute-start | bytes 1179656 | tf_op jit(solution)/shard_map/ppermute | solution.py:300
  66.2 9.2 %collective-permute-start.22 = (bf16[512,384]{1,0:T(8,128)(2,1)S(1)}, bf16[512,384]{1,0:T(8,128)(2,1)S(1)}, u32[]{:S(2)}, u32[]{:S(2)}) collective-permute-start(bf16[512,384]{1,0:T(8,128)(2,1)S(1)} %collective-permute-done.18.refs_0_), channel_id=1, source_target_pairs={{2,0},{0,4},{4,8},{8,12},{12,14},{14,10},{10,6},{6,2},{1,3},{5,1},... | collective-permute-start | bytes 1179656 | tf_op jit(solution)/shard_map/ppermute | solution.py:300
  68.9 9.4 %collective-permute-start.21 = (bf16[512,384]{1,0:T(8,128)(2,1)S(1)}, bf16[512,384]{1,0:T(8,128)(2,1)S(1)}, u32[]{:S(2)}, u32[]{:S(2)}) collective-permute-start(bf16[512,384]{1,0:T(8,128)(2,1)S(1)} %fusion.3), channel_id=1, source_target_pairs={{2,0},{0,4},{4,8},{8,12},{12,14},{14,10},{10,6},{6,2},{1,3},{5,1},... | collective-permute-start | bytes 1179656 | tf_op jit(solution)/shard_map/ppermute | solution.py:300
  81.7 10.2 %collective-permute-start.26 = (bf16[512,384]{1,0:T(8,128)(2,1)S(1)}, bf16[512,384]{1,0:T(8,128)(2,1)S(1)}, u32[]{:S(2)}, u32[]{:S(2)}) collective-permute-start(bf16[512,384]{1,0:T(8,128)(2,1)S(1)} %collective-permute-done.22.refs_0_), channel_id=1, source_target_pairs={{2,0},{0,4},{4,8},{8,12},{12,14},{14,10},{10,6},{6,2},{1,3},{5,1},... | collective-permute-start | bytes 1179656 | tf_op jit(solution)/shard_map/ppermute | solution.py:300
  86.2 8.3 %collective-permute-start.25 = (bf16[512,384]{1,0:T(8,128)(2,1)S(1)}, bf16[512,384]{1,0:T(8,128)(2,1)S(1)}, u32[]{:S(2)}, u32[]{:S(2)}) collective-permute-start(bf16[512,384]{1,0:T(8,128)(2,1)S(1)} %fusion.9), channel_id=1, source_target_pairs={{2,0},{0,4},{4,8},{8,12},{12,14},{14,10},{10,6},{6,2},{1,3},{5,1},... | collective-permute-start | bytes 1179656 | tf_op jit(solution)/shard_map/ppermute | solution.py:300
  94.5 8.5 %collective-permute-start.29 = (bf16[2,512,384]{2,1,0:T(8,128)(2,1)S(1)}, bf16[2,512,384]{2,1,0:T(8,128)(2,1)S(1)}, u32[]{:S(2)}, u32[]{:S(2)}) collective-permute-start(bf16[2,512,384]{2,1,0:T(8,128)(2,1)S(1)} %get-tuple-element.129), channel_id=1, source_target_pairs={{0,1},{1,0},{2,3},{3,2},{4,5},{5,4},{6,7},{7,6},{8,9},{9,8},{10,11... | collective-permute-start | bytes 2359304 | tf_op jit(solution)/shard_map/ppermute | solution.py:303
  95.1 7.8 %collective-permute-start.30 = (bf16[512,384]{1,0:T(8,128)(2,1)S(1)}, bf16[512,384]{1,0:T(8,128)(2,1)S(1)}, u32[]{:S(2)}, u32[]{:S(2)}) collective-permute-start(bf16[512,384]{1,0:T(8,128)(2,1)S(1)} %fusion.8), channel_id=1, source_target_pairs={{2,0},{0,4},{4,8},{8,12},{12,14},{14,10},{10,6},{6,2},{1,3},{5,1},... | collective-permute-start | bytes 1179656 | tf_op jit(solution)/shard_map/ppermute | solution.py:300
  103.3 7.8 %collective-permute-start.31 = (bf16[512,384]{1,0:T(8,128)(2,1)S(1)}, bf16[512,384]{1,0:T(8,128)(2,1)S(1)}, u32[]{:S(2)}, u32[]{:S(2)}) collective-permute-start(bf16[512,384]{1,0:T(8,128)(2,1)S(1)} %get-tuple-element.160), channel_id=1, source_target_pairs={{2,0},{0,4},{4,8},{8,12},{12,14},{14,10},{10,6},{6,2},{1,3},{5,1},... | collective-permute-start | bytes 1179656 | tf_op jit(solution)/shard_map/ppermute | solution.py:300
  111.1 8.3 %collective-permute-start.34 = (bf16[2,512,384]{2,1,0:T(8,128)(2,1)S(1)}, bf16[2,512,384]{2,1,0:T(8,128)(2,1)S(1)}, u32[]{:S(2)}, u32[]{:S(2)}) collective-permute-start(bf16[2,512,384]{2,1,0:T(8,128)(2,1)S(1)} %get-tuple-element.139), channel_id=1, source_target_pairs={{0,1},{1,0},{2,3},{3,2},{4,5},{5,4},{6,7},{7,6},{8,9},{9,8},{10,11... | collective-permute-start | bytes 2359304 | tf_op jit(solution)/shard_map/ppermute | solution.py:303
  112.1 13.1 %collective-permute-start.36 = (bf16[512,384]{1,0:T(8,128)(2,1)S(1)}, bf16[512,384]{1,0:T(8,128)(2,1)S(1)}, u32[]{:S(2)}, u32[]{:S(2)}) collective-permute-start(bf16[512,384]{1,0:T(8,128)(2,1)S(1)} %collective-permute-done.26.refs_0_), channel_id=1, source_target_pairs={{0,1},{1,0},{2,3},{3,2},{4,5},{5,4},{6,7},{7,6},{8,9},{9,8},{10,11... | collective-permute-start | bytes 1179656 | tf_op jit(solution)/shard_map/ppermute | solution.py:303
  119.7 8.5 %collective-permute-start.37 = (bf16[512,384]{1,0:T(8,128)(2,1)S(1)}, bf16[512,384]{1,0:T(8,128)(2,1)S(1)}, u32[]{:S(2)}, u32[]{:S(2)}) collective-permute-start(bf16[512,384]{1,0:T(8,128)(2,1)S(1)} %get-tuple-element.158), channel_id=1, source_target_pairs={{2,0},{0,4},{4,8},{8,12},{12,14},{14,10},{10,6},{6,2},{1,3},{5,1},... | collective-permute-start | bytes 1179656 | tf_op jit(solution)/shard_map/ppermute | solution.py:300
  120.4 8.8 %collective-permute-start.38 = (bf16[512,384]{1,0:T(8,128)(2,1)S(1)}, bf16[512,384]{1,0:T(8,128)(2,1)S(1)}, u32[]{:S(2)}, u32[]{:S(2)}) collective-permute-start(bf16[512,384]{1,0:T(8,128)(2,1)S(1)} %collective-permute-done.22.refs_0_), channel_id=1, source_target_pairs={{0,1},{1,0},{2,3},{3,2},{4,5},{5,4},{6,7},{7,6},{8,9},{9,8},{10,11... | collective-permute-start | bytes 1179656 | tf_op jit(solution)/shard_map/ppermute | solution.py:303
  120.4 8.8 %collective-permute-start.39 = (bf16[512,384]{1,0:T(8,128)(2,1)S(1)}, bf16[512,384]{1,0:T(8,128)(2,1)S(1)}, u32[]{:S(2)}, u32[]{:S(2)}) collective-permute-start(bf16[512,384]{1,0:T(8,128)(2,1)S(1)} %collective-permute-done.24.refs_1_), channel_id=1, source_target_pairs={{0,1},{1,0},{2,3},{3,2},{4,5},{5,4},{6,7},{7,6},{8,9},{9,8},{10,11... | collective-permute-start | bytes 1179656 | tf_op jit(solution)/shard_map/ppermute | solution.py:303
  124.7 8.8 %collective-permute-start.41 = (bf16[512,384]{1,0:T(8,128)(2,1)S(1)}, bf16[512,384]{1,0:T(8,128)(2,1)S(1)}, u32[]{:S(2)}, u32[]{:S(2)}) collective-permute-start(bf16[512,384]{1,0:T(8,128)(2,1)S(1)} %get-tuple-element.157), channel_id=1, source_target_pairs={{2,0},{0,4},{4,8},{8,12},{12,14},{14,10},{10,6},{6,2},{1,3},{5,1},... | collective-permute-start | bytes 1179656 | tf_op jit(solution)/shard_map/ppermute | solution.py:300
  (28 other events, 119.0 us)

commit v4 on v3

--- a/solution.py
+++ b/solution.py
@@ -28,9 +28,15 @@
     return pl.CostEstimate(flops=flops, bytes_accessed=nbytes, transcendentals=transcendentals)
 
 
-def attend_kernel(col_ref, row_ref, qkv_ref, attn_ref, out_ref, out_t_ref):
+def attend_kernel(row_ref, qkv_ref, attn_ref, out_ref, out_t_ref, column):
+    row = row_ref[...]
+
+    @pl.when(pl.program_id(0) == 0)
+    def _():
+        column[...] = jnp.broadcast_to(row, (HD, row.shape[1])).T
+
     scores = dot(qkv_ref[0], qkv_ref[1], NT) * FACTOR
-    scores = jnp.where(row_ref[...] <= col_ref[...], scores, -1e30)
+    scores = jnp.where(row <= column[:, :1], scores, -1e30)
     expd = jnp.exp(scores - jnp.max(scores, axis=1, keepdims=True))
     attn = (expd / jnp.sum(expd, axis=1, keepdims=True)).astype(jnp.bfloat16)
     attn_ref[0] = attn
@@ -46,7 +52,6 @@
         attend_kernel,
         grid=(heads,),
         in_specs=[
-            pl.BlockSpec((seq, 1), lambda h: (0, 0)),
             pl.BlockSpec((1, seq), lambda h: (0, 0)),
             pl.BlockSpec((3, seq, HD), lambda h: (0, 0, h)),
         ],
@@ -60,9 +65,10 @@
             jax.ShapeDtypeStruct((seq, columns), jnp.bfloat16),
             jax.ShapeDtypeStruct((columns, seq), jnp.bfloat16),
         ],
-        compiler_params=params(24),
+        scratch_shapes=[pltpu.VMEM((seq, HD), jnp.int32)],
+        compiler_params=params(60),
         cost_estimate=cost(4 * seq * seq * columns, 5 * MIB, heads * seq * seq),
-    )(positions[:, None], positions[None, :], qkv)
+    )(positions[None, :], qkv)
 
 
 def attend_back_kernel(qkv_ref, attn_ref, attended_ref, grad_ref, out_ref):
@@ -129,7 +135,7 @@
             scratch_shapes=[pltpu.VMEM((seq, columns), jnp.float32)],
         ),
         out_shape=jax.ShapeDtypeStruct((seq, columns), jnp.bfloat16 if last else jnp.float32),
-        compiler_params=params(40),
+        compiler_params=params(48),
         cost_estimate=cost(2 * seq * columns * part * count, MIB * count),
     )(plan, *[block for _, block in blocks], *[w_out] * count, *([] if first else [total]))
 
@@ -186,7 +192,7 @@
     )(plan, left, *[block for _, block in blocks], *([] if into is None else [into]))
 
 
-def terms_kernel(plan_ref, grad_ref, w_ref, *out_refs):
+def terms_kernel(receivers, plan_ref, grad_ref, w_ref, *out_refs):
     total = dot(grad_ref[0], w_ref[0], NT)
     total += dot(grad_ref[1], w_ref[1], NT)
     total += dot(grad_ref[2], w_ref[2], NT)
@@ -194,7 +200,7 @@
     part = total.shape[1] // 2
     step = pl.program_id(0)
     for i, out_ref in enumerate(out_refs):
-        core = plan_ref[0] if i == len(out_refs) - 1 else 1 - plan_ref[0]
+        core = 1 - plan_ref[0] if receivers[i] else plan_ref[0]
 
         @pl.when((step == i) & (core == 0))
         def _():
@@ -207,12 +213,13 @@
             out_ref[1] = total[:, part:]
 
 
-def terms(plan, place, count, grad, w, part):
+def terms(plan, place, receivers, grad, w, part):
     _, seq, columns = grad.shape
+    count = len(receivers)
     out = pl.BlockSpec((2, seq, part), lambda i, plan: (0, 0, 0))
     shape = jax.ShapeDtypeStruct((2, seq, part), jnp.bfloat16)
     return pl.pallas_call(
-        terms_kernel,
+        functools.partial(terms_kernel, receivers),
         grid_spec=pltpu.PrefetchScalarGridSpec(
             num_scalar_prefetch=1,
             grid=(count,),
@@ -306,11 +313,14 @@
         first = 1 if step == 0 else 4 * step - 1
         return [(first + i, array) for i, array in enumerate(arrays)]
 
-    def grad_out(index, some, into=None):
-        return weight_grad(index, attended_t, some, w_out.shape, into)
-
     def grad_qkv(index, some, into=None):
         return weight_grad(index, grad, some, w.shape, into)
+
+    def total(*values):
+        return sum(f32(value) for value in values[1:]) + f32(values[0])
+
+    def rounded_total(*values):
+        return total(*values).astype(jnp.bfloat16)
 
     qkv = saved_qkv.transpose(1, 0, 2)
     w = w_qkv.transpose(1, 0, 2)
@@ -320,10 +330,16 @@
     b1 = send(other)
     attn, attended, attended_t = attend(positions, qkv)
 
+    def grad_out_heads(index, some, so_far=None, last=False):
+        return grad_heads(index, w_out, some, so_far, last)
+
+    def grad_out(index, some, into=None):
+        return weight_grad(index, attended_t, some, w_out.shape, into)
+
     a1 = after(a1, attended)
     a2, a1x = send(a1), swapped(a1)
     g0 = blocks(0, out_grad, other)
-    grad_h = grad_heads(after(plan, a1), w_out, g0)
+    grad_h = grad_out_heads(after(plan, a1), g0)
 
     b1 = after(b1, grad_h)
     b2, b1x = send(b1), swapped(b1)
@@ -332,7 +348,7 @@
     a2 = after(a2, out)
     a3, a2x = send(a2), swapped(a2)
     g1 = blocks(1, a1, b1, a1x, b1x)
-    grad_h = grad_heads(after(plan, a2), w_out, g1, grad_h)
+    grad_h = grad_out_heads(after(plan, a2), g1, grad_h)
 
     b2 = after(b2, grad_h)
     b3, b2x = send(b2), swapped(b2)
@@ -340,84 +356,71 @@
 
     a3 = after(a3, out)
     a4, a3x = send(a3), swapped(a3)
-    g2 = blocks(2, a2, b2, a2x, b2x)
-    grad_h = grad_heads(after(plan, a3), w_out, g2, grad_h)
-
-    b3 = after(b3, grad_h)
-    b3x = swapped(b3)
-    inputs = after(inputs, b3)
+    inputs = after(inputs, a3)
     other = swapped(inputs)
     i1 = send(inputs)
-    out = grad_out(after(plan, b3), g2, out)
-
-    out, other, a3x, b3x, plan = together(out, other, a3x, b3x, plan)
+    g2 = blocks(2, a2, b2, a2x, b2x)
+    grad_h = grad_out_heads(after(plan, a3), g2, grad_h)
+
+    b3, grad_h, other, plan = together(b3, grad_h, other, plan)
+    b3x = swapped(b3)
     j1 = send(other)
     f0 = blocks(0, inputs, other)
+    out = grad_out(plan, g2, out)
+
+    out, a3x, b3x, plan = together(out, a3x, b3x, plan)
     g3 = blocks(3, a3, b3, a3x, b3x)
-    grad_h = grad_heads(plan, w_out, g3, grad_h)
-
-    grad_h, a4, plan = together(grad_h, a4, plan)
+    grad_h = grad_out_heads(plan, g3, grad_h)
+
+    grad_h, a4, i1, plan = together(grad_h, a4, i1, plan)
     a4x = swapped(a4)
-    out = grad_out(plan, g3, out)
-
-    out, a4x, i1, plan = together(out, a4x, i1, plan)
     i2, i1x = send(i1), swapped(i1)
+
+    a4x, j1, plan = together(a4x, j1, plan)
+    j2, j1x = send(j1), swapped(j1)
     g4 = blocks(4, a4, a4x)
-    grad_h = grad_heads(plan, w_out, g4, grad_h, last=True)
+    grad_h = grad_out_heads(plan, g4, grad_h, last=True)
     grad = attend_back(qkv, attn, attended, grad_h)
 
-    grad, j1, plan = together(grad, j1, plan)
-    j2, j1x = send(j1), swapped(j1)
-    (t4,) = terms(plan, 17, 1, grad, w, part)
-
-    t4, i2, plan = together(t4, i2, plan)
-    theirs = swapped(t4[0])
+    grad, i2, plan = together(grad, i2, plan)
     i3, i2x = send(i2), swapped(i2)
-    out = grad_out(plan, g4, out)
-
-    out, theirs, j2, plan = together(out, theirs, j2, plan)
-    m4 = send((f32(t4[1]) + f32(theirs)).astype(jnp.bfloat16))
+    t4, theirs3, t3 = terms(plan, 17, (0, 1, 0), grad, w, part)
+
+    t4, theirs3, t3, j2, i3, plan = together(t4, theirs3, t3, j2, i3, plan)
+    theirs4 = swapped(t4[0])
+    theirs3 = swapped(theirs3)
     j3, j2x = send(j2), swapped(j2)
-    theirs, t3 = terms(plan, 18, 2, grad, w, part)
-
-    theirs, t3, m4, i3, plan = together(theirs, t3, m4, i3, plan)
-    theirs = swapped(theirs)
     i4, i3x = send(i3), swapped(i3)
-    weight = grad_qkv(plan, f0)
-
-    weight, theirs, j3, plan = together(weight, theirs, j3, plan)
-    o3 = send((f32(t3[0]) + f32(theirs[0])).astype(jnp.bfloat16))
-    theirs2, t2 = terms(plan, 20, 2, grad, w, part)
-
-    theirs2, t2, o3, i4, plan = together(theirs2, t2, o3, i4, plan)
-    m3 = send((f32(t3[1]) + f32(theirs[1]) + f32(m4)).astype(jnp.bfloat16))
-    theirs = swapped(theirs2)
+    out = grad_out(plan, g3 + g4, out)
+
+    out, theirs4, theirs3, plan = together(out, theirs4, theirs3, plan)
+    m4 = send(rounded_total(t4[1], theirs4))
+    theirs2, t2 = terms(plan, 20, (1, 0), grad, w, part)
+
+    theirs2, t2, m4, j3, i4, plan = together(theirs2, t2, m4, j3, i4, plan)
+    o3 = send(rounded_total(t3[0], theirs3[0]))
+    m3 = send(rounded_total(t3[1], theirs3[1], m4))
+    theirs2 = swapped(theirs2)
     j3x = swapped(j3)
     i4x = swapped(i4)
-    weight = grad_qkv(plan, blocks(1, i1, j1, i1x, j1x), weight)
-
-    weight, theirs, m3, plan = together(weight, theirs, m3, plan)
-    o2 = send((f32(t2[0]) + f32(theirs[0]) + f32(o3)).astype(jnp.bfloat16))
-    theirs1, t1 = terms(plan, 22, 2, grad, w, part)
-
-    theirs1, t1, o2, plan = together(theirs1, t1, o2, plan)
-    m2 = send((f32(t2[1]) + f32(theirs[1]) + f32(m3)).astype(jnp.bfloat16))
-    theirs = swapped(theirs1)
-    weight = grad_qkv(plan, blocks(2, i2, j2, i2x, j2x), weight)
-
-    weight, theirs, m2, plan = together(weight, theirs, m2, plan)
-    o1 = send((f32(t1[0]) + f32(theirs[0]) + f32(o2)).astype(jnp.bfloat16))
-    (t0,) = terms(plan, 24, 1, grad, w, part)
-    weight = grad_qkv(plan, blocks(4, i4, i4x), weight)
-
-    weight, t0, o1, plan = together(weight, t0, o1, plan)
-    m1 = send((f32(t1[1]) + f32(theirs[1]) + f32(m2)).astype(jnp.bfloat16))
-    theirs = swapped((f32(t0[0]) + f32(o1)).astype(jnp.bfloat16))
-    weight = grad_qkv(plan, blocks(3, i3, j3, i3x, j3x), weight)
-
-    weight, theirs, m1 = together(weight, theirs, m1)
-    input_grad = f32(t0[1]) + f32(m1) + f32(theirs)
-    return input_grad.astype(jnp.bfloat16), weight.transpose(1, 0, 2), out
+    theirs1, t1, t0 = terms(plan, 22, (1, 0, 0), grad, w, part)
+
+    theirs1, t1, t0, theirs2, m3, o3, plan = together(theirs1, t1, t0, theirs2, m3, o3, plan)
+    o2 = send(rounded_total(t2[0], theirs2[0], o3))
+    m2 = send(rounded_total(t2[1], theirs2[1], m3))
+    theirs1 = swapped(theirs1)
+    some = f0 + blocks(1, i1, j1, i1x, j1x) + blocks(4, i4, i4x)
+    weight = grad_qkv(plan, some)
+
+    weight, theirs1, o2, m2, plan = together(weight, theirs1, o2, m2, plan)
+    o1 = send(rounded_total(t1[0], theirs1[0], o2))
+    m1 = send(rounded_total(t1[1], theirs1[1], m2))
+    some = blocks(2, i2, j2, i2x, j2x) + blocks(3, i3, j3, i3x, j3x)
+    weight = grad_qkv(plan, some, weight)
+
+    weight, o1, m1 = together(weight, o1, m1)
+    theirs = swapped(rounded_total(t0[0], o1))
+    return rounded_total(t0[1], m1, theirs), weight.transpose(1, 0, 2), out
 
 
 def solution(mesh):

time: 135 us -> 130 us (0.963)
  local copies, waits for them, and re-layouts: 9.96 us -> 1.87 us
  starting transfers between devices: 29.4 us -> 35.6 us
  Pallas kernels: 72.7 us -> 69.8 us
    ppermute x21, starting transfers between devices: 24.2 us -> 32.2 us  [send(): return lax.ppermute(x, 'gx', ring)]
    unnamed x20 -> x12, local copies, waits for them, and re-layouts: 7.63 us -> 1.08 us
    pallas_call x10 -> x6, Pallas kernels: 31.1 us -> 25.6 us  [weight_grad(): pl.pallas_call(functools.partial(weight_kernel, [place for place, _ in bl...]
    pallas_call x5, Pallas kernels: 9.24 us -> 14.4 us  [grad_heads(): pl.pallas_call(functools.partial(grad_heads_kernel, count, first, last),...]
    ppermute x21, waiting for transfers between devices: 15.2 us -> 18 us  [send(): return lax.ppermute(x, 'gx', ring)]
    pallas_call x6 -> x4, Pallas kernels: 28.4 us -> 25.9 us  [the longest x3 19.3 us: terms(): pl.pallas_call(functools.partial(terms_kernel, receivers), grid_spec=pltp...]
    ppermute x21, waiting for transfers between devices: 4.08 us -> 1.76 us  [swapped(): return lax.ppermute(x, 'gx', swap)]
    ppermute x21, starting transfers between devices: 5.24 us -> 3.43 us  [swapped(): return lax.ppermute(x, 'gx', swap)]
  transfers between devices with their start and end apart: 42 -> 42, of which waited for: 13 -> 10; matrix products, arithmetic and copies ran while one was open for 2% -> 1% of each run, Pallas kernels for 54% -> 54%
where the time goes in v4:
time: 130 us
  Pallas kernels  69.8 us (54%)
  starting transfers between devices  35.6 us (27%)
  waiting for transfers between devices  19.7 us (15%)
  other arithmetic  1.96 us (2%)
  local copies, waits for them, and re-layouts  1.87 us (1%)
    ppermute x21, starting transfers between devices, send(): return lax.ppermute(x, 'gx', ring)  32.2 us
    pallas_call x6, Pallas kernels, weight_grad(): pl.pallas_call(functools.partial(weight_kernel, [place for place, _ in bl...  25.6 us
    pallas_call x3, Pallas kernels, terms(): pl.pallas_call(functools.partial(terms_kernel, receivers), grid_spec=pltp...  19.3 us
    ppermute x21, waiting for transfers between devices, send(): return lax.ppermute(x, 'gx', ring)  18 us
    pallas_call x5, Pallas kernels, grad_heads(): pl.pallas_call(functools.partial(grad_heads_kernel, count, first, last),...  14.4 us
    pallas_call x1, Pallas kernels, attend(): pl.pallas_call(attend_kernel, grid=(heads,), in_specs=[pl.BlockSpec((1, s...  6.57 us
    pallas_call x1, Pallas kernels, attend_back(): pl.pallas_call(attend_back_kernel, grid=(columns // HD,), in_specs=[plane...  3.99 us
    ppermute x21, starting transfers between devices, swapped(): return lax.ppermute(x, 'gx', swap)  3.43 us
  transfers between devices with their start and end apart: 42, of which 10 were waited for; matrix products, arithmetic and copies ran while one was open for 1% of the time, Pallas kernels for 54%

profile of v4, /device:TPU:0, one launch (start us, length us, event | category | flops | bytes accessed | tf_op | source)
XLA Modules:
  0.0 130.0 jit_solution(18278357486965658432)
XLA Ops:
  1.1 2.6 %collective-permute-start.2 = (bf16[512,384]{1,0:T(8,128)(2,1)}, bf16[512,384]{1,0:T(8,128)(2,1)S(1)}, u32[]{:S(2)}, u32[]{:S(2)}) collective-permute-start(bf16[512,384]{1,0:T(8,128)(2,1)} %refs_0_.3), channel_id=1, source_target_pairs={{2,0},{0,4},{4,8},{8,12},{12,14},{14,10},{10,6},{6,2},{1,3},{5,1},... | collective-permute-start | bytes 1179656 | tf_op jit(solution)/shard_map/ppermute | solution.py:307
  3.8 1.9 %collective-permute-start.1 = (bf16[512,384]{1,0:T(8,128)(2,1)S(1)}, bf16[512,384]{1,0:T(8,128)(2,1)S(1)}, u32[]{:S(2)}, u32[]{:S(2)}) collective-permute-start(bf16[512,384]{1,0:T(8,128)(2,1)S(1)} %collective-permute-done.refs_1_), channel_id=1, source_target_pairs={{2,0},{0,4},{4,8},{8,12},{12,14},{14,10},{10,6},{6,2},{1,3},{5,1},... | collective-permute-start | bytes 1179656 | tf_op jit(solution)/shard_map/ppermute | solution.py:307
  5.7 6.6 %shard_map.94 = (bf16[4,512,512]{2,1,0:T(8,128)(2,1)}, bf16[512,512]{1,0:T(8,128)(2,1)}, bf16[512,512]{1,0:T(8,128)(2,1)}) custom-call(s32[1,512]{1,0:T(1,128)} %bitcast.53, bf16[3,512,512]{2,1,0:T(8,128)(2,1)} %bitcast.47), custom_call_target="tpu_custom_call" | custom-call | flops 131072 | bytes 1280 | tf_op jit(solution)/shard_map/pallas_call | solution.py:51
  15.6 2.4 %shard_map.95.refs_8_ = f32[512,512]{1,0:T(8,128)S(1)} custom-call(s32[25]{0:T(128)S(1)} %dynamic_slice.3.plan_ref, bf16[512,384]{1,0:T(8,128)(2,1)S(1)} %copy-done.3, bf16[512,384]{1,0:T(8,128)(2,1)S(1)} %collective-permute-done.refs_1_, bf16[512,6144]{1,0:T(8,128)(2,1)} %refs_3_.3, bf16[512,6144]{1,0:T(8,128)(2,1)} %refs_3_.3), custom_call_target="tpu_custom_call" | custom-call | flops 98304 | bytes 512 | tf_op jit(solution)/shard_map/pallas_call | solution.py:126
  20.1 2.0 %shard_map.96.refs_4_ = bf16[512,6144]{1,0:T(8,128)(2,1)} custom-call(s32[25]{0:T(128)S(1)} %dynamic_slice.3.plan_ref, bf16[512,512]{1,0:T(8,128)(2,1)S(1)} %copy-done, bf16[512,384]{1,0:T(8,128)(2,1)S(1)} %copy-done.3, bf16[512,384]{1,0:T(8,128)(2,1)S(1)} %collective-permute-done.refs_1_), custom_call_target="tpu_custom_call" | custom-call | flops 98304 | bytes 288 | tf_op jit(solution)/shard_map/pallas_call | solution.py:178
  23.8 3.2 %shard_map.97.refs_8_ = f32[512,512]{1,0:T(8,128)S(1)} custom-call(s32[25]{0:T(128)S(1)} %dynamic_slice.3.plan_ref, bf16[512,384]{1,0:T(8,128)(2,1)S(1)} %collective-permute-done.2.refs_0_, bf16[512,384]{1,0:T(8,128)(2,1)S(1)} %collective-permute-done.1.refs_1_, bf16[512,384]{1,0:T(8,128)(2,1)S(1)} %collective-permute-done.5.refs_2_, ...), custom_call_target="tpu_custom_call" | custom-call | flops 196608 | bytes 1024 | tf_op jit(solution)/shard_map/pallas_call | solution.py:126
  27.6 2.6 %shard_map.98.refs_4_ = bf16[512,6144]{1,0:T(8,128)(2,1)} custom-call(s32[25]{0:T(128)S(1)} %dynamic_slice.3.plan_ref, bf16[512,512]{1,0:T(8,128)(2,1)S(1)} %copy-done, bf16[512,384]{1,0:T(8,128)(2,1)S(1)} %collective-permute-done.2.refs_0_, bf16[512,384]{1,0:T(8,128)(2,1)S(1)} %collective-permute-done.1.refs_1_, ...), custom_call_target="tpu_custom_call", output_to_operand_aliasing={{}: (6, {})} | custom-call | flops 196608 | bytes 576 | tf_op jit(solution)/shard_map/pallas_call | solution.py:178
  32.2 3.2 %shard_map.99.refs_8_ = f32[512,512]{1,0:T(8,128)S(1)} custom-call(s32[25]{0:T(128)S(1)} %dynamic_slice.3.plan_ref, bf16[512,384]{1,0:T(8,128)(2,1)S(1)} %collective-permute-done.4.refs_0_, bf16[512,384]{1,0:T(8,128)(2,1)S(1)} %collective-permute-done.3.refs_1_, bf16[512,384]{1,0:T(8,128)(2,1)S(1)} %collective-permute-done.9.refs_2_, ...), custom_call_target="tpu_custom_call" | custom-call | flops 196608 | bytes 1024 | tf_op jit(solution)/shard_map/pallas_call | solution.py:126
  35.4 3.0 %collective-permute-done.7.refs_1_ = bf16[512,384]{1,0:T(8,128)(2,1)S(1)} collective-permute-done((bf16[512,384]{1,0:T(8,128)(2,1)S(1)}, bf16[512,384]{1,0:T(8,128)(2,1)S(1)}, u32[]{:S(2)}, u32[]{:S(2)}) %collective-permute-start.7) | collective-permute-done | bytes 393248 | tf_op jit(solution)/shard_map/ppermute | solution.py:307
  41.9 2.6 %shard_map.100.refs_6_ = bf16[512,6144]{1,0:T(8,128)(2,1)} custom-call(s32[25]{0:T(128)S(1)} %dynamic_slice.3.plan_ref, bf16[512,512]{1,0:T(8,128)(2,1)S(1)} %copy-done, bf16[512,384]{1,0:T(8,128)(2,1)S(1)} %collective-permute-done.4.refs_0_, bf16[512,384]{1,0:T(8,128)(2,1)S(1)} %collective-permute-done.3.refs_1_, ...), custom_call_target="tpu_custom_call", output_to_operand_aliasing={{}: (6, {})} | custom-call | flops 196608 | bytes 576 | tf_op jit(solution)/shard_map/pallas_call | solution.py:178
  44.5 3.2 %shard_map.101.refs_4_ = f32[512,512]{1,0:T(8,128)S(1)} custom-call(s32[25]{0:T(128)S(1)} %dynamic_slice.3.plan_ref, bf16[512,384]{1,0:T(8,128)(2,1)S(1)} %collective-permute-done.8.refs_0_, bf16[512,384]{1,0:T(8,128)(2,1)S(1)} %collective-permute-done.7.refs_1_, bf16[512,384]{1,0:T(8,128)(2,1)S(1)} %collective-permute-done.12.refs_2_, ...), custom_call_target="tpu_custom_call" | custom-call | flops 196608 | bytes 1024 | tf_op jit(solution)/shard_map/pallas_call | solution.py:126
  47.7 2.6 %collective-permute-done.14.refs_0_.refs_4_ = bf16[512,384]{1,0:T(8,128)(2,1)S(1)} collective-permute-done((bf16[512,384]{1,0:T(8,128)(2,1)S(1)}, bf16[512,384]{1,0:T(8,128)(2,1)S(1)}, u32[]{:S(2)}, u32[]{:S(2)}) %collective-permute-start.14) | collective-permute-done | bytes 393248 | tf_op jit(solution)/shard_map/ppermute | solution.py:307
  51.9 2.6 %collective-permute-done.17.refs_3_ = bf16[512,384]{1,0:T(8,128)(2,1)S(1)} collective-permute-done((bf16[512,384]{1,0:T(8,128)(2,1)S(1)}, bf16[512,384]{1,0:T(8,128)(2,1)S(1)}, u32[]{:S(2)}, u32[]{:S(2)}) %collective-permute-start.17) | collective-permute-done | bytes 393248 | tf_op jit(solution)/shard_map/ppermute | solution.py:307
  54.6 2.4 %shard_map.102.grad_ref = bf16[512,512]{1,0:T(8,128)(2,1)S(1)} custom-call(s32[25]{0:T(128)S(1)} %dynamic_slice.3.plan_ref, bf16[512,384]{1,0:T(8,128)(2,1)S(1)} %collective-permute-done.14.refs_0_.refs_4_, bf16[512,384]{1,0:T(8,128)(2,1)S(1)} %collective-permute-done.16.refs_1_.refs_5_, bf16[512,6144]{1,0:T(8,128)(2,1)} %refs_3_.3, ...), custom_call_target="tpu_custom_call" | custom-call | flops 98304 | bytes 512 | tf_op jit(solution)/shard_map/pallas_call | solution.py:126
  57.0 4.0 %shard_map.103.grad_ref.left_ref = bf16[3,512,512]{2,1,0:T(8,128)(2,1)S(1)} custom-call(bf16[3,512,512]{2,1,0:T(8,128)(2,1)S(1)} %bitcast.48, bf16[4,512,512]{2,1,0:T(8,128)(2,1)S(1)} %copy-done.1, bf16[512,512]{1,0:T(8,128)(2,1)S(1)} %copy-done.4, bf16[512,512]{1,0:T(8,128)(2,1)S(1)} %shard_map.102.grad_ref), custom_call_target="tpu_custom_call" | custom-call | flops 262144 | bytes 1536 | tf_op jit(solution)/shard_map/pallas_call | solution.py:91
  64.1 7.0 %shard_map.104 = (bf16[2,512,384]{2,1,0:T(8,128)(2,1)S(1)}, bf16[2,512,384]{2,1,0:T(8,128)(2,1)S(1)}, bf16[2,512,384]{2,1,0:T(8,128)(2,1)S(1)}) custom-call(s32[25]{0:T(128)S(1)} %dynamic_slice.3.plan_ref, bf16[3,512,512]{2,1,0:T(8,128)(2,1)S(1)} %shard_map.103.grad_ref.left_ref, bf16[3,6144,512]{2,1,0:T(8,128)(2,1)} %bitcast.49), custom_call_target="tpu_custom_call" | custom-call | flops 884736 | bytes 3840 | tf_op jit(solution)/shard_map/pallas_call | solution.py:221
  71.2 1.9 %collective-permute-done.19.refs_1_ = bf16[512,384]{1,0:T(8,128)(2,1)S(1)} collective-permute-done((bf16[512,384]{1,0:T(8,128)(2,1)S(1)}, bf16[512,384]{1,0:T(8,128)(2,1)S(1)}, u32[]{:S(2)}, u32[]{:S(2)}) %collective-permute-start.19) | collective-permute-done | bytes 393248 | tf_op jit(solution)/shard_map/ppermute | solution.py:307
  76.8 3.5 %shard_map.105 = bf16[512,6144]{1,0:T(8,128)(2,1)} custom-call(s32[25]{0:T(128)S(1)} %dynamic_slice.3.plan_ref, bf16[512,512]{1,0:T(8,128)(2,1)S(1)} %copy-done, bf16[512,384]{1,0:T(8,128)(2,1)S(1)} %collective-permute-done.8.refs_0_, bf16[512,384]{1,0:T(8,128)(2,1)S(1)} %collective-permute-done.7.refs_1_, ...), custom_call_target="tpu_custom_call", output_to_operand_aliasing={{}: (8, {})} | custom-call | flops 294912 | bytes 864 | tf_op jit(solution)/shard_map/pallas_call | solution.py:178
  80.9 5.3 %shard_map.106 = (bf16[2,512,384]{2,1,0:T(8,128)(2,1)S(1)}, bf16[2,512,384]{2,1,0:T(8,128)(2,1)S(1)}) custom-call(s32[25]{0:T(128)S(1)} %dynamic_slice.3.plan_ref, bf16[3,512,512]{2,1,0:T(8,128)(2,1)S(1)} %shard_map.103.grad_ref.left_ref, bf16[3,6144,512]{2,1,0:T(8,128)(2,1)} %bitcast.50), custom_call_target="tpu_custom_call" | custom-call | flops 589824 | bytes 2560 | tf_op jit(solution)/shard_map/pallas_call | solution.py:221
  86.2 3.7 %collective-permute-done.23 = bf16[512,384]{1,0:T(8,128)(2,1)S(1)} collective-permute-done((bf16[512,384]{1,0:T(8,128)(2,1)S(1)}, bf16[512,384]{1,0:T(8,128)(2,1)S(1)}, u32[]{:S(2)}, u32[]{:S(2)}) %collective-permute-start.23) | collective-permute-done | bytes 393248 | tf_op jit(solution)/shard_map/ppermute | solution.py:307
  93.3 7.0 %shard_map.107 = (bf16[2,512,384]{2,1,0:T(8,128)(2,1)S(1)}, bf16[2,512,384]{2,1,0:T(8,128)(2,1)S(1)}, bf16[2,512,384]{2,1,0:T(8,128)(2,1)S(1)}) custom-call(s32[25]{0:T(128)S(1)} %dynamic_slice.3.plan_ref, bf16[3,512,512]{2,1,0:T(8,128)(2,1)S(1)} %shard_map.103.grad_ref.left_ref, bf16[3,6144,512]{2,1,0:T(8,128)(2,1)} %bitcast.51), custom_call_target="tpu_custom_call" | custom-call | flops 884736 | bytes 3840 | tf_op jit(solution)/shard_map/pallas_call | solution.py:221
  106.5 7.5 %shard_map.108.refs_8_ = bf16[3,6144,512]{2,1,0:T(8,128)(2,1)} custom-call(s32[25]{0:T(128)S(1)} %dynamic_slice.3.plan_ref, bf16[3,512,512]{2,1,0:T(8,128)(2,1)S(1)} %shard_map.103.grad_ref.left_ref, bf16[512,384]{1,0:T(8,128)(2,1)S(1)} %copy-done.5, bf16[512,384]{1,0:T(8,128)(2,1)S(1)} %collective-permute-done.11.refs_1_, ...), custom_call_target="tpu_custom_call" | custom-call | flops 1179648 | bytes 3456 | tf_op jit(solution)/shard_map/pallas_call | solution.py:178
  118.4 7.5 %shard_map.109 = bf16[3,6144,512]{2,1,0:T(8,128)(2,1)} custom-call(s32[25]{0:T(128)S(1)} %dynamic_slice.3.plan_ref, bf16[3,512,512]{2,1,0:T(8,128)(2,1)S(1)} %shard_map.103.grad_ref.left_ref, bf16[512,384]{1,0:T(8,128)(2,1)S(1)} %collective-permute-done.18.refs_0_, ...), custom_call_target="tpu_custom_call", output_to_operand_aliasing={{}: (10, {})} | custom-call | flops 1179648 | bytes 3456 | tf_op jit(solution)/shard_map/pallas_call | solution.py:178
  127.4 1.7 %collective-permute-done.41 = bf16[512,384]{1,0:T(8,128)(2,1)S(1)} collective-permute-done((bf16[512,384]{1,0:T(8,128)(2,1)S(1)}, bf16[512,384]{1,0:T(8,128)(2,1)S(1)}, u32[]{:S(2)}, u32[]{:S(2)}) %collective-permute-start.41) | collective-permute-done | bytes 393248 | tf_op jit(solution)/shard_map/ppermute | solution.py:310
  (97 shorter events, 39.2 us)
Async XLA Ops:
  1.1 11.1 %collective-permute-start.2 = (bf16[512,384]{1,0:T(8,128)(2,1)}, bf16[512,384]{1,0:T(8,128)(2,1)S(1)}, u32[]{:S(2)}, u32[]{:S(2)}) collective-permute-start(bf16[512,384]{1,0:T(8,128)(2,1)} %refs_0_.3), channel_id=1, source_target_pairs={{2,0},{0,4},{4,8},{8,12},{12,14},{14,10},{10,6},{6,2},{1,3},{5,1},... | collective-permute-start | bytes 1179656 | tf_op jit(solution)/shard_map/ppermute | solution.py:307
  3.8 14.3 %collective-permute-start.1 = (bf16[512,384]{1,0:T(8,128)(2,1)S(1)}, bf16[512,384]{1,0:T(8,128)(2,1)S(1)}, u32[]{:S(2)}, u32[]{:S(2)}) collective-permute-start(bf16[512,384]{1,0:T(8,128)(2,1)S(1)} %collective-permute-done.refs_1_), channel_id=1, source_target_pairs={{2,0},{0,4},{4,8},{8,12},{12,14},{14,10},{10,6},{6,2},{1,3},{5,1},... | collective-permute-start | bytes 1179656 | tf_op jit(solution)/shard_map/ppermute | solution.py:307
  12.2 10.0 %collective-permute-start.4 = (bf16[512,384]{1,0:T(8,128)(2,1)S(1)}, bf16[512,384]{1,0:T(8,128)(2,1)S(1)}, u32[]{:S(2)}, u32[]{:S(2)}) collective-permute-start(bf16[512,384]{1,0:T(8,128)(2,1)S(1)} %collective-permute-done.2.refs_0_), channel_id=1, source_target_pairs={{2,0},{0,4},{4,8},{8,12},{12,14},{14,10},{10,6},{6,2},{1,3},{5,1},... | collective-permute-start | bytes 1179656 | tf_op jit(solution)/shard_map/ppermute | solution.py:307
  32.1 12.3 %collective-permute-start.12 = (bf16[512,384]{1,0:T(8,128)(2,1)S(1)}, bf16[512,384]{1,0:T(8,128)(2,1)S(1)}, u32[]{:S(2)}, u32[]{:S(2)}) collective-permute-start(bf16[512,384]{1,0:T(8,128)(2,1)S(1)} %collective-permute-done.8.refs_0_), channel_id=1, source_target_pairs={{0,1},{1,0},{2,3},{3,2},{4,5},{5,4},{6,7},{7,6},{8,9},{9,8},{10,11... | collective-permute-start | bytes 1179656 | tf_op jit(solution)/shard_map/ppermute | solution.py:310
  38.3 9.4 %collective-permute-start.15 = (bf16[512,384]{1,0:T(8,128)(2,1)S(1)}, bf16[512,384]{1,0:T(8,128)(2,1)S(1)}, u32[]{:S(2)}, u32[]{:S(2)}) collective-permute-start(bf16[512,384]{1,0:T(8,128)(2,1)S(1)} %copy-done.5), channel_id=1, source_target_pairs={{2,0},{0,4},{4,8},{8,12},{12,14},{14,10},{10,6},{6,2},{1,3},{5,1},... | collective-permute-start | bytes 1179656 | tf_op jit(solution)/shard_map/ppermute | solution.py:307
  39.9 10.4 %collective-permute-start.14 = (bf16[512,384]{1,0:T(8,128)(2,1)S(1)}, bf16[512,384]{1,0:T(8,128)(2,1)S(1)}, u32[]{:S(2)}, u32[]{:S(2)}) collective-permute-start(bf16[512,384]{1,0:T(8,128)(2,1)S(1)} %collective-permute-done.8.refs_0_), channel_id=1, source_target_pairs={{2,0},{0,4},{4,8},{8,12},{12,14},{14,10},{10,6},{6,2},{1,3},{5,1},... | collective-permute-start | bytes 1179656 | tf_op jit(solution)/shard_map/ppermute | solution.py:307
  41.4 13.1 %collective-permute-start.17 = (bf16[512,384]{1,0:T(8,128)(2,1)S(1)}, bf16[512,384]{1,0:T(8,128)(2,1)S(1)}, u32[]{:S(2)}, u32[]{:S(2)}) collective-permute-start(bf16[512,384]{1,0:T(8,128)(2,1)S(1)} %collective-permute-done.11.refs_1_), channel_id=1, source_target_pairs={{2,0},{0,4},{4,8},{8,12},{12,14},{14,10},{10,6},{6,2},{1,3},{5,1},... | collective-permute-start | bytes 1179656 | tf_op jit(solution)/shard_map/ppermute | solution.py:307
  50.3 10.6 %collective-permute-start.18 = (bf16[512,384]{1,0:T(8,128)(2,1)S(1)}, bf16[512,384]{1,0:T(8,128)(2,1)S(1)}, u32[]{:S(2)}, u32[]{:S(2)}) collective-permute-start(bf16[512,384]{1,0:T(8,128)(2,1)S(1)} %collective-permute-done.15.refs_2_), channel_id=1, source_target_pairs={{2,0},{0,4},{4,8},{8,12},{12,14},{14,10},{10,6},{6,2},{1,3},{5,1},... | collective-permute-start | bytes 1179656 | tf_op jit(solution)/shard_map/ppermute | solution.py:307
  61.0 10.2 %collective-permute-start.20 = (bf16[512,384]{1,0:T(8,128)(2,1)S(1)}, bf16[512,384]{1,0:T(8,128)(2,1)S(1)}, u32[]{:S(2)}, u32[]{:S(2)}) collective-permute-start(bf16[512,384]{1,0:T(8,128)(2,1)S(1)} %collective-permute-done.18.refs_0_), channel_id=1, source_target_pairs={{2,0},{0,4},{4,8},{8,12},{12,14},{14,10},{10,6},{6,2},{1,3},{5,1},... | collective-permute-start | bytes 1179656 | tf_op jit(solution)/shard_map/ppermute | solution.py:307
  62.6 10.4 %collective-permute-start.19 = (bf16[512,384]{1,0:T(8,128)(2,1)S(1)}, bf16[512,384]{1,0:T(8,128)(2,1)S(1)}, u32[]{:S(2)}, u32[]{:S(2)}) collective-permute-start(bf16[512,384]{1,0:T(8,128)(2,1)S(1)} %collective-permute-done.17.refs_3_), channel_id=1, source_target_pairs={{2,0},{0,4},{4,8},{8,12},{12,14},{14,10},{10,6},{6,2},{1,3},{5,1},... | collective-permute-start | bytes 1179656 | tf_op jit(solution)/shard_map/ppermute | solution.py:307
  73.7 12.5 %collective-permute-start.24 = (bf16[512,384]{1,0:T(8,128)(2,1)S(1)}, bf16[512,384]{1,0:T(8,128)(2,1)S(1)}, u32[]{:S(2)}, u32[]{:S(2)}) collective-permute-start(bf16[512,384]{1,0:T(8,128)(2,1)S(1)} %collective-permute-done.19.refs_1_), channel_id=1, source_target_pairs={{2,0},{0,4},{4,8},{8,12},{12,14},{14,10},{10,6},{6,2},{1,3},{5,1},... | collective-permute-start | bytes 1179656 | tf_op jit(solution)/shard_map/ppermute | solution.py:307
  75.2 10.9 %collective-permute-start.25 = (bf16[512,384]{1,0:T(8,128)(2,1)S(1)}, bf16[512,384]{1,0:T(8,128)(2,1)S(1)}, u32[]{:S(2)}, u32[]{:S(2)}) collective-permute-start(bf16[512,384]{1,0:T(8,128)(2,1)S(1)} %collective-permute-done.20.refs_4_), channel_id=1, source_target_pairs={{2,0},{0,4},{4,8},{8,12},{12,14},{14,10},{10,6},{6,2},{1,3},{5,1},... | collective-permute-start | bytes 1179656 | tf_op jit(solution)/shard_map/ppermute | solution.py:307
  80.4 9.5 %collective-permute-start.23 = (bf16[512,384]{1,0:T(8,128)(2,1)S(1)}, bf16[512,384]{1,0:T(8,128)(2,1)S(1)}, u32[]{:S(2)}, u32[]{:S(2)}) collective-permute-start(bf16[512,384]{1,0:T(8,128)(2,1)S(1)} %fusion.7), channel_id=1, source_target_pairs={{2,0},{0,4},{4,8},{8,12},{12,14},{14,10},{10,6},{6,2},{1,3},{5,1},... | collective-permute-start | bytes 1179656 | tf_op jit(solution)/shard_map/ppermute | solution.py:307
  89.9 12.2 %collective-permute-start.26 = (bf16[2,512,384]{2,1,0:T(8,128)(2,1)S(1)}, bf16[2,512,384]{2,1,0:T(8,128)(2,1)S(1)}, u32[]{:S(2)}, u32[]{:S(2)}) collective-permute-start(bf16[2,512,384]{2,1,0:T(8,128)(2,1)S(1)} %get-tuple-element.122), channel_id=1, source_target_pairs={{0,1},{1,0},{2,3},{3,2},{4,5},{5,4},{6,7},{7,6},{8,9},{9,8},{10,11... | collective-permute-start | bytes 2359304 | tf_op jit(solution)/shard_map/ppermute | solution.py:310
  90.0 10.4 %collective-permute-start.28 = (bf16[512,384]{1,0:T(8,128)(2,1)S(1)}, bf16[512,384]{1,0:T(8,128)(2,1)S(1)}, u32[]{:S(2)}, u32[]{:S(2)}) collective-permute-start(bf16[512,384]{1,0:T(8,128)(2,1)S(1)} %fusion.8), channel_id=1, source_target_pairs={{2,0},{0,4},{4,8},{8,12},{12,14},{14,10},{10,6},{6,2},{1,3},{5,1},... | collective-permute-start | bytes 1179656 | tf_op jit(solution)/shard_map/ppermute | solution.py:307
  91.8 10.3 %collective-permute-start.27 = (bf16[512,384]{1,0:T(8,128)(2,1)S(1)}, bf16[512,384]{1,0:T(8,128)(2,1)S(1)}, u32[]{:S(2)}, u32[]{:S(2)}) collective-permute-start(bf16[512,384]{1,0:T(8,128)(2,1)S(1)} %fusion.6), channel_id=1, source_target_pairs={{2,0},{0,4},{4,8},{8,12},{12,14},{14,10},{10,6},{6,2},{1,3},{5,1},... | collective-permute-start | bytes 1179656 | tf_op jit(solution)/shard_map/ppermute | solution.py:307
  93.3 11.1 %collective-permute-start.29 = (bf16[512,384]{1,0:T(8,128)(2,1)S(1)}, bf16[512,384]{1,0:T(8,128)(2,1)S(1)}, u32[]{:S(2)}, u32[]{:S(2)}) collective-permute-start(bf16[512,384]{1,0:T(8,128)(2,1)S(1)} %collective-permute-done.15.refs_2_), channel_id=1, source_target_pairs={{0,1},{1,0},{2,3},{3,2},{4,5},{5,4},{6,7},{7,6},{8,9},{9,8},{10,11... | collective-permute-start | bytes 1179656 | tf_op jit(solution)/shard_map/ppermute | solution.py:310
  102.0 12.9 %collective-permute-start.32 = (bf16[2,512,384]{2,1,0:T(8,128)(2,1)S(1)}, bf16[2,512,384]{2,1,0:T(8,128)(2,1)S(1)}, u32[]{:S(2)}, u32[]{:S(2)}) collective-permute-start(bf16[2,512,384]{2,1,0:T(8,128)(2,1)S(1)} %get-tuple-element.128), channel_id=1, source_target_pairs={{0,1},{1,0},{2,3},{3,2},{4,5},{5,4},{6,7},{7,6},{8,9},{9,8},{10,11... | collective-permute-start | bytes 2359304 | tf_op jit(solution)/shard_map/ppermute | solution.py:310
  102.8 11.1 %collective-permute-start.33 = (bf16[512,384]{1,0:T(8,128)(2,1)S(1)}, bf16[512,384]{1,0:T(8,128)(2,1)S(1)}, u32[]{:S(2)}, u32[]{:S(2)}) collective-permute-start(bf16[512,384]{1,0:T(8,128)(2,1)S(1)} %get-tuple-element.148), channel_id=1, source_target_pairs={{2,0},{0,4},{4,8},{8,12},{12,14},{14,10},{10,6},{6,2},{1,3},{5,1},... | collective-permute-start | bytes 1179656 | tf_op jit(solution)/shard_map/ppermute | solution.py:307
  104.5 10.4 %collective-permute-start.34 = (bf16[512,384]{1,0:T(8,128)(2,1)S(1)}, bf16[512,384]{1,0:T(8,128)(2,1)S(1)}, u32[]{:S(2)}, u32[]{:S(2)}) collective-permute-start(bf16[512,384]{1,0:T(8,128)(2,1)S(1)} %get-tuple-element.147), channel_id=1, source_target_pairs={{2,0},{0,4},{4,8},{8,12},{12,14},{14,10},{10,6},{6,2},{1,3},{5,1},... | collective-permute-start | bytes 1179656 | tf_op jit(solution)/shard_map/ppermute | solution.py:307
  106.0 10.8 %collective-permute-start.35 = (bf16[512,384]{1,0:T(8,128)(2,1)S(1)}, bf16[512,384]{1,0:T(8,128)(2,1)S(1)}, u32[]{:S(2)}, u32[]{:S(2)}) collective-permute-start(bf16[512,384]{1,0:T(8,128)(2,1)S(1)} %collective-permute-done.18.refs_0_), channel_id=1, source_target_pairs={{0,1},{1,0},{2,3},{3,2},{4,5},{5,4},{6,7},{7,6},{8,9},{9,8},{10,11... | collective-permute-start | bytes 1179656 | tf_op jit(solution)/shard_map/ppermute | solution.py:310
  106.0 12.4 %collective-permute-start.36 = (bf16[512,384]{1,0:T(8,128)(2,1)S(1)}, bf16[512,384]{1,0:T(8,128)(2,1)S(1)}, u32[]{:S(2)}, u32[]{:S(2)}) collective-permute-start(bf16[512,384]{1,0:T(8,128)(2,1)S(1)} %collective-permute-done.19.refs_1_), channel_id=1, source_target_pairs={{0,1},{1,0},{2,3},{3,2},{4,5},{5,4},{6,7},{7,6},{8,9},{9,8},{10,11... | collective-permute-start | bytes 1179656 | tf_op jit(solution)/shard_map/ppermute | solution.py:310
  115.2 10.7 %collective-permute-start.39 = (bf16[512,384]{1,0:T(8,128)(2,1)S(1)}, bf16[512,384]{1,0:T(8,128)(2,1)S(1)}, u32[]{:S(2)}, u32[]{:S(2)}) collective-permute-start(bf16[512,384]{1,0:T(8,128)(2,1)S(1)} %get-tuple-element.146), channel_id=1, source_target_pairs={{2,0},{0,4},{4,8},{8,12},{12,14},{14,10},{10,6},{6,2},{1,3},{5,1},... | collective-permute-start | bytes 1179656 | tf_op jit(solution)/shard_map/ppermute | solution.py:307
  116.8 10.4 %collective-permute-start.40 = (bf16[512,384]{1,0:T(8,128)(2,1)S(1)}, bf16[512,384]{1,0:T(8,128)(2,1)S(1)}, u32[]{:S(2)}, u32[]{:S(2)}) collective-permute-start(bf16[512,384]{1,0:T(8,128)(2,1)S(1)} %get-tuple-element.145), channel_id=1, source_target_pairs={{2,0},{0,4},{4,8},{8,12},{12,14},{14,10},{10,6},{6,2},{1,3},{5,1},... | collective-permute-start | bytes 1179656 | tf_op jit(solution)/shard_map/ppermute | solution.py:307
  (24 other events, 140.7 us)

commit v5 on v4

--- a/solution.py
+++ b/solution.py
@@ -100,24 +100,25 @@
 
 
 def grad_heads_kernel(count, first, last, plan_ref, *refs):
-    blocks, weights, rest = refs[:count], refs[count : 2 * count], refs[2 * count :]
+    blocks, (weight_ref, *rest) = refs[:count], refs[count:]
     out_ref, total = rest[-2:]
-    for i, (block, weight) in enumerate(zip(blocks, weights)):
-        term = dot(block[...], weight[...], NT)
-        if i:
-            total[...] += term
-        else:
-            total[...] = term if first else rest[0][...] + term
-    out_ref[...] = total[...].astype(jnp.bfloat16) if last else total[...]
+    for i, block in enumerate(blocks):
+
+        @pl.when(pl.program_id(0) == i)
+        def _():
+            term = dot(block[...], weight_ref[...], NT)
+            if i:
+                total[...] += term
+            else:
+                total[...] = term if first else rest[0][...] + term
+            if i == count - 1:
+                out_ref[...] = total[...].astype(out_ref.dtype)
 
 
 def grad_heads(plan, w_out, blocks, total=None, last=False):
     columns = w_out.shape[0]
     seq, part = blocks[0][1].shape
-    count = len(blocks)
-
-    def weight(place):
-        return pl.BlockSpec((columns, part), lambda step, plan: (0, plan[place]))
+    count, place = len(blocks), blocks[0][0]
 
     def whole(shape):
         return pl.BlockSpec(shape, lambda step, plan: (0, 0))
@@ -127,9 +128,9 @@
         functools.partial(grad_heads_kernel, count, first, last),
         grid_spec=pltpu.PrefetchScalarGridSpec(
             num_scalar_prefetch=1,
-            grid=(1,),
+            grid=(count,),
             in_specs=[whole((seq, part))] * count
-            + [weight(place) for place, _ in blocks]
+            + [pl.BlockSpec((columns, part), lambda step, plan: (0, plan[place + step]))]
             + [whole((seq, columns))] * (not first),
             out_specs=whole((seq, columns)),
             scratch_shapes=[pltpu.VMEM((seq, columns), jnp.float32)],
@@ -137,7 +138,7 @@
         out_shape=jax.ShapeDtypeStruct((seq, columns), jnp.bfloat16 if last else jnp.float32),
         compiler_params=params(48),
         cost_estimate=cost(2 * seq * columns * part * count, MIB * count),
-    )(plan, *[block for _, block in blocks], *[w_out] * count, *([] if first else [total]))
+    )(plan, *[block for _, block in blocks], w_out, *([] if first else [total]))
 
 
 SLOTS = 4
@@ -192,34 +193,30 @@
     )(plan, left, *[block for _, block in blocks], *([] if into is None else [into]))
 
 
-def terms_kernel(receivers, plan_ref, grad_ref, w_ref, *out_refs):
+def terms_kernel(plan_ref, grad_ref, w_ref, theirs_ref, mine_ref):
     total = dot(grad_ref[0], w_ref[0], NT)
     total += dot(grad_ref[1], w_ref[1], NT)
     total += dot(grad_ref[2], w_ref[2], NT)
     total = total.astype(jnp.bfloat16)
     part = total.shape[1] // 2
-    step = pl.program_id(0)
-    for i, out_ref in enumerate(out_refs):
-        core = 1 - plan_ref[0] if receivers[i] else plan_ref[0]
-
-        @pl.when((step == i) & (core == 0))
-        def _():
-            out_ref[0] = total[:, part:]
-            out_ref[1] = total[:, :part]
-
-        @pl.when((step == i) & (core == 1))
-        def _():
-            out_ref[0] = total[:, :part]
-            out_ref[1] = total[:, part:]
-
-
-def terms(plan, place, receivers, grad, w, part):
+
+    @pl.when(plan_ref[0] == 0)
+    def _():
+        mine_ref[0] = total[:, :part]
+        theirs_ref[0] = total[:, part:]
+
+    @pl.when(plan_ref[0] == 1)
+    def _():
+        mine_ref[0] = total[:, part:]
+        theirs_ref[0] = total[:, :part]
+
+
+def terms(plan, place, count, grad, w, part):
     _, seq, columns = grad.shape
-    count = len(receivers)
-    out = pl.BlockSpec((2, seq, part), lambda i, plan: (0, 0, 0))
-    shape = jax.ShapeDtypeStruct((2, seq, part), jnp.bfloat16)
+    out = pl.BlockSpec((1, seq, part), lambda i, plan: (i, 0, 0))
+    shape = jax.ShapeDtypeStruct((count, seq, part), jnp.bfloat16)
     return pl.pallas_call(
-        functools.partial(terms_kernel, receivers),
+        terms_kernel,
         grid_spec=pltpu.PrefetchScalarGridSpec(
             num_scalar_prefetch=1,
             grid=(count,),
@@ -227,9 +224,9 @@
                 pl.BlockSpec((3, seq, columns), lambda i, plan: (0, 0, 0)),
                 pl.BlockSpec((3, 2 * part, columns), lambda i, plan: (0, plan[place + i], 0)),
             ],
-            out_specs=[out] * count,
+            out_specs=[out, out],
         ),
-        out_shape=[shape] * count,
+        out_shape=[shape, shape],
         compiler_params=params(48),
         cost_estimate=cost(12 * seq * columns * part * count, 5 * MIB * count),
     )(plan, grad, w)
@@ -265,14 +262,12 @@
 
     blocks = [2 * chip(0) + core, 2 * chip(0) + 1 - core]
     for step in range(1, chips // 2):
-        behind, ahead = (-step, step) if core == 0 else (step, -step)
-        blocks += [2 * chip(behind) + core, 2 * chip(behind) + 1 - core]
-        blocks += [2 * chip(ahead) + 1 - core, 2 * chip(ahead) + core]
+        for shard in (core, 1 - core):
+            blocks += [2 * chip(-step) + shard, 2 * chip(step) + shard]
     blocks += [2 * chip(chips // 2) + core, 2 * chip(chips // 2) + 1 - core]
     summed = [chip(chips // 2)]
     for step in range(chips // 2 - 1, 0, -1):
-        ahead = step if core == 0 else -step
-        summed += [chip(-ahead), chip(ahead)]
+        summed += [chip(step), chip(-step)]
     return [core] + blocks + summed + [chip(0)]
 
 
@@ -293,21 +288,27 @@
     if part % 128 or n != 16:
         return plain(n, inputs, out_grad, w_qkv, w_out, saved_qkv, positions)
     order = ring_order(n // 2)
-    chips = range(n // 2)
-    ring = [(2 * order[i], 2 * order[i - 1]) for i in chips]
-    ring = [(j, i) for i, j in ring] + [(i + 1, j + 1) for i, j in ring]
+    hops = [(2 * order[i - 1], 2 * order[i]) for i in range(n // 2)]
+    ahead = [(i + core, j + core) for i, j in hops for core in range(2)]
+    back = [(j, i) for i, j in ahead]
+    apart = [(i, j) for i, j in hops] + [(j + 1, i + 1) for i, j in hops]
     swap = [(i, i ^ 1) for i in range(n)]
     plans = [plan_of(order, i) for i in range(n)]
     size = len(plans[0])
     plan = lax.dynamic_slice(
         jnp.array(sum(plans, []), jnp.int32), (lax.axis_index("gx") * size,), (size,)
     )
-
-    def send(x):
-        return lax.ppermute(x, "gx", ring)
-
-    def swapped(x):
-        return lax.ppermute(x, "gx", swap)
+    on_first = lax.axis_index("gx") % 2 == 0
+
+    def both_ways(right, left):
+        return lax.ppermute(right, "gx", ahead), lax.ppermute(left, "gx", back)
+
+    def one_way(right, left):
+        return lax.ppermute(jnp.where(on_first, right, left), "gx", apart)
+
+    def swapped(*arrays):
+        found = [lax.ppermute(x, "gx", swap) for x in arrays]
+        return found if len(found) > 1 else found[0]
 
     def blocks(step, *arrays):
         first = 1 if step == 0 else 4 * step - 1
@@ -325,102 +326,101 @@
     qkv = saved_qkv.transpose(1, 0, 2)
     w = w_qkv.transpose(1, 0, 2)
 
-    a1 = send(out_grad)
-    other = swapped(out_grad)
-    b1 = send(other)
-    attn, attended, attended_t = attend(positions, qkv)
-
     def grad_out_heads(index, some, so_far=None, last=False):
         return grad_heads(index, w_out, some, so_far, last)
 
     def grad_out(index, some, into=None):
         return weight_grad(index, attended_t, some, w_out.shape, into)
 
-    a1 = after(a1, attended)
-    a2, a1x = send(a1), swapped(a1)
+    r1, l1 = both_ways(out_grad, out_grad)
+    other = swapped(out_grad)
+    attn, attended, attended_t = attend(positions, qkv)
+
+    r1, l1, attended, plan = together(r1, l1, attended, plan)
+    r2, l2 = both_ways(r1, l1)
+    g1 = blocks(1, r1, l1, *swapped(r1, l1))
     g0 = blocks(0, out_grad, other)
-    grad_h = grad_out_heads(after(plan, a1), g0)
-
-    b1 = after(b1, grad_h)
-    b2, b1x = send(b1), swapped(b1)
-    out = grad_out(after(plan, b1), g0)
-
-    a2 = after(a2, out)
-    a3, a2x = send(a2), swapped(a2)
-    g1 = blocks(1, a1, b1, a1x, b1x)
-    grad_h = grad_out_heads(after(plan, a2), g1, grad_h)
-
-    b2 = after(b2, grad_h)
-    b3, b2x = send(b2), swapped(b2)
-    out = grad_out(after(plan, b2), g1, out)
-
-    a3 = after(a3, out)
-    a4, a3x = send(a3), swapped(a3)
-    inputs = after(inputs, a3)
+    grad_h = grad_out_heads(plan, g0)
+    out = grad_out(plan, g0)
+
+    r2, l2, grad_h, out, plan = together(r2, l2, grad_h, out, plan)
+    r3, l3 = both_ways(r2, l2)
+    g2 = blocks(2, r2, l2, *swapped(r2, l2))
+    grad_h = grad_out_heads(plan, g1, grad_h)
+    out = grad_out(plan, g1, out)
+
+    r3, l3, grad_h, out, plan = together(r3, l3, grad_h, out, plan)
+    x4 = one_way(r3, l3)
+    r3x, l3x = swapped(r3, l3)
+    g3 = blocks(3, r3, l3, r3x, l3x)
+    grad_h = grad_out_heads(plan, g2, grad_h)
+
+    grad_h, r3x, l3x, inputs, plan = together(grad_h, r3x, l3x, inputs, plan)
+    i1, j1 = both_ways(inputs, inputs)
+    out = grad_out(plan, g2, out)
+    grad_h = grad_out_heads(plan, g3, grad_h)
+
+    x4, grad_h, out, plan = together(x4, grad_h, out, plan)
+    x4x = swapped(x4)
     other = swapped(inputs)
-    i1 = send(inputs)
-    g2 = blocks(2, a2, b2, a2x, b2x)
-    grad_h = grad_out_heads(after(plan, a3), g2, grad_h)
-
-    b3, grad_h, other, plan = together(b3, grad_h, other, plan)
-    b3x = swapped(b3)
-    j1 = send(other)
-    f0 = blocks(0, inputs, other)
-    out = grad_out(plan, g2, out)
-
-    out, a3x, b3x, plan = together(out, a3x, b3x, plan)
-    g3 = blocks(3, a3, b3, a3x, b3x)
-    grad_h = grad_out_heads(plan, g3, grad_h)
-
-    grad_h, a4, i1, plan = together(grad_h, a4, i1, plan)
-    a4x = swapped(a4)
-    i2, i1x = send(i1), swapped(i1)
-
-    a4x, j1, plan = together(a4x, j1, plan)
-    j2, j1x = send(j1), swapped(j1)
-    g4 = blocks(4, a4, a4x)
+    g4 = blocks(4, x4, x4x)
     grad_h = grad_out_heads(plan, g4, grad_h, last=True)
     grad = attend_back(qkv, attn, attended, grad_h)
 
-    grad, i2, plan = together(grad, i2, plan)
-    i3, i2x = send(i2), swapped(i2)
-    t4, theirs3, t3 = terms(plan, 17, (0, 1, 0), grad, w, part)
-
-    t4, theirs3, t3, j2, i3, plan = together(t4, theirs3, t3, j2, i3, plan)
-    theirs4 = swapped(t4[0])
+    grad, i1, j1, other, plan = together(grad, i1, j1, other, plan)
+    i2, j2 = both_ways(i1, j1)
+    i1x, j1x = swapped(i1, j1)
+    f0 = blocks(0, inputs, other)
+
+    theirs3, mine3 = terms(plan, 17, 3, grad, w, part)
+
+    theirs3, mine3, i2, j2, i1x, j1x, plan = together(theirs3, mine3, i2, j2, i1x, j1x, plan)
     theirs3 = swapped(theirs3)
-    j3, j2x = send(j2), swapped(j2)
-    i4, i3x = send(i3), swapped(i3)
+    i3, j3 = both_ways(i2, j2)
+    i2x, j2x = swapped(i2, j2)
     out = grad_out(plan, g3 + g4, out)
 
-    out, theirs4, theirs3, plan = together(out, theirs4, theirs3, plan)
-    m4 = send(rounded_total(t4[1], theirs4))
-    theirs2, t2 = terms(plan, 20, (1, 0), grad, w, part)
-
-    theirs2, t2, m4, j3, i4, plan = together(theirs2, t2, m4, j3, i4, plan)
-    o3 = send(rounded_total(t3[0], theirs3[0]))
-    m3 = send(rounded_total(t3[1], theirs3[1], m4))
+    out, theirs3, plan = together(out, theirs3, plan)
+    low = rounded_total(mine3[0], theirs3[0])
+    s4 = one_way(low, low)
+    theirs2, mine2 = terms(plan, 20, 2, grad, w, part)
+
+    theirs2, mine2, s4, i3, j3, i2x, j2x, plan = together(
+        theirs2, mine2, s4, i3, j3, i2x, j2x, plan
+    )
+    nothing = jnp.zeros_like(s4)
+    s3, u3 = both_ways(
+        rounded_total(mine3[1], theirs3[1], jnp.where(on_first, s4, nothing)),
+        rounded_total(mine3[2], theirs3[2], jnp.where(on_first, nothing, s4)),
+    )
     theirs2 = swapped(theirs2)
-    j3x = swapped(j3)
+    i4 = one_way(i3, j3)
+    i3x, j3x = swapped(i3, j3)
+    theirs1, mine1 = terms(plan, 22, 3, grad, w, part)
+
+    theirs1, mine1, theirs2, s3, u3, i4, i3x, plan = together(
+        theirs1, mine1, theirs2, s3, u3, i4, i3x, plan
+    )
+    s2, u2 = both_ways(
+        rounded_total(mine2[0], theirs2[0], s3), rounded_total(mine2[1], theirs2[1], u3)
+    )
+    theirs1 = swapped(theirs1)
     i4x = swapped(i4)
-    theirs1, t1, t0 = terms(plan, 22, (1, 0, 0), grad, w, part)
-
-    theirs1, t1, t0, theirs2, m3, o3, plan = together(theirs1, t1, t0, theirs2, m3, o3, plan)
-    o2 = send(rounded_total(t2[0], theirs2[0], o3))
-    m2 = send(rounded_total(t2[1], theirs2[1], m3))
-    theirs1 = swapped(theirs1)
-    some = f0 + blocks(1, i1, j1, i1x, j1x) + blocks(4, i4, i4x)
+    some = f0 + blocks(1, i1, j1, i1x, j1x) + blocks(2, i2, j2, i2x, j2x)[:2]
     weight = grad_qkv(plan, some)
 
-    weight, theirs1, o2, m2, plan = together(weight, theirs1, o2, m2, plan)
-    o1 = send(rounded_total(t1[0], theirs1[0], o2))
-    m1 = send(rounded_total(t1[1], theirs1[1], m2))
-    some = blocks(2, i2, j2, i2x, j2x) + blocks(3, i3, j3, i3x, j3x)
+    weight, theirs1, s2, u2, i4x, j3x, plan = together(
+        weight, theirs1, s2, u2, i4x, j3x, plan
+    )
+    s1, u1 = both_ways(
+        rounded_total(mine1[0], theirs1[0], s2), rounded_total(mine1[1], theirs1[1], u2)
+    )
+    some = blocks(2, i2, j2, i2x, j2x)[2:] + blocks(3, i3, j3, i3x, j3x) + blocks(4, i4, i4x)
     weight = grad_qkv(plan, some, weight)
 
-    weight, o1, m1 = together(weight, o1, m1)
-    theirs = swapped(rounded_total(t0[0], o1))
-    return rounded_total(t0[1], m1, theirs), weight.transpose(1, 0, 2), out
+    weight, s1, u1 = together(weight, s1, u1)
+    input_grad = rounded_total(mine1[2], theirs1[2], s1, u1)
+    return input_grad, weight.transpose(1, 0, 2), out
 
 
 def solution(mesh):

time: 130 us -> 132 us (1.015)
  starting transfers between devices: 35.6 us -> 29.6 us
  Pallas kernels: 69.8 us -> 74.2 us
  waiting for transfers between devices: 19.7 us -> 23.8 us
    ppermute x42 -> x40, starting transfers between devices: 35.6 us -> 29.6 us  [the longest x18 19.5 us: both_ways(): return (lax.ppermute(right, 'gx', ahead), lax.ppermute(left, 'gx', back))]
    ppermute x42 -> x40, waiting for transfers between devices: 19.7 us -> 23.8 us  [the longest x18 21.2 us: both_ways(): return (lax.ppermute(right, 'gx', ahead), lax.ppermute(left, 'gx', back))]
    pallas_call x5, Pallas kernels: 14.4 us -> 17.7 us  [grad_heads(): pl.pallas_call(functools.partial(grad_heads_kernel, count, first, last),...]
  transfers between devices with their start and end apart: 42 -> 40, of which waited for: 10 -> 17; matrix products, arithmetic and copies ran while one was open for 1% -> 1% of each run, Pallas kernels for 54% -> 56%
where the time goes in v5:
time: 132 us; the launch traced here: 131 us
  Pallas kernels  74.2 us (56%)
  starting transfers between devices  29.6 us (22%)
  waiting for transfers between devices  23.8 us (18%)
  other arithmetic  2.09 us (2%)
    pallas_call x6, Pallas kernels, weight_grad(): pl.pallas_call(functools.partial(weight_kernel, [place for place, _ in bl...  26.7 us
    ppermute x18, waiting for transfers between devices, both_ways(): return (lax.ppermute(right, 'gx', ahead), lax.ppermute(left, 'gx', back))  21.2 us
    ppermute x18, starting transfers between devices, both_ways(): return (lax.ppermute(right, 'gx', ahead), lax.ppermute(left, 'gx', back))  19.5 us
    pallas_call x3, Pallas kernels, terms(): pl.pallas_call(terms_kernel, grid_spec=pltpu.PrefetchScalarGridSpec(num_s...  19.3 us
    pallas_call x5, Pallas kernels, grad_heads(): pl.pallas_call(functools.partial(grad_heads_kernel, count, first, last),...  17.7 us
    pallas_call x1, Pallas kernels, attend(): pl.pallas_call(attend_kernel, grid=(heads,), in_specs=[pl.BlockSpec((1, s...  6.57 us
    ppermute x19, starting transfers between devices, swapped(): found = [lax.ppermute(x, 'gx', swap) for x in arrays]  5.31 us
    ppermute x3, starting transfers between devices, one_way(): return lax.ppermute(jnp.where(on_first, right, left), 'gx', apart)  4.77 us
  transfers between devices with their start and end apart: 40, of which 17 were waited for; matrix products, arithmetic and copies ran while one was open for 1% of the time, Pallas kernels for 56%

profile of v5, /device:TPU:0, one launch (start us, length us, event | category | flops | bytes accessed | tf_op | source)
XLA Modules:
  0.0 131.5 jit_solution(5248960157885189777)
XLA Ops:
  0.6 3.0 %collective-permute-start.1 = (bf16[512,384]{1,0:T(8,128)(2,1)}, bf16[512,384]{1,0:T(8,128)(2,1)S(1)}, u32[]{:S(2)}, u32[]{:S(2)}) collective-permute-start(bf16[512,384]{1,0:T(8,128)(2,1)} %refs_0_.3), channel_id=1, source_target_pairs={{0,2},{1,3},{4,0},{5,1},{8,4},{9,5},{12,8},{13,9},{14,12},{15,13},... | collective-permute-start | bytes 1179656 | tf_op jit(solution)/shard_map/ppermute | solution.py:304
  3.8 6.6 %shard_map.94 = (bf16[4,512,512]{2,1,0:T(8,128)(2,1)}, bf16[512,512]{1,0:T(8,128)(2,1)}, bf16[512,512]{1,0:T(8,128)(2,1)}) custom-call(s32[1,512]{1,0:T(1,128)} %bitcast.54, bf16[3,512,512]{2,1,0:T(8,128)(2,1)} %bitcast.48), custom_call_target="tpu_custom_call" | custom-call | flops 131072 | bytes 1280 | tf_op jit(solution)/shard_map/pallas_call | solution.py:51
  11.1 1.9 %collective-permute-done.1.refs_1_ = bf16[512,384]{1,0:T(8,128)(2,1)S(1)} collective-permute-done((bf16[512,384]{1,0:T(8,128)(2,1)}, bf16[512,384]{1,0:T(8,128)(2,1)S(1)}, u32[]{:S(2)}, u32[]{:S(2)}) %collective-permute-start.1) | collective-permute-done | bytes 393248 | tf_op jit(solution)/shard_map/ppermute | solution.py:304
  17.0 2.5 %shard_map.95.refs_5_ = f32[512,512]{1,0:T(8,128)S(1)} custom-call(s32[25]{0:T(128)S(1)} %dynamic_slice.3.plan_ref, bf16[512,384]{1,0:T(8,128)(2,1)S(1)} %copy-done.2, bf16[512,384]{1,0:T(8,128)(2,1)S(1)} %collective-permute-done.4.refs_1_, bf16[512,6144]{1,0:T(8,128)(2,1)} %refs_2_.3), custom_call_target="tpu_custom_call" | custom-call | flops 98304 | bytes 512 | tf_op jit(solution)/shard_map/pallas_call | solution.py:127
  19.5 2.0 %shard_map.96.refs_4_ = bf16[512,6144]{1,0:T(8,128)(2,1)} custom-call(s32[25]{0:T(128)S(1)} %dynamic_slice.3.plan_ref, bf16[512,512]{1,0:T(8,128)(2,1)S(1)} %copy-done, bf16[512,384]{1,0:T(8,128)(2,1)S(1)} %copy-done.2, bf16[512,384]{1,0:T(8,128)(2,1)S(1)} %collective-permute-done.4.refs_1_), custom_call_target="tpu_custom_call" | custom-call | flops 98304 | bytes 288 | tf_op jit(solution)/shard_map/pallas_call | solution.py:179
  21.6 2.5 %collective-permute-done.2.refs_0_ = bf16[512,384]{1,0:T(8,128)(2,1)S(1)} collective-permute-done((bf16[512,384]{1,0:T(8,128)(2,1)S(1)}, bf16[512,384]{1,0:T(8,128)(2,1)S(1)}, u32[]{:S(2)}, u32[]{:S(2)}) %collective-permute-start.2) | collective-permute-done | bytes 393248 | tf_op jit(solution)/shard_map/ppermute | solution.py:304
  27.2 4.3 %shard_map.97.refs_5_ = f32[512,512]{1,0:T(8,128)S(1)} custom-call(s32[25]{0:T(128)S(1)} %dynamic_slice.3.plan_ref, bf16[512,384]{1,0:T(8,128)(2,1)S(1)} %collective-permute-done.refs_0_, bf16[512,384]{1,0:T(8,128)(2,1)S(1)} %collective-permute-done.1.refs_1_, bf16[512,384]{1,0:T(8,128)(2,1)} %collective-permute-done.7.refs_2_, ...), custom_call_target="tpu_custom_call" | custom-call | flops 196608 | bytes 1024 | tf_op jit(solution)/shard_map/pallas_call | solution.py:127
  31.5 3.2 %shard_map.98.refs_4_ = bf16[512,6144]{1,0:T(8,128)(2,1)} custom-call(s32[25]{0:T(128)S(1)} %dynamic_slice.3.plan_ref, bf16[512,512]{1,0:T(8,128)(2,1)S(1)} %copy-done, bf16[512,384]{1,0:T(8,128)(2,1)S(1)} %collective-permute-done.refs_0_, bf16[512,384]{1,0:T(8,128)(2,1)S(1)} %collective-permute-done.1.refs_1_, ...), custom_call_target="tpu_custom_call", output_to_operand_aliasing={{}: (6, {})} | custom-call | flops 196608 | bytes 576 | tf_op jit(solution)/shard_map/pallas_call | solution.py:179
  36.9 4.2 %shard_map.99.refs_5_ = f32[512,512]{1,0:T(8,128)S(1)} custom-call(s32[25]{0:T(128)S(1)} %dynamic_slice.3.plan_ref, bf16[512,384]{1,0:T(8,128)(2,1)S(1)} %collective-permute-done.2.refs_0_, bf16[512,384]{1,0:T(8,128)(2,1)} %collective-permute-done.3.refs_1_, bf16[512,384]{1,0:T(8,128)(2,1)S(1)} %collective-permute-done.10.refs_2_, ...), custom_call_target="tpu_custom_call" | custom-call | flops 196608 | bytes 1024 | tf_op jit(solution)/shard_map/pallas_call | solution.py:127
  41.2 3.1 %shard_map.101.refs_6_ = bf16[512,6144]{1,0:T(8,128)(2,1)} custom-call(s32[25]{0:T(128)S(1)} %dynamic_slice.3.plan_ref, bf16[512,512]{1,0:T(8,128)(2,1)S(1)} %copy-done, bf16[512,384]{1,0:T(8,128)(2,1)S(1)} %collective-permute-done.2.refs_0_, bf16[512,384]{1,0:T(8,128)(2,1)} %collective-permute-done.3.refs_1_, ...), custom_call_target="tpu_custom_call", output_to_operand_aliasing={{}: (6, {})} | custom-call | flops 196608 | bytes 576 | tf_op jit(solution)/shard_map/pallas_call | solution.py:179
  44.2 4.1 %shard_map.100.refs_3_ = f32[512,512]{1,0:T(8,128)S(1)} custom-call(s32[25]{0:T(128)S(1)} %dynamic_slice.3.plan_ref, bf16[512,384]{1,0:T(8,128)(2,1)S(1)} %collective-permute-done.5.refs_0_, bf16[512,384]{1,0:T(8,128)(2,1)S(1)} %collective-permute-done.6.refs_1_, bf16[512,384]{1,0:T(8,128)(2,1)S(1)} %collective-permute-done.12.refs_2_, ...), custom_call_target="tpu_custom_call" | custom-call | flops 196608 | bytes 1024 | tf_op jit(solution)/shard_map/pallas_call | solution.py:127
  50.9 2.6 %shard_map.102.grad_ref = bf16[512,512]{1,0:T(8,128)(2,1)S(1)} custom-call(s32[25]{0:T(128)S(1)} %dynamic_slice.3.plan_ref, bf16[512,384]{1,0:T(8,128)(2,1)S(1)} %collective-permute-done.9.refs_0_.refs_4_, bf16[512,384]{1,0:T(8,128)(2,1)S(1)} %collective-permute-done.14.refs_1_.refs_5_, bf16[512,6144]{1,0:T(8,128)(2,1)} %refs_2_.3, ...), custom_call_target="tpu_custom_call" | custom-call | flops 98304 | bytes 512 | tf_op jit(solution)/shard_map/pallas_call | solution.py:127
  53.6 4.0 %shard_map.103.grad_ref.left_ref = bf16[3,512,512]{2,1,0:T(8,128)(2,1)S(1)} custom-call(bf16[3,512,512]{2,1,0:T(8,128)(2,1)S(1)} %bitcast.49, bf16[4,512,512]{2,1,0:T(8,128)(2,1)S(1)} %copy-done.1, bf16[512,512]{1,0:T(8,128)(2,1)S(1)} %copy-done.4, bf16[512,512]{1,0:T(8,128)(2,1)S(1)} %shard_map.102.grad_ref), custom_call_target="tpu_custom_call" | custom-call | flops 262144 | bytes 1536 | tf_op jit(solution)/shard_map/pallas_call | solution.py:91
  57.6 2.4 %collective-permute-done.16.refs_3_ = bf16[512,384]{1,0:T(8,128)(2,1)S(1)} collective-permute-done((bf16[512,384]{1,0:T(8,128)(2,1)S(1)}, bf16[512,384]{1,0:T(8,128)(2,1)S(1)}, u32[]{:S(2)}, u32[]{:S(2)}) %collective-permute-start.16) | collective-permute-done | bytes 393248 | tf_op jit(solution)/shard_map/ppermute | solution.py:304
  63.1 7.0 %shard_map.104 = (bf16[3,512,384]{2,1,0:T(8,128)(2,1)S(1)}, bf16[3,512,384]{2,1,0:T(8,128)(2,1)S(1)}) custom-call(s32[25]{0:T(128)S(1)} %dynamic_slice.3.plan_ref, bf16[3,512,512]{2,1,0:T(8,128)(2,1)S(1)} %shard_map.103.grad_ref.left_ref, bf16[3,6144,512]{2,1,0:T(8,128)(2,1)} %bitcast.50), custom_call_target="tpu_custom_call" | custom-call | flops 884736 | bytes 3840 | tf_op jit(solution)/shard_map/pallas_call | solution.py:218
  70.1 2.3 %collective-permute-done.18.refs_6_ = bf16[512,384]{1,0:T(8,128)(2,1)S(1)} collective-permute-done((bf16[512,384]{1,0:T(8,128)(2,1)S(1)}, bf16[512,384]{1,0:T(8,128)(2,1)S(1)}, u32[]{:S(2)}, u32[]{:S(2)}) %collective-permute-start.18) | collective-permute-done | bytes 393248 | tf_op jit(solution)/shard_map/ppermute | solution.py:304
  75.8 3.5 %shard_map.105 = bf16[512,6144]{1,0:T(8,128)(2,1)} custom-call(s32[25]{0:T(128)S(1)} %dynamic_slice.3.plan_ref, bf16[512,512]{1,0:T(8,128)(2,1)S(1)} %copy-done, bf16[512,384]{1,0:T(8,128)(2,1)S(1)} %collective-permute-done.5.refs_0_, bf16[512,384]{1,0:T(8,128)(2,1)S(1)} %collective-permute-done.6.refs_1_, ...), custom_call_target="tpu_custom_call", output_to_operand_aliasing={{}: (8, {})} | custom-call | flops 294912 | bytes 864 | tf_op jit(solution)/shard_map/pallas_call | solution.py:179
  81.1 5.3 %shard_map.106 = (bf16[2,512,384]{2,1,0:T(8,128)(2,1)S(1)}, bf16[2,512,384]{2,1,0:T(8,128)(2,1)S(1)}) custom-call(s32[25]{0:T(128)S(1)} %dynamic_slice.3.plan_ref, bf16[3,512,512]{2,1,0:T(8,128)(2,1)S(1)} %shard_map.103.grad_ref.left_ref, bf16[3,6144,512]{2,1,0:T(8,128)(2,1)} %bitcast.51), custom_call_target="tpu_custom_call" | custom-call | flops 589824 | bytes 2560 | tf_op jit(solution)/shard_map/pallas_call | solution.py:218
  89.1 1.9 %collective-permute-start.28 = (bf16[2,512,384]{2,1,0:T(8,128)(2,1)S(1)}, bf16[2,512,384]{2,1,0:T(8,128)(2,1)S(1)}, u32[]{:S(2)}, u32[]{:S(2)}) collective-permute-start(bf16[2,512,384]{2,1,0:T(8,128)(2,1)S(1)} %get-tuple-element.116), channel_id=1, source_target_pairs={{0,1},{1,0},{2,3},{3,2},{4,5},{5,4},{6,7},{7,6},{8,9},{9,8},{10,11... | collective-permute-start | bytes 2359304 | tf_op jit(solution)/shard_map/ppermute | solution.py:310
  95.0 7.0 %shard_map.107 = (bf16[3,512,384]{2,1,0:T(8,128)(2,1)S(1)}, bf16[3,512,384]{2,1,0:T(8,128)(2,1)S(1)}) custom-call(s32[25]{0:T(128)S(1)} %dynamic_slice.3.plan_ref, bf16[3,512,512]{2,1,0:T(8,128)(2,1)S(1)} %shard_map.103.grad_ref.left_ref, bf16[3,6144,512]{2,1,0:T(8,128)(2,1)} %bitcast.52), custom_call_target="tpu_custom_call" | custom-call | flops 884736 | bytes 3840 | tf_op jit(solution)/shard_map/pallas_call | solution.py:218
  102.7 2.3 %collective-permute-done.30 = bf16[512,384]{1,0:T(8,128)(2,1)S(1)} collective-permute-done((bf16[512,384]{1,0:T(8,128)(2,1)S(1)}, bf16[512,384]{1,0:T(8,128)(2,1)S(1)}, u32[]{:S(2)}, u32[]{:S(2)}) %collective-permute-start.30) | collective-permute-done | bytes 393248 | tf_op jit(solution)/shard_map/ppermute | solution.py:304
  105.0 2.2 %collective-permute-done.29 = bf16[512,384]{1,0:T(8,128)(2,1)S(1)} collective-permute-done((bf16[512,384]{1,0:T(8,128)(2,1)S(1)}, bf16[512,384]{1,0:T(8,128)(2,1)S(1)}, u32[]{:S(2)}, u32[]{:S(2)}) %collective-permute-start.29) | collective-permute-done | bytes 393248 | tf_op jit(solution)/shard_map/ppermute | solution.py:304
  110.2 7.5 %shard_map.108.refs_8_ = bf16[3,6144,512]{2,1,0:T(8,128)(2,1)} custom-call(s32[25]{0:T(128)S(1)} %dynamic_slice.3.plan_ref, bf16[3,512,512]{2,1,0:T(8,128)(2,1)S(1)} %shard_map.103.grad_ref.left_ref, bf16[512,384]{1,0:T(8,128)(2,1)S(1)} %copy-done.5, bf16[512,384]{1,0:T(8,128)(2,1)S(1)} %collective-permute-done.17.refs_1_, ...), custom_call_target="tpu_custom_call" | custom-call | flops 1179648 | bytes 3456 | tf_op jit(solution)/shard_map/pallas_call | solution.py:179
  121.8 7.5 %shard_map.109 = bf16[3,6144,512]{2,1,0:T(8,128)(2,1)} custom-call(s32[25]{0:T(128)S(1)} %dynamic_slice.3.plan_ref, bf16[3,512,512]{2,1,0:T(8,128)(2,1)S(1)} %shard_map.103.grad_ref.left_ref, bf16[512,384]{1,0:T(8,128)(2,1)S(1)} %collective-permute-done.26.refs_0_, ...), custom_call_target="tpu_custom_call", output_to_operand_aliasing={{}: (10, {})} | custom-call | flops 1179648 | bytes 3456 | tf_op jit(solution)/shard_map/pallas_call | solution.py:179
  (92 shorter events, 37.6 us)
Async XLA Ops:
  0.6 12.4 %collective-permute-start.1 = (bf16[512,384]{1,0:T(8,128)(2,1)}, bf16[512,384]{1,0:T(8,128)(2,1)S(1)}, u32[]{:S(2)}, u32[]{:S(2)}) collective-permute-start(bf16[512,384]{1,0:T(8,128)(2,1)} %refs_0_.3), channel_id=1, source_target_pairs={{0,2},{1,3},{4,0},{5,1},{8,4},{9,5},{12,8},{13,9},{14,12},{15,13},... | collective-permute-start | bytes 1179656 | tf_op jit(solution)/shard_map/ppermute | solution.py:304
  3.7 10.8 %collective-permute-start = (bf16[512,384]{1,0:T(8,128)(2,1)}, bf16[512,384]{1,0:T(8,128)(2,1)S(1)}, u32[]{:S(2)}, u32[]{:S(2)}) collective-permute-start(bf16[512,384]{1,0:T(8,128)(2,1)} %refs_0_.3), channel_id=1, source_target_pairs={{2,0},{3,1},{0,4},{1,5},{4,8},{5,9},{8,12},{9,13},{12,14},{13,15},... | collective-permute-start | bytes 1179656 | tf_op jit(solution)/shard_map/ppermute | solution.py:304
  3.8 13.2 %collective-permute-start.4 = (bf16[512,384]{1,0:T(8,128)(2,1)}, bf16[512,384]{1,0:T(8,128)(2,1)S(1)}, u32[]{:S(2)}, u32[]{:S(2)}) collective-permute-start(bf16[512,384]{1,0:T(8,128)(2,1)} %refs_0_.3), channel_id=1, source_target_pairs={{0,1},{1,0},{2,3},{3,2},{4,5},{5,4},{6,7},{7,6},{8,9},{9,8},{10,11... | collective-permute-start | bytes 1179656 | tf_op jit(solution)/shard_map/ppermute | solution.py:310
  16.5 10.7 %collective-permute-start.8 = (bf16[512,384]{1,0:T(8,128)(2,1)S(1)}, bf16[512,384]{1,0:T(8,128)(2,1)}, u32[]{:S(2)}, u32[]{:S(2)}) collective-permute-start(bf16[512,384]{1,0:T(8,128)(2,1)S(1)} %collective-permute-done.1.refs_1_), channel_id=1, source_target_pairs={{0,1},{1,0},{2,3},{3,2},{4,5},{5,4},{6,7},{7,6},{8,9},{9,8},{10,11... | collective-permute-start | bytes 1179656 | tf_op jit(solution)/shard_map/ppermute | solution.py:310
  26.7 10.2 %collective-permute-start.10 = (bf16[512,384]{1,0:T(8,128)(2,1)S(1)}, bf16[512,384]{1,0:T(8,128)(2,1)S(1)}, u32[]{:S(2)}, u32[]{:S(2)}) collective-permute-start(bf16[512,384]{1,0:T(8,128)(2,1)S(1)} %collective-permute-done.2.refs_0_), channel_id=1, source_target_pairs={{0,1},{1,0},{2,3},{3,2},{4,5},{5,4},{6,7},{7,6},{8,9},{9,8},{10,11... | collective-permute-start | bytes 1179656 | tf_op jit(solution)/shard_map/ppermute | solution.py:310
  35.3 13.0 %collective-permute-start.9 = (bf16[512,384]{1,0:T(8,128)(2,1)S(1)}, bf16[512,384]{1,0:T(8,128)(2,1)S(1)}, u32[]{:S(2)}, u32[]{:S(2)}) collective-permute-start(bf16[512,384]{1,0:T(8,128)(2,1)S(1)} %broadcast_select_fusion.1), channel_id=1, source_target_pairs={{2,0},{0,4},{4,8},{8,12},{12,14},{14,10},{10,6},{6,2},{1,3},{5,1},... | collective-permute-start | bytes 1179656 | tf_op jit(solution)/shard_map/ppermute | solution.py:307
  48.9 11.1 %collective-permute-start.16 = (bf16[512,384]{1,0:T(8,128)(2,1)S(1)}, bf16[512,384]{1,0:T(8,128)(2,1)S(1)}, u32[]{:S(2)}, u32[]{:S(2)}) collective-permute-start(bf16[512,384]{1,0:T(8,128)(2,1)S(1)} %copy-done.5), channel_id=1, source_target_pairs={{0,2},{1,3},{4,0},{5,1},{8,4},{9,5},{12,8},{13,9},{14,12},{15,13},... | collective-permute-start | bytes 1179656 | tf_op jit(solution)/shard_map/ppermute | solution.py:304
  49.7 11.2 %collective-permute-start.15 = (bf16[512,384]{1,0:T(8,128)(2,1)S(1)}, bf16[512,384]{1,0:T(8,128)(2,1)S(1)}, u32[]{:S(2)}, u32[]{:S(2)}) collective-permute-start(bf16[512,384]{1,0:T(8,128)(2,1)S(1)} %copy-done.5), channel_id=1, source_target_pairs={{2,0},{3,1},{0,4},{1,5},{4,8},{5,9},{8,12},{9,13},{12,14},{13,15},... | collective-permute-start | bytes 1179656 | tf_op jit(solution)/shard_map/ppermute | solution.py:304
  60.8 11.5 %collective-permute-start.18 = (bf16[512,384]{1,0:T(8,128)(2,1)S(1)}, bf16[512,384]{1,0:T(8,128)(2,1)S(1)}, u32[]{:S(2)}, u32[]{:S(2)}) collective-permute-start(bf16[512,384]{1,0:T(8,128)(2,1)S(1)} %collective-permute-done.15.refs_2_), channel_id=1, source_target_pairs={{2,0},{3,1},{0,4},{1,5},{4,8},{5,9},{8,12},{9,13},{12,14},{13,15},... | collective-permute-start | bytes 1179656 | tf_op jit(solution)/shard_map/ppermute | solution.py:304
  61.8 10.6 %collective-permute-start.21 = (bf16[512,384]{1,0:T(8,128)(2,1)S(1)}, bf16[512,384]{1,0:T(8,128)(2,1)S(1)}, u32[]{:S(2)}, u32[]{:S(2)}) collective-permute-start(bf16[512,384]{1,0:T(8,128)(2,1)S(1)} %collective-permute-done.16.refs_3_), channel_id=1, source_target_pairs={{0,1},{1,0},{2,3},{3,2},{4,5},{5,4},{6,7},{7,6},{8,9},{9,8},{10,11... | collective-permute-start | bytes 1179656 | tf_op jit(solution)/shard_map/ppermute | solution.py:310
  62.0 11.3 %collective-permute-start.19 = (bf16[512,384]{1,0:T(8,128)(2,1)S(1)}, bf16[512,384]{1,0:T(8,128)(2,1)S(1)}, u32[]{:S(2)}, u32[]{:S(2)}) collective-permute-start(bf16[512,384]{1,0:T(8,128)(2,1)S(1)} %collective-permute-done.16.refs_3_), channel_id=1, source_target_pairs={{0,2},{1,3},{4,0},{5,1},{8,4},{9,5},{12,8},{13,9},{14,12},{15,13},... | collective-permute-start | bytes 1179656 | tf_op jit(solution)/shard_map/ppermute | solution.py:304
  73.3 13.1 %collective-permute-start.26 = (bf16[512,384]{1,0:T(8,128)(2,1)S(1)}, bf16[512,384]{1,0:T(8,128)(2,1)S(1)}, u32[]{:S(2)}, u32[]{:S(2)}) collective-permute-start(bf16[512,384]{1,0:T(8,128)(2,1)S(1)} %collective-permute-done.18.refs_6_), channel_id=1, source_target_pairs={{0,1},{1,0},{2,3},{3,2},{4,5},{5,4},{6,7},{7,6},{8,9},{9,8},{10,11... | collective-permute-start | bytes 1179656 | tf_op jit(solution)/shard_map/ppermute | solution.py:310
  73.8 12.6 %collective-permute-start.24 = (bf16[512,384]{1,0:T(8,128)(2,1)S(1)}, bf16[512,384]{1,0:T(8,128)(2,1)S(1)}, u32[]{:S(2)}, u32[]{:S(2)}) collective-permute-start(bf16[512,384]{1,0:T(8,128)(2,1)S(1)} %collective-permute-done.18.refs_6_), channel_id=1, source_target_pairs={{2,0},{3,1},{0,4},{1,5},{4,8},{5,9},{8,12},{9,13},{12,14},{13,15},... | collective-permute-start | bytes 1179656 | tf_op jit(solution)/shard_map/ppermute | solution.py:304
  75.4 11.0 %collective-permute-start.27 = (bf16[512,384]{1,0:T(8,128)(2,1)S(1)}, bf16[512,384]{1,0:T(8,128)(2,1)S(1)}, u32[]{:S(2)}, u32[]{:S(2)}) collective-permute-start(bf16[512,384]{1,0:T(8,128)(2,1)S(1)} %collective-permute-done.19.refs_7_), channel_id=1, source_target_pairs={{0,1},{1,0},{2,3},{3,2},{4,5},{5,4},{6,7},{7,6},{8,9},{9,8},{10,11... | collective-permute-start | bytes 1179656 | tf_op jit(solution)/shard_map/ppermute | solution.py:310
  75.4 11.9 %collective-permute-start.25 = (bf16[512,384]{1,0:T(8,128)(2,1)S(1)}, bf16[512,384]{1,0:T(8,128)(2,1)S(1)}, u32[]{:S(2)}, u32[]{:S(2)}) collective-permute-start(bf16[512,384]{1,0:T(8,128)(2,1)S(1)} %collective-permute-done.19.refs_7_), channel_id=1, source_target_pairs={{0,2},{1,3},{4,0},{5,1},{8,4},{9,5},{12,8},{13,9},{14,12},{15,13},... | collective-permute-start | bytes 1179656 | tf_op jit(solution)/shard_map/ppermute | solution.py:304
  89.1 18.2 %collective-permute-start.28 = (bf16[2,512,384]{2,1,0:T(8,128)(2,1)S(1)}, bf16[2,512,384]{2,1,0:T(8,128)(2,1)S(1)}, u32[]{:S(2)}, u32[]{:S(2)}) collective-permute-start(bf16[2,512,384]{2,1,0:T(8,128)(2,1)S(1)} %get-tuple-element.116), channel_id=1, source_target_pairs={{0,1},{1,0},{2,3},{3,2},{4,5},{5,4},{6,7},{7,6},{8,9},{9,8},{10,11... | collective-permute-start | bytes 2359304 | tf_op jit(solution)/shard_map/ppermute | solution.py:310
  91.0 11.7 %collective-permute-start.31 = (bf16[512,384]{1,0:T(8,128)(2,1)S(1)}, bf16[512,384]{1,0:T(8,128)(2,1)S(1)}, u32[]{:S(2)}, u32[]{:S(2)}) collective-permute-start(bf16[512,384]{1,0:T(8,128)(2,1)S(1)} %broadcast_select_fusion), channel_id=1, source_target_pairs={{2,0},{0,4},{4,8},{8,12},{12,14},{14,10},{10,6},{6,2},{1,3},{5,1},... | collective-permute-start | bytes 1179656 | tf_op jit(solution)/shard_map/ppermute | solution.py:307
  92.9 12.1 %collective-permute-start.30 = (bf16[512,384]{1,0:T(8,128)(2,1)S(1)}, bf16[512,384]{1,0:T(8,128)(2,1)S(1)}, u32[]{:S(2)}, u32[]{:S(2)}) collective-permute-start(bf16[512,384]{1,0:T(8,128)(2,1)S(1)} %get-tuple-element.145), channel_id=1, source_target_pairs={{0,2},{1,3},{4,0},{5,1},{8,4},{9,5},{12,8},{13,9},{14,12},{15,13},... | collective-permute-start | bytes 1179656 | tf_op jit(solution)/shard_map/ppermute | solution.py:304
  93.5 13.8 %collective-permute-start.29 = (bf16[512,384]{1,0:T(8,128)(2,1)S(1)}, bf16[512,384]{1,0:T(8,128)(2,1)S(1)}, u32[]{:S(2)}, u32[]{:S(2)}) collective-permute-start(bf16[512,384]{1,0:T(8,128)(2,1)S(1)} %get-tuple-element.146), channel_id=1, source_target_pairs={{2,0},{3,1},{0,4},{1,5},{4,8},{5,9},{8,12},{9,13},{12,14},{13,15},... | collective-permute-start | bytes 1179656 | tf_op jit(solution)/shard_map/ppermute | solution.py:304
  95.0 12.3 %collective-permute-start.32 = (bf16[512,384]{1,0:T(8,128)(2,1)S(1)}, bf16[512,384]{1,0:T(8,128)(2,1)S(1)}, u32[]{:S(2)}, u32[]{:S(2)}) collective-permute-start(bf16[512,384]{1,0:T(8,128)(2,1)S(1)} %collective-permute-done.24.refs_2_), channel_id=1, source_target_pairs={{0,1},{1,0},{2,3},{3,2},{4,5},{5,4},{6,7},{7,6},{8,9},{9,8},{10,11... | collective-permute-start | bytes 1179656 | tf_op jit(solution)/shard_map/ppermute | solution.py:310
  107.3 12.1 %collective-permute-start.33 = (bf16[3,512,384]{2,1,0:T(8,128)(2,1)S(1)}, bf16[3,512,384]{2,1,0:T(8,128)(2,1)S(1)}, u32[]{:S(2)}, u32[]{:S(2)}) collective-permute-start(bf16[3,512,384]{2,1,0:T(8,128)(2,1)S(1)} %get-tuple-element.124), channel_id=1, source_target_pairs={{0,1},{1,0},{2,3},{3,2},{4,5},{5,4},{6,7},{7,6},{8,9},{9,8},{10,11... | collective-permute-start | bytes 3538952 | tf_op jit(solution)/shard_map/ppermute | solution.py:310
  107.3 10.4 %collective-permute-start.37 = (bf16[512,384]{1,0:T(8,128)(2,1)S(1)}, bf16[512,384]{1,0:T(8,128)(2,1)S(1)}, u32[]{:S(2)}, u32[]{:S(2)}) collective-permute-start(bf16[512,384]{1,0:T(8,128)(2,1)S(1)} %collective-permute-done.25.refs_3_), channel_id=1, source_target_pairs={{0,1},{1,0},{2,3},{3,2},{4,5},{5,4},{6,7},{7,6},{8,9},{9,8},{10,11... | collective-permute-start | bytes 1179656 | tf_op jit(solution)/shard_map/ppermute | solution.py:310
  108.1 11.1 %collective-permute-start.35 = (bf16[512,384]{1,0:T(8,128)(2,1)S(1)}, bf16[512,384]{1,0:T(8,128)(2,1)S(1)}, u32[]{:S(2)}, u32[]{:S(2)}) collective-permute-start(bf16[512,384]{1,0:T(8,128)(2,1)S(1)} %get-tuple-element.149), channel_id=1, source_target_pairs={{0,2},{1,3},{4,0},{5,1},{8,4},{9,5},{12,8},{13,9},{14,12},{15,13},... | collective-permute-start | bytes 1179656 | tf_op jit(solution)/shard_map/ppermute | solution.py:304
  108.6 10.8 %collective-permute-start.34 = (bf16[512,384]{1,0:T(8,128)(2,1)S(1)}, bf16[512,384]{1,0:T(8,128)(2,1)S(1)}, u32[]{:S(2)}, u32[]{:S(2)}) collective-permute-start(bf16[512,384]{1,0:T(8,128)(2,1)S(1)} %get-tuple-element.150), channel_id=1, source_target_pairs={{2,0},{3,1},{0,4},{1,5},{4,8},{5,9},{8,12},{9,13},{12,14},{13,15},... | collective-permute-start | bytes 1179656 | tf_op jit(solution)/shard_map/ppermute | solution.py:304
  (22 other events, 175.8 us)

commit v6 on v5

--- a/solution.py
+++ b/solution.py
@@ -100,25 +100,24 @@
 
 
 def grad_heads_kernel(count, first, last, plan_ref, *refs):
-    blocks, (weight_ref, *rest) = refs[:count], refs[count:]
+    blocks, weights, rest = refs[:count], refs[count : 2 * count], refs[2 * count :]
     out_ref, total = rest[-2:]
-    for i, block in enumerate(blocks):
-
-        @pl.when(pl.program_id(0) == i)
-        def _():
-            term = dot(block[...], weight_ref[...], NT)
-            if i:
-                total[...] += term
-            else:
-                total[...] = term if first else rest[0][...] + term
-            if i == count - 1:
-                out_ref[...] = total[...].astype(out_ref.dtype)
+    for i, (block, weight) in enumerate(zip(blocks, weights)):
+        term = dot(block[...], weight[...], NT)
+        if i:
+            total[...] += term
+        else:
+            total[...] = term if first else rest[0][...] + term
+    out_ref[...] = total[...].astype(jnp.bfloat16) if last else total[...]
 
 
 def grad_heads(plan, w_out, blocks, total=None, last=False):
     columns = w_out.shape[0]
     seq, part = blocks[0][1].shape
-    count, place = len(blocks), blocks[0][0]
+    count = len(blocks)
+
+    def weight(place):
+        return pl.BlockSpec((columns, part), lambda step, plan: (0, plan[place]))
 
     def whole(shape):
         return pl.BlockSpec(shape, lambda step, plan: (0, 0))
@@ -128,17 +127,17 @@
         functools.partial(grad_heads_kernel, count, first, last),
         grid_spec=pltpu.PrefetchScalarGridSpec(
             num_scalar_prefetch=1,
-            grid=(count,),
+            grid=(1,),
             in_specs=[whole((seq, part))] * count
-            + [pl.BlockSpec((columns, part), lambda step, plan: (0, plan[place + step]))]
+            + [weight(place) for place, _ in blocks]
             + [whole((seq, columns))] * (not first),
             out_specs=whole((seq, columns)),
             scratch_shapes=[pltpu.VMEM((seq, columns), jnp.float32)],
         ),
         out_shape=jax.ShapeDtypeStruct((seq, columns), jnp.bfloat16 if last else jnp.float32),
-        compiler_params=params(48),
+        compiler_params=params(40),
         cost_estimate=cost(2 * seq * columns * part * count, MIB * count),
-    )(plan, *[block for _, block in blocks], w_out, *([] if first else [total]))
+    )(plan, *[block for _, block in blocks], *[w_out] * count, *([] if first else [total]))
 
 
 SLOTS = 4
@@ -268,7 +267,12 @@
     summed = [chip(chips // 2)]
     for step in range(chips // 2 - 1, 0, -1):
         summed += [chip(step), chip(-step)]
-    return [core] + blocks + summed + [chip(0)]
+    apart = blocks[:2]
+    for step in range(1, chips // 2):
+        behind = step if core else -step
+        for shard, first in ((core, behind), (1 - core, -behind)):
+            apart += [2 * chip(first) + shard, 2 * chip(-first) + shard]
+    return [core] + blocks + summed + [chip(0)] + apart + blocks[-2:]
 
 
 def after(x, *others):
@@ -292,6 +296,7 @@
     ahead = [(i + core, j + core) for i, j in hops for core in range(2)]
     back = [(j, i) for i, j in ahead]
     apart = [(i, j) for i, j in hops] + [(j + 1, i + 1) for i, j in hops]
+    crossed = [(j, i) for i, j in apart]
     swap = [(i, i ^ 1) for i in range(n)]
     plans = [plan_of(order, i) for i in range(n)]
     size = len(plans[0])
@@ -306,6 +311,12 @@
     def one_way(right, left):
         return lax.ppermute(jnp.where(on_first, right, left), "gx", apart)
 
+    def first_chain(x):
+        return lax.ppermute(x, "gx", apart)
+
+    def second_chain(x):
+        return lax.ppermute(x, "gx", crossed)
+
     def swapped(*arrays):
         found = [lax.ppermute(x, "gx", swap) for x in arrays]
         return found if len(found) > 1 else found[0]
@@ -313,6 +324,9 @@
     def blocks(step, *arrays):
         first = 1 if step == 0 else 4 * step - 1
         return [(first + i, array) for i, array in enumerate(arrays)]
+
+    def in_blocks(step, *arrays):
+        return [(place + 24, array) for place, array in blocks(step, *arrays)]
 
     def grad_qkv(index, some, into=None):
         return weight_grad(index, grad, some, w.shape, into)
@@ -351,71 +365,66 @@
 
     r3, l3, grad_h, out, plan = together(r3, l3, grad_h, out, plan)
     x4 = one_way(r3, l3)
+    i1 = first_chain(after(inputs, r3))
     r3x, l3x = swapped(r3, l3)
     g3 = blocks(3, r3, l3, r3x, l3x)
     grad_h = grad_out_heads(plan, g2, grad_h)
 
-    grad_h, r3x, l3x, inputs, plan = together(grad_h, r3x, l3x, inputs, plan)
-    i1, j1 = both_ways(inputs, inputs)
+    grad_h, r3x, l3x, plan = together(grad_h, r3x, l3x, plan)
     out = grad_out(plan, g2, out)
     grad_h = grad_out_heads(plan, g3, grad_h)
 
-    x4, grad_h, out, plan = together(x4, grad_h, out, plan)
-    x4x = swapped(x4)
-    other = swapped(inputs)
+    x4, i1, grad_h, out, plan = together(x4, i1, grad_h, out, plan)
+    x4x, other = swapped(x4, inputs)
+    i2, j1 = first_chain(i1), second_chain(inputs)
+    f0 = in_blocks(0, inputs, other)
     g4 = blocks(4, x4, x4x)
     grad_h = grad_out_heads(plan, g4, grad_h, last=True)
     grad = attend_back(qkv, attn, attended, grad_h)
 
-    grad, i1, j1, other, plan = together(grad, i1, j1, other, plan)
-    i2, j2 = both_ways(i1, j1)
+    grad, i2, j1, other, plan = together(grad, i2, j1, other, plan)
+    i3, j2 = first_chain(i2), second_chain(j1)
     i1x, j1x = swapped(i1, j1)
-    f0 = blocks(0, inputs, other)
-
     theirs3, mine3 = terms(plan, 17, 3, grad, w, part)
 
-    theirs3, mine3, i2, j2, i1x, j1x, plan = together(theirs3, mine3, i2, j2, i1x, j1x, plan)
+    theirs3, mine3, i3, j2, i1x, j1x, plan = together(theirs3, mine3, i3, j2, i1x, j1x, plan)
     theirs3 = swapped(theirs3)
-    i3, j3 = both_ways(i2, j2)
+    i4, j3 = first_chain(i3), second_chain(j2)
     i2x, j2x = swapped(i2, j2)
     out = grad_out(plan, g3 + g4, out)
 
     out, theirs3, plan = together(out, theirs3, plan)
     low = rounded_total(mine3[0], theirs3[0])
-    s4 = one_way(low, low)
+    s4 = first_chain(low)
     theirs2, mine2 = terms(plan, 20, 2, grad, w, part)
 
-    theirs2, mine2, s4, i3, j3, i2x, j2x, plan = together(
-        theirs2, mine2, s4, i3, j3, i2x, j2x, plan
+    theirs2, mine2, s4, i4, j3, i2x, j2x, plan = together(
+        theirs2, mine2, s4, i4, j3, i2x, j2x, plan
     )
     nothing = jnp.zeros_like(s4)
     s3, u3 = both_ways(
         rounded_total(mine3[1], theirs3[1], jnp.where(on_first, s4, nothing)),
         rounded_total(mine3[2], theirs3[2], jnp.where(on_first, nothing, s4)),
     )
-    theirs2 = swapped(theirs2)
-    i4 = one_way(i3, j3)
-    i3x, j3x = swapped(i3, j3)
+    theirs2, i3x = swapped(theirs2, i3)
     theirs1, mine1 = terms(plan, 22, 3, grad, w, part)
 
-    theirs1, mine1, theirs2, s3, u3, i4, i3x, plan = together(
-        theirs1, mine1, theirs2, s3, u3, i4, i3x, plan
+    theirs1, mine1, theirs2, s3, u3, i3x, plan = together(
+        theirs1, mine1, theirs2, s3, u3, i3x, plan
     )
     s2, u2 = both_ways(
         rounded_total(mine2[0], theirs2[0], s3), rounded_total(mine2[1], theirs2[1], u3)
     )
-    theirs1 = swapped(theirs1)
-    i4x = swapped(i4)
-    some = f0 + blocks(1, i1, j1, i1x, j1x) + blocks(2, i2, j2, i2x, j2x)[:2]
+    theirs1, i4x, j3x = swapped(theirs1, i4, j3)
+    some = f0 + in_blocks(1, i1, j1, i1x, j1x) + in_blocks(2, i2, j2, i2x, j2x)[:2]
     weight = grad_qkv(plan, some)
 
-    weight, theirs1, s2, u2, i4x, j3x, plan = together(
-        weight, theirs1, s2, u2, i4x, j3x, plan
-    )
+    weight, theirs1, s2, u2, i4x, j3x, plan = together(weight, theirs1, s2, u2, i4x, j3x, plan)
     s1, u1 = both_ways(
         rounded_total(mine1[0], theirs1[0], s2), rounded_total(mine1[1], theirs1[1], u2)
     )
-    some = blocks(2, i2, j2, i2x, j2x)[2:] + blocks(3, i3, j3, i3x, j3x) + blocks(4, i4, i4x)
+    some = in_blocks(2, i2, j2, i2x, j2x)[2:]
+    some += in_blocks(3, i3, j3, i3x, j3x) + in_blocks(4, i4, i4x)
     weight = grad_qkv(plan, some, weight)
 
     weight, s1, u1 = together(weight, s1, u1)

time: 132 us -> 130 us (0.985)
  local copies, waits for them, and re-layouts: 0.78 us -> 7.36 us
  Pallas kernels: 74.2 us -> 67.7 us
  waiting for transfers between devices: 23.8 us -> 20.9 us
    ppermute x0 -> x8, starting transfers between devices: none -> 10.9 us  [the longest x5 7.29 us: first_chain(): return lax.ppermute(x, 'gx', apart)]
    ppermute x18 -> x12, waiting for transfers between devices: 21.2 us -> 13.4 us  [both_ways(): return (lax.ppermute(right, 'gx', ahead), lax.ppermute(left, 'gx', back))]
    ppermute x0 -> x8, waiting for transfers between devices: none -> 7.5 us  [the longest x5 5.27 us: first_chain(): return lax.ppermute(x, 'gx', apart)]
    pallas_call x5, Pallas kernels: 17.7 us -> 10.4 us  [grad_heads(): pl.pallas_call(functools.partial(grad_heads_kernel, count, first, last),...]
    unnamed x12 -> x22, local copies, waits for them, and re-layouts: 0.03 us -> 6.6 us
    ppermute x18 -> x12, starting transfers between devices: 19.5 us -> 13.4 us  [both_ways(): return (lax.ppermute(right, 'gx', ahead), lax.ppermute(left, 'gx', back))]
    ppermute x3 -> x1, starting transfers between devices: 4.77 us -> 1.57 us  [one_way(): return lax.ppermute(jnp.where(on_first, right, left), 'gx', apart)]
    ppermute x3 -> x1, waiting for transfers between devices: 2.49 us -> 0.01 us  [one_way(): return lax.ppermute(jnp.where(on_first, right, left), 'gx', apart)]
  transfers between devices with their start and end apart: 40 -> 40, of which waited for: 17 -> 14; matrix products, arithmetic and copies ran while one was open for 1% -> 1% of each run, Pallas kernels for 56% -> 52%
where the time goes in v6:
time: 130 us; the launch traced here: 129 us
  Pallas kernels  67.7 us (52%)
  starting transfers between devices  30.5 us (23%)
  waiting for transfers between devices  20.9 us (16%)
  local copies, waits for them, and re-layouts  7.36 us (6%)
  other arithmetic  2.04 us (2%)
    pallas_call x6, Pallas kernels, weight_grad(): pl.pallas_call(functools.partial(weight_kernel, [place for place, _ in bl...  27.5 us
    pallas_call x3, Pallas kernels, terms(): pl.pallas_call(terms_kernel, grid_spec=pltpu.PrefetchScalarGridSpec(num_s...  19.3 us
    ppermute x12, starting transfers between devices, both_ways(): return (lax.ppermute(right, 'gx', ahead), lax.ppermute(left, 'gx', back))  13.4 us
    ppermute x12, waiting for transfers between devices, both_ways(): return (lax.ppermute(right, 'gx', ahead), lax.ppermute(left, 'gx', back))  13.4 us
    pallas_call x5, Pallas kernels, grad_heads(): pl.pallas_call(functools.partial(grad_heads_kernel, count, first, last),...  10.4 us
    ppermute x5, starting transfers between devices, first_chain(): return lax.ppermute(x, 'gx', apart)  7.29 us
    unnamed x22, local copies, waits for them, and re-layouts  6.6 us
    pallas_call x1, Pallas kernels, attend(): pl.pallas_call(attend_kernel, grid=(heads,), in_specs=[pl.BlockSpec((1, s...  6.57 us
  transfers between devices with their start and end apart: 40, of which 14 were waited for; matrix products, arithmetic and copies ran while one was open for 1% of the time, Pallas kernels for 52%

profile of v6, /device:TPU:0, one launch (start us, length us, event | category | flops | bytes accessed | tf_op | source)
XLA Modules:
  0.0 129.5 jit_solution(11017349468175216518)
XLA Ops:
  0.6 3.0 %collective-permute-start.1 = (bf16[512,384]{1,0:T(8,128)(2,1)}, bf16[512,384]{1,0:T(8,128)(2,1)S(1)}, u32[]{:S(2)}, u32[]{:S(2)}) collective-permute-start(bf16[512,384]{1,0:T(8,128)(2,1)} %refs_0_.4), channel_id=1, source_target_pairs={{0,2},{1,3},{4,0},{5,1},{8,4},{9,5},{12,8},{13,9},{14,12},{15,13},... | collective-permute-start | bytes 1179656 | tf_op jit(solution)/shard_map/ppermute | solution.py:309
  3.8 6.6 %shard_map.94 = (bf16[4,512,512]{2,1,0:T(8,128)(2,1)}, bf16[512,512]{1,0:T(8,128)(2,1)}, bf16[512,512]{1,0:T(8,128)(2,1)}) custom-call(s32[1,512]{1,0:T(1,128)} %bitcast.54, bf16[3,512,512]{2,1,0:T(8,128)(2,1)} %bitcast.48), custom_call_target="tpu_custom_call" | custom-call | flops 131072 | bytes 1280 | tf_op jit(solution)/shard_map/pallas_call | solution.py:51
  11.1 1.9 %collective-permute-done.1.refs_1_ = bf16[512,384]{1,0:T(8,128)(2,1)S(1)} collective-permute-done((bf16[512,384]{1,0:T(8,128)(2,1)}, bf16[512,384]{1,0:T(8,128)(2,1)S(1)}, u32[]{:S(2)}, u32[]{:S(2)}) %collective-permute-start.1) | collective-permute-done | bytes 393248 | tf_op jit(solution)/shard_map/ppermute | solution.py:309
  17.1 2.8 %copy-done = bf16[512,6144]{1,0:T(8,128)(2,1)S(1)} copy-done((bf16[512,6144]{1,0:T(8,128)(2,1)S(1)}, bf16[512,6144]{1,0:T(8,128)(2,1)}, u32[]{:S(2)}) %copy-start) | copy-done | bytes 6291480
  21.2 2.0 %shard_map.96.refs_4_ = bf16[512,6144]{1,0:T(8,128)(2,1)} custom-call(s32[41]{0:T(128)S(1)} %dynamic_slice.3.plan_ref, bf16[512,512]{1,0:T(8,128)(2,1)S(1)} %copy-done.3, bf16[512,384]{1,0:T(8,128)(2,1)S(1)} %copy-done.6, bf16[512,384]{1,0:T(8,128)(2,1)S(1)} %collective-permute-done.4.refs_1_), custom_call_target="tpu_custom_call" | custom-call | flops 98304 | bytes 288 | tf_op jit(solution)/shard_map/pallas_call | solution.py:178
  27.2 2.8 %copy-done.1 = bf16[512,6144]{1,0:T(8,128)(2,1)S(1)} copy-done((bf16[512,6144]{1,0:T(8,128)(2,1)S(1)}, bf16[512,6144]{1,0:T(8,128)(2,1)}, u32[]{:S(2)}) %copy-start.1) | copy-done | bytes 6291480
  30.0 3.0 %shard_map.97.refs_8_ = f32[512,512]{1,0:T(8,128)S(1)} custom-call(s32[41]{0:T(128)S(1)} %dynamic_slice.3.plan_ref, bf16[512,384]{1,0:T(8,128)(2,1)} %collective-permute-done.refs_0_, bf16[512,384]{1,0:T(8,128)(2,1)S(1)} %collective-permute-done.1.refs_1_, bf16[512,384]{1,0:T(8,128)(2,1)} %collective-permute-done.7.refs_2_, ...), custom_call_target="tpu_custom_call" | custom-call | flops 196608 | bytes 1024 | tf_op jit(solution)/shard_map/pallas_call | solution.py:126
  33.0 3.4 %shard_map.98.refs_4_ = bf16[512,6144]{1,0:T(8,128)(2,1)} custom-call(s32[41]{0:T(128)S(1)} %dynamic_slice.3.plan_ref, bf16[512,512]{1,0:T(8,128)(2,1)S(1)} %copy-done.3, bf16[512,384]{1,0:T(8,128)(2,1)} %collective-permute-done.refs_0_, bf16[512,384]{1,0:T(8,128)(2,1)S(1)} %collective-permute-done.1.refs_1_, ...), custom_call_target="tpu_custom_call", output_to_operand_aliasing={{}: (6, {})} | custom-call | flops 196608 | bytes 576 | tf_op jit(solution)/shard_map/pallas_call | solution.py:178
  40.3 2.8 %shard_map.99.refs_8_ = f32[512,512]{1,0:T(8,128)S(1)} custom-call(s32[41]{0:T(128)S(1)} %dynamic_slice.3.plan_ref, bf16[512,384]{1,0:T(8,128)(2,1)S(1)} %collective-permute-done.2.refs_0_, bf16[512,384]{1,0:T(8,128)(2,1)S(1)} %collective-permute-done.3.refs_1_, bf16[512,384]{1,0:T(8,128)(2,1)} %collective-permute-done.11.refs_2_, ...), custom_call_target="tpu_custom_call" | custom-call | flops 196608 | bytes 1024 | tf_op jit(solution)/shard_map/pallas_call | solution.py:126
  43.1 3.1 %shard_map.101.refs_6_ = bf16[512,6144]{1,0:T(8,128)(2,1)} custom-call(s32[41]{0:T(128)S(1)} %dynamic_slice.3.plan_ref, bf16[512,512]{1,0:T(8,128)(2,1)S(1)} %copy-done.3, bf16[512,384]{1,0:T(8,128)(2,1)S(1)} %collective-permute-done.2.refs_0_, bf16[512,384]{1,0:T(8,128)(2,1)S(1)} %collective-permute-done.3.refs_1_, ...), custom_call_target="tpu_custom_call", output_to_operand_aliasing={{}: (6, {})} | custom-call | flops 196608 | bytes 576 | tf_op jit(solution)/shard_map/pallas_call | solution.py:178
  46.2 1.9 %shard_map.100.refs_4_ = f32[512,512]{1,0:T(8,128)S(1)} custom-call(s32[41]{0:T(128)S(1)} %dynamic_slice.3.plan_ref, bf16[512,384]{1,0:T(8,128)(2,1)S(1)} %collective-permute-done.5.refs_0_, bf16[512,384]{1,0:T(8,128)(2,1)S(1)} %collective-permute-done.6.refs_1_, bf16[512,384]{1,0:T(8,128)(2,1)S(1)} %collective-permute-done.13.refs_2_, ...), custom_call_target="tpu_custom_call" | custom-call | flops 196608 | bytes 1024 | tf_op jit(solution)/shard_map/pallas_call | solution.py:126
  54.1 4.0 %shard_map.103.grad_ref.left_ref = bf16[3,512,512]{2,1,0:T(8,128)(2,1)S(1)} custom-call(bf16[3,512,512]{2,1,0:T(8,128)(2,1)S(1)} %bitcast.49, bf16[4,512,512]{2,1,0:T(8,128)(2,1)S(1)} %copy-done.4, bf16[512,512]{1,0:T(8,128)(2,1)S(1)} %copy-done.7, bf16[512,512]{1,0:T(8,128)(2,1)S(1)} %shard_map.102.grad_ref), custom_call_target="tpu_custom_call" | custom-call | flops 262144 | bytes 1536 | tf_op jit(solution)/shard_map/pallas_call | solution.py:91
  58.1 2.2 %collective-permute-done.17.refs_3_ = bf16[512,384]{1,0:T(8,128)(2,1)S(1)} collective-permute-done((bf16[512,384]{1,0:T(8,128)(2,1)S(1)}, bf16[512,384]{1,0:T(8,128)(2,1)S(1)}, u32[]{:S(2)}, u32[]{:S(2)}) %collective-permute-start.17) | collective-permute-done | bytes 393248 | tf_op jit(solution)/shard_map/ppermute | solution.py:318
  63.8 7.0 %shard_map.104 = (bf16[3,512,384]{2,1,0:T(8,128)(2,1)S(1)}, bf16[3,512,384]{2,1,0:T(8,128)(2,1)S(1)}) custom-call(s32[41]{0:T(128)S(1)} %dynamic_slice.3.plan_ref, bf16[3,512,512]{2,1,0:T(8,128)(2,1)S(1)} %shard_map.103.grad_ref.left_ref, bf16[3,6144,512]{2,1,0:T(8,128)(2,1)} %bitcast.50), custom_call_target="tpu_custom_call" | custom-call | flops 884736 | bytes 3840 | tf_op jit(solution)/shard_map/pallas_call | solution.py:217
  75.6 3.5 %shard_map.105 = bf16[512,6144]{1,0:T(8,128)(2,1)} custom-call(s32[41]{0:T(128)S(1)} %dynamic_slice.3.plan_ref, bf16[512,512]{1,0:T(8,128)(2,1)S(1)} %copy-done.3, bf16[512,384]{1,0:T(8,128)(2,1)S(1)} %collective-permute-done.5.refs_0_, bf16[512,384]{1,0:T(8,128)(2,1)S(1)} %collective-permute-done.6.refs_1_, ...), custom_call_target="tpu_custom_call", output_to_operand_aliasing={{}: (8, {})} | custom-call | flops 294912 | bytes 864 | tf_op jit(solution)/shard_map/pallas_call | solution.py:178
  79.2 1.6 %collective-permute-start.24 = (bf16[512,384]{1,0:T(8,128)(2,1)S(1)}, bf16[512,384]{1,0:T(8,128)(2,1)S(1)}, u32[]{:S(2)}, u32[]{:S(2)}) collective-permute-start(bf16[512,384]{1,0:T(8,128)(2,1)S(1)} %fusion.8), channel_id=1, source_target_pairs={{2,0},{0,4},{4,8},{8,12},{12,14},{14,10},{10,6},{6,2},{1,3},{5,1},... | collective-permute-start | bytes 1179656 | tf_op jit(solution)/shard_map/ppermute | solution.py:315
  80.8 5.3 %shard_map.106 = (bf16[2,512,384]{2,1,0:T(8,128)(2,1)S(1)}, bf16[2,512,384]{2,1,0:T(8,128)(2,1)S(1)}) custom-call(s32[41]{0:T(128)S(1)} %dynamic_slice.3.plan_ref, bf16[3,512,512]{2,1,0:T(8,128)(2,1)S(1)} %shard_map.103.grad_ref.left_ref, bf16[3,6144,512]{2,1,0:T(8,128)(2,1)} %bitcast.51), custom_call_target="tpu_custom_call" | custom-call | flops 589824 | bytes 2560 | tf_op jit(solution)/shard_map/pallas_call | solution.py:217
  86.2 2.6 %collective-permute-done.24 = bf16[512,384]{1,0:T(8,128)(2,1)S(1)} collective-permute-done((bf16[512,384]{1,0:T(8,128)(2,1)S(1)}, bf16[512,384]{1,0:T(8,128)(2,1)S(1)}, u32[]{:S(2)}, u32[]{:S(2)}) %collective-permute-start.24) | collective-permute-done | bytes 393248 | tf_op jit(solution)/shard_map/ppermute | solution.py:315
  92.0 7.0 %shard_map.107 = (bf16[3,512,384]{2,1,0:T(8,128)(2,1)S(1)}, bf16[3,512,384]{2,1,0:T(8,128)(2,1)S(1)}) custom-call(s32[41]{0:T(128)S(1)} %dynamic_slice.3.plan_ref, bf16[3,512,512]{2,1,0:T(8,128)(2,1)S(1)} %shard_map.103.grad_ref.left_ref, bf16[3,6144,512]{2,1,0:T(8,128)(2,1)} %bitcast.52), custom_call_target="tpu_custom_call" | custom-call | flops 884736 | bytes 3840 | tf_op jit(solution)/shard_map/pallas_call | solution.py:217
  99.0 2.5 %collective-permute-done.31 = bf16[512,384]{1,0:T(8,128)(2,1)S(1)} collective-permute-done((bf16[512,384]{1,0:T(8,128)(2,1)S(1)}, bf16[512,384]{1,0:T(8,128)(2,1)S(1)}, u32[]{:S(2)}, u32[]{:S(2)}) %collective-permute-start.31) | collective-permute-done | bytes 393248 | tf_op jit(solution)/shard_map/ppermute | solution.py:309
  103.3 1.9 %collective-permute-start.35 = (bf16[512,384]{1,0:T(8,128)(2,1)S(1)}, bf16[512,384]{1,0:T(8,128)(2,1)S(1)}, u32[]{:S(2)}, u32[]{:S(2)}) collective-permute-start(bf16[512,384]{1,0:T(8,128)(2,1)S(1)} %get-tuple-element.147), channel_id=1, source_target_pairs={{0,2},{1,3},{4,0},{5,1},{8,4},{9,5},{12,8},{13,9},{14,12},{15,13},... | collective-permute-start | bytes 1179656 | tf_op jit(solution)/shard_map/ppermute | solution.py:309
  105.3 8.1 %shard_map.108.refs_8_ = bf16[3,6144,512]{2,1,0:T(8,128)(2,1)} custom-call(s32[41]{0:T(128)S(1)} %dynamic_slice.3.plan_ref, bf16[3,512,512]{2,1,0:T(8,128)(2,1)S(1)} %shard_map.103.grad_ref.left_ref, bf16[512,384]{1,0:T(8,128)(2,1)S(1)} %copy-done.8, bf16[512,384]{1,0:T(8,128)(2,1)S(1)} %copy-done.10, bf16[512,384]{1,0:T(8,128)(2,1)S(1)} %collective-permute-done.10.refs_2_, ...), custom_call_target="tpu_custom_call" | custom-call | flops 1179648 | bytes 3456 | tf_op jit(solution)/shard_map/pallas_call | solution.py:178
  116.7 1.8 %collective-permute-start.39 = (bf16[512,384]{1,0:T(8,128)(2,1)S(1)}, bf16[512,384]{1,0:T(8,128)(2,1)S(1)}, u32[]{:S(2)}, u32[]{:S(2)}) collective-permute-start(bf16[512,384]{1,0:T(8,128)(2,1)S(1)} %get-tuple-element.145), channel_id=1, source_target_pairs={{0,2},{1,3},{4,0},{5,1},{8,4},{9,5},{12,8},{13,9},{14,12},{15,13},... | collective-permute-start | bytes 1179656 | tf_op jit(solution)/shard_map/ppermute | solution.py:309
  118.7 7.5 %shard_map.109 = bf16[3,6144,512]{2,1,0:T(8,128)(2,1)} custom-call(s32[41]{0:T(128)S(1)} %dynamic_slice.3.plan_ref, bf16[3,512,512]{2,1,0:T(8,128)(2,1)S(1)} %shard_map.103.grad_ref.left_ref, bf16[512,384]{1,0:T(8,128)(2,1)S(1)} %collective-permute-done.27.refs_0_, ...), custom_call_target="tpu_custom_call", output_to_operand_aliasing={{}: (10, {})} | custom-call | flops 1179648 | bytes 3456 | tf_op jit(solution)/shard_map/pallas_call | solution.py:178
  (101 shorter events, 40.2 us)
Async XLA Ops:
  0.6 12.4 %collective-permute-start.1 = (bf16[512,384]{1,0:T(8,128)(2,1)}, bf16[512,384]{1,0:T(8,128)(2,1)S(1)}, u32[]{:S(2)}, u32[]{:S(2)}) collective-permute-start(bf16[512,384]{1,0:T(8,128)(2,1)} %refs_0_.4), channel_id=1, source_target_pairs={{0,2},{1,3},{4,0},{5,1},{8,4},{9,5},{12,8},{13,9},{14,12},{15,13},... | collective-permute-start | bytes 1179656 | tf_op jit(solution)/shard_map/ppermute | solution.py:309
  3.7 10.9 %collective-permute-start = (bf16[512,384]{1,0:T(8,128)(2,1)}, bf16[512,384]{1,0:T(8,128)(2,1)}, u32[]{:S(2)}, u32[]{:S(2)}) collective-permute-start(bf16[512,384]{1,0:T(8,128)(2,1)} %refs_0_.4), channel_id=1, source_target_pairs={{2,0},{3,1},{0,4},{1,5},{4,8},{5,9},{8,12},{9,13},{12,14},{13,15},... | collective-permute-start | bytes 1179656 | tf_op jit(solution)/shard_map/ppermute | solution.py:309
  3.8 13.3 %collective-permute-start.4 = (bf16[512,384]{1,0:T(8,128)(2,1)}, bf16[512,384]{1,0:T(8,128)(2,1)S(1)}, u32[]{:S(2)}, u32[]{:S(2)}) collective-permute-start(bf16[512,384]{1,0:T(8,128)(2,1)} %refs_0_.4), channel_id=1, source_target_pairs={{0,1},{1,0},{2,3},{3,2},{4,5},{5,4},{6,7},{7,6},{8,9},{9,8},{10,11... | collective-permute-start | bytes 1179656 | tf_op jit(solution)/shard_map/ppermute | solution.py:321
  16.6 10.6 %collective-permute-start.8 = (bf16[512,384]{1,0:T(8,128)(2,1)S(1)}, bf16[512,384]{1,0:T(8,128)(2,1)}, u32[]{:S(2)}, u32[]{:S(2)}) collective-permute-start(bf16[512,384]{1,0:T(8,128)(2,1)S(1)} %collective-permute-done.1.refs_1_), channel_id=1, source_target_pairs={{0,1},{1,0},{2,3},{3,2},{4,5},{5,4},{6,7},{7,6},{8,9},{9,8},{10,11... | collective-permute-start | bytes 1179656 | tf_op jit(solution)/shard_map/ppermute | solution.py:321
  24.7 11.8 %collective-permute-start.5 = (bf16[512,384]{1,0:T(8,128)(2,1)S(1)}, bf16[512,384]{1,0:T(8,128)(2,1)S(1)}, u32[]{:S(2)}, u32[]{:S(2)}) collective-permute-start(bf16[512,384]{1,0:T(8,128)(2,1)S(1)} %collective-permute-done.2.refs_0_), channel_id=1, source_target_pairs={{2,0},{3,1},{0,4},{1,5},{4,8},{5,9},{8,12},{9,13},{12,14},{13,15},... | collective-permute-start | bytes 1179656 | tf_op jit(solution)/shard_map/ppermute | solution.py:309
  26.7 12.0 %collective-permute-start.11 = (bf16[512,384]{1,0:T(8,128)(2,1)S(1)}, bf16[512,384]{1,0:T(8,128)(2,1)}, u32[]{:S(2)}, u32[]{:S(2)}) collective-permute-start(bf16[512,384]{1,0:T(8,128)(2,1)S(1)} %collective-permute-done.2.refs_0_), channel_id=1, source_target_pairs={{0,1},{1,0},{2,3},{3,2},{4,5},{5,4},{6,7},{7,6},{8,9},{9,8},{10,11... | collective-permute-start | bytes 1179656 | tf_op jit(solution)/shard_map/ppermute | solution.py:321
  26.7 13.6 %collective-permute-start.12 = (bf16[512,384]{1,0:T(8,128)(2,1)S(1)}, bf16[512,384]{1,0:T(8,128)(2,1)S(1)}, u32[]{:S(2)}, u32[]{:S(2)}) collective-permute-start(bf16[512,384]{1,0:T(8,128)(2,1)S(1)} %collective-permute-done.3.refs_1_), channel_id=1, source_target_pairs={{0,1},{1,0},{2,3},{3,2},{4,5},{5,4},{6,7},{7,6},{8,9},{9,8},{10,11... | collective-permute-start | bytes 1179656 | tf_op jit(solution)/shard_map/ppermute | solution.py:321
  37.1 11.0 %collective-permute-start.9 = (bf16[512,384]{1,0:T(8,128)(2,1)S(1)}, bf16[512,384]{1,0:T(8,128)(2,1)S(1)}, u32[]{:S(2)}, u32[]{:S(2)}) collective-permute-start(bf16[512,384]{1,0:T(8,128)(2,1)S(1)} %broadcast_select_fusion), channel_id=1, source_target_pairs={{2,0},{0,4},{4,8},{8,12},{12,14},{14,10},{10,6},{6,2},{1,3},{5,1},... | collective-permute-start | bytes 1179656 | tf_op jit(solution)/shard_map/ppermute | solution.py:312
  38.7 10.5 %collective-permute-start.10 = (bf16[512,384]{1,0:T(8,128)(2,1)S(1)}, bf16[512,384]{1,0:T(8,128)(2,1)S(1)}, u32[]{:S(2)}, u32[]{:S(2)}) collective-permute-start(bf16[512,384]{1,0:T(8,128)(2,1)S(1)} %copy-done.8), channel_id=1, source_target_pairs={{2,0},{0,4},{4,8},{8,12},{12,14},{14,10},{10,6},{6,2},{1,3},{5,1},... | collective-permute-start | bytes 1179656 | tf_op jit(solution)/shard_map/ppermute | solution.py:315
  49.2 11.1 %collective-permute-start.17 = (bf16[512,384]{1,0:T(8,128)(2,1)S(1)}, bf16[512,384]{1,0:T(8,128)(2,1)S(1)}, u32[]{:S(2)}, u32[]{:S(2)}) collective-permute-start(bf16[512,384]{1,0:T(8,128)(2,1)S(1)} %copy-done.8), channel_id=1, source_target_pairs={{0,2},{4,0},{8,4},{12,8},{14,12},{10,14},{6,10},{2,6},{3,1},{1,5},... | collective-permute-start | bytes 1179656 | tf_op jit(solution)/shard_map/ppermute | solution.py:318
  52.5 18.2 %collective-permute-start.21 = (bf16[512,384]{1,0:T(8,128)(2,1)S(1)}, bf16[512,384]{1,0:T(8,128)(2,1)}, u32[]{:S(2)}, u32[]{:S(2)}) collective-permute-start(bf16[512,384]{1,0:T(8,128)(2,1)S(1)} %collective-permute-done.10.refs_2_), channel_id=1, source_target_pairs={{0,1},{1,0},{2,3},{3,2},{4,5},{5,4},{6,7},{7,6},{8,9},{9,8},{10,11... | collective-permute-start | bytes 1179656 | tf_op jit(solution)/shard_map/ppermute | solution.py:321
  61.1 11.3 %collective-permute-start.19 = (bf16[512,384]{1,0:T(8,128)(2,1)}, bf16[512,384]{1,0:T(8,128)(2,1)S(1)}, u32[]{:S(2)}, u32[]{:S(2)}) collective-permute-start(bf16[512,384]{1,0:T(8,128)(2,1)} %collective-permute-done.16.refs_6_), channel_id=1, source_target_pairs={{2,0},{0,4},{4,8},{8,12},{12,14},{14,10},{10,6},{6,2},{1,3},{5,1},... | collective-permute-start | bytes 1179656 | tf_op jit(solution)/shard_map/ppermute | solution.py:315
  73.1 13.1 %collective-permute-start.27 = (bf16[512,384]{1,0:T(8,128)(2,1)}, bf16[512,384]{1,0:T(8,128)(2,1)S(1)}, u32[]{:S(2)}, u32[]{:S(2)}) collective-permute-start(bf16[512,384]{1,0:T(8,128)(2,1)} %collective-permute-done.16.refs_6_), channel_id=1, source_target_pairs={{0,1},{1,0},{2,3},{3,2},{4,5},{5,4},{6,7},{7,6},{8,9},{9,8},{10,11... | collective-permute-start | bytes 1179656 | tf_op jit(solution)/shard_map/ppermute | solution.py:321
  73.1 13.1 %collective-permute-start.28 = (bf16[512,384]{1,0:T(8,128)(2,1)S(1)}, bf16[512,384]{1,0:T(8,128)(2,1)S(1)}, u32[]{:S(2)}, u32[]{:S(2)}) collective-permute-start(bf16[512,384]{1,0:T(8,128)(2,1)S(1)} %collective-permute-done.20.refs_7_), channel_id=1, source_target_pairs={{0,1},{1,0},{2,3},{3,2},{4,5},{5,4},{6,7},{7,6},{8,9},{9,8},{10,11... | collective-permute-start | bytes 1179656 | tf_op jit(solution)/shard_map/ppermute | solution.py:321
  73.6 12.6 %collective-permute-start.26 = (bf16[512,384]{1,0:T(8,128)(2,1)S(1)}, bf16[512,384]{1,0:T(8,128)(2,1)S(1)}, u32[]{:S(2)}, u32[]{:S(2)}) collective-permute-start(bf16[512,384]{1,0:T(8,128)(2,1)S(1)} %collective-permute-done.20.refs_7_), channel_id=1, source_target_pairs={{0,2},{4,0},{8,4},{12,8},{14,12},{10,14},{6,10},{2,6},{3,1},{1,5},... | collective-permute-start | bytes 1179656 | tf_op jit(solution)/shard_map/ppermute | solution.py:318
  74.7 11.5 %collective-permute-start.25 = (bf16[512,384]{1,0:T(8,128)(2,1)S(1)}, bf16[512,384]{1,0:T(8,128)(2,1)S(1)}, u32[]{:S(2)}, u32[]{:S(2)}) collective-permute-start(bf16[512,384]{1,0:T(8,128)(2,1)S(1)} %collective-permute-done.19.refs_2_), channel_id=1, source_target_pairs={{2,0},{0,4},{4,8},{8,12},{12,14},{14,10},{10,6},{6,2},{1,3},{5,1},... | collective-permute-start | bytes 1179656 | tf_op jit(solution)/shard_map/ppermute | solution.py:315
  88.8 13.5 %collective-permute-start.29 = (bf16[2,512,384]{2,1,0:T(8,128)(2,1)S(1)}, bf16[2,512,384]{2,1,0:T(8,128)(2,1)S(1)}, u32[]{:S(2)}, u32[]{:S(2)}) collective-permute-start(bf16[2,512,384]{2,1,0:T(8,128)(2,1)S(1)} %get-tuple-element.116), channel_id=1, source_target_pairs={{0,1},{1,0},{2,3},{3,2},{4,5},{5,4},{6,7},{7,6},{8,9},{9,8},{10,11... | collective-permute-start | bytes 2359304 | tf_op jit(solution)/shard_map/ppermute | solution.py:321
  90.0 11.6 %collective-permute-start.31 = (bf16[512,384]{1,0:T(8,128)(2,1)S(1)}, bf16[512,384]{1,0:T(8,128)(2,1)S(1)}, u32[]{:S(2)}, u32[]{:S(2)}) collective-permute-start(bf16[512,384]{1,0:T(8,128)(2,1)S(1)} %get-tuple-element.143), channel_id=1, source_target_pairs={{0,2},{1,3},{4,0},{5,1},{8,4},{9,5},{12,8},{13,9},{14,12},{15,13},... | collective-permute-start | bytes 1179656 | tf_op jit(solution)/shard_map/ppermute | solution.py:309
  91.2 11.1 %collective-permute-start.30 = (bf16[512,384]{1,0:T(8,128)(2,1)S(1)}, bf16[512,384]{1,0:T(8,128)(2,1)S(1)}, u32[]{:S(2)}, u32[]{:S(2)}) collective-permute-start(bf16[512,384]{1,0:T(8,128)(2,1)S(1)} %get-tuple-element.144), channel_id=1, source_target_pairs={{2,0},{3,1},{0,4},{1,5},{4,8},{5,9},{8,12},{9,13},{12,14},{13,15},... | collective-permute-start | bytes 1179656 | tf_op jit(solution)/shard_map/ppermute | solution.py:309
  102.4 14.0 %collective-permute-start.33 = (bf16[3,512,384]{2,1,0:T(8,128)(2,1)S(1)}, bf16[3,512,384]{2,1,0:T(8,128)(2,1)S(1)}, u32[]{:S(2)}, u32[]{:S(2)}) collective-permute-start(bf16[3,512,384]{2,1,0:T(8,128)(2,1)S(1)} %get-tuple-element.121), channel_id=1, source_target_pairs={{0,1},{1,0},{2,3},{3,2},{4,5},{5,4},{6,7},{7,6},{8,9},{9,8},{10,11... | collective-permute-start | bytes 3538952 | tf_op jit(solution)/shard_map/ppermute | solution.py:321
  102.4 11.0 %collective-permute-start.36 = (bf16[512,384]{1,0:T(8,128)(2,1)S(1)}, bf16[512,384]{1,0:T(8,128)(2,1)S(1)}, u32[]{:S(2)}, u32[]{:S(2)}) collective-permute-start(bf16[512,384]{1,0:T(8,128)(2,1)S(1)} %collective-permute-done.25.refs_6_), channel_id=1, source_target_pairs={{0,1},{1,0},{2,3},{3,2},{4,5},{5,4},{6,7},{7,6},{8,9},{9,8},{10,11... | collective-permute-start | bytes 1179656 | tf_op jit(solution)/shard_map/ppermute | solution.py:321
  102.9 10.5 %collective-permute-start.37 = (bf16[512,384]{1,0:T(8,128)(2,1)S(1)}, bf16[512,384]{1,0:T(8,128)(2,1)S(1)}, u32[]{:S(2)}, u32[]{:S(2)}) collective-permute-start(bf16[512,384]{1,0:T(8,128)(2,1)S(1)} %collective-permute-done.26.refs_3_), channel_id=1, source_target_pairs={{0,1},{1,0},{2,3},{3,2},{4,5},{5,4},{6,7},{7,6},{8,9},{9,8},{10,11... | collective-permute-start | bytes 1179656 | tf_op jit(solution)/shard_map/ppermute | solution.py:321
  103.3 11.5 %collective-permute-start.35 = (bf16[512,384]{1,0:T(8,128)(2,1)S(1)}, bf16[512,384]{1,0:T(8,128)(2,1)S(1)}, u32[]{:S(2)}, u32[]{:S(2)}) collective-permute-start(bf16[512,384]{1,0:T(8,128)(2,1)S(1)} %get-tuple-element.147), channel_id=1, source_target_pairs={{0,2},{1,3},{4,0},{5,1},{8,4},{9,5},{12,8},{13,9},{14,12},{15,13},... | collective-permute-start | bytes 1179656 | tf_op jit(solution)/shard_map/ppermute | solution.py:309
  105.2 11.2 %collective-permute-start.34 = (bf16[512,384]{1,0:T(8,128)(2,1)S(1)}, bf16[512,384]{1,0:T(8,128)(2,1)S(1)}, u32[]{:S(2)}, u32[]{:S(2)}) collective-permute-start(bf16[512,384]{1,0:T(8,128)(2,1)S(1)} %get-tuple-element.148), channel_id=1, source_target_pairs={{2,0},{3,1},{0,4},{1,5},{4,8},{5,9},{8,12},{9,13},{12,14},{13,15},... | collective-permute-start | bytes 1179656 | tf_op jit(solution)/shard_map/ppermute | solution.py:309
  (27 other events, 191.7 us)

commit v7 on v6

--- a/solution.py
+++ b/solution.py
@@ -135,61 +135,74 @@
             scratch_shapes=[pltpu.VMEM((seq, columns), jnp.float32)],
         ),
         out_shape=jax.ShapeDtypeStruct((seq, columns), jnp.bfloat16 if last else jnp.float32),
-        compiler_params=params(40),
+        compiler_params=params(48),
         cost_estimate=cost(2 * seq * columns * part * count, MIB * count),
     )(plan, *[block for _, block in blocks], *[w_out] * count, *([] if first else [total]))
 
 
-SLOTS = 4
-
-
-def weight_kernel(places, turn, plan_ref, left_ref, *refs):
+def weight_out_kernel(places, plan_ref, left_ref, *refs):
     out_ref, held, sems = refs[-3:]
+    for i in range(len(places)):
+        held[i] = dot(left_ref[...], refs[i][...]).astype(jnp.bfloat16)
+    width = held.shape[2]
     copies = []
-    for i, (place, block) in enumerate(zip(places, refs)):
-        width = block.shape[1]
-        slot = i % SLOTS
-        if i >= SLOTS:
-            copies[i - SLOTS].wait()
-        if turn:
-            turned = block[...].T
-            for k in range(3):
-                held[slot, k] = dot(turned, left_ref[k]).astype(jnp.bfloat16)
-        else:
-            held[slot] = dot(left_ref[...], block[...]).astype(jnp.bfloat16)
+    for i, place in enumerate(places):
         start = pl.multiple_of(plan_ref[place] * width, 128)
-        copy = pltpu.make_async_copy(
-            held.at[slot], out_ref.at[:, pl.ds(start, width)], sems.at[slot]
+        copies.append(
+            pltpu.make_async_copy(held.at[i], out_ref.at[:, pl.ds(start, width)], sems.at[i])
         )
-        copy.start()
-        copies.append(copy)
-    for copy in copies[-SLOTS:]:
+        copies[i].start()
+    for copy in copies:
         copy.wait()
 
 
-def weight_grad(plan, left, blocks, shape, into=None):
-    turn = left.ndim == 3
+def weight_out(plan, left, blocks, shape, into=None):
     seq, part = blocks[0][1].shape
     count = len(blocks)
-    held = (3, part, left.shape[2]) if turn else (left.shape[0], part)
     vmem = pl.BlockSpec(memory_space=pltpu.VMEM)
     rest = pl.BlockSpec(memory_space=pl.ANY)
-    size = math.prod(held) * count
-    return pl.pallas_call(
-        functools.partial(weight_kernel, [place for place, _ in blocks], turn),
+    size = left.shape[0] * part * count
+    return pl.pallas_call(
+        functools.partial(weight_out_kernel, [place for place, _ in blocks]),
         in_specs=[pl.BlockSpec(memory_space=pltpu.SMEM)]
         + [vmem] * (1 + count)
         + [rest] * (into is not None),
         out_specs=rest,
         out_shape=jax.ShapeDtypeStruct(shape, jnp.bfloat16),
         scratch_shapes=[
-            pltpu.VMEM((SLOTS, *held), jnp.bfloat16),
-            pltpu.SemaphoreType.DMA((SLOTS,)),
+            pltpu.VMEM((count, left.shape[0], part), jnp.bfloat16),
+            pltpu.SemaphoreType.DMA((count,)),
         ],
         input_output_aliases={} if into is None else {2 + count: 0},
         compiler_params=params(40),
         cost_estimate=cost(2 * seq * size, 3 * size),
     )(plan, left, *[block for _, block in blocks], *([] if into is None else [into]))
+
+
+def weight_qkv_kernel(grad_ref, block_ref, *refs):
+    turned = block_ref[...].T
+    for k in range(3):
+        refs[-1][k] = dot(turned, grad_ref[k]).astype(jnp.bfloat16)
+
+
+def weight_qkv(grad, full_in, width, first, count, into=None):
+    _, seq, columns = grad.shape
+    features = full_in.shape[1]
+    given = [] if into is None else [into]
+    return pl.pallas_call(
+        weight_qkv_kernel,
+        grid=(count,),
+        in_specs=[
+            pl.BlockSpec((3, seq, columns), lambda i: (0, 0, 0)),
+            pl.BlockSpec((seq, width), lambda i: (0, first + i)),
+        ]
+        + [pl.BlockSpec(memory_space=pl.ANY)] * len(given),
+        out_specs=pl.BlockSpec((3, width, columns), lambda i: (0, first + i, 0)),
+        out_shape=jax.ShapeDtypeStruct((3, features, columns), jnp.bfloat16),
+        input_output_aliases={2: 0} if given else {},
+        compiler_params=params(56),
+        cost_estimate=cost(6 * seq * columns * width * count, 5 * MIB * count),
+    )(grad, full_in, *given)
 
 
 def terms_kernel(plan_ref, grad_ref, w_ref, theirs_ref, mine_ref):
@@ -267,12 +280,7 @@
     summed = [chip(chips // 2)]
     for step in range(chips // 2 - 1, 0, -1):
         summed += [chip(step), chip(-step)]
-    apart = blocks[:2]
-    for step in range(1, chips // 2):
-        behind = step if core else -step
-        for shard, first in ((core, behind), (1 - core, -behind)):
-            apart += [2 * chip(first) + shard, 2 * chip(-first) + shard]
-    return [core] + blocks + summed + [chip(0)] + apart + blocks[-2:]
+    return [core] + blocks + summed + [chip(0)]
 
 
 def after(x, *others):
@@ -296,7 +304,6 @@
     ahead = [(i + core, j + core) for i, j in hops for core in range(2)]
     back = [(j, i) for i, j in ahead]
     apart = [(i, j) for i, j in hops] + [(j + 1, i + 1) for i, j in hops]
-    crossed = [(j, i) for i, j in apart]
     swap = [(i, i ^ 1) for i in range(n)]
     plans = [plan_of(order, i) for i in range(n)]
     size = len(plans[0])
@@ -311,11 +318,8 @@
     def one_way(right, left):
         return lax.ppermute(jnp.where(on_first, right, left), "gx", apart)
 
-    def first_chain(x):
+    def both_apart(x):
         return lax.ppermute(x, "gx", apart)
-
-    def second_chain(x):
-        return lax.ppermute(x, "gx", crossed)
 
     def swapped(*arrays):
         found = [lax.ppermute(x, "gx", swap) for x in arrays]
@@ -325,12 +329,6 @@
         first = 1 if step == 0 else 4 * step - 1
         return [(first + i, array) for i, array in enumerate(arrays)]
 
-    def in_blocks(step, *arrays):
-        return [(place + 24, array) for place, array in blocks(step, *arrays)]
-
-    def grad_qkv(index, some, into=None):
-        return weight_grad(index, grad, some, w.shape, into)
-
     def total(*values):
         return sum(f32(value) for value in values[1:]) + f32(values[0])
 
@@ -344,14 +342,15 @@
         return grad_heads(index, w_out, some, so_far, last)
 
     def grad_out(index, some, into=None):
-        return weight_grad(index, attended_t, some, w_out.shape, into)
+        return weight_out(index, attended_t, some, w_out.shape, into)
 
     r1, l1 = both_ways(out_grad, out_grad)
     other = swapped(out_grad)
     attn, attended, attended_t = attend(positions, qkv)
 
-    r1, l1, attended, plan = together(r1, l1, attended, plan)
+    r1, l1, attended, inputs, plan = together(r1, l1, attended, inputs, plan)
     r2, l2 = both_ways(r1, l1)
+    full_in = lax.all_gather(inputs, "gx", axis=1, tiled=True)
     g1 = blocks(1, r1, l1, *swapped(r1, l1))
     g0 = blocks(0, out_grad, other)
     grad_h = grad_out_heads(plan, g0)
@@ -365,67 +364,56 @@
 
     r3, l3, grad_h, out, plan = together(r3, l3, grad_h, out, plan)
     x4 = one_way(r3, l3)
-    i1 = first_chain(after(inputs, r3))
     r3x, l3x = swapped(r3, l3)
     g3 = blocks(3, r3, l3, r3x, l3x)
     grad_h = grad_out_heads(plan, g2, grad_h)
 
     grad_h, r3x, l3x, plan = together(grad_h, r3x, l3x, plan)
+    grad_h = grad_out_heads(plan, g3, grad_h)
+
+    x4, grad_h, plan = together(x4, grad_h, plan)
+    x4x = swapped(x4)
     out = grad_out(plan, g2, out)
-    grad_h = grad_out_heads(plan, g3, grad_h)
-
-    x4, i1, grad_h, out, plan = together(x4, i1, grad_h, out, plan)
-    x4x, other = swapped(x4, inputs)
-    i2, j1 = first_chain(i1), second_chain(inputs)
-    f0 = in_blocks(0, inputs, other)
+
+    x4x, out, plan = together(x4x, out, plan)
     g4 = blocks(4, x4, x4x)
     grad_h = grad_out_heads(plan, g4, grad_h, last=True)
     grad = attend_back(qkv, attn, attended, grad_h)
 
-    grad, i2, j1, other, plan = together(grad, i2, j1, other, plan)
-    i3, j2 = first_chain(i2), second_chain(j1)
-    i1x, j1x = swapped(i1, j1)
     theirs3, mine3 = terms(plan, 17, 3, grad, w, part)
 
-    theirs3, mine3, i3, j2, i1x, j1x, plan = together(theirs3, mine3, i3, j2, i1x, j1x, plan)
+    theirs3, mine3, plan = together(theirs3, mine3, plan)
     theirs3 = swapped(theirs3)
-    i4, j3 = first_chain(i3), second_chain(j2)
-    i2x, j2x = swapped(i2, j2)
     out = grad_out(plan, g3 + g4, out)
 
     out, theirs3, plan = together(out, theirs3, plan)
-    low = rounded_total(mine3[0], theirs3[0])
-    s4 = first_chain(low)
+    s4 = both_apart(rounded_total(mine3[0], theirs3[0]))
     theirs2, mine2 = terms(plan, 20, 2, grad, w, part)
 
-    theirs2, mine2, s4, i4, j3, i2x, j2x, plan = together(
-        theirs2, mine2, s4, i4, j3, i2x, j2x, plan
-    )
+    theirs2, mine2, s4, plan = together(theirs2, mine2, s4, plan)
     nothing = jnp.zeros_like(s4)
     s3, u3 = both_ways(
         rounded_total(mine3[1], theirs3[1], jnp.where(on_first, s4, nothing)),
         rounded_total(mine3[2], theirs3[2], jnp.where(on_first, nothing, s4)),
     )
-    theirs2, i3x = swapped(theirs2, i3)
+    theirs2 = swapped(theirs2)
     theirs1, mine1 = terms(plan, 22, 3, grad, w, part)
 
-    theirs1, mine1, theirs2, s3, u3, i3x, plan = together(
-        theirs1, mine1, theirs2, s3, u3, i3x, plan
+    theirs1, mine1, theirs2, s3, u3, full_in, plan = together(
+        theirs1, mine1, theirs2, s3, u3, full_in, plan
     )
     s2, u2 = both_ways(
         rounded_total(mine2[0], theirs2[0], s3), rounded_total(mine2[1], theirs2[1], u3)
     )
-    theirs1, i4x, j3x = swapped(theirs1, i4, j3)
-    some = f0 + in_blocks(1, i1, j1, i1x, j1x) + in_blocks(2, i2, j2, i2x, j2x)[:2]
-    weight = grad_qkv(plan, some)
-
-    weight, theirs1, s2, u2, i4x, j3x, plan = together(weight, theirs1, s2, u2, i4x, j3x, plan)
+    theirs1 = swapped(theirs1)
+    half = n // 4
+    weight = weight_qkv(grad, full_in, 2 * part, 0, half)
+
+    weight, theirs1, s2, u2 = together(weight, theirs1, s2, u2)
     s1, u1 = both_ways(
         rounded_total(mine1[0], theirs1[0], s2), rounded_total(mine1[1], theirs1[1], u2)
     )
-    some = in_blocks(2, i2, j2, i2x, j2x)[2:]
-    some += in_blocks(3, i3, j3, i3x, j3x) + in_blocks(4, i4, i4x)
-    weight = grad_qkv(plan, some, weight)
+    weight = weight_qkv(grad, full_in, 2 * part, half, half, weight)
 
     weight, s1, u1 = together(weight, s1, u1)
     input_grad = rounded_total(mine1[2], theirs1[2], s1, u1)

time: 130 us -> 146 us (1.12)
  between operations: 0.99 us -> 14.3 us
  Pallas kernels: 67.7 us -> 76.8 us
  local copies, waits for them, and re-layouts: 7.36 us -> 1.87 us
  starting transfers between devices: 30.5 us -> 27.3 us
    ppermute x12, waiting for transfers between devices: 13.4 us -> 21.4 us  [both_ways(): return (lax.ppermute(right, 'gx', ahead), lax.ppermute(left, 'gx', back))]
    ppermute x8 -> x1, waiting for transfers between devices: 7.5 us -> 0.01 us  [both_apart(): return lax.ppermute(x, 'gx', apart)]
    unnamed x22 -> x14, local copies, waits for them, and re-layouts: 6.6 us -> 1.11 us
    pallas_call x5, Pallas kernels: 10.4 us -> 15.5 us  [grad_heads(): pl.pallas_call(functools.partial(grad_heads_kernel, count, first, last),...]
    pallas_call x6, Pallas kernels: 27.5 us -> 31.3 us  [the longest x2 18.3 us: weight_qkv(): pl.pallas_call(weight_qkv_kernel, grid=(count,), in_specs=[pl.BlockSpec((...]
    ppermute x8 -> x1, starting transfers between devices: 10.9 us -> 7.87 us  [both_apart(): return lax.ppermute(x, 'gx', apart)]
    ppermute x19 -> x11, starting transfers between devices: 4.59 us -> 2.35 us  [swapped(): found = [lax.ppermute(x, 'gx', swap) for x in arrays]]
  transfers between devices with their start and end apart: 40 -> 26, of which waited for: 14 -> 10; matrix products, arithmetic and copies ran while one was open for 1% -> 2% of each run, Pallas kernels for 52% -> 53%
where the time goes in v7:
time: 146 us; the launch traced here: 145 us
  Pallas kernels  76.8 us (53%)
  starting transfers between devices  27.3 us (19%)
  waiting for transfers between devices  21.5 us (15%)
  between operations  14.3 us (10%)
  other arithmetic  3.36 us (2%)
  local copies, waits for them, and re-layouts  1.87 us (1%)
    ppermute x12, waiting for transfers between devices, both_ways(): return (lax.ppermute(right, 'gx', ahead), lax.ppermute(left, 'gx', back))  21.4 us
    pallas_call x3, Pallas kernels, terms(): pl.pallas_call(terms_kernel, grid_spec=pltpu.PrefetchScalarGridSpec(num_s...  19.4 us
    pallas_call x2, Pallas kernels, weight_qkv(): pl.pallas_call(weight_qkv_kernel, grid=(count,), in_specs=[pl.BlockSpec((...  18.3 us
    pallas_call x5, Pallas kernels, grad_heads(): pl.pallas_call(functools.partial(grad_heads_kernel, count, first, last),...  15.5 us
    ppermute x12, starting transfers between devices, both_ways(): return (lax.ppermute(right, 'gx', ahead), lax.ppermute(left, 'gx', back))  14.7 us
    pallas_call x4, Pallas kernels, weight_out(): pl.pallas_call(functools.partial(weight_out_kernel, [place for place, _ i...  13.1 us
    ppermute x1, starting transfers between devices, both_apart(): return lax.ppermute(x, 'gx', apart)  7.87 us
    pallas_call x1, Pallas kernels, attend(): pl.pallas_call(attend_kernel, grid=(heads,), in_specs=[pl.BlockSpec((1, s...  6.62 us
  transfers between devices with their start and end apart: 26, of which 10 were waited for; matrix products, arithmetic and copies ran while one was open for 2% of the time, Pallas kernels for 53%

profile of v7, /device:TPU:0, one launch (start us, length us, event | category | flops | bytes accessed | tf_op | source)
XLA Modules:
  0.0 145.2 jit_solution(14361330890776624873)
XLA Ops:
  7.2 3.0 %collective-permute-start.1 = (bf16[512,384]{1,0:T(8,128)(2,1)}, bf16[512,384]{1,0:T(8,128)(2,1)S(1)}, u32[]{:S(2)}, u32[]{:S(2)}) collective-permute-start(bf16[512,384]{1,0:T(8,128)(2,1)} %refs_0_.3), channel_id=1, source_target_pairs={{0,2},{1,3},{4,0},{5,1},{8,4},{9,5},{12,8},{13,9},{14,12},{15,13},... | collective-permute-start | bytes 1179656 | tf_op jit(solution)/shard_map/ppermute | solution.py:316
  10.4 6.6 %shard_map.94 = (bf16[4,512,512]{2,1,0:T(8,128)(2,1)}, bf16[512,512]{1,0:T(8,128)(2,1)}, bf16[512,512]{1,0:T(8,128)(2,1)}) custom-call(s32[1,512]{1,0:T(1,128)} %bitcast.54, bf16[3,512,512]{2,1,0:T(8,128)(2,1)} %bitcast.48), custom_call_target="tpu_custom_call" | custom-call | flops 131072 | bytes 1280 | tf_op jit(solution)/shard_map/pallas_call | solution.py:51
  17.7 1.9 %collective-permute-done.1.refs_1_ = bf16[512,384]{1,0:T(8,128)(2,1)S(1)} collective-permute-done((bf16[512,384]{1,0:T(8,128)(2,1)}, bf16[512,384]{1,0:T(8,128)(2,1)S(1)}, u32[]{:S(2)}, u32[]{:S(2)}) %collective-permute-start.1) | collective-permute-done | bytes 393248 | tf_op jit(solution)/shard_map/ppermute | solution.py:316
  23.8 2.4 %shard_map.95.refs_8_ = f32[512,512]{1,0:T(8,128)S(1)} custom-call(s32[25]{0:T(128)S(1)} %dynamic_slice.3.plan_ref, bf16[512,384]{1,0:T(8,128)(2,1)S(1)} %copy-done.4, bf16[512,384]{1,0:T(8,128)(2,1)S(1)} %collective-permute-done.4.refs_1_, bf16[512,6144]{1,0:T(8,128)(2,1)} %refs_3_.3, bf16[512,6144]{1,0:T(8,128)(2,1)} %refs_3_.3), custom_call_target="tpu_custom_call" | custom-call | flops 98304 | bytes 512 | tf_op jit(solution)/shard_map/pallas_call | solution.py:126
  26.2 2.1 %shard_map.96.refs_4_ = bf16[512,6144]{1,0:T(8,128)(2,1)} custom-call(s32[25]{0:T(128)S(1)} %dynamic_slice.3.plan_ref, bf16[512,512]{1,0:T(8,128)(2,1)S(1)} %copy-done.1, bf16[512,384]{1,0:T(8,128)(2,1)S(1)} %copy-done.4, bf16[512,384]{1,0:T(8,128)(2,1)S(1)} %collective-permute-done.4.refs_1_), custom_call_target="tpu_custom_call" | custom-call | flops 98304 | bytes 288 | tf_op jit(solution)/shard_map/pallas_call | solution.py:165
  28.4 5.6 %collective-permute-done.2.refs_0_ = bf16[512,384]{1,0:T(8,128)(2,1)S(1)} collective-permute-done((bf16[512,384]{1,0:T(8,128)(2,1)}, bf16[512,384]{1,0:T(8,128)(2,1)S(1)}, u32[]{:S(2)}, u32[]{:S(2)}) %collective-permute-start.2) | collective-permute-done | bytes 393248 | tf_op jit(solution)/shard_map/ppermute | solution.py:316
  37.7 3.6 %shard_map.97.refs_8_ = f32[512,512]{1,0:T(8,128)S(1)} custom-call(s32[25]{0:T(128)S(1)} %dynamic_slice.3.plan_ref, bf16[512,384]{1,0:T(8,128)(2,1)} %collective-permute-done.refs_0_, bf16[512,384]{1,0:T(8,128)(2,1)S(1)} %collective-permute-done.1.refs_1_, bf16[512,384]{1,0:T(8,128)(2,1)} %collective-permute-done.7.refs_2_, ...), custom_call_target="tpu_custom_call" | custom-call | flops 196608 | bytes 1024 | tf_op jit(solution)/shard_map/pallas_call | solution.py:126
  41.2 3.7 %shard_map.98.refs_4_ = bf16[512,6144]{1,0:T(8,128)(2,1)} custom-call(s32[25]{0:T(128)S(1)} %dynamic_slice.3.plan_ref, bf16[512,512]{1,0:T(8,128)(2,1)S(1)} %copy-done.1, bf16[512,384]{1,0:T(8,128)(2,1)} %collective-permute-done.refs_0_, bf16[512,384]{1,0:T(8,128)(2,1)S(1)} %collective-permute-done.1.refs_1_, ...), custom_call_target="tpu_custom_call", output_to_operand_aliasing={{}: (6, {})} | custom-call | flops 196608 | bytes 576 | tf_op jit(solution)/shard_map/pallas_call | solution.py:165
  44.9 5.4 %collective-permute-done.5.refs_0_ = bf16[512,384]{1,0:T(8,128)(2,1)S(1)} collective-permute-done((bf16[512,384]{1,0:T(8,128)(2,1)S(1)}, bf16[512,384]{1,0:T(8,128)(2,1)S(1)}, u32[]{:S(2)}, u32[]{:S(2)}) %collective-permute-start.5) | collective-permute-done | bytes 393248 | tf_op jit(solution)/shard_map/ppermute | solution.py:316
  50.3 2.5 %collective-permute-done.6.refs_1_ = bf16[512,384]{1,0:T(8,128)(2,1)S(1)} collective-permute-done((bf16[512,384]{1,0:T(8,128)(2,1)}, bf16[512,384]{1,0:T(8,128)(2,1)S(1)}, u32[]{:S(2)}, u32[]{:S(2)}) %collective-permute-start.6) | collective-permute-done | bytes 393248 | tf_op jit(solution)/shard_map/ppermute | solution.py:316
  53.3 2.4 %collective-permute-start.9 = (bf16[512,384]{1,0:T(8,128)(2,1)S(1)}, bf16[512,384]{1,0:T(8,128)(2,1)S(1)}, u32[]{:S(2)}, u32[]{:S(2)}) collective-permute-start(bf16[512,384]{1,0:T(8,128)(2,1)S(1)} %broadcast_select_fusion), channel_id=1, source_target_pairs={{2,0},{0,4},{4,8},{8,12},{12,14},{14,10},{10,6},{6,2},{1,3},{5,1},... | collective-permute-start | bytes 1179656 | tf_op jit(solution)/shard_map/ppermute | solution.py:319
  55.7 3.3 %shard_map.99.refs_8_ = f32[512,512]{1,0:T(8,128)S(1)} custom-call(s32[25]{0:T(128)S(1)} %dynamic_slice.3.plan_ref, bf16[512,384]{1,0:T(8,128)(2,1)S(1)} %collective-permute-done.2.refs_0_, bf16[512,384]{1,0:T(8,128)(2,1)} %collective-permute-done.3.refs_1_, bf16[512,384]{1,0:T(8,128)(2,1)S(1)} %collective-permute-done.10.refs_2_, ...), custom_call_target="tpu_custom_call" | custom-call | flops 196608 | bytes 1024 | tf_op jit(solution)/shard_map/pallas_call | solution.py:126
  59.1 3.5 %shard_map.100.refs_4_ = f32[512,512]{1,0:T(8,128)S(1)} custom-call(s32[25]{0:T(128)S(1)} %dynamic_slice.3.plan_ref, bf16[512,384]{1,0:T(8,128)(2,1)S(1)} %collective-permute-done.5.refs_0_, bf16[512,384]{1,0:T(8,128)(2,1)S(1)} %collective-permute-done.6.refs_1_, bf16[512,384]{1,0:T(8,128)(2,1)S(1)} %collective-permute-done.12.refs_2_, ...), custom_call_target="tpu_custom_call" | custom-call | flops 196608 | bytes 1024 | tf_op jit(solution)/shard_map/pallas_call | solution.py:126
  62.7 3.5 %shard_map.101.refs_6_ = bf16[512,6144]{1,0:T(8,128)(2,1)} custom-call(s32[25]{0:T(128)S(1)} %dynamic_slice.3.plan_ref, bf16[512,512]{1,0:T(8,128)(2,1)S(1)} %copy-done.1, bf16[512,384]{1,0:T(8,128)(2,1)S(1)} %collective-permute-done.2.refs_0_, bf16[512,384]{1,0:T(8,128)(2,1)} %collective-permute-done.3.refs_1_, ...), custom_call_target="tpu_custom_call", output_to_operand_aliasing={{}: (6, {})} | custom-call | flops 196608 | bytes 576 | tf_op jit(solution)/shard_map/pallas_call | solution.py:165
  66.2 2.7 %shard_map.102.grad_ref = bf16[512,512]{1,0:T(8,128)(2,1)S(1)} custom-call(s32[25]{0:T(128)S(1)} %dynamic_slice.3.plan_ref, bf16[512,384]{1,0:T(8,128)(2,1)S(1)} %collective-permute-done.9.refs_0_.refs_4_, bf16[512,384]{1,0:T(8,128)(2,1)S(1)} %collective-permute-done.14.refs_1_.refs_5_, bf16[512,6144]{1,0:T(8,128)(2,1)} %refs_3_.3, ...), custom_call_target="tpu_custom_call" | custom-call | flops 98304 | bytes 512 | tf_op jit(solution)/shard_map/pallas_call | solution.py:126
  68.9 4.0 %shard_map.103.grad_ref = bf16[3,512,512]{2,1,0:T(8,128)(2,1)S(1)} custom-call(bf16[3,512,512]{2,1,0:T(8,128)(2,1)S(1)} %bitcast.49, bf16[4,512,512]{2,1,0:T(8,128)(2,1)S(1)} %copy-done.2, bf16[512,512]{1,0:T(8,128)(2,1)S(1)} %copy-done.5, bf16[512,512]{1,0:T(8,128)(2,1)S(1)} %shard_map.102.grad_ref), custom_call_target="tpu_custom_call" | custom-call | flops 262144 | bytes 1536 | tf_op jit(solution)/shard_map/pallas_call | solution.py:91
  72.9 7.0 %shard_map.104 = (bf16[3,512,384]{2,1,0:T(8,128)(2,1)S(1)}, bf16[3,512,384]{2,1,0:T(8,128)(2,1)S(1)}) custom-call(s32[25]{0:T(128)S(1)} %dynamic_slice.3.plan_ref, bf16[3,512,512]{2,1,0:T(8,128)(2,1)S(1)} %shard_map.103.grad_ref, bf16[3,6144,512]{2,1,0:T(8,128)(2,1)} %bitcast.50), custom_call_target="tpu_custom_call" | custom-call | flops 884736 | bytes 3840 | tf_op jit(solution)/shard_map/pallas_call | solution.py:230
  80.4 3.8 %shard_map.105 = bf16[512,6144]{1,0:T(8,128)(2,1)} custom-call(s32[25]{0:T(128)S(1)} %dynamic_slice.3.plan_ref, bf16[512,512]{1,0:T(8,128)(2,1)S(1)} %copy-done.1, bf16[512,384]{1,0:T(8,128)(2,1)S(1)} %collective-permute-done.5.refs_0_, bf16[512,384]{1,0:T(8,128)(2,1)S(1)} %collective-permute-done.6.refs_1_, ...), custom_call_target="tpu_custom_call", output_to_operand_aliasing={{}: (8, {})} | custom-call | flops 294912 | bytes 864 | tf_op jit(solution)/shard_map/pallas_call | solution.py:165
  84.4 7.9 %collective-permute-start.16 = (bf16[512,384]{1,0:T(8,128)(2,1)S(1)}, bf16[512,384]{1,0:T(8,128)(2,1)S(1)}, u32[]{:S(2)}, u32[]{:S(2)}) collective-permute-start(bf16[512,384]{1,0:T(8,128)(2,1)S(1)} %fusion.8), channel_id=1, source_target_pairs={{2,0},{0,4},{4,8},{8,12},{12,14},{14,10},{10,6},{6,2},{1,3},{5,1},... | collective-permute-start | bytes 1179656 | tf_op jit(solution)/shard_map/ppermute | solution.py:322
  92.2 5.5 %shard_map.106 = (bf16[2,512,384]{2,1,0:T(8,128)(2,1)S(1)}, bf16[2,512,384]{2,1,0:T(8,128)(2,1)S(1)}) custom-call(s32[25]{0:T(128)S(1)} %dynamic_slice.3.plan_ref, bf16[3,512,512]{2,1,0:T(8,128)(2,1)S(1)} %shard_map.103.grad_ref, bf16[3,6144,512]{2,1,0:T(8,128)(2,1)} %bitcast.51), custom_call_target="tpu_custom_call" | custom-call | flops 589824 | bytes 2560 | tf_op jit(solution)/shard_map/pallas_call | solution.py:230
  100.5 6.9 %shard_map.107 = (bf16[3,512,384]{2,1,0:T(8,128)(2,1)S(1)}, bf16[3,512,384]{2,1,0:T(8,128)(2,1)S(1)}) custom-call(s32[25]{0:T(128)S(1)} %dynamic_slice.3.plan_ref, bf16[3,512,512]{2,1,0:T(8,128)(2,1)S(1)} %shard_map.103.grad_ref, bf16[3,6144,512]{2,1,0:T(8,128)(2,1)} %bitcast.52), custom_call_target="tpu_custom_call" | custom-call | flops 884736 | bytes 3840 | tf_op jit(solution)/shard_map/pallas_call | solution.py:230
  112.1 1.9 %collective-permute-start.22 = (bf16[512,384]{1,0:T(8,128)(2,1)S(1)}, bf16[512,384]{1,0:T(8,128)(2,1)S(1)}, u32[]{:S(2)}, u32[]{:S(2)}) collective-permute-start(bf16[512,384]{1,0:T(8,128)(2,1)S(1)} %get-tuple-element.117), channel_id=1, source_target_pairs={{0,2},{1,3},{4,0},{5,1},{8,4},{9,5},{12,8},{13,9},{14,12},{15,13},... | collective-permute-start | bytes 1179656 | tf_op jit(solution)/shard_map/ppermute | solution.py:316
  114.6 9.1 %shard_map.108.refs_0_ = bf16[3,6144,512]{2,1,0:T(8,128)(2,1)} custom-call(bf16[3,512,512]{2,1,0:T(8,128)(2,1)} %copy-done, bf16[512,6144]{1,0:T(8,128)(2,1)} %all-gather.2.cloned.1.call-done.block_ref), custom_call_target="tpu_custom_call" | custom-call | flops 1179648 | bytes 5120 | tf_op jit(solution)/shard_map/pallas_call | solution.py:192
  127.5 9.1 %shard_map.109 = bf16[3,6144,512]{2,1,0:T(8,128)(2,1)} custom-call(bf16[3,512,512]{2,1,0:T(8,128)(2,1)} %copy-done, bf16[512,6144]{1,0:T(8,128)(2,1)} %all-gather.2.cloned.1.call-done.block_ref, bf16[3,6144,512]{2,1,0:T(8,128)(2,1)} %shard_map.108.refs_0_), custom_call_target="tpu_custom_call", output_to_operand_aliasing={{}: (2, {})} | custom-call | flops 1179648 | bytes 5120 | tf_op jit(solution)/shard_map/pallas_call | solution.py:192
  (66 shorter events, 23.6 us)
Async XLA Ops:
  7.2 103.2 %all-gather.2.cloned.1.call-start = ((), (), s32[]{:S(2)}) async-start(), calls=%async_computation | async-start | bytes 6684672 | tf_op jit(solution)/shard_map/all_gather | solution.py:353
  7.2 12.4 %collective-permute-start.1 = (bf16[512,384]{1,0:T(8,128)(2,1)}, bf16[512,384]{1,0:T(8,128)(2,1)S(1)}, u32[]{:S(2)}, u32[]{:S(2)}) collective-permute-start(bf16[512,384]{1,0:T(8,128)(2,1)} %refs_0_.3), channel_id=1, source_target_pairs={{0,2},{1,3},{4,0},{5,1},{8,4},{9,5},{12,8},{13,9},{14,12},{15,13},... | collective-permute-start | bytes 1179656 | tf_op jit(solution)/shard_map/ppermute | solution.py:316
  10.2 10.9 %collective-permute-start = (bf16[512,384]{1,0:T(8,128)(2,1)}, bf16[512,384]{1,0:T(8,128)(2,1)}, u32[]{:S(2)}, u32[]{:S(2)}) collective-permute-start(bf16[512,384]{1,0:T(8,128)(2,1)} %refs_0_.3), channel_id=1, source_target_pairs={{2,0},{3,1},{0,4},{1,5},{4,8},{5,9},{8,12},{9,13},{12,14},{13,15},... | collective-permute-start | bytes 1179656 | tf_op jit(solution)/shard_map/ppermute | solution.py:316
  21.2 12.7 %collective-permute-start.2 = (bf16[512,384]{1,0:T(8,128)(2,1)}, bf16[512,384]{1,0:T(8,128)(2,1)S(1)}, u32[]{:S(2)}, u32[]{:S(2)}) collective-permute-start(bf16[512,384]{1,0:T(8,128)(2,1)} %collective-permute-done.refs_0_), channel_id=1, source_target_pairs={{2,0},{3,1},{0,4},{1,5},{4,8},{5,9},{8,12},{9,13},{12,14},{13,15},... | collective-permute-start | bytes 1179656 | tf_op jit(solution)/shard_map/ppermute | solution.py:316
  21.7 12.9 %collective-permute-start.3 = (bf16[512,384]{1,0:T(8,128)(2,1)S(1)}, bf16[512,384]{1,0:T(8,128)(2,1)}, u32[]{:S(2)}, u32[]{:S(2)}) collective-permute-start(bf16[512,384]{1,0:T(8,128)(2,1)S(1)} %collective-permute-done.1.refs_1_), channel_id=1, source_target_pairs={{0,2},{1,3},{4,0},{5,1},{8,4},{9,5},{12,8},{13,9},{14,12},{15,13},... | collective-permute-start | bytes 1179656 | tf_op jit(solution)/shard_map/ppermute | solution.py:316
  23.3 13.8 %collective-permute-start.7 = (bf16[512,384]{1,0:T(8,128)(2,1)}, bf16[512,384]{1,0:T(8,128)(2,1)}, u32[]{:S(2)}, u32[]{:S(2)}) collective-permute-start(bf16[512,384]{1,0:T(8,128)(2,1)} %collective-permute-done.refs_0_), channel_id=1, source_target_pairs={{0,1},{1,0},{2,3},{3,2},{4,5},{5,4},{6,7},{7,6},{8,9},{9,8},{10,11... | collective-permute-start | bytes 1179656 | tf_op jit(solution)/shard_map/ppermute | solution.py:325
  23.3 14.3 %collective-permute-start.8 = (bf16[512,384]{1,0:T(8,128)(2,1)S(1)}, bf16[512,384]{1,0:T(8,128)(2,1)}, u32[]{:S(2)}, u32[]{:S(2)}) collective-permute-start(bf16[512,384]{1,0:T(8,128)(2,1)S(1)} %collective-permute-done.1.refs_1_), channel_id=1, source_target_pairs={{0,1},{1,0},{2,3},{3,2},{4,5},{5,4},{6,7},{7,6},{8,9},{9,8},{10,11... | collective-permute-start | bytes 1179656 | tf_op jit(solution)/shard_map/ppermute | solution.py:325
  34.6 15.7 %collective-permute-start.5 = (bf16[512,384]{1,0:T(8,128)(2,1)S(1)}, bf16[512,384]{1,0:T(8,128)(2,1)S(1)}, u32[]{:S(2)}, u32[]{:S(2)}) collective-permute-start(bf16[512,384]{1,0:T(8,128)(2,1)S(1)} %collective-permute-done.2.refs_0_), channel_id=1, source_target_pairs={{2,0},{3,1},{0,4},{1,5},{4,8},{5,9},{8,12},{9,13},{12,14},{13,15},... | collective-permute-start | bytes 1179656 | tf_op jit(solution)/shard_map/ppermute | solution.py:316
  36.1 16.7 %collective-permute-start.6 = (bf16[512,384]{1,0:T(8,128)(2,1)}, bf16[512,384]{1,0:T(8,128)(2,1)S(1)}, u32[]{:S(2)}, u32[]{:S(2)}) collective-permute-start(bf16[512,384]{1,0:T(8,128)(2,1)} %collective-permute-done.3.refs_1_), channel_id=1, source_target_pairs={{0,2},{1,3},{4,0},{5,1},{8,4},{9,5},{12,8},{13,9},{14,12},{15,13},... | collective-permute-start | bytes 1179656 | tf_op jit(solution)/shard_map/ppermute | solution.py:316
  37.1 18.6 %collective-permute-start.10 = (bf16[512,384]{1,0:T(8,128)(2,1)S(1)}, bf16[512,384]{1,0:T(8,128)(2,1)S(1)}, u32[]{:S(2)}, u32[]{:S(2)}) collective-permute-start(bf16[512,384]{1,0:T(8,128)(2,1)S(1)} %collective-permute-done.2.refs_0_), channel_id=1, source_target_pairs={{0,1},{1,0},{2,3},{3,2},{4,5},{5,4},{6,7},{7,6},{8,9},{9,8},{10,11... | collective-permute-start | bytes 1179656 | tf_op jit(solution)/shard_map/ppermute | solution.py:325
  37.1 18.6 %collective-permute-start.11 = (bf16[512,384]{1,0:T(8,128)(2,1)}, bf16[512,384]{1,0:T(8,128)(2,1)S(1)}, u32[]{:S(2)}, u32[]{:S(2)}) collective-permute-start(bf16[512,384]{1,0:T(8,128)(2,1)} %collective-permute-done.3.refs_1_), channel_id=1, source_target_pairs={{0,1},{1,0},{2,3},{3,2},{4,5},{5,4},{6,7},{7,6},{8,9},{9,8},{10,11... | collective-permute-start | bytes 1179656 | tf_op jit(solution)/shard_map/ppermute | solution.py:325
  52.8 6.3 %collective-permute-start.12 = (bf16[512,384]{1,0:T(8,128)(2,1)S(1)}, bf16[512,384]{1,0:T(8,128)(2,1)S(1)}, u32[]{:S(2)}, u32[]{:S(2)}) collective-permute-start(bf16[512,384]{1,0:T(8,128)(2,1)S(1)} %collective-permute-done.5.refs_0_), channel_id=1, source_target_pairs={{0,1},{1,0},{2,3},{3,2},{4,5},{5,4},{6,7},{7,6},{8,9},{9,8},{10,11... | collective-permute-start | bytes 1179656 | tf_op jit(solution)/shard_map/ppermute | solution.py:325
  52.8 6.3 %collective-permute-start.13 = (bf16[512,384]{1,0:T(8,128)(2,1)S(1)}, bf16[512,384]{1,0:T(8,128)(2,1)S(1)}, u32[]{:S(2)}, u32[]{:S(2)}) collective-permute-start(bf16[512,384]{1,0:T(8,128)(2,1)S(1)} %collective-permute-done.6.refs_1_), channel_id=1, source_target_pairs={{0,1},{1,0},{2,3},{3,2},{4,5},{5,4},{6,7},{7,6},{8,9},{9,8},{10,11... | collective-permute-start | bytes 1179656 | tf_op jit(solution)/shard_map/ppermute | solution.py:325
  53.3 9.3 %collective-permute-start.9 = (bf16[512,384]{1,0:T(8,128)(2,1)S(1)}, bf16[512,384]{1,0:T(8,128)(2,1)S(1)}, u32[]{:S(2)}, u32[]{:S(2)}) collective-permute-start(bf16[512,384]{1,0:T(8,128)(2,1)S(1)} %broadcast_select_fusion), channel_id=1, source_target_pairs={{2,0},{0,4},{4,8},{8,12},{12,14},{14,10},{10,6},{6,2},{1,3},{5,1},... | collective-permute-start | bytes 1179656 | tf_op jit(solution)/shard_map/ppermute | solution.py:319
  79.9 4.4 %collective-permute-start.15 = (bf16[3,512,384]{2,1,0:T(8,128)(2,1)S(1)}, bf16[3,512,384]{2,1,0:T(8,128)(2,1)S(1)}, u32[]{:S(2)}, u32[]{:S(2)}) collective-permute-start(bf16[3,512,384]{2,1,0:T(8,128)(2,1)S(1)} %get-tuple-element.86), channel_id=1, source_target_pairs={{0,1},{1,0},{2,3},{3,2},{4,5},{5,4},{6,7},{7,6},{8,9},{9,8},{10,11... | collective-permute-start | bytes 3538952 | tf_op jit(solution)/shard_map/ppermute | solution.py:325
  84.4 13.4 %collective-permute-start.16 = (bf16[512,384]{1,0:T(8,128)(2,1)S(1)}, bf16[512,384]{1,0:T(8,128)(2,1)S(1)}, u32[]{:S(2)}, u32[]{:S(2)}) collective-permute-start(bf16[512,384]{1,0:T(8,128)(2,1)S(1)} %fusion.8), channel_id=1, source_target_pairs={{2,0},{0,4},{4,8},{8,12},{12,14},{14,10},{10,6},{6,2},{1,3},{5,1},... | collective-permute-start | bytes 1179656 | tf_op jit(solution)/shard_map/ppermute | solution.py:322
  97.8 12.5 %collective-permute-start.17 = (bf16[2,512,384]{2,1,0:T(8,128)(2,1)S(1)}, bf16[2,512,384]{2,1,0:T(8,128)(2,1)}, u32[]{:S(2)}, u32[]{:S(2)}) collective-permute-start(bf16[2,512,384]{2,1,0:T(8,128)(2,1)S(1)} %get-tuple-element.95), channel_id=1, source_target_pairs={{0,1},{1,0},{2,3},{3,2},{4,5},{5,4},{6,7},{7,6},{8,9},{9,8},{10,11... | collective-permute-start | bytes 2359304 | tf_op jit(solution)/shard_map/ppermute | solution.py:325
  98.2 12.1 %collective-permute-start.19 = (bf16[512,384]{1,0:T(8,128)(2,1)S(1)}, bf16[512,384]{1,0:T(8,128)(2,1)}, u32[]{:S(2)}, u32[]{:S(2)}) collective-permute-start(bf16[512,384]{1,0:T(8,128)(2,1)S(1)} %get-tuple-element.113), channel_id=1, source_target_pairs={{0,2},{1,3},{4,0},{5,1},{8,4},{9,5},{12,8},{13,9},{14,12},{15,13},... | collective-permute-start | bytes 1179656 | tf_op jit(solution)/shard_map/ppermute | solution.py:316
  98.8 11.5 %collective-permute-start.18 = (bf16[512,384]{1,0:T(8,128)(2,1)S(1)}, bf16[512,384]{1,0:T(8,128)(2,1)}, u32[]{:S(2)}, u32[]{:S(2)}) collective-permute-start(bf16[512,384]{1,0:T(8,128)(2,1)S(1)} %get-tuple-element.114), channel_id=1, source_target_pairs={{2,0},{3,1},{0,4},{1,5},{4,8},{5,9},{8,12},{9,13},{12,14},{13,15},... | collective-permute-start | bytes 1179656 | tf_op jit(solution)/shard_map/ppermute | solution.py:316
  110.3 14.8 %collective-permute-start.20 = (bf16[3,512,384]{2,1,0:T(8,128)(2,1)}, bf16[3,512,384]{2,1,0:T(8,128)(2,1)S(1)}, u32[]{:S(2)}, u32[]{:S(2)}) collective-permute-start(bf16[3,512,384]{2,1,0:T(8,128)(2,1)} %copy-done.6), channel_id=1, source_target_pairs={{0,1},{1,0},{2,3},{3,2},{4,5},{5,4},{6,7},{7,6},{8,9},{9,8},{10,11... | collective-permute-start | bytes 3538952 | tf_op jit(solution)/shard_map/ppermute | solution.py:325
  112.1 12.2 %collective-permute-start.22 = (bf16[512,384]{1,0:T(8,128)(2,1)S(1)}, bf16[512,384]{1,0:T(8,128)(2,1)S(1)}, u32[]{:S(2)}, u32[]{:S(2)}) collective-permute-start(bf16[512,384]{1,0:T(8,128)(2,1)S(1)} %get-tuple-element.117), channel_id=1, source_target_pairs={{0,2},{1,3},{4,0},{5,1},{8,4},{9,5},{12,8},{13,9},{14,12},{15,13},... | collective-permute-start | bytes 1179656 | tf_op jit(solution)/shard_map/ppermute | solution.py:316
  113.9 11.2 %collective-permute-start.21 = (bf16[512,384]{1,0:T(8,128)(2,1)S(1)}, bf16[512,384]{1,0:T(8,128)(2,1)S(1)}, u32[]{:S(2)}, u32[]{:S(2)}) collective-permute-start(bf16[512,384]{1,0:T(8,128)(2,1)S(1)} %get-tuple-element.118), channel_id=1, source_target_pairs={{2,0},{3,1},{0,4},{1,5},{4,8},{5,9},{8,12},{9,13},{12,14},{13,15},... | collective-permute-start | bytes 1179656 | tf_op jit(solution)/shard_map/ppermute | solution.py:316
  125.5 11.2 %collective-permute-start.24 = (bf16[512,384]{1,0:T(8,128)(2,1)S(1)}, bf16[512,384]{1,0:T(8,128)(2,1)S(1)}, u32[]{:S(2)}, u32[]{:S(2)}) collective-permute-start(bf16[512,384]{1,0:T(8,128)(2,1)S(1)} %get-tuple-element.115), channel_id=1, source_target_pairs={{0,2},{1,3},{4,0},{5,1},{8,4},{9,5},{12,8},{13,9},{14,12},{15,13},... | collective-permute-start | bytes 1179656 | tf_op jit(solution)/shard_map/ppermute | solution.py:316
  127.3 10.1 %collective-permute-start.23 = (bf16[512,384]{1,0:T(8,128)(2,1)S(1)}, bf16[512,384]{1,0:T(8,128)(2,1)S(1)}, u32[]{:S(2)}, u32[]{:S(2)}) collective-permute-start(bf16[512,384]{1,0:T(8,128)(2,1)S(1)} %get-tuple-element.116), channel_id=1, source_target_pairs={{2,0},{3,1},{0,4},{1,5},{4,8},{5,9},{8,12},{9,13},{12,14},{13,15},... | collective-permute-start | bytes 1179656 | tf_op jit(solution)/shard_map/ppermute | solution.py:316
  (9 other events, 59.0 us)
Sparse Core Ops, SparseCore 0:
  21.3 74.4 all-gather.1

commit v8 on v6

--- a/solution.py
+++ b/solution.py
@@ -143,18 +143,17 @@
 SLOTS = 4
 
 
-def weight_kernel(places, turn, plan_ref, left_ref, *refs):
+def weight_kernel(places, turned, plan_ref, left_ref, *refs):
     out_ref, held, sems = refs[-3:]
     copies = []
     for i, (place, block) in enumerate(zip(places, refs)):
-        width = block.shape[1]
+        width = block.shape[0 if turned else 1]
         slot = i % SLOTS
         if i >= SLOTS:
             copies[i - SLOTS].wait()
-        if turn:
-            turned = block[...].T
+        if turned:
             for k in range(3):
-                held[slot, k] = dot(turned, left_ref[k]).astype(jnp.bfloat16)
+                held[slot, k] = dot(block[...], left_ref[k]).astype(jnp.bfloat16)
         else:
             held[slot] = dot(left_ref[...], block[...]).astype(jnp.bfloat16)
         start = pl.multiple_of(plan_ref[place] * width, 128)
@@ -168,15 +167,15 @@
 
 
 def weight_grad(plan, left, blocks, shape, into=None):
-    turn = left.ndim == 3
-    seq, part = blocks[0][1].shape
+    turned = left.ndim == 3
+    seq, part = blocks[0][1].shape[::-1] if turned else blocks[0][1].shape
     count = len(blocks)
-    held = (3, part, left.shape[2]) if turn else (left.shape[0], part)
+    held = (3, part, left.shape[2]) if turned else (left.shape[0], part)
     vmem = pl.BlockSpec(memory_space=pltpu.VMEM)
     rest = pl.BlockSpec(memory_space=pl.ANY)
     size = math.prod(held) * count
     return pl.pallas_call(
-        functools.partial(weight_kernel, [place for place, _ in blocks], turn),
+        functools.partial(weight_kernel, [place for place, _ in blocks], turned),
         in_specs=[pl.BlockSpec(memory_space=pltpu.SMEM)]
         + [vmem] * (1 + count)
         + [rest] * (into is not None),
@@ -339,6 +338,7 @@
 
     qkv = saved_qkv.transpose(1, 0, 2)
     w = w_qkv.transpose(1, 0, 2)
+    inputs = inputs.T
 
     def grad_out_heads(index, some, so_far=None, last=False):
         return grad_heads(index, w_out, some, so_far, last)
@@ -354,13 +354,12 @@
     r2, l2 = both_ways(r1, l1)
     g1 = blocks(1, r1, l1, *swapped(r1, l1))
     g0 = blocks(0, out_grad, other)
-    grad_h = grad_out_heads(plan, g0)
     out = grad_out(plan, g0)
 
-    r2, l2, grad_h, out, plan = together(r2, l2, grad_h, out, plan)
+    r2, l2, out, plan = together(r2, l2, out, plan)
     r3, l3 = both_ways(r2, l2)
     g2 = blocks(2, r2, l2, *swapped(r2, l2))
-    grad_h = grad_out_heads(plan, g1, grad_h)
+    grad_h = grad_out_heads(plan, g0 + g1)
     out = grad_out(plan, g1, out)
 
     r3, l3, grad_h, out, plan = together(r3, l3, grad_h, out, plan)
@@ -371,10 +370,9 @@
     grad_h = grad_out_heads(plan, g2, grad_h)
 
     grad_h, r3x, l3x, plan = together(grad_h, r3x, l3x, plan)
-    out = grad_out(plan, g2, out)
     grad_h = grad_out_heads(plan, g3, grad_h)
 
-    x4, i1, grad_h, out, plan = together(x4, i1, grad_h, out, plan)
+    x4, i1, grad_h, plan = together(x4, i1, grad_h, plan)
     x4x, other = swapped(x4, inputs)
     i2, j1 = first_chain(i1), second_chain(inputs)
     f0 = in_blocks(0, inputs, other)
@@ -382,7 +380,10 @@
     grad_h = grad_out_heads(plan, g4, grad_h, last=True)
     grad = attend_back(qkv, attn, attended, grad_h)
 
-    grad, i2, j1, other, plan = together(grad, i2, j1, other, plan)
+    grad, plan = together(grad, plan)
+    out = grad_out(plan, g2, out)
+
+    out, i2, j1, other, plan = together(out, i2, j1, other, plan)
     i3, j2 = first_chain(i2), second_chain(j1)
     i1x, j1x = swapped(i1, j1)
     theirs3, mine3 = terms(plan, 17, 3, grad, w, part)

time: 130 us -> 131 us (level)
  waiting for transfers between devices: 20.9 us -> 24.9 us
  local copies, waits for them, and re-layouts: 7.36 us -> 5.19 us
    ppermute x12, waiting for transfers between devices: 13.4 us -> 16.4 us  [both_ways(): return (lax.ppermute(right, 'gx', ahead), lax.ppermute(left, 'gx', back))]
    ppermute x5, waiting for transfers between devices: 5.27 us -> 7.86 us  [first_chain(): return lax.ppermute(x, 'gx', apart)]
    unnamed x22 -> x41, local copies, waits for them, and re-layouts: 6.6 us -> 4.43 us
    ppermute x3, waiting for transfers between devices: 2.22 us -> 0.58 us  [second_chain(): return lax.ppermute(x, 'gx', crossed)]
    pallas_call x5 -> x4, Pallas kernels: 10.4 us -> 9.96 us  [grad_heads(): pl.pallas_call(functools.partial(grad_heads_kernel, count, first, last),...]
  transfers between devices with their start and end apart: 40 -> 40, of which waited for: 14 -> 14; matrix products, arithmetic and copies ran while one was open for 1% -> 3% of each run, Pallas kernels for 52% -> 52%
where the time goes in v8:
time: 131 us; the launch traced here: 130 us
  Pallas kernels  67.6 us (52%)
  starting transfers between devices  29.4 us (22%)
  waiting for transfers between devices  24.9 us (19%)
  local copies, waits for them, and re-layouts  5.19 us (4%)
  other arithmetic  2.04 us (2%)
    pallas_call x6, Pallas kernels, weight_grad(): pl.pallas_call(functools.partial(weight_kernel, [place for place, _ in bl...  27.8 us
    pallas_call x3, Pallas kernels, terms(): pl.pallas_call(terms_kernel, grid_spec=pltpu.PrefetchScalarGridSpec(num_s...  19.3 us
    ppermute x12, waiting for transfers between devices, both_ways(): return (lax.ppermute(right, 'gx', ahead), lax.ppermute(left, 'gx', back))  16.4 us
    ppermute x12, starting transfers between devices, both_ways(): return (lax.ppermute(right, 'gx', ahead), lax.ppermute(left, 'gx', back))  13.4 us
    pallas_call x4, Pallas kernels, grad_heads(): pl.pallas_call(functools.partial(grad_heads_kernel, count, first, last),...  9.96 us
    ppermute x5, waiting for transfers between devices, first_chain(): return lax.ppermute(x, 'gx', apart)  7.86 us
    pallas_call x1, Pallas kernels, attend(): pl.pallas_call(attend_kernel, grid=(heads,), in_specs=[pl.BlockSpec((1, s...  6.58 us
    ppermute x5, starting transfers between devices, first_chain(): return lax.ppermute(x, 'gx', apart)  6.09 us
  transfers between devices with their start and end apart: 40, of which 14 were waited for; matrix products, arithmetic and copies ran while one was open for 3% of the time, Pallas kernels for 52%

profile of v8, /device:TPU:0, one launch (start us, length us, event | category | flops | bytes accessed | tf_op | source)
XLA Modules:
  0.0 130.3 jit_solution(2450513517642052920)
XLA Ops:
  0.6 3.0 %collective-permute-start.1 = (bf16[512,384]{1,0:T(8,128)(2,1)}, bf16[512,384]{1,0:T(8,128)(2,1)}, u32[]{:S(2)}, u32[]{:S(2)}) collective-permute-start(bf16[512,384]{1,0:T(8,128)(2,1)} %refs_0_.3), channel_id=1, source_target_pairs={{0,2},{1,3},{4,0},{5,1},{8,4},{9,5},{12,8},{13,9},{14,12},{15,13},... | collective-permute-start | bytes 1179656 | tf_op jit(solution)/shard_map/ppermute | solution.py:308
  3.8 6.6 %shard_map.94 = (bf16[4,512,512]{2,1,0:T(8,128)(2,1)}, bf16[512,512]{1,0:T(8,128)(2,1)}, bf16[512,512]{1,0:T(8,128)(2,1)}) custom-call(s32[1,512]{1,0:T(1,128)} %bitcast.61, bf16[3,512,512]{2,1,0:T(8,128)(2,1)} %bitcast.51), custom_call_target="tpu_custom_call" | custom-call | flops 131072 | bytes 1280 | tf_op jit(solution)/shard_map/pallas_call | solution.py:51
  11.1 2.0 %collective-permute-done.1.refs_3_.refs_1_ = bf16[512,384]{1,0:T(8,128)(2,1)} collective-permute-done((bf16[512,384]{1,0:T(8,128)(2,1)}, bf16[512,384]{1,0:T(8,128)(2,1)}, u32[]{:S(2)}, u32[]{:S(2)}) %collective-permute-start.1) | collective-permute-done | bytes 393248 | tf_op jit(solution)/shard_map/ppermute | solution.py:308
  15.0 1.6 %collective-permute-start.3 = (bf16[512,384]{1,0:T(8,128)(2,1)}, bf16[512,384]{1,0:T(8,128)(2,1)}, u32[]{:S(2)}, u32[]{:S(2)}) collective-permute-start(bf16[512,384]{1,0:T(8,128)(2,1)} %collective-permute-done.1.refs_3_.refs_1_), channel_id=1, source_target_pairs={{0,2},{1,3},{4,0},{5,1},{8,4},{9,5},{12,8},{13,9},{14,12},{15,13},... | collective-permute-start | bytes 1179656 | tf_op jit(solution)/shard_map/ppermute | solution.py:308
  18.3 2.0 %shard_map.95.refs_4_ = bf16[512,6144]{1,0:T(8,128)(2,1)} custom-call(s32[41]{0:T(128)S(1)} %dynamic_slice.3.plan_ref, bf16[512,512]{1,0:T(8,128)(2,1)S(1)} %copy-done, bf16[512,384]{1,0:T(8,128)(2,1)S(1)} %copy-done.3, bf16[512,384]{1,0:T(8,128)(2,1)S(1)} %collective-permute-done.4.refs_1_), custom_call_target="tpu_custom_call" | custom-call | flops 98304 | bytes 288 | tf_op jit(solution)/shard_map/pallas_call | solution.py:177
  20.3 4.2 %collective-permute-done.2.refs_0_ = bf16[512,384]{1,0:T(8,128)(2,1)} collective-permute-done((bf16[512,384]{1,0:T(8,128)(2,1)}, bf16[512,384]{1,0:T(8,128)(2,1)}, u32[]{:S(2)}, u32[]{:S(2)}) %collective-permute-start.2) | collective-permute-done | bytes 393248 | tf_op jit(solution)/shard_map/ppermute | solution.py:308
  27.0 2.1 %copy.14 = bf16[512,384]{0,1:T(8,128)(2,1)} copy(bf16[512,384]{1,0:T(8,128)(2,1)} %param.7) | data formatting | bytes 786432 | tf_op args[0]
  29.7 3.7 %shard_map.97.refs_4_ = bf16[512,6144]{1,0:T(8,128)(2,1)} custom-call(s32[41]{0:T(128)S(1)} %dynamic_slice.3.plan_ref, bf16[512,512]{1,0:T(8,128)(2,1)S(1)} %copy-done.1, bf16[512,384]{1,0:T(8,128)(2,1)} %collective-permute-done.refs_2_.refs_0_, bf16[512,384]{1,0:T(8,128)(2,1)} %collective-permute-done.1.refs_3_.refs_1_, ...), custom_call_target="tpu_custom_call", output_to_operand_aliasing={{}: (6, {})} | custom-call | flops 196608 | bytes 576 | tf_op jit(solution)/shard_map/pallas_call | solution.py:177
  33.4 3.7 %shard_map.96.refs_8_ = f32[512,512]{1,0:T(8,128)S(1)} custom-call(s32[41]{0:T(128)S(1)} %dynamic_slice.3.plan_ref, bf16[512,384]{1,0:T(8,128)(2,1)S(1)} %copy-done.4, bf16[512,384]{1,0:T(8,128)(2,1)S(1)} %copy-done.6, bf16[512,384]{1,0:T(8,128)(2,1)} %collective-permute-done.refs_2_.refs_0_, bf16[512,384]{1,0:T(8,128)(2,1)} %collective-permute-done.1.refs_3_.refs_1_, ...), custom_call_target="tpu_custom_call" | custom-call | flops 294912 | bytes 1536 | tf_op jit(solution)/shard_map/pallas_call | solution.py:126
  39.4 1.6 %collective-permute-start.10 = (bf16[384,512]{1,0:T(8,128)(2,1)S(1)}, bf16[384,512]{1,0:T(8,128)(2,1)S(1)}, u32[]{:S(2)}, u32[]{:S(2)}) collective-permute-start(bf16[384,512]{1,0:T(8,128)(2,1)S(1)} %bitcast.53), channel_id=1, source_target_pairs={{2,0},{0,4},{4,8},{8,12},{12,14},{14,10},{10,6},{6,2},{1,3},{5,1},... | collective-permute-start | bytes 1179656 | tf_op jit(solution)/shard_map/ppermute | solution.py:314
  40.9 3.0 %shard_map.98.refs_8_ = f32[512,512]{1,0:T(8,128)S(1)} custom-call(s32[41]{0:T(128)S(1)} %dynamic_slice.3.plan_ref, bf16[512,384]{1,0:T(8,128)(2,1)} %collective-permute-done.2.refs_0_, bf16[512,384]{1,0:T(8,128)(2,1)} %collective-permute-done.3.refs_1_, bf16[512,384]{1,0:T(8,128)(2,1)} %collective-permute-done.11.refs_2_, ...), custom_call_target="tpu_custom_call" | custom-call | flops 196608 | bytes 1024 | tf_op jit(solution)/shard_map/pallas_call | solution.py:126
  44.0 1.9 %shard_map.99.refs_4_ = f32[512,512]{1,0:T(8,128)S(1)} custom-call(s32[41]{0:T(128)S(1)} %dynamic_slice.3.plan_ref, bf16[512,384]{1,0:T(8,128)(2,1)S(1)} %collective-permute-done.5.refs_0_, bf16[512,384]{1,0:T(8,128)(2,1)S(1)} %collective-permute-done.6.refs_1_, bf16[512,384]{1,0:T(8,128)(2,1)S(1)} %collective-permute-done.13.refs_2_, ...), custom_call_target="tpu_custom_call" | custom-call | flops 196608 | bytes 1024 | tf_op jit(solution)/shard_map/pallas_call | solution.py:126
  46.0 3.9 %collective-permute-done.10.refs_2_ = bf16[384,512]{1,0:T(8,128)(2,1)S(1)} collective-permute-done((bf16[384,512]{1,0:T(8,128)(2,1)S(1)}, bf16[384,512]{1,0:T(8,128)(2,1)S(1)}, u32[]{:S(2)}, u32[]{:S(2)}) %collective-permute-start.10) | collective-permute-done | bytes 393248 | tf_op jit(solution)/shard_map/ppermute | solution.py:314
  54.1 4.0 %shard_map.101.grad_ref.left_ref = bf16[3,512,512]{2,1,0:T(8,128)(2,1)S(1)} custom-call(bf16[3,512,512]{2,1,0:T(8,128)(2,1)S(1)} %bitcast.52, bf16[4,512,512]{2,1,0:T(8,128)(2,1)S(1)} %copy-done.2, bf16[512,512]{1,0:T(8,128)(2,1)S(1)} %copy-done.13, bf16[512,512]{1,0:T(8,128)(2,1)S(1)} %shard_map.100.grad_ref), custom_call_target="tpu_custom_call" | custom-call | flops 262144 | bytes 1536 | tf_op jit(solution)/shard_map/pallas_call | solution.py:91
  58.1 3.3 %shard_map.102.refs_6_ = bf16[512,6144]{1,0:T(8,128)(2,1)} custom-call(s32[41]{0:T(128)S(1)} %dynamic_slice.3.plan_ref, bf16[512,512]{1,0:T(8,128)(2,1)S(1)} %copy-done.1, bf16[512,384]{1,0:T(8,128)(2,1)} %collective-permute-done.2.refs_0_, bf16[512,384]{1,0:T(8,128)(2,1)} %collective-permute-done.3.refs_1_, ...), custom_call_target="tpu_custom_call", output_to_operand_aliasing={{}: (6, {})} | custom-call | flops 196608 | bytes 576 | tf_op jit(solution)/shard_map/pallas_call | solution.py:177
  65.3 7.0 %shard_map.103 = (bf16[3,512,384]{2,1,0:T(8,128)(2,1)S(1)}, bf16[3,512,384]{2,1,0:T(8,128)(2,1)S(1)}) custom-call(s32[41]{0:T(128)S(1)} %dynamic_slice.3.plan_ref, bf16[3,512,512]{2,1,0:T(8,128)(2,1)S(1)} %shard_map.101.grad_ref.left_ref, bf16[3,6144,512]{2,1,0:T(8,128)(2,1)} %bitcast.57), custom_call_target="tpu_custom_call" | custom-call | flops 884736 | bytes 3840 | tf_op jit(solution)/shard_map/pallas_call | solution.py:216
  76.7 3.5 %shard_map.104 = bf16[512,6144]{1,0:T(8,128)(2,1)} custom-call(s32[41]{0:T(128)S(1)} %dynamic_slice.3.plan_ref, bf16[512,512]{1,0:T(8,128)(2,1)S(1)} %copy-done.1, bf16[512,384]{1,0:T(8,128)(2,1)S(1)} %collective-permute-done.5.refs_0_, bf16[512,384]{1,0:T(8,128)(2,1)S(1)} %collective-permute-done.6.refs_1_, ...), custom_call_target="tpu_custom_call", output_to_operand_aliasing={{}: (8, {})} | custom-call | flops 294912 | bytes 864 | tf_op jit(solution)/shard_map/pallas_call | solution.py:177
  81.9 5.3 %shard_map.105 = (bf16[2,512,384]{2,1,0:T(8,128)(2,1)S(1)}, bf16[2,512,384]{2,1,0:T(8,128)(2,1)S(1)}) custom-call(s32[41]{0:T(128)S(1)} %dynamic_slice.3.plan_ref, bf16[3,512,512]{2,1,0:T(8,128)(2,1)S(1)} %shard_map.101.grad_ref.left_ref, bf16[3,6144,512]{2,1,0:T(8,128)(2,1)} %bitcast.58), custom_call_target="tpu_custom_call" | custom-call | flops 589824 | bytes 2560 | tf_op jit(solution)/shard_map/pallas_call | solution.py:216
  87.3 2.9 %collective-permute-done.24 = bf16[512,384]{1,0:T(8,128)(2,1)S(1)} collective-permute-done((bf16[512,384]{1,0:T(8,128)(2,1)S(1)}, bf16[512,384]{1,0:T(8,128)(2,1)S(1)}, u32[]{:S(2)}, u32[]{:S(2)}) %collective-permute-start.24) | collective-permute-done | bytes 393248 | tf_op jit(solution)/shard_map/ppermute | solution.py:314
  93.2 7.0 %shard_map.106 = (bf16[3,512,384]{2,1,0:T(8,128)(2,1)S(1)}, bf16[3,512,384]{2,1,0:T(8,128)(2,1)S(1)}) custom-call(s32[41]{0:T(128)S(1)} %dynamic_slice.3.plan_ref, bf16[3,512,512]{2,1,0:T(8,128)(2,1)S(1)} %shard_map.101.grad_ref.left_ref, bf16[3,6144,512]{2,1,0:T(8,128)(2,1)} %bitcast.59), custom_call_target="tpu_custom_call" | custom-call | flops 884736 | bytes 3840 | tf_op jit(solution)/shard_map/pallas_call | solution.py:216
  100.2 2.5 %collective-permute-done.31 = bf16[512,384]{1,0:T(8,128)(2,1)S(1)} collective-permute-done((bf16[512,384]{1,0:T(8,128)(2,1)S(1)}, bf16[512,384]{1,0:T(8,128)(2,1)S(1)}, u32[]{:S(2)}, u32[]{:S(2)}) %collective-permute-start.31) | collective-permute-done | bytes 393248 | tf_op jit(solution)/shard_map/ppermute | solution.py:308
  106.4 8.0 %shard_map.107.refs_8_ = bf16[3,6144,512]{2,1,0:T(8,128)(2,1)} custom-call(s32[41]{0:T(128)S(1)} %dynamic_slice.3.plan_ref, bf16[3,512,512]{2,1,0:T(8,128)(2,1)S(1)} %shard_map.101.grad_ref.left_ref, bf16[384,512]{1,0:T(8,128)(2,1)S(1)} %bitcast.56, bf16[384,512]{1,0:T(8,128)(2,1)S(1)} %copy-done.17, bf16[384,512]{1,0:T(8,128)(2,1)S(1)} %copy-done.15, ...), custom_call_target="tpu_custom_call" | custom-call | flops 1179648 | bytes 3456 | tf_op jit(solution)/shard_map/pallas_call | solution.py:177
  117.4 1.8 %collective-permute-start.39 = (bf16[512,384]{1,0:T(8,128)(2,1)S(1)}, bf16[512,384]{1,0:T(8,128)(2,1)S(1)}, u32[]{:S(2)}, u32[]{:S(2)}) collective-permute-start(bf16[512,384]{1,0:T(8,128)(2,1)S(1)} %get-tuple-element.145), channel_id=1, source_target_pairs={{0,2},{1,3},{4,0},{5,1},{8,4},{9,5},{12,8},{13,9},{14,12},{15,13},... | collective-permute-start | bytes 1179656 | tf_op jit(solution)/shard_map/ppermute | solution.py:308
  119.5 7.3 %shard_map.108 = bf16[3,6144,512]{2,1,0:T(8,128)(2,1)} custom-call(s32[41]{0:T(128)S(1)} %dynamic_slice.3.plan_ref, bf16[3,512,512]{2,1,0:T(8,128)(2,1)S(1)} %shard_map.101.grad_ref.left_ref, bf16[384,512]{1,0:T(8,128)(2,1)S(1)} %collective-permute-done.27.refs_0_, ...), custom_call_target="tpu_custom_call", output_to_operand_aliasing={{}: (10, {})} | custom-call | flops 1179648 | bytes 3456 | tf_op jit(solution)/shard_map/pallas_call | solution.py:177
  (120 shorter events, 37.3 us)
Async XLA Ops:
  0.6 12.5 %collective-permute-start.1 = (bf16[512,384]{1,0:T(8,128)(2,1)}, bf16[512,384]{1,0:T(8,128)(2,1)}, u32[]{:S(2)}, u32[]{:S(2)}) collective-permute-start(bf16[512,384]{1,0:T(8,128)(2,1)} %refs_0_.3), channel_id=1, source_target_pairs={{0,2},{1,3},{4,0},{5,1},{8,4},{9,5},{12,8},{13,9},{14,12},{15,13},... | collective-permute-start | bytes 1179656 | tf_op jit(solution)/shard_map/ppermute | solution.py:308
  3.7 10.9 %collective-permute-start = (bf16[512,384]{1,0:T(8,128)(2,1)}, bf16[512,384]{1,0:T(8,128)(2,1)}, u32[]{:S(2)}, u32[]{:S(2)}) collective-permute-start(bf16[512,384]{1,0:T(8,128)(2,1)} %refs_0_.3), channel_id=1, source_target_pairs={{2,0},{3,1},{0,4},{1,5},{4,8},{5,9},{8,12},{9,13},{12,14},{13,15},... | collective-permute-start | bytes 1179656 | tf_op jit(solution)/shard_map/ppermute | solution.py:308
  3.8 13.3 %collective-permute-start.4 = (bf16[512,384]{1,0:T(8,128)(2,1)}, bf16[512,384]{1,0:T(8,128)(2,1)S(1)}, u32[]{:S(2)}, u32[]{:S(2)}) collective-permute-start(bf16[512,384]{1,0:T(8,128)(2,1)} %refs_0_.3), channel_id=1, source_target_pairs={{0,1},{1,0},{2,3},{3,2},{4,5},{5,4},{6,7},{7,6},{8,9},{9,8},{10,11... | collective-permute-start | bytes 1179656 | tf_op jit(solution)/shard_map/ppermute | solution.py:320
  16.6 12.5 %collective-permute-start.7 = (bf16[512,384]{1,0:T(8,128)(2,1)}, bf16[512,384]{1,0:T(8,128)(2,1)}, u32[]{:S(2)}, u32[]{:S(2)}) collective-permute-start(bf16[512,384]{1,0:T(8,128)(2,1)} %collective-permute-done.refs_2_.refs_0_), channel_id=1, source_target_pairs={{0,1},{1,0},{2,3},{3,2},{4,5},{5,4},{6,7},{7,6},{8,9},{9,8},{10,11... | collective-permute-start | bytes 1179656 | tf_op jit(solution)/shard_map/ppermute | solution.py:320
  16.6 13.1 %collective-permute-start.8 = (bf16[512,384]{1,0:T(8,128)(2,1)}, bf16[512,384]{1,0:T(8,128)(2,1)}, u32[]{:S(2)}, u32[]{:S(2)}) collective-permute-start(bf16[512,384]{1,0:T(8,128)(2,1)} %collective-permute-done.1.refs_3_.refs_1_), channel_id=1, source_target_pairs={{0,1},{1,0},{2,3},{3,2},{4,5},{5,4},{6,7},{7,6},{8,9},{9,8},{10,11... | collective-permute-start | bytes 1179656 | tf_op jit(solution)/shard_map/ppermute | solution.py:320
  25.0 12.2 %collective-permute-start.5 = (bf16[512,384]{1,0:T(8,128)(2,1)}, bf16[512,384]{1,0:T(8,128)(2,1)S(1)}, u32[]{:S(2)}, u32[]{:S(2)}) collective-permute-start(bf16[512,384]{1,0:T(8,128)(2,1)} %collective-permute-done.2.refs_0_), channel_id=1, source_target_pairs={{2,0},{3,1},{0,4},{1,5},{4,8},{5,9},{8,12},{9,13},{12,14},{13,15},... | collective-permute-start | bytes 1179656 | tf_op jit(solution)/shard_map/ppermute | solution.py:308
  26.5 10.7 %collective-permute-start.6 = (bf16[512,384]{1,0:T(8,128)(2,1)}, bf16[512,384]{1,0:T(8,128)(2,1)S(1)}, u32[]{:S(2)}, u32[]{:S(2)}) collective-permute-start(bf16[512,384]{1,0:T(8,128)(2,1)} %collective-permute-done.3.refs_1_), channel_id=1, source_target_pairs={{0,2},{1,3},{4,0},{5,1},{8,4},{9,5},{12,8},{13,9},{14,12},{15,13},... | collective-permute-start | bytes 1179656 | tf_op jit(solution)/shard_map/ppermute | solution.py:308
  27.0 12.4 %collective-permute-start.11 = (bf16[512,384]{1,0:T(8,128)(2,1)}, bf16[512,384]{1,0:T(8,128)(2,1)}, u32[]{:S(2)}, u32[]{:S(2)}) collective-permute-start(bf16[512,384]{1,0:T(8,128)(2,1)} %collective-permute-done.2.refs_0_), channel_id=1, source_target_pairs={{0,1},{1,0},{2,3},{3,2},{4,5},{5,4},{6,7},{7,6},{8,9},{9,8},{10,11... | collective-permute-start | bytes 1179656 | tf_op jit(solution)/shard_map/ppermute | solution.py:320
  29.1 11.8 %collective-permute-start.12 = (bf16[512,384]{1,0:T(8,128)(2,1)}, bf16[512,384]{1,0:T(8,128)(2,1)S(1)}, u32[]{:S(2)}, u32[]{:S(2)}) collective-permute-start(bf16[512,384]{1,0:T(8,128)(2,1)} %collective-permute-done.3.refs_1_), channel_id=1, source_target_pairs={{0,1},{1,0},{2,3},{3,2},{4,5},{5,4},{6,7},{7,6},{8,9},{9,8},{10,11... | collective-permute-start | bytes 1179656 | tf_op jit(solution)/shard_map/ppermute | solution.py:320
  49.8 11.6 %collective-permute-start.18 = (bf16[384,512]{1,0:T(8,128)(2,1)S(1)}, bf16[384,512]{1,0:T(8,128)(2,1)S(1)}, u32[]{:S(2)}, u32[]{:S(2)}) collective-permute-start(bf16[384,512]{1,0:T(8,128)(2,1)S(1)} %bitcast.54), channel_id=1, source_target_pairs={{0,1},{1,0},{2,3},{3,2},{4,5},{5,4},{6,7},{7,6},{8,9},{9,8},{10,11... | collective-permute-start | bytes 1179656 | tf_op jit(solution)/shard_map/ppermute | solution.py:320
  50.4 11.8 %collective-permute-start.17 = (bf16[384,512]{1,0:T(8,128)(2,1)S(1)}, bf16[384,512]{1,0:T(8,128)(2,1)}, u32[]{:S(2)}, u32[]{:S(2)}) collective-permute-start(bf16[384,512]{1,0:T(8,128)(2,1)S(1)} %bitcast.55), channel_id=1, source_target_pairs={{0,2},{4,0},{8,4},{12,8},{14,12},{10,14},{6,10},{2,6},{3,1},{1,5},... | collective-permute-start | bytes 1179656 | tf_op jit(solution)/shard_map/ppermute | solution.py:317
  52.4 19.9 %collective-permute-start.21 = (bf16[384,512]{1,0:T(8,128)(2,1)S(1)}, bf16[384,512]{1,0:T(8,128)(2,1)}, u32[]{:S(2)}, u32[]{:S(2)}) collective-permute-start(bf16[384,512]{1,0:T(8,128)(2,1)S(1)} %collective-permute-done.10.refs_2_), channel_id=1, source_target_pairs={{0,1},{1,0},{2,3},{3,2},{4,5},{5,4},{6,7},{7,6},{8,9},{9,8},{10,11... | collective-permute-start | bytes 1179656 | tf_op jit(solution)/shard_map/ppermute | solution.py:320
  62.2 11.2 %collective-permute-start.19 = (bf16[384,512]{1,0:T(8,128)(2,1)}, bf16[384,512]{1,0:T(8,128)(2,1)S(1)}, u32[]{:S(2)}, u32[]{:S(2)}) collective-permute-start(bf16[384,512]{1,0:T(8,128)(2,1)} %collective-permute-done.16.refs_6_), channel_id=1, source_target_pairs={{2,0},{0,4},{4,8},{8,12},{12,14},{14,10},{10,6},{6,2},{1,3},{5,1},... | collective-permute-start | bytes 1179656 | tf_op jit(solution)/shard_map/ppermute | solution.py:314
  74.2 13.0 %collective-permute-start.27 = (bf16[384,512]{1,0:T(8,128)(2,1)}, bf16[384,512]{1,0:T(8,128)(2,1)S(1)}, u32[]{:S(2)}, u32[]{:S(2)}) collective-permute-start(bf16[384,512]{1,0:T(8,128)(2,1)} %collective-permute-done.16.refs_6_), channel_id=1, source_target_pairs={{0,1},{1,0},{2,3},{3,2},{4,5},{5,4},{6,7},{7,6},{8,9},{9,8},{10,11... | collective-permute-start | bytes 1179656 | tf_op jit(solution)/shard_map/ppermute | solution.py:320
  74.4 12.8 %collective-permute-start.28 = (bf16[384,512]{1,0:T(8,128)(2,1)S(1)}, bf16[384,512]{1,0:T(8,128)(2,1)S(1)}, u32[]{:S(2)}, u32[]{:S(2)}) collective-permute-start(bf16[384,512]{1,0:T(8,128)(2,1)S(1)} %collective-permute-done.20.refs_7_), channel_id=1, source_target_pairs={{0,1},{1,0},{2,3},{3,2},{4,5},{5,4},{6,7},{7,6},{8,9},{9,8},{10,11... | collective-permute-start | bytes 1179656 | tf_op jit(solution)/shard_map/ppermute | solution.py:320
  74.7 12.5 %collective-permute-start.26 = (bf16[384,512]{1,0:T(8,128)(2,1)S(1)}, bf16[384,512]{1,0:T(8,128)(2,1)S(1)}, u32[]{:S(2)}, u32[]{:S(2)}) collective-permute-start(bf16[384,512]{1,0:T(8,128)(2,1)S(1)} %collective-permute-done.20.refs_7_), channel_id=1, source_target_pairs={{0,2},{4,0},{8,4},{12,8},{14,12},{10,14},{6,10},{2,6},{3,1},{1,5},... | collective-permute-start | bytes 1179656 | tf_op jit(solution)/shard_map/ppermute | solution.py:317
  76.0 11.2 %collective-permute-start.25 = (bf16[384,512]{1,0:T(8,128)(2,1)S(1)}, bf16[384,512]{1,0:T(8,128)(2,1)S(1)}, u32[]{:S(2)}, u32[]{:S(2)}) collective-permute-start(bf16[384,512]{1,0:T(8,128)(2,1)S(1)} %collective-permute-done.19.refs_2_), channel_id=1, source_target_pairs={{2,0},{0,4},{4,8},{8,12},{12,14},{14,10},{10,6},{6,2},{1,3},{5,1},... | collective-permute-start | bytes 1179656 | tf_op jit(solution)/shard_map/ppermute | solution.py:314
  90.2 13.2 %collective-permute-start.29 = (bf16[2,512,384]{2,1,0:T(8,128)(2,1)S(1)}, bf16[2,512,384]{2,1,0:T(8,128)(2,1)S(1)}, u32[]{:S(2)}, u32[]{:S(2)}) collective-permute-start(bf16[2,512,384]{2,1,0:T(8,128)(2,1)S(1)} %get-tuple-element.116), channel_id=1, source_target_pairs={{0,1},{1,0},{2,3},{3,2},{4,5},{5,4},{6,7},{7,6},{8,9},{9,8},{10,11... | collective-permute-start | bytes 2359304 | tf_op jit(solution)/shard_map/ppermute | solution.py:320
  91.1 11.6 %collective-permute-start.31 = (bf16[512,384]{1,0:T(8,128)(2,1)S(1)}, bf16[512,384]{1,0:T(8,128)(2,1)S(1)}, u32[]{:S(2)}, u32[]{:S(2)}) collective-permute-start(bf16[512,384]{1,0:T(8,128)(2,1)S(1)} %get-tuple-element.143), channel_id=1, source_target_pairs={{0,2},{1,3},{4,0},{5,1},{8,4},{9,5},{12,8},{13,9},{14,12},{15,13},... | collective-permute-start | bytes 1179656 | tf_op jit(solution)/shard_map/ppermute | solution.py:308
  92.4 11.0 %collective-permute-start.30 = (bf16[512,384]{1,0:T(8,128)(2,1)S(1)}, bf16[512,384]{1,0:T(8,128)(2,1)S(1)}, u32[]{:S(2)}, u32[]{:S(2)}) collective-permute-start(bf16[512,384]{1,0:T(8,128)(2,1)S(1)} %get-tuple-element.144), channel_id=1, source_target_pairs={{2,0},{3,1},{0,4},{1,5},{4,8},{5,9},{8,12},{9,13},{12,14},{13,15},... | collective-permute-start | bytes 1179656 | tf_op jit(solution)/shard_map/ppermute | solution.py:308
  103.4 13.8 %collective-permute-start.33 = (bf16[3,512,384]{2,1,0:T(8,128)(2,1)S(1)}, bf16[3,512,384]{2,1,0:T(8,128)(2,1)S(1)}, u32[]{:S(2)}, u32[]{:S(2)}) collective-permute-start(bf16[3,512,384]{2,1,0:T(8,128)(2,1)S(1)} %get-tuple-element.121), channel_id=1, source_target_pairs={{0,1},{1,0},{2,3},{3,2},{4,5},{5,4},{6,7},{7,6},{8,9},{9,8},{10,11... | collective-permute-start | bytes 3538952 | tf_op jit(solution)/shard_map/ppermute | solution.py:320
  103.4 11.0 %collective-permute-start.36 = (bf16[384,512]{1,0:T(8,128)(2,1)S(1)}, bf16[384,512]{1,0:T(8,128)(2,1)S(1)}, u32[]{:S(2)}, u32[]{:S(2)}) collective-permute-start(bf16[384,512]{1,0:T(8,128)(2,1)S(1)} %collective-permute-done.25.refs_6_), channel_id=1, source_target_pairs={{0,1},{1,0},{2,3},{3,2},{4,5},{5,4},{6,7},{7,6},{8,9},{9,8},{10,11... | collective-permute-start | bytes 1179656 | tf_op jit(solution)/shard_map/ppermute | solution.py:320
  104.3 11.5 %collective-permute-start.35 = (bf16[512,384]{1,0:T(8,128)(2,1)S(1)}, bf16[512,384]{1,0:T(8,128)(2,1)S(1)}, u32[]{:S(2)}, u32[]{:S(2)}) collective-permute-start(bf16[512,384]{1,0:T(8,128)(2,1)S(1)} %get-tuple-element.147), channel_id=1, source_target_pairs={{0,2},{1,3},{4,0},{5,1},{8,4},{9,5},{12,8},{13,9},{14,12},{15,13},... | collective-permute-start | bytes 1179656 | tf_op jit(solution)/shard_map/ppermute | solution.py:308
  105.8 11.3 %collective-permute-start.34 = (bf16[512,384]{1,0:T(8,128)(2,1)S(1)}, bf16[512,384]{1,0:T(8,128)(2,1)S(1)}, u32[]{:S(2)}, u32[]{:S(2)}) collective-permute-start(bf16[512,384]{1,0:T(8,128)(2,1)S(1)} %get-tuple-element.148), channel_id=1, source_target_pairs={{2,0},{3,1},{0,4},{1,5},{4,8},{5,9},{8,12},{9,13},{12,14},{13,15},... | collective-permute-start | bytes 1179656 | tf_op jit(solution)/shard_map/ppermute | solution.py:308
  (36 other events, 255.9 us)

commit v9 on v6

--- a/solution.py
+++ b/solution.py
@@ -347,25 +347,27 @@
         return weight_grad(index, attended_t, some, w_out.shape, into)
 
     r1, l1 = both_ways(out_grad, out_grad)
+    i1 = first_chain(inputs)
     other = swapped(out_grad)
     attn, attended, attended_t = attend(positions, qkv)
 
-    r1, l1, attended, plan = together(r1, l1, attended, plan)
+    r1, l1, i1, attended, plan = together(r1, l1, i1, attended, plan)
     r2, l2 = both_ways(r1, l1)
+    i2 = first_chain(i1)
     g1 = blocks(1, r1, l1, *swapped(r1, l1))
     g0 = blocks(0, out_grad, other)
-    grad_h = grad_out_heads(plan, g0)
     out = grad_out(plan, g0)
 
-    r2, l2, grad_h, out, plan = together(r2, l2, grad_h, out, plan)
+    r2, l2, i2, out, plan = together(r2, l2, i2, out, plan)
     r3, l3 = both_ways(r2, l2)
+    i3 = first_chain(i2)
     g2 = blocks(2, r2, l2, *swapped(r2, l2))
-    grad_h = grad_out_heads(plan, g1, grad_h)
+    grad_h = grad_out_heads(plan, g0 + g1)
     out = grad_out(plan, g1, out)
 
-    r3, l3, grad_h, out, plan = together(r3, l3, grad_h, out, plan)
+    r3, l3, i3, grad_h, out, plan = together(r3, l3, i3, grad_h, out, plan)
     x4 = one_way(r3, l3)
-    i1 = first_chain(after(inputs, r3))
+    j1 = second_chain(after(inputs, r3))
     r3x, l3x = swapped(r3, l3)
     g3 = blocks(3, r3, l3, r3x, l3x)
     grad_h = grad_out_heads(plan, g2, grad_h)
@@ -374,52 +376,53 @@
     out = grad_out(plan, g2, out)
     grad_h = grad_out_heads(plan, g3, grad_h)
 
-    x4, i1, grad_h, out, plan = together(x4, i1, grad_h, out, plan)
+    x4, j1, grad_h, out, plan = together(x4, j1, grad_h, out, plan)
     x4x, other = swapped(x4, inputs)
-    i2, j1 = first_chain(i1), second_chain(inputs)
+    i4, j2 = first_chain(i3), second_chain(j1)
     f0 = in_blocks(0, inputs, other)
     g4 = blocks(4, x4, x4x)
     grad_h = grad_out_heads(plan, g4, grad_h, last=True)
     grad = attend_back(qkv, attn, attended, grad_h)
 
-    grad, i2, j1, other, plan = together(grad, i2, j1, other, plan)
-    i3, j2 = first_chain(i2), second_chain(j1)
-    i1x, j1x = swapped(i1, j1)
+    grad, plan = together(grad, plan)
+    out = grad_out(plan, g3, out)
+
+    out, i4, j2, other, plan = together(out, i4, j2, other, plan)
+    j3 = second_chain(j2)
+    i1x, i2x = swapped(i1, i2)
     theirs3, mine3 = terms(plan, 17, 3, grad, w, part)
 
-    theirs3, mine3, i3, j2, i1x, j1x, plan = together(theirs3, mine3, i3, j2, i1x, j1x, plan)
+    theirs3, mine3, j3, i1x, i2x, plan = together(theirs3, mine3, j3, i1x, i2x, plan)
     theirs3 = swapped(theirs3)
-    i4, j3 = first_chain(i3), second_chain(j2)
-    i2x, j2x = swapped(i2, j2)
-    out = grad_out(plan, g3 + g4, out)
-
-    out, theirs3, plan = together(out, theirs3, plan)
+    i3x, j1x = swapped(i3, j1)
+    out = grad_out(plan, g4, out)
+
+    out, theirs3, i3x, j1x, plan = together(out, theirs3, i3x, j1x, plan)
     low = rounded_total(mine3[0], theirs3[0])
     s4 = first_chain(low)
+    i4x, j2x = swapped(i4, j2)
     theirs2, mine2 = terms(plan, 20, 2, grad, w, part)
 
-    theirs2, mine2, s4, i4, j3, i2x, j2x, plan = together(
-        theirs2, mine2, s4, i4, j3, i2x, j2x, plan
-    )
+    theirs2, mine2, s4, i4x, j2x, plan = together(theirs2, mine2, s4, i4x, j2x, plan)
     nothing = jnp.zeros_like(s4)
     s3, u3 = both_ways(
         rounded_total(mine3[1], theirs3[1], jnp.where(on_first, s4, nothing)),
         rounded_total(mine3[2], theirs3[2], jnp.where(on_first, nothing, s4)),
     )
-    theirs2, i3x = swapped(theirs2, i3)
+    theirs2, j3x = swapped(theirs2, j3)
     theirs1, mine1 = terms(plan, 22, 3, grad, w, part)
 
-    theirs1, mine1, theirs2, s3, u3, i3x, plan = together(
-        theirs1, mine1, theirs2, s3, u3, i3x, plan
+    theirs1, mine1, theirs2, s3, u3, j3x, plan = together(
+        theirs1, mine1, theirs2, s3, u3, j3x, plan
     )
     s2, u2 = both_ways(
         rounded_total(mine2[0], theirs2[0], s3), rounded_total(mine2[1], theirs2[1], u3)
     )
-    theirs1, i4x, j3x = swapped(theirs1, i4, j3)
+    theirs1 = swapped(theirs1)
     some = f0 + in_blocks(1, i1, j1, i1x, j1x) + in_blocks(2, i2, j2, i2x, j2x)[:2]
     weight = grad_qkv(plan, some)
 
-    weight, theirs1, s2, u2, i4x, j3x, plan = together(weight, theirs1, s2, u2, i4x, j3x, plan)
+    weight, theirs1, s2, u2, plan = together(weight, theirs1, s2, u2, plan)
     s1, u1 = both_ways(
         rounded_total(mine1[0], theirs1[0], s2), rounded_total(mine1[1], theirs1[1], u2)
     )

time: 130 us -> 135 us (1.038)
  waiting for transfers between devices: 20.9 us -> 28.5 us
  local copies, waits for them, and re-layouts: 7.36 us -> 4.9 us
  starting transfers between devices: 30.5 us -> 28.3 us
  Pallas kernels: 67.7 us -> 69.2 us
    ppermute x12, waiting for transfers between devices: 13.4 us -> 18.8 us  [both_ways(): return (lax.ppermute(right, 'gx', ahead), lax.ppermute(left, 'gx', back))]
    unnamed x22 -> x48, local copies, waits for them, and re-layouts: 6.6 us -> 4.14 us
    ppermute x3, waiting for transfers between devices: 2.22 us -> 0.01 us  [second_chain(): return lax.ppermute(x, 'gx', crossed)]
    pallas_call x6 -> x7, Pallas kernels: 27.5 us -> 29.5 us  [weight_grad(): pl.pallas_call(functools.partial(weight_kernel, [place for place, _ in bl...]
    ppermute x5, waiting for transfers between devices: 5.27 us -> 6.95 us  [first_chain(): return lax.ppermute(x, 'gx', apart)]
    ppermute x3, starting transfers between devices: 3.58 us -> 5.16 us  [second_chain(): return lax.ppermute(x, 'gx', crossed)]
    ppermute x19, waiting for transfers between devices: 0.05 us -> 1.42 us  [swapped(): found = [lax.ppermute(x, 'gx', swap) for x in arrays]]
    pallas_call x5 -> x4, Pallas kernels: 10.4 us -> 9.84 us  [grad_heads(): pl.pallas_call(functools.partial(grad_heads_kernel, count, first, last),...]
  transfers between devices with their start and end apart: 40 -> 40, of which waited for: 14 -> 17; matrix products, arithmetic and copies ran while one was open for 1% -> 1% of each run, Pallas kernels for 52% -> 52%
where the time goes in v9:
time: 135 us; the launch traced here: 134 us
  Pallas kernels  69.2 us (51%)
  waiting for transfers between devices  28.5 us (21%)
  starting transfers between devices  28.3 us (21%)
  local copies, waits for them, and re-layouts  4.9 us (4%)
  other arithmetic  2.04 us (2%)
    pallas_call x7, Pallas kernels, weight_grad(): pl.pallas_call(functools.partial(weight_kernel, [place for place, _ in bl...  29.5 us
    pallas_call x3, Pallas kernels, terms(): pl.pallas_call(terms_kernel, grid_spec=pltpu.PrefetchScalarGridSpec(num_s...  19.3 us
    ppermute x12, waiting for transfers between devices, both_ways(): return (lax.ppermute(right, 'gx', ahead), lax.ppermute(left, 'gx', back))  18.8 us
    ppermute x12, starting transfers between devices, both_ways(): return (lax.ppermute(right, 'gx', ahead), lax.ppermute(left, 'gx', back))  12.3 us
    pallas_call x4, Pallas kernels, grad_heads(): pl.pallas_call(functools.partial(grad_heads_kernel, count, first, last),...  9.84 us
    ppermute x5, waiting for transfers between devices, first_chain(): return lax.ppermute(x, 'gx', apart)  6.95 us
    pallas_call x1, Pallas kernels, attend(): pl.pallas_call(attend_kernel, grid=(heads,), in_specs=[pl.BlockSpec((1, s...  6.58 us
    ppermute x5, starting transfers between devices, first_chain(): return lax.ppermute(x, 'gx', apart)  6.19 us
  transfers between devices with their start and end apart: 40, of which 17 were waited for; matrix products, arithmetic and copies ran while one was open for 1% of the time, Pallas kernels for 52%

profile of v9, /device:TPU:0, one launch (start us, length us, event | category | flops | bytes accessed | tf_op | source)
XLA Modules:
  0.0 134.1 jit_solution(12858402016370534872)
XLA Ops:
  0.6 3.1 %collective-permute-start.2 = (bf16[512,384]{1,0:T(8,128)(2,1)}, bf16[512,384]{1,0:T(8,128)(2,1)}, u32[]{:S(2)}, u32[]{:S(2)}) collective-permute-start(bf16[512,384]{1,0:T(8,128)(2,1)} %refs_0_.5), channel_id=1, source_target_pairs={{2,0},{0,4},{4,8},{8,12},{12,14},{14,10},{10,6},{6,2},{1,3},{5,1},... | collective-permute-start | bytes 1179656 | tf_op jit(solution)/shard_map/ppermute | solution.py:315
  3.7 2.0 %collective-permute-start = (bf16[512,384]{1,0:T(8,128)(2,1)}, bf16[512,384]{1,0:T(8,128)(2,1)}, u32[]{:S(2)}, u32[]{:S(2)}) collective-permute-start(bf16[512,384]{1,0:T(8,128)(2,1)} %refs_0_.4), channel_id=1, source_target_pairs={{2,0},{3,1},{0,4},{1,5},{4,8},{5,9},{8,12},{9,13},{12,14},{13,15},... | collective-permute-start | bytes 1179656 | tf_op jit(solution)/shard_map/ppermute | solution.py:309
  5.7 6.6 %shard_map.94 = (bf16[4,512,512]{2,1,0:T(8,128)(2,1)}, bf16[512,512]{1,0:T(8,128)(2,1)}, bf16[512,512]{1,0:T(8,128)(2,1)}) custom-call(s32[1,512]{1,0:T(1,128)} %bitcast.56, bf16[3,512,512]{2,1,0:T(8,128)(2,1)} %bitcast.50), custom_call_target="tpu_custom_call" | custom-call | flops 131072 | bytes 1280 | tf_op jit(solution)/shard_map/pallas_call | solution.py:51
  13.3 2.8 %collective-permute-done.1.refs_3_.refs_1_ = bf16[512,384]{1,0:T(8,128)(2,1)} collective-permute-done((bf16[512,384]{1,0:T(8,128)(2,1)}, bf16[512,384]{1,0:T(8,128)(2,1)}, u32[]{:S(2)}, u32[]{:S(2)}) %collective-permute-start.1) | collective-permute-done | bytes 393248 | tf_op jit(solution)/shard_map/ppermute | solution.py:309
  16.1 2.1 %collective-permute-done.refs_2_.refs_0_ = bf16[512,384]{1,0:T(8,128)(2,1)} collective-permute-done((bf16[512,384]{1,0:T(8,128)(2,1)}, bf16[512,384]{1,0:T(8,128)(2,1)}, u32[]{:S(2)}, u32[]{:S(2)}) %collective-permute-start) | collective-permute-done | bytes 393248 | tf_op jit(solution)/shard_map/ppermute | solution.py:309
  18.2 2.1 %collective-permute-start.5 = (bf16[512,384]{1,0:T(8,128)(2,1)}, bf16[512,384]{1,0:T(8,128)(2,1)}, u32[]{:S(2)}, u32[]{:S(2)}) collective-permute-start(bf16[512,384]{1,0:T(8,128)(2,1)} %collective-permute-done.2.refs_2_), channel_id=1, source_target_pairs={{2,0},{0,4},{4,8},{8,12},{12,14},{14,10},{10,6},{6,2},{1,3},{5,1},... | collective-permute-start | bytes 1179656 | tf_op jit(solution)/shard_map/ppermute | solution.py:315
  23.8 2.0 %shard_map.95.refs_4_ = bf16[512,6144]{1,0:T(8,128)(2,1)} custom-call(s32[41]{0:T(128)S(1)} %dynamic_slice.3.plan_ref, bf16[512,512]{1,0:T(8,128)(2,1)S(1)} %copy-done, bf16[512,384]{1,0:T(8,128)(2,1)S(1)} %copy-done.3, bf16[512,384]{1,0:T(8,128)(2,1)S(1)} %collective-permute-done.6.refs_1_), custom_call_target="tpu_custom_call" | custom-call | flops 98304 | bytes 288 | tf_op jit(solution)/shard_map/pallas_call | solution.py:178
  25.9 4.3 %collective-permute-done.5.refs_6_ = bf16[512,384]{1,0:T(8,128)(2,1)} collective-permute-done((bf16[512,384]{1,0:T(8,128)(2,1)}, bf16[512,384]{1,0:T(8,128)(2,1)}, u32[]{:S(2)}, u32[]{:S(2)}) %collective-permute-start.5) | collective-permute-done | bytes 393248 | tf_op jit(solution)/shard_map/ppermute | solution.py:315
  30.2 4.2 %collective-permute-done.3.refs_0_ = bf16[512,384]{1,0:T(8,128)(2,1)} collective-permute-done((bf16[512,384]{1,0:T(8,128)(2,1)}, bf16[512,384]{1,0:T(8,128)(2,1)}, u32[]{:S(2)}, u32[]{:S(2)}) %collective-permute-start.3) | collective-permute-done | bytes 393248 | tf_op jit(solution)/shard_map/ppermute | solution.py:309
  39.4 3.3 %shard_map.97.refs_4_ = bf16[512,6144]{1,0:T(8,128)(2,1)} custom-call(s32[41]{0:T(128)S(1)} %dynamic_slice.3.plan_ref, bf16[512,512]{1,0:T(8,128)(2,1)S(1)} %copy-done.1, bf16[512,384]{1,0:T(8,128)(2,1)} %collective-permute-done.refs_2_.refs_0_, bf16[512,384]{1,0:T(8,128)(2,1)} %collective-permute-done.1.refs_3_.refs_1_, ...), custom_call_target="tpu_custom_call", output_to_operand_aliasing={{}: (6, {})} | custom-call | flops 196608 | bytes 576 | tf_op jit(solution)/shard_map/pallas_call | solution.py:178
  42.8 3.6 %shard_map.96.refs_8_ = f32[512,512]{1,0:T(8,128)S(1)} custom-call(s32[41]{0:T(128)S(1)} %dynamic_slice.3.plan_ref, bf16[512,384]{1,0:T(8,128)(2,1)S(1)} %copy-done.4, bf16[512,384]{1,0:T(8,128)(2,1)S(1)} %copy-done.6, bf16[512,384]{1,0:T(8,128)(2,1)} %collective-permute-done.refs_2_.refs_0_, bf16[512,384]{1,0:T(8,128)(2,1)} %collective-permute-done.1.refs_3_.refs_1_, ...), custom_call_target="tpu_custom_call" | custom-call | flops 294912 | bytes 1536 | tf_op jit(solution)/shard_map/pallas_call | solution.py:126
  46.5 3.5 %collective-permute-done.7.refs_0_ = bf16[512,384]{1,0:T(8,128)(2,1)S(1)} collective-permute-done((bf16[512,384]{1,0:T(8,128)(2,1)}, bf16[512,384]{1,0:T(8,128)(2,1)S(1)}, u32[]{:S(2)}, u32[]{:S(2)}) %collective-permute-start.7) | collective-permute-done | bytes 393248 | tf_op jit(solution)/shard_map/ppermute | solution.py:309
  52.6 3.0 %shard_map.98.refs_8_ = f32[512,512]{1,0:T(8,128)S(1)} custom-call(s32[41]{0:T(128)S(1)} %dynamic_slice.3.plan_ref, bf16[512,384]{1,0:T(8,128)(2,1)} %collective-permute-done.3.refs_0_, bf16[512,384]{1,0:T(8,128)(2,1)} %collective-permute-done.4.refs_1_, bf16[512,384]{1,0:T(8,128)(2,1)} %collective-permute-done.14.refs_2_, ...), custom_call_target="tpu_custom_call" | custom-call | flops 196608 | bytes 1024 | tf_op jit(solution)/shard_map/pallas_call | solution.py:126
  55.7 3.3 %shard_map.100.refs_4_ = bf16[512,6144]{1,0:T(8,128)(2,1)} custom-call(s32[41]{0:T(128)S(1)} %dynamic_slice.3.plan_ref, bf16[512,512]{1,0:T(8,128)(2,1)S(1)} %copy-done.1, bf16[512,384]{1,0:T(8,128)(2,1)} %collective-permute-done.3.refs_0_, bf16[512,384]{1,0:T(8,128)(2,1)} %collective-permute-done.4.refs_1_, ...), custom_call_target="tpu_custom_call", output_to_operand_aliasing={{}: (6, {})} | custom-call | flops 196608 | bytes 576 | tf_op jit(solution)/shard_map/pallas_call | solution.py:178
  66.9 4.0 %shard_map.102.grad_ref.left_ref = bf16[3,512,512]{2,1,0:T(8,128)(2,1)S(1)} custom-call(bf16[3,512,512]{2,1,0:T(8,128)(2,1)S(1)} %bitcast.51, bf16[4,512,512]{2,1,0:T(8,128)(2,1)S(1)} %copy-done.2, bf16[512,512]{1,0:T(8,128)(2,1)S(1)} %copy-done.11, bf16[512,512]{1,0:T(8,128)(2,1)S(1)} %shard_map.101.grad_ref), custom_call_target="tpu_custom_call" | custom-call | flops 262144 | bytes 1536 | tf_op jit(solution)/shard_map/pallas_call | solution.py:91
  70.9 2.6 %shard_map.103.refs_2_ = bf16[512,6144]{1,0:T(8,128)(2,1)} custom-call(s32[41]{0:T(128)S(1)} %dynamic_slice.3.plan_ref, bf16[512,512]{1,0:T(8,128)(2,1)S(1)} %copy-done.1, bf16[512,384]{1,0:T(8,128)(2,1)S(1)} %collective-permute-done.7.refs_0_, bf16[512,384]{1,0:T(8,128)(2,1)S(1)} %collective-permute-done.8.refs_1_, ...), custom_call_target="tpu_custom_call", output_to_operand_aliasing={{}: (6, {})} | custom-call | flops 196608 | bytes 576 | tf_op jit(solution)/shard_map/pallas_call | solution.py:178
  76.3 7.0 %shard_map.104 = (bf16[3,512,384]{2,1,0:T(8,128)(2,1)S(1)}, bf16[3,512,384]{2,1,0:T(8,128)(2,1)S(1)}) custom-call(s32[41]{0:T(128)S(1)} %dynamic_slice.3.plan_ref, bf16[3,512,512]{2,1,0:T(8,128)(2,1)S(1)} %shard_map.102.grad_ref.left_ref, bf16[3,6144,512]{2,1,0:T(8,128)(2,1)} %bitcast.52), custom_call_target="tpu_custom_call" | custom-call | flops 884736 | bytes 3840 | tf_op jit(solution)/shard_map/pallas_call | solution.py:217
  84.5 2.0 %shard_map.105 = bf16[512,6144]{1,0:T(8,128)(2,1)} custom-call(s32[41]{0:T(128)S(1)} %dynamic_slice.3.plan_ref, bf16[512,512]{1,0:T(8,128)(2,1)S(1)} %copy-done.1, bf16[512,384]{1,0:T(8,128)(2,1)S(1)} %collective-permute-done.12.refs_0_, bf16[512,384]{1,0:T(8,128)(2,1)S(1)} %collective-permute-done.18.refs_1_, ...), custom_call_target="tpu_custom_call", output_to_operand_aliasing={{}: (4, {})} | custom-call | flops 98304 | bytes 288 | tf_op jit(solution)/shard_map/pallas_call | solution.py:178
  88.5 5.3 %shard_map.106 = (bf16[2,512,384]{2,1,0:T(8,128)(2,1)S(1)}, bf16[2,512,384]{2,1,0:T(8,128)(2,1)S(1)}) custom-call(s32[41]{0:T(128)S(1)} %dynamic_slice.3.plan_ref, bf16[3,512,512]{2,1,0:T(8,128)(2,1)S(1)} %shard_map.102.grad_ref.left_ref, bf16[3,6144,512]{2,1,0:T(8,128)(2,1)} %bitcast.53), custom_call_target="tpu_custom_call" | custom-call | flops 589824 | bytes 2560 | tf_op jit(solution)/shard_map/pallas_call | solution.py:217
  93.9 2.0 %collective-permute-done.28 = bf16[512,384]{1,0:T(8,128)(2,1)S(1)} collective-permute-done((bf16[512,384]{1,0:T(8,128)(2,1)S(1)}, bf16[512,384]{1,0:T(8,128)(2,1)S(1)}, u32[]{:S(2)}, u32[]{:S(2)}) %collective-permute-start.28) | collective-permute-done | bytes 393248 | tf_op jit(solution)/shard_map/ppermute | solution.py:315
  98.8 7.0 %shard_map.107 = (bf16[3,512,384]{2,1,0:T(8,128)(2,1)S(1)}, bf16[3,512,384]{2,1,0:T(8,128)(2,1)S(1)}) custom-call(s32[41]{0:T(128)S(1)} %dynamic_slice.3.plan_ref, bf16[3,512,512]{2,1,0:T(8,128)(2,1)S(1)} %shard_map.102.grad_ref.left_ref, bf16[3,6144,512]{2,1,0:T(8,128)(2,1)} %bitcast.54), custom_call_target="tpu_custom_call" | custom-call | flops 884736 | bytes 3840 | tf_op jit(solution)/shard_map/pallas_call | solution.py:217
  105.8 2.0 %collective-permute-done.33 = bf16[512,384]{1,0:T(8,128)(2,1)S(1)} collective-permute-done((bf16[512,384]{1,0:T(8,128)(2,1)S(1)}, bf16[512,384]{1,0:T(8,128)(2,1)S(1)}, u32[]{:S(2)}, u32[]{:S(2)}) %collective-permute-start.33) | collective-permute-done | bytes 393248 | tf_op jit(solution)/shard_map/ppermute | solution.py:309
  111.6 8.3 %shard_map.108.refs_8_ = bf16[3,6144,512]{2,1,0:T(8,128)(2,1)} custom-call(s32[41]{0:T(128)S(1)} %dynamic_slice.3.plan_ref, bf16[3,512,512]{2,1,0:T(8,128)(2,1)S(1)} %shard_map.102.grad_ref.left_ref, bf16[512,384]{1,0:T(8,128)(2,1)S(1)} %copy-done.17, bf16[512,384]{1,0:T(8,128)(2,1)S(1)} %copy-done.21, bf16[512,384]{1,0:T(8,128)(2,1)} %collective-permute-done.2.refs_2_, ...), custom_call_target="tpu_custom_call" | custom-call | flops 1179648 | bytes 3456 | tf_op jit(solution)/shard_map/pallas_call | solution.py:178
  124.1 7.9 %shard_map.109 = bf16[3,6144,512]{2,1,0:T(8,128)(2,1)} custom-call(s32[41]{0:T(128)S(1)} %dynamic_slice.3.plan_ref, bf16[3,512,512]{2,1,0:T(8,128)(2,1)S(1)} %shard_map.102.grad_ref.left_ref, bf16[512,384]{1,0:T(8,128)(2,1)S(1)} %copy-done.15, bf16[512,384]{1,0:T(8,128)(2,1)S(1)} %collective-permute-done.30.refs_1_, ...), custom_call_target="tpu_custom_call", output_to_operand_aliasing={{}: (10, {})} | custom-call | flops 1179648 | bytes 3456 | tf_op jit(solution)/shard_map/pallas_call | solution.py:178
  (128 shorter events, 38.9 us)
Async XLA Ops:
  0.6 12.6 %collective-permute-start.2 = (bf16[512,384]{1,0:T(8,128)(2,1)}, bf16[512,384]{1,0:T(8,128)(2,1)}, u32[]{:S(2)}, u32[]{:S(2)}) collective-permute-start(bf16[512,384]{1,0:T(8,128)(2,1)} %refs_0_.5), channel_id=1, source_target_pairs={{2,0},{0,4},{4,8},{8,12},{12,14},{14,10},{10,6},{6,2},{1,3},{5,1},... | collective-permute-start | bytes 1179656 | tf_op jit(solution)/shard_map/ppermute | solution.py:315
  3.7 12.4 %collective-permute-start.1 = (bf16[512,384]{1,0:T(8,128)(2,1)}, bf16[512,384]{1,0:T(8,128)(2,1)}, u32[]{:S(2)}, u32[]{:S(2)}) collective-permute-start(bf16[512,384]{1,0:T(8,128)(2,1)} %refs_0_.4), channel_id=1, source_target_pairs={{0,2},{1,3},{4,0},{5,1},{8,4},{9,5},{12,8},{13,9},{14,12},{15,13},... | collective-permute-start | bytes 1179656 | tf_op jit(solution)/shard_map/ppermute | solution.py:309
  3.7 14.4 %collective-permute-start = (bf16[512,384]{1,0:T(8,128)(2,1)}, bf16[512,384]{1,0:T(8,128)(2,1)}, u32[]{:S(2)}, u32[]{:S(2)}) collective-permute-start(bf16[512,384]{1,0:T(8,128)(2,1)} %refs_0_.4), channel_id=1, source_target_pairs={{2,0},{3,1},{0,4},{1,5},{4,8},{5,9},{8,12},{9,13},{12,14},{13,15},... | collective-permute-start | bytes 1179656 | tf_op jit(solution)/shard_map/ppermute | solution.py:309
  5.7 16.5 %collective-permute-start.6 = (bf16[512,384]{1,0:T(8,128)(2,1)}, bf16[512,384]{1,0:T(8,128)(2,1)S(1)}, u32[]{:S(2)}, u32[]{:S(2)}) collective-permute-start(bf16[512,384]{1,0:T(8,128)(2,1)} %refs_0_.4), channel_id=1, source_target_pairs={{0,1},{1,0},{2,3},{3,2},{4,5},{5,4},{6,7},{7,6},{8,9},{9,8},{10,11... | collective-permute-start | bytes 1179656 | tf_op jit(solution)/shard_map/ppermute | solution.py:321
  18.2 12.1 %collective-permute-start.5 = (bf16[512,384]{1,0:T(8,128)(2,1)}, bf16[512,384]{1,0:T(8,128)(2,1)}, u32[]{:S(2)}, u32[]{:S(2)}) collective-permute-start(bf16[512,384]{1,0:T(8,128)(2,1)} %collective-permute-done.2.refs_2_), channel_id=1, source_target_pairs={{2,0},{0,4},{4,8},{8,12},{12,14},{14,10},{10,6},{6,2},{1,3},{5,1},... | collective-permute-start | bytes 1179656 | tf_op jit(solution)/shard_map/ppermute | solution.py:315
  20.2 14.2 %collective-permute-start.3 = (bf16[512,384]{1,0:T(8,128)(2,1)}, bf16[512,384]{1,0:T(8,128)(2,1)}, u32[]{:S(2)}, u32[]{:S(2)}) collective-permute-start(bf16[512,384]{1,0:T(8,128)(2,1)} %collective-permute-done.refs_2_.refs_0_), channel_id=1, source_target_pairs={{2,0},{3,1},{0,4},{1,5},{4,8},{5,9},{8,12},{9,13},{12,14},{13,15},... | collective-permute-start | bytes 1179656 | tf_op jit(solution)/shard_map/ppermute | solution.py:309
  20.9 13.5 %collective-permute-start.4 = (bf16[512,384]{1,0:T(8,128)(2,1)}, bf16[512,384]{1,0:T(8,128)(2,1)}, u32[]{:S(2)}, u32[]{:S(2)}) collective-permute-start(bf16[512,384]{1,0:T(8,128)(2,1)} %collective-permute-done.1.refs_3_.refs_1_), channel_id=1, source_target_pairs={{0,2},{1,3},{4,0},{5,1},{8,4},{9,5},{12,8},{13,9},{14,12},{15,13},... | collective-permute-start | bytes 1179656 | tf_op jit(solution)/shard_map/ppermute | solution.py:309
  22.3 14.6 %collective-permute-start.10 = (bf16[512,384]{1,0:T(8,128)(2,1)}, bf16[512,384]{1,0:T(8,128)(2,1)S(1)}, u32[]{:S(2)}, u32[]{:S(2)}) collective-permute-start(bf16[512,384]{1,0:T(8,128)(2,1)} %collective-permute-done.refs_2_.refs_0_), channel_id=1, source_target_pairs={{0,1},{1,0},{2,3},{3,2},{4,5},{5,4},{6,7},{7,6},{8,9},{9,8},{10,11... | collective-permute-start | bytes 1179656 | tf_op jit(solution)/shard_map/ppermute | solution.py:321
  22.3 15.3 %collective-permute-start.11 = (bf16[512,384]{1,0:T(8,128)(2,1)}, bf16[512,384]{1,0:T(8,128)(2,1)}, u32[]{:S(2)}, u32[]{:S(2)}) collective-permute-start(bf16[512,384]{1,0:T(8,128)(2,1)} %collective-permute-done.1.refs_3_.refs_1_), channel_id=1, source_target_pairs={{0,1},{1,0},{2,3},{3,2},{4,5},{5,4},{6,7},{7,6},{8,9},{9,8},{10,11... | collective-permute-start | bytes 1179656 | tf_op jit(solution)/shard_map/ppermute | solution.py:321
  34.4 12.0 %collective-permute-start.9 = (bf16[512,384]{1,0:T(8,128)(2,1)}, bf16[512,384]{1,0:T(8,128)(2,1)}, u32[]{:S(2)}, u32[]{:S(2)}) collective-permute-start(bf16[512,384]{1,0:T(8,128)(2,1)} %collective-permute-done.5.refs_6_), channel_id=1, source_target_pairs={{2,0},{0,4},{4,8},{8,12},{12,14},{14,10},{10,6},{6,2},{1,3},{5,1},... | collective-permute-start | bytes 1179656 | tf_op jit(solution)/shard_map/ppermute | solution.py:315
  34.8 15.2 %collective-permute-start.7 = (bf16[512,384]{1,0:T(8,128)(2,1)}, bf16[512,384]{1,0:T(8,128)(2,1)S(1)}, u32[]{:S(2)}, u32[]{:S(2)}) collective-permute-start(bf16[512,384]{1,0:T(8,128)(2,1)} %collective-permute-done.3.refs_0_), channel_id=1, source_target_pairs={{2,0},{3,1},{0,4},{1,5},{4,8},{5,9},{8,12},{9,13},{12,14},{13,15},... | collective-permute-start | bytes 1179656 | tf_op jit(solution)/shard_map/ppermute | solution.py:309
  36.5 13.5 %collective-permute-start.8 = (bf16[512,384]{1,0:T(8,128)(2,1)}, bf16[512,384]{1,0:T(8,128)(2,1)S(1)}, u32[]{:S(2)}, u32[]{:S(2)}) collective-permute-start(bf16[512,384]{1,0:T(8,128)(2,1)} %collective-permute-done.4.refs_1_), channel_id=1, source_target_pairs={{0,2},{1,3},{4,0},{5,1},{8,4},{9,5},{12,8},{13,9},{14,12},{15,13},... | collective-permute-start | bytes 1179656 | tf_op jit(solution)/shard_map/ppermute | solution.py:309
  37.6 13.3 %collective-permute-start.14 = (bf16[512,384]{1,0:T(8,128)(2,1)}, bf16[512,384]{1,0:T(8,128)(2,1)}, u32[]{:S(2)}, u32[]{:S(2)}) collective-permute-start(bf16[512,384]{1,0:T(8,128)(2,1)} %collective-permute-done.3.refs_0_), channel_id=1, source_target_pairs={{0,1},{1,0},{2,3},{3,2},{4,5},{5,4},{6,7},{7,6},{8,9},{9,8},{10,11... | collective-permute-start | bytes 1179656 | tf_op jit(solution)/shard_map/ppermute | solution.py:321
  37.6 15.1 %collective-permute-start.15 = (bf16[512,384]{1,0:T(8,128)(2,1)}, bf16[512,384]{1,0:T(8,128)(2,1)S(1)}, u32[]{:S(2)}, u32[]{:S(2)}) collective-permute-start(bf16[512,384]{1,0:T(8,128)(2,1)} %collective-permute-done.4.refs_1_), channel_id=1, source_target_pairs={{0,1},{1,0},{2,3},{3,2},{4,5},{5,4},{6,7},{7,6},{8,9},{9,8},{10,11... | collective-permute-start | bytes 1179656 | tf_op jit(solution)/shard_map/ppermute | solution.py:321
  50.6 11.7 %collective-permute-start.12 = (bf16[512,384]{1,0:T(8,128)(2,1)S(1)}, bf16[512,384]{1,0:T(8,128)(2,1)S(1)}, u32[]{:S(2)}, u32[]{:S(2)}) collective-permute-start(bf16[512,384]{1,0:T(8,128)(2,1)S(1)} %broadcast_select_fusion), channel_id=1, source_target_pairs={{2,0},{0,4},{4,8},{8,12},{12,14},{14,10},{10,6},{6,2},{1,3},{5,1},... | collective-permute-start | bytes 1179656 | tf_op jit(solution)/shard_map/ppermute | solution.py:312
  50.9 11.4 %collective-permute-start.13 = (bf16[512,384]{1,0:T(8,128)(2,1)S(1)}, bf16[512,384]{1,0:T(8,128)(2,1)S(1)}, u32[]{:S(2)}, u32[]{:S(2)}) collective-permute-start(bf16[512,384]{1,0:T(8,128)(2,1)S(1)} %copy-done.16), channel_id=1, source_target_pairs={{0,2},{4,0},{8,4},{12,8},{14,12},{10,14},{6,10},{2,6},{3,1},{1,5},... | collective-permute-start | bytes 1179656 | tf_op jit(solution)/shard_map/ppermute | solution.py:318
  62.8 11.9 %collective-permute-start.19 = (bf16[512,384]{1,0:T(8,128)(2,1)}, bf16[512,384]{1,0:T(8,128)(2,1)S(1)}, u32[]{:S(2)}, u32[]{:S(2)}) collective-permute-start(bf16[512,384]{1,0:T(8,128)(2,1)} %collective-permute-done.9.refs_2_), channel_id=1, source_target_pairs={{2,0},{0,4},{4,8},{8,12},{12,14},{14,10},{10,6},{6,2},{1,3},{5,1},... | collective-permute-start | bytes 1179656 | tf_op jit(solution)/shard_map/ppermute | solution.py:315
  63.0 11.7 %collective-permute-start.20 = (bf16[512,384]{1,0:T(8,128)(2,1)S(1)}, bf16[512,384]{1,0:T(8,128)(2,1)}, u32[]{:S(2)}, u32[]{:S(2)}) collective-permute-start(bf16[512,384]{1,0:T(8,128)(2,1)S(1)} %collective-permute-done.13.refs_3_), channel_id=1, source_target_pairs={{0,2},{4,0},{8,4},{12,8},{14,12},{10,14},{6,10},{2,6},{3,1},{1,5},... | collective-permute-start | bytes 1179656 | tf_op jit(solution)/shard_map/ppermute | solution.py:318
  64.8 18.5 %collective-permute-start.23 = (bf16[512,384]{1,0:T(8,128)(2,1)}, bf16[512,384]{1,0:T(8,128)(2,1)}, u32[]{:S(2)}, u32[]{:S(2)}) collective-permute-start(bf16[512,384]{1,0:T(8,128)(2,1)} %collective-permute-done.2.refs_2_), channel_id=1, source_target_pairs={{0,1},{1,0},{2,3},{3,2},{4,5},{5,4},{6,7},{7,6},{8,9},{9,8},{10,11... | collective-permute-start | bytes 1179656 | tf_op jit(solution)/shard_map/ppermute | solution.py:321
  64.8 18.5 %collective-permute-start.24 = (bf16[512,384]{1,0:T(8,128)(2,1)}, bf16[512,384]{1,0:T(8,128)(2,1)S(1)}, u32[]{:S(2)}, u32[]{:S(2)}) collective-permute-start(bf16[512,384]{1,0:T(8,128)(2,1)} %collective-permute-done.5.refs_6_), channel_id=1, source_target_pairs={{0,1},{1,0},{2,3},{3,2},{4,5},{5,4},{6,7},{7,6},{8,9},{9,8},{10,11... | collective-permute-start | bytes 1179656 | tf_op jit(solution)/shard_map/ppermute | solution.py:321
  95.9 13.3 %collective-permute-start.31 = (bf16[2,512,384]{2,1,0:T(8,128)(2,1)S(1)}, bf16[2,512,384]{2,1,0:T(8,128)(2,1)S(1)}, u32[]{:S(2)}, u32[]{:S(2)}) collective-permute-start(bf16[2,512,384]{2,1,0:T(8,128)(2,1)S(1)} %get-tuple-element.119), channel_id=1, source_target_pairs={{0,1},{1,0},{2,3},{3,2},{4,5},{5,4},{6,7},{7,6},{8,9},{9,8},{10,11... | collective-permute-start | bytes 2359304 | tf_op jit(solution)/shard_map/ppermute | solution.py:321
  109.2 12.6 %collective-permute-start.35 = (bf16[3,512,384]{2,1,0:T(8,128)(2,1)S(1)}, bf16[3,512,384]{2,1,0:T(8,128)(2,1)S(1)}, u32[]{:S(2)}, u32[]{:S(2)}) collective-permute-start(bf16[3,512,384]{2,1,0:T(8,128)(2,1)S(1)} %get-tuple-element.125), channel_id=1, source_target_pairs={{0,1},{1,0},{2,3},{3,2},{4,5},{5,4},{6,7},{7,6},{8,9},{9,8},{10,11... | collective-permute-start | bytes 3538952 | tf_op jit(solution)/shard_map/ppermute | solution.py:321
  109.5 11.6 %collective-permute-start.37 = (bf16[512,384]{1,0:T(8,128)(2,1)S(1)}, bf16[512,384]{1,0:T(8,128)(2,1)S(1)}, u32[]{:S(2)}, u32[]{:S(2)}) collective-permute-start(bf16[512,384]{1,0:T(8,128)(2,1)S(1)} %get-tuple-element.149), channel_id=1, source_target_pairs={{0,2},{1,3},{4,0},{5,1},{8,4},{9,5},{12,8},{13,9},{14,12},{15,13},... | collective-permute-start | bytes 1179656 | tf_op jit(solution)/shard_map/ppermute | solution.py:309
  110.5 11.2 %collective-permute-start.36 = (bf16[512,384]{1,0:T(8,128)(2,1)S(1)}, bf16[512,384]{1,0:T(8,128)(2,1)S(1)}, u32[]{:S(2)}, u32[]{:S(2)}) collective-permute-start(bf16[512,384]{1,0:T(8,128)(2,1)S(1)} %get-tuple-element.150), channel_id=1, source_target_pairs={{2,0},{3,1},{0,4},{1,5},{4,8},{5,9},{8,12},{9,13},{12,14},{13,15},... | collective-permute-start | bytes 1179656 | tf_op jit(solution)/shard_map/ppermute | solution.py:309
  (40 other events, 263.3 us)

commit v10 on v6

--- a/solution.py
+++ b/solution.py
@@ -304,6 +304,7 @@
         jnp.array(sum(plans, []), jnp.int32), (lax.axis_index("gx") * size,), (size,)
     )
     on_first = lax.axis_index("gx") % 2 == 0
+    half = inputs.shape[0] // 2
 
     def both_ways(right, left):
         return lax.ppermute(right, "gx", ahead), lax.ppermute(left, "gx", back)
@@ -354,13 +355,12 @@
     r2, l2 = both_ways(r1, l1)
     g1 = blocks(1, r1, l1, *swapped(r1, l1))
     g0 = blocks(0, out_grad, other)
-    grad_h = grad_out_heads(plan, g0)
     out = grad_out(plan, g0)
 
-    r2, l2, grad_h, out, plan = together(r2, l2, grad_h, out, plan)
+    r2, l2, out, plan = together(r2, l2, out, plan)
     r3, l3 = both_ways(r2, l2)
     g2 = blocks(2, r2, l2, *swapped(r2, l2))
-    grad_h = grad_out_heads(plan, g1, grad_h)
+    grad_h = grad_out_heads(plan, g0 + g1)
     out = grad_out(plan, g1, out)
 
     r3, l3, grad_h, out, plan = together(r3, l3, grad_h, out, plan)
@@ -382,7 +382,10 @@
     grad_h = grad_out_heads(plan, g4, grad_h, last=True)
     grad = attend_back(qkv, attn, attended, grad_h)
 
-    grad, i2, j1, other, plan = together(grad, i2, j1, other, plan)
+    grad, plan = together(grad, plan)
+    out = grad_out(plan, g3, out)
+
+    out, i2, j1, other, plan = together(out, i2, j1, other, plan)
     i3, j2 = first_chain(i2), second_chain(j1)
     i1x, j1x = swapped(i1, j1)
     theirs3, mine3 = terms(plan, 17, 3, grad, w, part)
@@ -391,20 +394,20 @@
     theirs3 = swapped(theirs3)
     i4, j3 = first_chain(i3), second_chain(j2)
     i2x, j2x = swapped(i2, j2)
-    out = grad_out(plan, g3 + g4, out)
+    out = grad_out(plan, g4, out)
 
     out, theirs3, plan = together(out, theirs3, plan)
     low = rounded_total(mine3[0], theirs3[0])
-    s4 = first_chain(low)
+    s4, u4 = both_ways(low[:half], low[half:])
     theirs2, mine2 = terms(plan, 20, 2, grad, w, part)
 
-    theirs2, mine2, s4, i4, j3, i2x, j2x, plan = together(
-        theirs2, mine2, s4, i4, j3, i2x, j2x, plan
-    )
-    nothing = jnp.zeros_like(s4)
+    theirs2, mine2, s4, u4, i4, j3, i2x, j2x, plan = together(
+        theirs2, mine2, s4, u4, i4, j3, i2x, j2x, plan
+    )
+    s4 = jnp.pad(s4, ((0, half), (0, 0)))
+    u4 = jnp.pad(u4, ((half, 0), (0, 0)))
     s3, u3 = both_ways(
-        rounded_total(mine3[1], theirs3[1], jnp.where(on_first, s4, nothing)),
-        rounded_total(mine3[2], theirs3[2], jnp.where(on_first, nothing, s4)),
+        rounded_total(mine3[1], theirs3[1], s4), rounded_total(mine3[2], theirs3[2], u4)
     )
     theirs2, i3x = swapped(theirs2, i3)
     theirs1, mine1 = terms(plan, 22, 3, grad, w, part)

time: 130 us -> 129 us (level)
  local copies, waits for them, and re-layouts: 7.36 us -> 3.07 us
  waiting for transfers between devices: 20.9 us -> 22.9 us
    ppermute x12 -> x14, waiting for transfers between devices: 13.4 us -> 18.5 us  [both_ways(): return (lax.ppermute(right, 'gx', ahead), lax.ppermute(left, 'gx', back))]
    unnamed x22 -> x38, local copies, waits for them, and re-layouts: 6.6 us -> 2.27 us
    ppermute x5 -> x4, starting transfers between devices: 7.29 us -> 5.16 us  [first_chain(): return lax.ppermute(x, 'gx', apart)]
    ppermute x12 -> x14, starting transfers between devices: 13.4 us -> 15.5 us  [both_ways(): return (lax.ppermute(right, 'gx', ahead), lax.ppermute(left, 'gx', back))]
    ppermute x3, waiting for transfers between devices: 2.22 us -> 0.37 us  [second_chain(): return lax.ppermute(x, 'gx', crossed)]
    pallas_call x6 -> x7, Pallas kernels: 27.5 us -> 29.2 us  [weight_grad(): pl.pallas_call(functools.partial(weight_kernel, [place for place, _ in bl...]
    ppermute x5 -> x4, waiting for transfers between devices: 5.27 us -> 4 us  [first_chain(): return lax.ppermute(x, 'gx', apart)]
    pallas_call x5 -> x4, Pallas kernels: 10.4 us -> 9.96 us  [grad_heads(): pl.pallas_call(functools.partial(grad_heads_kernel, count, first, last),...]
  transfers between devices with their start and end apart: 40 -> 41, of which waited for: 14 -> 15; matrix products, arithmetic and copies ran while one was open for 1% -> 1% of each run, Pallas kernels for 52% -> 54%
where the time goes in v10:
time: 129 us; the launch traced here: 128 us
  Pallas kernels  69 us (53%)
  starting transfers between devices  30.3 us (23%)
  waiting for transfers between devices  22.9 us (18%)
  local copies, waits for them, and re-layouts  3.07 us (2%)
  other arithmetic  1.97 us (2%)
    pallas_call x7, Pallas kernels, weight_grad(): pl.pallas_call(functools.partial(weight_kernel, [place for place, _ in bl...  29.2 us
    pallas_call x3, Pallas kernels, terms(): pl.pallas_call(terms_kernel, grid_spec=pltpu.PrefetchScalarGridSpec(num_s...  19.3 us
    ppermute x14, waiting for transfers between devices, both_ways(): return (lax.ppermute(right, 'gx', ahead), lax.ppermute(left, 'gx', back))  18.5 us
    ppermute x14, starting transfers between devices, both_ways(): return (lax.ppermute(right, 'gx', ahead), lax.ppermute(left, 'gx', back))  15.5 us
    pallas_call x4, Pallas kernels, grad_heads(): pl.pallas_call(functools.partial(grad_heads_kernel, count, first, last),...  9.96 us
    pallas_call x1, Pallas kernels, attend(): pl.pallas_call(attend_kernel, grid=(heads,), in_specs=[pl.BlockSpec((1, s...  6.57 us
    ppermute x4, starting transfers between devices, first_chain(): return lax.ppermute(x, 'gx', apart)  5.16 us
    ppermute x19, starting transfers between devices, swapped(): found = [lax.ppermute(x, 'gx', swap) for x in arrays]  4.04 us
  transfers between devices with their start and end apart: 41, of which 15 were waited for; matrix products, arithmetic and copies ran while one was open for 1% of the time, Pallas kernels for 54%

profile of v10, /device:TPU:0, one launch (start us, length us, event | category | flops | bytes accessed | tf_op | source)
XLA Modules:
  0.0 128.2 jit_solution(15147957545551443106)
XLA Ops:
  0.6 3.0 %collective-permute-start.1 = (bf16[512,384]{1,0:T(8,128)(2,1)}, bf16[512,384]{1,0:T(8,128)(2,1)}, u32[]{:S(2)}, u32[]{:S(2)}) collective-permute-start(bf16[512,384]{1,0:T(8,128)(2,1)} %refs_0_.4), channel_id=1, source_target_pairs={{0,2},{1,3},{4,0},{5,1},{8,4},{9,5},{12,8},{13,9},{14,12},{15,13},... | collective-permute-start | bytes 1179656 | tf_op jit(solution)/shard_map/ppermute | solution.py:310
  3.8 6.6 %shard_map.94 = (bf16[4,512,512]{2,1,0:T(8,128)(2,1)}, bf16[512,512]{1,0:T(8,128)(2,1)}, bf16[512,512]{1,0:T(8,128)(2,1)}) custom-call(s32[1,512]{1,0:T(1,128)} %bitcast.58, bf16[3,512,512]{2,1,0:T(8,128)(2,1)} %bitcast.52), custom_call_target="tpu_custom_call" | custom-call | flops 131072 | bytes 1280 | tf_op jit(solution)/shard_map/pallas_call | solution.py:51
  11.1 2.0 %collective-permute-done.1.refs_3_.refs_1_ = bf16[512,384]{1,0:T(8,128)(2,1)} collective-permute-done((bf16[512,384]{1,0:T(8,128)(2,1)}, bf16[512,384]{1,0:T(8,128)(2,1)}, u32[]{:S(2)}, u32[]{:S(2)}) %collective-permute-start.1) | collective-permute-done | bytes 393248 | tf_op jit(solution)/shard_map/ppermute | solution.py:310
  15.0 1.6 %collective-permute-start.3 = (bf16[512,384]{1,0:T(8,128)(2,1)}, bf16[512,384]{1,0:T(8,128)(2,1)}, u32[]{:S(2)}, u32[]{:S(2)}) collective-permute-start(bf16[512,384]{1,0:T(8,128)(2,1)} %collective-permute-done.1.refs_3_.refs_1_), channel_id=1, source_target_pairs={{0,2},{1,3},{4,0},{5,1},{8,4},{9,5},{12,8},{13,9},{14,12},{15,13},... | collective-permute-start | bytes 1179656 | tf_op jit(solution)/shard_map/ppermute | solution.py:310
  18.3 2.0 %shard_map.95.refs_4_ = bf16[512,6144]{1,0:T(8,128)(2,1)} custom-call(s32[41]{0:T(128)S(1)} %dynamic_slice.3.plan_ref, bf16[512,512]{1,0:T(8,128)(2,1)S(1)} %copy-done, bf16[512,384]{1,0:T(8,128)(2,1)S(1)} %copy-done.3, bf16[512,384]{1,0:T(8,128)(2,1)S(1)} %collective-permute-done.4.refs_1_), custom_call_target="tpu_custom_call" | custom-call | flops 98304 | bytes 288 | tf_op jit(solution)/shard_map/pallas_call | solution.py:178
  20.3 4.2 %collective-permute-done.2.refs_0_ = bf16[512,384]{1,0:T(8,128)(2,1)} collective-permute-done((bf16[512,384]{1,0:T(8,128)(2,1)}, bf16[512,384]{1,0:T(8,128)(2,1)}, u32[]{:S(2)}, u32[]{:S(2)}) %collective-permute-start.2) | collective-permute-done | bytes 393248 | tf_op jit(solution)/shard_map/ppermute | solution.py:310
  27.6 3.7 %shard_map.97.refs_4_ = bf16[512,6144]{1,0:T(8,128)(2,1)} custom-call(s32[41]{0:T(128)S(1)} %dynamic_slice.3.plan_ref, bf16[512,512]{1,0:T(8,128)(2,1)S(1)} %copy-done.1, bf16[512,384]{1,0:T(8,128)(2,1)} %collective-permute-done.refs_2_.refs_0_, bf16[512,384]{1,0:T(8,128)(2,1)} %collective-permute-done.1.refs_3_.refs_1_, ...), custom_call_target="tpu_custom_call", output_to_operand_aliasing={{}: (6, {})} | custom-call | flops 196608 | bytes 576 | tf_op jit(solution)/shard_map/pallas_call | solution.py:178
  31.3 3.7 %shard_map.96.refs_8_ = f32[512,512]{1,0:T(8,128)S(1)} custom-call(s32[41]{0:T(128)S(1)} %dynamic_slice.3.plan_ref, bf16[512,384]{1,0:T(8,128)(2,1)S(1)} %copy-done.4, bf16[512,384]{1,0:T(8,128)(2,1)S(1)} %copy-done.6, bf16[512,384]{1,0:T(8,128)(2,1)} %collective-permute-done.refs_2_.refs_0_, bf16[512,384]{1,0:T(8,128)(2,1)} %collective-permute-done.1.refs_3_.refs_1_, ...), custom_call_target="tpu_custom_call" | custom-call | flops 294912 | bytes 1536 | tf_op jit(solution)/shard_map/pallas_call | solution.py:126
  38.9 3.0 %shard_map.98.refs_8_ = f32[512,512]{1,0:T(8,128)S(1)} custom-call(s32[41]{0:T(128)S(1)} %dynamic_slice.3.plan_ref, bf16[512,384]{1,0:T(8,128)(2,1)} %collective-permute-done.2.refs_0_, bf16[512,384]{1,0:T(8,128)(2,1)} %collective-permute-done.3.refs_1_, bf16[512,384]{1,0:T(8,128)(2,1)} %collective-permute-done.11.refs_2_, ...), custom_call_target="tpu_custom_call" | custom-call | flops 196608 | bytes 1024 | tf_op jit(solution)/shard_map/pallas_call | solution.py:126
  41.9 3.3 %shard_map.100.refs_4_ = bf16[512,6144]{1,0:T(8,128)(2,1)} custom-call(s32[41]{0:T(128)S(1)} %dynamic_slice.3.plan_ref, bf16[512,512]{1,0:T(8,128)(2,1)S(1)} %copy-done.1, bf16[512,384]{1,0:T(8,128)(2,1)} %collective-permute-done.2.refs_0_, bf16[512,384]{1,0:T(8,128)(2,1)} %collective-permute-done.3.refs_1_, ...), custom_call_target="tpu_custom_call", output_to_operand_aliasing={{}: (6, {})} | custom-call | flops 196608 | bytes 576 | tf_op jit(solution)/shard_map/pallas_call | solution.py:178
  45.2 1.9 %shard_map.99.refs_4_ = f32[512,512]{1,0:T(8,128)S(1)} custom-call(s32[41]{0:T(128)S(1)} %dynamic_slice.3.plan_ref, bf16[512,384]{1,0:T(8,128)(2,1)S(1)} %collective-permute-done.5.refs_0_, bf16[512,384]{1,0:T(8,128)(2,1)S(1)} %collective-permute-done.6.refs_1_, bf16[512,384]{1,0:T(8,128)(2,1)S(1)} %collective-permute-done.13.refs_2_, ...), custom_call_target="tpu_custom_call" | custom-call | flops 196608 | bytes 1024 | tf_op jit(solution)/shard_map/pallas_call | solution.py:126
  52.7 4.0 %shard_map.102.grad_ref.left_ref = bf16[3,512,512]{2,1,0:T(8,128)(2,1)S(1)} custom-call(bf16[3,512,512]{2,1,0:T(8,128)(2,1)S(1)} %bitcast.53, bf16[4,512,512]{2,1,0:T(8,128)(2,1)S(1)} %copy-done.2, bf16[512,512]{1,0:T(8,128)(2,1)S(1)} %copy-done.8, bf16[512,512]{1,0:T(8,128)(2,1)S(1)} %shard_map.101.grad_ref), custom_call_target="tpu_custom_call" | custom-call | flops 262144 | bytes 1536 | tf_op jit(solution)/shard_map/pallas_call | solution.py:91
  56.7 2.6 %shard_map.103.refs_2_ = bf16[512,6144]{1,0:T(8,128)(2,1)} custom-call(s32[41]{0:T(128)S(1)} %dynamic_slice.3.plan_ref, bf16[512,512]{1,0:T(8,128)(2,1)S(1)} %copy-done.1, bf16[512,384]{1,0:T(8,128)(2,1)S(1)} %collective-permute-done.5.refs_0_, bf16[512,384]{1,0:T(8,128)(2,1)S(1)} %collective-permute-done.6.refs_1_, ...), custom_call_target="tpu_custom_call", output_to_operand_aliasing={{}: (6, {})} | custom-call | flops 196608 | bytes 576 | tf_op jit(solution)/shard_map/pallas_call | solution.py:178
  62.8 7.0 %shard_map.104 = (bf16[3,512,384]{2,1,0:T(8,128)(2,1)S(1)}, bf16[3,512,384]{2,1,0:T(8,128)(2,1)S(1)}) custom-call(s32[41]{0:T(128)S(1)} %dynamic_slice.3.plan_ref, bf16[3,512,512]{2,1,0:T(8,128)(2,1)S(1)} %shard_map.102.grad_ref.left_ref, bf16[3,6144,512]{2,1,0:T(8,128)(2,1)} %bitcast.54), custom_call_target="tpu_custom_call" | custom-call | flops 884736 | bytes 3840 | tf_op jit(solution)/shard_map/pallas_call | solution.py:217
  69.8 1.7 %collective-permute-done.19.refs_2_ = bf16[512,384]{1,0:T(8,128)(2,1)S(1)} collective-permute-done((bf16[512,384]{1,0:T(8,128)(2,1)}, bf16[512,384]{1,0:T(8,128)(2,1)S(1)}, u32[]{:S(2)}, u32[]{:S(2)}) %collective-permute-start.19) | collective-permute-done | bytes 393248 | tf_op jit(solution)/shard_map/ppermute | solution.py:316
  74.7 2.0 %shard_map.105 = bf16[512,6144]{1,0:T(8,128)(2,1)} custom-call(s32[41]{0:T(128)S(1)} %dynamic_slice.3.plan_ref, bf16[512,512]{1,0:T(8,128)(2,1)S(1)} %copy-done.1, bf16[512,384]{1,0:T(8,128)(2,1)S(1)} %collective-permute-done.9.refs_0_, bf16[512,384]{1,0:T(8,128)(2,1)S(1)} %collective-permute-done.15.refs_1_, ...), custom_call_target="tpu_custom_call", output_to_operand_aliasing={{}: (4, {})} | custom-call | flops 98304 | bytes 288 | tf_op jit(solution)/shard_map/pallas_call | solution.py:178
  78.9 5.3 %shard_map.106 = (bf16[2,512,384]{2,1,0:T(8,128)(2,1)S(1)}, bf16[2,512,384]{2,1,0:T(8,128)(2,1)S(1)}) custom-call(s32[41]{0:T(128)S(1)} %dynamic_slice.3.plan_ref, bf16[3,512,512]{2,1,0:T(8,128)(2,1)S(1)} %shard_map.102.grad_ref.left_ref, bf16[3,6144,512]{2,1,0:T(8,128)(2,1)} %bitcast.55), custom_call_target="tpu_custom_call" | custom-call | flops 589824 | bytes 2560 | tf_op jit(solution)/shard_map/pallas_call | solution.py:217
  84.3 1.7 %collective-permute-done.26.refs_6_ = bf16[512,384]{1,0:T(8,128)(2,1)S(1)} collective-permute-done((bf16[512,384]{1,0:T(8,128)(2,1)S(1)}, bf16[512,384]{1,0:T(8,128)(2,1)S(1)}, u32[]{:S(2)}, u32[]{:S(2)}) %collective-permute-start.26) | collective-permute-done | bytes 393248 | tf_op jit(solution)/shard_map/ppermute | solution.py:316
  86.0 2.4 %collective-permute-done.25 = bf16[256,384]{1,0:T(8,128)(2,1)S(1)} collective-permute-done((bf16[256,384]{1,0:T(8,128)(2,1)S(1)}, bf16[256,384]{1,0:T(8,128)(2,1)S(1)}, u32[]{:S(2)}, u32[]{:S(2)}) %collective-permute-start.25) | collective-permute-done | bytes 196640 | tf_op jit(solution)/shard_map/ppermute | solution.py:310
  91.3 7.0 %shard_map.107 = (bf16[3,512,384]{2,1,0:T(8,128)(2,1)S(1)}, bf16[3,512,384]{2,1,0:T(8,128)(2,1)S(1)}) custom-call(s32[41]{0:T(128)S(1)} %dynamic_slice.3.plan_ref, bf16[3,512,512]{2,1,0:T(8,128)(2,1)S(1)} %shard_map.102.grad_ref.left_ref, bf16[3,6144,512]{2,1,0:T(8,128)(2,1)} %bitcast.56), custom_call_target="tpu_custom_call" | custom-call | flops 884736 | bytes 3840 | tf_op jit(solution)/shard_map/pallas_call | solution.py:217
  98.3 2.2 %collective-permute-done.32 = bf16[512,384]{1,0:T(8,128)(2,1)S(1)} collective-permute-done((bf16[512,384]{1,0:T(8,128)(2,1)S(1)}, bf16[512,384]{1,0:T(8,128)(2,1)S(1)}, u32[]{:S(2)}, u32[]{:S(2)}) %collective-permute-start.32) | collective-permute-done | bytes 393248 | tf_op jit(solution)/shard_map/ppermute | solution.py:310
  102.4 1.8 %collective-permute-start.36 = (bf16[512,384]{1,0:T(8,128)(2,1)S(1)}, bf16[512,384]{1,0:T(8,128)(2,1)S(1)}, u32[]{:S(2)}, u32[]{:S(2)}) collective-permute-start(bf16[512,384]{1,0:T(8,128)(2,1)S(1)} %get-tuple-element.151), channel_id=1, source_target_pairs={{0,2},{1,3},{4,0},{5,1},{8,4},{9,5},{12,8},{13,9},{14,12},{15,13},... | collective-permute-start | bytes 1179656 | tf_op jit(solution)/shard_map/ppermute | solution.py:310
  104.5 8.1 %shard_map.108.refs_8_ = bf16[3,6144,512]{2,1,0:T(8,128)(2,1)} custom-call(s32[41]{0:T(128)S(1)} %dynamic_slice.3.plan_ref, bf16[3,512,512]{2,1,0:T(8,128)(2,1)S(1)} %shard_map.102.grad_ref.left_ref, bf16[512,384]{1,0:T(8,128)(2,1)S(1)} %copy-done.10, bf16[512,384]{1,0:T(8,128)(2,1)S(1)} %copy-done.16, bf16[512,384]{1,0:T(8,128)(2,1)S(1)} %copy-done.12, ...), custom_call_target="tpu_custom_call" | custom-call | flops 1179648 | bytes 3456 | tf_op jit(solution)/shard_map/pallas_call | solution.py:178
  117.8 7.5 %shard_map.109 = bf16[3,6144,512]{2,1,0:T(8,128)(2,1)} custom-call(s32[41]{0:T(128)S(1)} %dynamic_slice.3.plan_ref, bf16[3,512,512]{2,1,0:T(8,128)(2,1)S(1)} %shard_map.102.grad_ref.left_ref, bf16[512,384]{1,0:T(8,128)(2,1)S(1)} %collective-permute-done.28.refs_0_, ...), custom_call_target="tpu_custom_call", output_to_operand_aliasing={{}: (10, {})} | custom-call | flops 1179648 | bytes 3456 | tf_op jit(solution)/shard_map/pallas_call | solution.py:178
  (121 shorter events, 38.8 us)
Async XLA Ops:
  0.6 12.5 %collective-permute-start.1 = (bf16[512,384]{1,0:T(8,128)(2,1)}, bf16[512,384]{1,0:T(8,128)(2,1)}, u32[]{:S(2)}, u32[]{:S(2)}) collective-permute-start(bf16[512,384]{1,0:T(8,128)(2,1)} %refs_0_.4), channel_id=1, source_target_pairs={{0,2},{1,3},{4,0},{5,1},{8,4},{9,5},{12,8},{13,9},{14,12},{15,13},... | collective-permute-start | bytes 1179656 | tf_op jit(solution)/shard_map/ppermute | solution.py:310
  3.7 10.9 %collective-permute-start = (bf16[512,384]{1,0:T(8,128)(2,1)}, bf16[512,384]{1,0:T(8,128)(2,1)}, u32[]{:S(2)}, u32[]{:S(2)}) collective-permute-start(bf16[512,384]{1,0:T(8,128)(2,1)} %refs_0_.4), channel_id=1, source_target_pairs={{2,0},{3,1},{0,4},{1,5},{4,8},{5,9},{8,12},{9,13},{12,14},{13,15},... | collective-permute-start | bytes 1179656 | tf_op jit(solution)/shard_map/ppermute | solution.py:310
  3.8 13.3 %collective-permute-start.4 = (bf16[512,384]{1,0:T(8,128)(2,1)}, bf16[512,384]{1,0:T(8,128)(2,1)S(1)}, u32[]{:S(2)}, u32[]{:S(2)}) collective-permute-start(bf16[512,384]{1,0:T(8,128)(2,1)} %refs_0_.4), channel_id=1, source_target_pairs={{0,1},{1,0},{2,3},{3,2},{4,5},{5,4},{6,7},{7,6},{8,9},{9,8},{10,11... | collective-permute-start | bytes 1179656 | tf_op jit(solution)/shard_map/ppermute | solution.py:322
  16.6 10.4 %collective-permute-start.7 = (bf16[512,384]{1,0:T(8,128)(2,1)}, bf16[512,384]{1,0:T(8,128)(2,1)}, u32[]{:S(2)}, u32[]{:S(2)}) collective-permute-start(bf16[512,384]{1,0:T(8,128)(2,1)} %collective-permute-done.refs_2_.refs_0_), channel_id=1, source_target_pairs={{0,1},{1,0},{2,3},{3,2},{4,5},{5,4},{6,7},{7,6},{8,9},{9,8},{10,11... | collective-permute-start | bytes 1179656 | tf_op jit(solution)/shard_map/ppermute | solution.py:322
  16.6 11.0 %collective-permute-start.8 = (bf16[512,384]{1,0:T(8,128)(2,1)}, bf16[512,384]{1,0:T(8,128)(2,1)}, u32[]{:S(2)}, u32[]{:S(2)}) collective-permute-start(bf16[512,384]{1,0:T(8,128)(2,1)} %collective-permute-done.1.refs_3_.refs_1_), channel_id=1, source_target_pairs={{0,1},{1,0},{2,3},{3,2},{4,5},{5,4},{6,7},{7,6},{8,9},{9,8},{10,11... | collective-permute-start | bytes 1179656 | tf_op jit(solution)/shard_map/ppermute | solution.py:322
  27.0 11.8 %collective-permute-start.12 = (bf16[512,384]{1,0:T(8,128)(2,1)}, bf16[512,384]{1,0:T(8,128)(2,1)S(1)}, u32[]{:S(2)}, u32[]{:S(2)}) collective-permute-start(bf16[512,384]{1,0:T(8,128)(2,1)} %collective-permute-done.3.refs_1_), channel_id=1, source_target_pairs={{0,1},{1,0},{2,3},{3,2},{4,5},{5,4},{6,7},{7,6},{8,9},{9,8},{10,11... | collective-permute-start | bytes 1179656 | tf_op jit(solution)/shard_map/ppermute | solution.py:322
  35.7 11.4 %collective-permute-start.9 = (bf16[512,384]{1,0:T(8,128)(2,1)S(1)}, bf16[512,384]{1,0:T(8,128)(2,1)S(1)}, u32[]{:S(2)}, u32[]{:S(2)}) collective-permute-start(bf16[512,384]{1,0:T(8,128)(2,1)S(1)} %broadcast_select_fusion), channel_id=1, source_target_pairs={{2,0},{0,4},{4,8},{8,12},{12,14},{14,10},{10,6},{6,2},{1,3},{5,1},... | collective-permute-start | bytes 1179656 | tf_op jit(solution)/shard_map/ppermute | solution.py:313
  37.3 10.5 %collective-permute-start.10 = (bf16[512,384]{1,0:T(8,128)(2,1)S(1)}, bf16[512,384]{1,0:T(8,128)(2,1)S(1)}, u32[]{:S(2)}, u32[]{:S(2)}) collective-permute-start(bf16[512,384]{1,0:T(8,128)(2,1)S(1)} %copy-done.9), channel_id=1, source_target_pairs={{2,0},{0,4},{4,8},{8,12},{12,14},{14,10},{10,6},{6,2},{1,3},{5,1},... | collective-permute-start | bytes 1179656 | tf_op jit(solution)/shard_map/ppermute | solution.py:316
  47.8 11.5 %collective-permute-start.17 = (bf16[512,384]{1,0:T(8,128)(2,1)S(1)}, bf16[512,384]{1,0:T(8,128)(2,1)S(1)}, u32[]{:S(2)}, u32[]{:S(2)}) collective-permute-start(bf16[512,384]{1,0:T(8,128)(2,1)S(1)} %copy-done.9), channel_id=1, source_target_pairs={{0,2},{4,0},{8,4},{12,8},{14,12},{10,14},{6,10},{2,6},{3,1},{1,5},... | collective-permute-start | bytes 1179656 | tf_op jit(solution)/shard_map/ppermute | solution.py:319
  49.5 10.6 %collective-permute-start.16 = (bf16[512,384]{1,0:T(8,128)(2,1)S(1)}, bf16[512,384]{1,0:T(8,128)(2,1)}, u32[]{:S(2)}, u32[]{:S(2)}) collective-permute-start(bf16[512,384]{1,0:T(8,128)(2,1)S(1)} %collective-permute-done.10.refs_2_), channel_id=1, source_target_pairs={{2,0},{0,4},{4,8},{8,12},{12,14},{14,10},{10,6},{6,2},{1,3},{5,1},... | collective-permute-start | bytes 1179656 | tf_op jit(solution)/shard_map/ppermute | solution.py:316
  51.1 18.7 %collective-permute-start.21 = (bf16[512,384]{1,0:T(8,128)(2,1)S(1)}, bf16[512,384]{1,0:T(8,128)(2,1)}, u32[]{:S(2)}, u32[]{:S(2)}) collective-permute-start(bf16[512,384]{1,0:T(8,128)(2,1)S(1)} %collective-permute-done.10.refs_2_), channel_id=1, source_target_pairs={{0,1},{1,0},{2,3},{3,2},{4,5},{5,4},{6,7},{7,6},{8,9},{9,8},{10,11... | collective-permute-start | bytes 1179656 | tf_op jit(solution)/shard_map/ppermute | solution.py:322
  60.1 11.4 %collective-permute-start.19 = (bf16[512,384]{1,0:T(8,128)(2,1)}, bf16[512,384]{1,0:T(8,128)(2,1)S(1)}, u32[]{:S(2)}, u32[]{:S(2)}) collective-permute-start(bf16[512,384]{1,0:T(8,128)(2,1)} %collective-permute-done.16.refs_6_), channel_id=1, source_target_pairs={{2,0},{0,4},{4,8},{8,12},{12,14},{14,10},{10,6},{6,2},{1,3},{5,1},... | collective-permute-start | bytes 1179656 | tf_op jit(solution)/shard_map/ppermute | solution.py:316
  72.3 13.6 %collective-permute-start.29 = (bf16[512,384]{1,0:T(8,128)(2,1)S(1)}, bf16[512,384]{1,0:T(8,128)(2,1)S(1)}, u32[]{:S(2)}, u32[]{:S(2)}) collective-permute-start(bf16[512,384]{1,0:T(8,128)(2,1)S(1)} %collective-permute-done.20.refs_7_), channel_id=1, source_target_pairs={{0,1},{1,0},{2,3},{3,2},{4,5},{5,4},{6,7},{7,6},{8,9},{9,8},{10,11... | collective-permute-start | bytes 1179656 | tf_op jit(solution)/shard_map/ppermute | solution.py:322
  72.6 13.4 %collective-permute-start.27 = (bf16[512,384]{1,0:T(8,128)(2,1)S(1)}, bf16[512,384]{1,0:T(8,128)(2,1)S(1)}, u32[]{:S(2)}, u32[]{:S(2)}) collective-permute-start(bf16[512,384]{1,0:T(8,128)(2,1)S(1)} %collective-permute-done.20.refs_7_), channel_id=1, source_target_pairs={{0,2},{4,0},{8,4},{12,8},{14,12},{10,14},{6,10},{2,6},{3,1},{1,5},... | collective-permute-start | bytes 1179656 | tf_op jit(solution)/shard_map/ppermute | solution.py:319
  74.2 11.8 %collective-permute-start.26 = (bf16[512,384]{1,0:T(8,128)(2,1)S(1)}, bf16[512,384]{1,0:T(8,128)(2,1)S(1)}, u32[]{:S(2)}, u32[]{:S(2)}) collective-permute-start(bf16[512,384]{1,0:T(8,128)(2,1)S(1)} %collective-permute-done.19.refs_2_), channel_id=1, source_target_pairs={{2,0},{0,4},{4,8},{8,12},{12,14},{14,10},{10,6},{6,2},{1,3},{5,1},... | collective-permute-start | bytes 1179656 | tf_op jit(solution)/shard_map/ppermute | solution.py:316
  76.9 11.5 %collective-permute-start.25 = (bf16[256,384]{1,0:T(8,128)(2,1)S(1)}, bf16[256,384]{1,0:T(8,128)(2,1)S(1)}, u32[]{:S(2)}, u32[]{:S(2)}) collective-permute-start(bf16[256,384]{1,0:T(8,128)(2,1)S(1)} %get-tuple-element.153), channel_id=1, source_target_pairs={{0,2},{1,3},{4,0},{5,1},{8,4},{9,5},{12,8},{13,9},{14,12},{15,13},... | collective-permute-start | bytes 589832 | tf_op jit(solution)/shard_map/ppermute | solution.py:310
  88.4 13.0 %collective-permute-start.30 = (bf16[2,512,384]{2,1,0:T(8,128)(2,1)S(1)}, bf16[2,512,384]{2,1,0:T(8,128)(2,1)S(1)}, u32[]{:S(2)}, u32[]{:S(2)}) collective-permute-start(bf16[2,512,384]{2,1,0:T(8,128)(2,1)S(1)} %get-tuple-element.119), channel_id=1, source_target_pairs={{0,1},{1,0},{2,3},{3,2},{4,5},{5,4},{6,7},{7,6},{8,9},{9,8},{10,11... | collective-permute-start | bytes 2359304 | tf_op jit(solution)/shard_map/ppermute | solution.py:322
  89.2 11.3 %collective-permute-start.32 = (bf16[512,384]{1,0:T(8,128)(2,1)S(1)}, bf16[512,384]{1,0:T(8,128)(2,1)S(1)}, u32[]{:S(2)}, u32[]{:S(2)}) collective-permute-start(bf16[512,384]{1,0:T(8,128)(2,1)S(1)} %get-tuple-element.149), channel_id=1, source_target_pairs={{0,2},{1,3},{4,0},{5,1},{8,4},{9,5},{12,8},{13,9},{14,12},{15,13},... | collective-permute-start | bytes 1179656 | tf_op jit(solution)/shard_map/ppermute | solution.py:310
  90.7 10.7 %collective-permute-start.31 = (bf16[512,384]{1,0:T(8,128)(2,1)S(1)}, bf16[512,384]{1,0:T(8,128)(2,1)S(1)}, u32[]{:S(2)}, u32[]{:S(2)}) collective-permute-start(bf16[512,384]{1,0:T(8,128)(2,1)S(1)} %get-tuple-element.150), channel_id=1, source_target_pairs={{2,0},{3,1},{0,4},{1,5},{4,8},{5,9},{8,12},{9,13},{12,14},{13,15},... | collective-permute-start | bytes 1179656 | tf_op jit(solution)/shard_map/ppermute | solution.py:310
  101.4 13.9 %collective-permute-start.34 = (bf16[3,512,384]{2,1,0:T(8,128)(2,1)S(1)}, bf16[3,512,384]{2,1,0:T(8,128)(2,1)S(1)}, u32[]{:S(2)}, u32[]{:S(2)}) collective-permute-start(bf16[3,512,384]{2,1,0:T(8,128)(2,1)S(1)} %get-tuple-element.125), channel_id=1, source_target_pairs={{0,1},{1,0},{2,3},{3,2},{4,5},{5,4},{6,7},{7,6},{8,9},{9,8},{10,11... | collective-permute-start | bytes 3538952 | tf_op jit(solution)/shard_map/ppermute | solution.py:322
  101.5 11.1 %collective-permute-start.37 = (bf16[512,384]{1,0:T(8,128)(2,1)S(1)}, bf16[512,384]{1,0:T(8,128)(2,1)S(1)}, u32[]{:S(2)}, u32[]{:S(2)}) collective-permute-start(bf16[512,384]{1,0:T(8,128)(2,1)S(1)} %collective-permute-done.26.refs_6_), channel_id=1, source_target_pairs={{0,1},{1,0},{2,3},{3,2},{4,5},{5,4},{6,7},{7,6},{8,9},{9,8},{10,11... | collective-permute-start | bytes 1179656 | tf_op jit(solution)/shard_map/ppermute | solution.py:322
  102.0 10.6 %collective-permute-start.38 = (bf16[512,384]{1,0:T(8,128)(2,1)S(1)}, bf16[512,384]{1,0:T(8,128)(2,1)S(1)}, u32[]{:S(2)}, u32[]{:S(2)}) collective-permute-start(bf16[512,384]{1,0:T(8,128)(2,1)S(1)} %collective-permute-done.27.refs_3_), channel_id=1, source_target_pairs={{0,1},{1,0},{2,3},{3,2},{4,5},{5,4},{6,7},{7,6},{8,9},{9,8},{10,11... | collective-permute-start | bytes 1179656 | tf_op jit(solution)/shard_map/ppermute | solution.py:322
  102.4 11.5 %collective-permute-start.36 = (bf16[512,384]{1,0:T(8,128)(2,1)S(1)}, bf16[512,384]{1,0:T(8,128)(2,1)S(1)}, u32[]{:S(2)}, u32[]{:S(2)}) collective-permute-start(bf16[512,384]{1,0:T(8,128)(2,1)S(1)} %get-tuple-element.151), channel_id=1, source_target_pairs={{0,2},{1,3},{4,0},{5,1},{8,4},{9,5},{12,8},{13,9},{14,12},{15,13},... | collective-permute-start | bytes 1179656 | tf_op jit(solution)/shard_map/ppermute | solution.py:310
  104.2 11.2 %collective-permute-start.35 = (bf16[512,384]{1,0:T(8,128)(2,1)S(1)}, bf16[512,384]{1,0:T(8,128)(2,1)S(1)}, u32[]{:S(2)}, u32[]{:S(2)}) collective-permute-start(bf16[512,384]{1,0:T(8,128)(2,1)S(1)} %get-tuple-element.152), channel_id=1, source_target_pairs={{2,0},{3,1},{0,4},{1,5},{4,8},{5,9},{8,12},{9,13},{12,14},{13,15},... | collective-permute-start | bytes 1179656 | tf_op jit(solution)/shard_map/ppermute | solution.py:310
  (36 other events, 246.1 us)

commit v11 on v10

--- a/solution.py
+++ b/solution.py
@@ -355,13 +355,13 @@
     r2, l2 = both_ways(r1, l1)
     g1 = blocks(1, r1, l1, *swapped(r1, l1))
     g0 = blocks(0, out_grad, other)
-    out = grad_out(plan, g0)
+    out = grad_out(plan, g0 + g1)
 
     r2, l2, out, plan = together(r2, l2, out, plan)
     r3, l3 = both_ways(r2, l2)
     g2 = blocks(2, r2, l2, *swapped(r2, l2))
-    grad_h = grad_out_heads(plan, g0 + g1)
-    out = grad_out(plan, g1, out)
+    out = grad_out(plan, g2, out)
+    grad_h = grad_out_heads(after(plan, out), g0 + g1)
 
     r3, l3, grad_h, out, plan = together(r3, l3, grad_h, out, plan)
     x4 = one_way(r3, l3)
@@ -371,8 +371,8 @@
     grad_h = grad_out_heads(plan, g2, grad_h)
 
     grad_h, r3x, l3x, plan = together(grad_h, r3x, l3x, plan)
-    out = grad_out(plan, g2, out)
     grad_h = grad_out_heads(plan, g3, grad_h)
+    out = grad_out(plan, g3, out)
 
     x4, i1, grad_h, out, plan = together(x4, i1, grad_h, out, plan)
     x4x, other = swapped(x4, inputs)
@@ -383,46 +383,49 @@
     grad = attend_back(qkv, attn, attended, grad_h)
 
     grad, plan = together(grad, plan)
-    out = grad_out(plan, g3, out)
-
-    out, i2, j1, other, plan = together(out, i2, j1, other, plan)
+    theirs4, mine4 = terms(plan, 17, 1, grad, w, part)
+
+    theirs4, mine4, i2, j1, other, plan = together(theirs4, mine4, i2, j1, other, plan)
     i3, j2 = first_chain(i2), second_chain(j1)
+    theirs4 = swapped(theirs4)
     i1x, j1x = swapped(i1, j1)
-    theirs3, mine3 = terms(plan, 17, 3, grad, w, part)
-
-    theirs3, mine3, i3, j2, i1x, j1x, plan = together(theirs3, mine3, i3, j2, i1x, j1x, plan)
+    theirs3, mine3 = terms(plan, 18, 2, grad, w, part)
+    out = grad_out(after(plan, mine3), g4, out)
+
+    theirs3, mine3, theirs4, out, i3, j2, i1x, j1x, plan = together(
+        theirs3, mine3, theirs4, out, i3, j2, i1x, j1x, plan
+    )
+    low = rounded_total(mine4[0], theirs4[0])
+    s4, u4 = both_ways(low[:half], low[half:])
     theirs3 = swapped(theirs3)
     i4, j3 = first_chain(i3), second_chain(j2)
-    i2x, j2x = swapped(i2, j2)
-    out = grad_out(plan, g4, out)
-
-    out, theirs3, plan = together(out, theirs3, plan)
-    low = rounded_total(mine3[0], theirs3[0])
-    s4, u4 = both_ways(low[:half], low[half:])
     theirs2, mine2 = terms(plan, 20, 2, grad, w, part)
 
-    theirs2, mine2, s4, u4, i4, j3, i2x, j2x, plan = together(
-        theirs2, mine2, s4, u4, i4, j3, i2x, j2x, plan
+    theirs2, mine2, theirs3, s4, u4, i4, j3, plan = together(
+        theirs2, mine2, theirs3, s4, u4, i4, j3, plan
     )
     s4 = jnp.pad(s4, ((0, half), (0, 0)))
     u4 = jnp.pad(u4, ((half, 0), (0, 0)))
     s3, u3 = both_ways(
-        rounded_total(mine3[1], theirs3[1], s4), rounded_total(mine3[2], theirs3[2], u4)
-    )
-    theirs2, i3x = swapped(theirs2, i3)
+        rounded_total(mine3[0], theirs3[0], s4), rounded_total(mine3[1], theirs3[1], u4)
+    )
+    theirs2, i2x, j2x = swapped(theirs2, i2, j2)
     theirs1, mine1 = terms(plan, 22, 3, grad, w, part)
 
-    theirs1, mine1, theirs2, s3, u3, i3x, plan = together(
-        theirs1, mine1, theirs2, s3, u3, i3x, plan
+    theirs1, mine1, theirs2, s3, u3, i2x, j2x, plan = together(
+        theirs1, mine1, theirs2, s3, u3, i2x, j2x, plan
     )
     s2, u2 = both_ways(
         rounded_total(mine2[0], theirs2[0], s3), rounded_total(mine2[1], theirs2[1], u3)
     )
-    theirs1, i4x, j3x = swapped(theirs1, i4, j3)
+    theirs1, i3x = swapped(theirs1, i3)
+    i4x, j3x = swapped(i4, j3)
     some = f0 + in_blocks(1, i1, j1, i1x, j1x) + in_blocks(2, i2, j2, i2x, j2x)[:2]
     weight = grad_qkv(plan, some)
 
-    weight, theirs1, s2, u2, i4x, j3x, plan = together(weight, theirs1, s2, u2, i4x, j3x, plan)
+    weight, theirs1, s2, u2, i3x, i4x, j3x, plan = together(
+        weight, theirs1, s2, u2, i3x, i4x, j3x, plan
+    )
     s1, u1 = both_ways(
         rounded_total(mine1[0], theirs1[0], s2), rounded_total(mine1[1], theirs1[1], u2)
     )

time: 129 us -> 133 us (1.031)
  waiting for transfers between devices: 22.9 us -> 25.4 us
    ppermute x14, waiting for transfers between devices: 18.5 us -> 21.5 us  [both_ways(): return (lax.ppermute(right, 'gx', ahead), lax.ppermute(left, 'gx', back))]
    ppermute x3, starting transfers between devices: 3.98 us -> 1.39 us  [second_chain(): return lax.ppermute(x, 'gx', crossed)]
    pallas_call x3 -> x4, Pallas kernels: 19.3 us -> 21.4 us  [terms(): pl.pallas_call(terms_kernel, grid_spec=pltpu.PrefetchScalarGridSpec(num_s...]
    ppermute x19 -> x20, starting transfers between devices: 4.04 us -> 5.68 us  [swapped(): found = [lax.ppermute(x, 'gx', swap) for x in arrays]]
    pallas_call x7 -> x6, Pallas kernels: 29.2 us -> 27.7 us  [weight_grad(): pl.pallas_call(functools.partial(weight_kernel, [place for place, _ in bl...]
    unnamed x38 -> x42, local copies, waits for them, and re-layouts: 2.27 us -> 3.14 us
  transfers between devices with their start and end apart: 41 -> 42, of which waited for: 15 -> 15; matrix products, arithmetic and copies ran while one was open for 1% -> 1% of each run, Pallas kernels for 54% -> 52%
where the time goes in v11:
time: 133 us
  Pallas kernels  69.3 us (52%)
  starting transfers between devices  31.1 us (23%)
  waiting for transfers between devices  25.4 us (19%)
  local copies, waits for them, and re-layouts  3.94 us (3%)
  other arithmetic  1.97 us (1%)
    pallas_call x6, Pallas kernels, weight_grad(): pl.pallas_call(functools.partial(weight_kernel, [place for place, _ in bl...  27.7 us
    ppermute x14, waiting for transfers between devices, both_ways(): return (lax.ppermute(right, 'gx', ahead), lax.ppermute(left, 'gx', back))  21.5 us
    pallas_call x4, Pallas kernels, terms(): pl.pallas_call(terms_kernel, grid_spec=pltpu.PrefetchScalarGridSpec(num_s...  21.4 us
    ppermute x14, starting transfers between devices, both_ways(): return (lax.ppermute(right, 'gx', ahead), lax.ppermute(left, 'gx', back))  16.1 us
    pallas_call x4, Pallas kernels, grad_heads(): pl.pallas_call(functools.partial(grad_heads_kernel, count, first, last),...  9.71 us
    pallas_call x1, Pallas kernels, attend(): pl.pallas_call(attend_kernel, grid=(heads,), in_specs=[pl.BlockSpec((1, s...  6.58 us
    ppermute x4, starting transfers between devices, first_chain(): return lax.ppermute(x, 'gx', apart)  6.25 us
    ppermute x20, starting transfers between devices, swapped(): found = [lax.ppermute(x, 'gx', swap) for x in arrays]  5.68 us
  transfers between devices with their start and end apart: 42, of which 15 were waited for; matrix products, arithmetic and copies ran while one was open for 1% of the time, Pallas kernels for 52%

profile of v11, /device:TPU:0, one launch (start us, length us, event | category | flops | bytes accessed | tf_op | source)
XLA Modules:
  0.0 132.9 jit_solution(2660524960719373042)
XLA Ops:
  0.6 3.0 %collective-permute-start.1 = (bf16[512,384]{1,0:T(8,128)(2,1)}, bf16[512,384]{1,0:T(8,128)(2,1)S(1)}, u32[]{:S(2)}, u32[]{:S(2)}) collective-permute-start(bf16[512,384]{1,0:T(8,128)(2,1)} %refs_0_.4), channel_id=1, source_target_pairs={{0,2},{1,3},{4,0},{5,1},{8,4},{9,5},{12,8},{13,9},{14,12},{15,13},... | collective-permute-start | bytes 1179656 | tf_op jit(solution)/shard_map/ppermute | solution.py:310
  3.8 6.6 %shard_map.94 = (bf16[4,512,512]{2,1,0:T(8,128)(2,1)}, bf16[512,512]{1,0:T(8,128)(2,1)}, bf16[512,512]{1,0:T(8,128)(2,1)}) custom-call(s32[1,512]{1,0:T(1,128)} %bitcast.59, bf16[3,512,512]{2,1,0:T(8,128)(2,1)} %bitcast.52), custom_call_target="tpu_custom_call" | custom-call | flops 131072 | bytes 1280 | tf_op jit(solution)/shard_map/pallas_call | solution.py:51
  11.1 1.9 %collective-permute-done.1.refs_3_ = bf16[512,384]{1,0:T(8,128)(2,1)S(1)} collective-permute-done((bf16[512,384]{1,0:T(8,128)(2,1)}, bf16[512,384]{1,0:T(8,128)(2,1)S(1)}, u32[]{:S(2)}, u32[]{:S(2)}) %collective-permute-start.1) | collective-permute-done | bytes 393248 | tf_op jit(solution)/shard_map/ppermute | solution.py:310
  20.2 4.1 %shard_map.95.refs_4_ = bf16[512,6144]{1,0:T(8,128)(2,1)} custom-call(s32[41]{0:T(128)S(1)} %dynamic_slice.3.plan_ref, bf16[512,512]{1,0:T(8,128)(2,1)S(1)} %copy-done, bf16[512,384]{1,0:T(8,128)(2,1)S(1)} %copy-done.3, bf16[512,384]{1,0:T(8,128)(2,1)S(1)} %copy-done.8, bf16[512,384]{1,0:T(8,128)(2,1)} %collective-permute-done.refs_2_, ...), custom_call_target="tpu_custom_call" | custom-call | flops 294912 | bytes 864 | tf_op jit(solution)/shard_map/pallas_call | solution.py:178
  24.3 2.1 %collective-permute-done.2.refs_0_ = bf16[512,384]{1,0:T(8,128)(2,1)} collective-permute-done((bf16[512,384]{1,0:T(8,128)(2,1)}, bf16[512,384]{1,0:T(8,128)(2,1)}, u32[]{:S(2)}, u32[]{:S(2)}) %collective-permute-start.2) | collective-permute-done | bytes 393248 | tf_op jit(solution)/shard_map/ppermute | solution.py:310
  29.0 3.5 %shard_map.96.refs_4_ = bf16[512,6144]{1,0:T(8,128)(2,1)} custom-call(s32[41]{0:T(128)S(1)} %dynamic_slice.3.plan_ref, bf16[512,512]{1,0:T(8,128)(2,1)S(1)} %copy-done.1, bf16[512,384]{1,0:T(8,128)(2,1)} %collective-permute-done.2.refs_0_, bf16[512,384]{1,0:T(8,128)(2,1)} %collective-permute-done.3.refs_1_, ...), custom_call_target="tpu_custom_call", output_to_operand_aliasing={{}: (6, {})} | custom-call | flops 196608 | bytes 576 | tf_op jit(solution)/shard_map/pallas_call | solution.py:178
  32.7 3.4 %shard_map.97.refs_8_ = f32[512,512]{1,0:T(8,128)S(1)} custom-call(s32[41]{0:T(128)S(1)} %dynamic_slice.3.plan_ref, bf16[512,384]{1,0:T(8,128)(2,1)S(1)} %copy-done.4, bf16[512,384]{1,0:T(8,128)(2,1)S(1)} %copy-done.9, bf16[512,384]{1,0:T(8,128)(2,1)} %collective-permute-done.refs_2_, bf16[512,384]{1,0:T(8,128)(2,1)S(1)} %copy-done.6, ...), custom_call_target="tpu_custom_call" | custom-call | flops 294912 | bytes 1536 | tf_op jit(solution)/shard_map/pallas_call | solution.py:126
  36.0 2.1 %collective-permute-done.7.refs_0_ = bf16[512,384]{1,0:T(8,128)(2,1)S(1)} collective-permute-done((bf16[512,384]{1,0:T(8,128)(2,1)}, bf16[512,384]{1,0:T(8,128)(2,1)S(1)}, u32[]{:S(2)}, u32[]{:S(2)}) %collective-permute-start.7) | collective-permute-done | bytes 393248 | tf_op jit(solution)/shard_map/ppermute | solution.py:310
  40.0 1.6 %collective-permute-start.11 = (bf16[512,384]{1,0:T(8,128)(2,1)S(1)}, bf16[512,384]{1,0:T(8,128)(2,1)S(1)}, u32[]{:S(2)}, u32[]{:S(2)}) collective-permute-start(bf16[512,384]{1,0:T(8,128)(2,1)S(1)} %broadcast_select_fusion), channel_id=1, source_target_pairs={{2,0},{0,4},{4,8},{8,12},{12,14},{14,10},{10,6},{6,2},{1,3},{5,1},... | collective-permute-start | bytes 1179656 | tf_op jit(solution)/shard_map/ppermute | solution.py:313
  43.2 3.2 %shard_map.98.refs_8_ = f32[512,512]{1,0:T(8,128)S(1)} custom-call(s32[41]{0:T(128)S(1)} %dynamic_slice.3.plan_ref, bf16[512,384]{1,0:T(8,128)(2,1)} %collective-permute-done.2.refs_0_, bf16[512,384]{1,0:T(8,128)(2,1)} %collective-permute-done.3.refs_1_, bf16[512,384]{1,0:T(8,128)(2,1)} %collective-permute-done.9.refs_2_, ...), custom_call_target="tpu_custom_call" | custom-call | flops 196608 | bytes 1024 | tf_op jit(solution)/shard_map/pallas_call | solution.py:126
  46.4 1.9 %shard_map.99.refs_4_ = f32[512,512]{1,0:T(8,128)S(1)} custom-call(s32[41]{0:T(128)S(1)} %dynamic_slice.3.plan_ref, bf16[512,384]{1,0:T(8,128)(2,1)S(1)} %collective-permute-done.7.refs_0_, bf16[512,384]{1,0:T(8,128)(2,1)S(1)} %collective-permute-done.8.refs_1_, bf16[512,384]{1,0:T(8,128)(2,1)S(1)} %collective-permute-done.13.refs_2_, ...), custom_call_target="tpu_custom_call" | custom-call | flops 196608 | bytes 1024 | tf_op jit(solution)/shard_map/pallas_call | solution.py:126
  48.3 2.6 %shard_map.100.refs_2_ = bf16[512,6144]{1,0:T(8,128)(2,1)} custom-call(s32[41]{0:T(128)S(1)} %dynamic_slice.3.plan_ref, bf16[512,512]{1,0:T(8,128)(2,1)S(1)} %copy-done.1, bf16[512,384]{1,0:T(8,128)(2,1)S(1)} %collective-permute-done.7.refs_0_, bf16[512,384]{1,0:T(8,128)(2,1)S(1)} %collective-permute-done.8.refs_1_, ...), custom_call_target="tpu_custom_call", output_to_operand_aliasing={{}: (6, {})} | custom-call | flops 196608 | bytes 576 | tf_op jit(solution)/shard_map/pallas_call | solution.py:178
  56.8 4.0 %shard_map.102.grad_ref.left_ref = bf16[3,512,512]{2,1,0:T(8,128)(2,1)S(1)} custom-call(bf16[3,512,512]{2,1,0:T(8,128)(2,1)S(1)} %bitcast.53, bf16[4,512,512]{2,1,0:T(8,128)(2,1)S(1)} %copy-done.2, bf16[512,512]{1,0:T(8,128)(2,1)S(1)} %copy-done.15, bf16[512,512]{1,0:T(8,128)(2,1)S(1)} %shard_map.101.grad_ref), custom_call_target="tpu_custom_call" | custom-call | flops 262144 | bytes 1536 | tf_op jit(solution)/shard_map/pallas_call | solution.py:91
  60.8 3.7 %shard_map.103 = (bf16[1,512,384]{2,1,0:T(8,128)(2,1)S(1)}, bf16[1,512,384]{2,1,0:T(8,128)(2,1)S(1)}) custom-call(s32[41]{0:T(128)S(1)} %dynamic_slice.3.plan_ref, bf16[3,512,512]{2,1,0:T(8,128)(2,1)S(1)} %shard_map.102.grad_ref.left_ref, bf16[3,6144,512]{2,1,0:T(8,128)(2,1)} %bitcast.54), custom_call_target="tpu_custom_call" | custom-call | flops 294912 | bytes 1280 | tf_op jit(solution)/shard_map/pallas_call | solution.py:217
  67.2 5.3 %shard_map.104 = (bf16[2,512,384]{2,1,0:T(8,128)(2,1)S(1)}, bf16[2,512,384]{2,1,0:T(8,128)(2,1)S(1)}) custom-call(s32[41]{0:T(128)S(1)} %dynamic_slice.3.plan_ref, bf16[3,512,512]{2,1,0:T(8,128)(2,1)S(1)} %shard_map.102.grad_ref.left_ref, bf16[3,6144,512]{2,1,0:T(8,128)(2,1)} %bitcast.55), custom_call_target="tpu_custom_call" | custom-call | flops 589824 | bytes 2560 | tf_op jit(solution)/shard_map/pallas_call | solution.py:217
  72.5 2.0 %shard_map.105 = bf16[512,6144]{1,0:T(8,128)(2,1)} custom-call(s32[41]{0:T(128)S(1)} %dynamic_slice.3.plan_ref, bf16[512,512]{1,0:T(8,128)(2,1)S(1)} %copy-done.1, bf16[512,384]{1,0:T(8,128)(2,1)S(1)} %collective-permute-done.11.refs_0_, bf16[512,384]{1,0:T(8,128)(2,1)S(1)} %collective-permute-done.15.refs_1_, ...), custom_call_target="tpu_custom_call", output_to_operand_aliasing={{}: (4, {})} | custom-call | flops 98304 | bytes 288 | tf_op jit(solution)/shard_map/pallas_call | solution.py:178
  74.6 1.9 %collective-permute-done.20.refs_2_ = bf16[512,384]{1,0:T(8,128)(2,1)S(1)} collective-permute-done((bf16[512,384]{1,0:T(8,128)(2,1)}, bf16[512,384]{1,0:T(8,128)(2,1)S(1)}, u32[]{:S(2)}, u32[]{:S(2)}) %collective-permute-start.20) | collective-permute-done | bytes 393248 | tf_op jit(solution)/shard_map/ppermute | solution.py:316
  81.4 5.3 %shard_map.106 = (bf16[2,512,384]{2,1,0:T(8,128)(2,1)S(1)}, bf16[2,512,384]{2,1,0:T(8,128)(2,1)S(1)}) custom-call(s32[41]{0:T(128)S(1)} %dynamic_slice.3.plan_ref, bf16[3,512,512]{2,1,0:T(8,128)(2,1)S(1)} %shard_map.102.grad_ref.left_ref, bf16[3,6144,512]{2,1,0:T(8,128)(2,1)} %bitcast.56), custom_call_target="tpu_custom_call" | custom-call | flops 589824 | bytes 2560 | tf_op jit(solution)/shard_map/pallas_call | solution.py:217
  86.8 5.9 %collective-permute-done.26 = bf16[256,384]{1,0:T(8,128)(2,1)S(1)} collective-permute-done((bf16[256,384]{1,0:T(8,128)(2,1)S(1)}, bf16[256,384]{1,0:T(8,128)(2,1)S(1)}, u32[]{:S(2)}, u32[]{:S(2)}) %collective-permute-start.26) | collective-permute-done | bytes 196640 | tf_op jit(solution)/shard_map/ppermute | solution.py:310
  95.7 7.0 %shard_map.107 = (bf16[3,512,384]{2,1,0:T(8,128)(2,1)S(1)}, bf16[3,512,384]{2,1,0:T(8,128)(2,1)S(1)}) custom-call(s32[41]{0:T(128)S(1)} %dynamic_slice.3.plan_ref, bf16[3,512,512]{2,1,0:T(8,128)(2,1)S(1)} %shard_map.102.grad_ref.left_ref, bf16[3,6144,512]{2,1,0:T(8,128)(2,1)} %bitcast.57), custom_call_target="tpu_custom_call" | custom-call | flops 884736 | bytes 3840 | tf_op jit(solution)/shard_map/pallas_call | solution.py:217
  102.7 2.4 %collective-permute-done.31 = bf16[512,384]{1,0:T(8,128)(2,1)S(1)} collective-permute-done((bf16[512,384]{1,0:T(8,128)(2,1)S(1)}, bf16[512,384]{1,0:T(8,128)(2,1)S(1)}, u32[]{:S(2)}, u32[]{:S(2)}) %collective-permute-start.31) | collective-permute-done | bytes 393248 | tf_op jit(solution)/shard_map/ppermute | solution.py:310
  110.4 7.9 %shard_map.108.refs_8_ = bf16[3,6144,512]{2,1,0:T(8,128)(2,1)} custom-call(s32[41]{0:T(128)S(1)} %dynamic_slice.3.plan_ref, bf16[3,512,512]{2,1,0:T(8,128)(2,1)S(1)} %shard_map.102.grad_ref.left_ref, bf16[512,384]{1,0:T(8,128)(2,1)S(1)} %copy-done.16, bf16[512,384]{1,0:T(8,128)(2,1)S(1)} %collective-permute-done.18.refs_1_, ...), custom_call_target="tpu_custom_call" | custom-call | flops 1179648 | bytes 3456 | tf_op jit(solution)/shard_map/pallas_call | solution.py:178
  118.3 1.9 %collective-permute-done.35 = bf16[512,384]{1,0:T(8,128)(2,1)S(1)} collective-permute-done((bf16[512,384]{1,0:T(8,128)(2,1)S(1)}, bf16[512,384]{1,0:T(8,128)(2,1)S(1)}, u32[]{:S(2)}, u32[]{:S(2)}) %collective-permute-start.35) | collective-permute-done | bytes 393248 | tf_op jit(solution)/shard_map/ppermute | solution.py:310
  122.6 7.5 %shard_map.109 = bf16[3,6144,512]{2,1,0:T(8,128)(2,1)} custom-call(s32[41]{0:T(128)S(1)} %dynamic_slice.3.plan_ref, bf16[3,512,512]{2,1,0:T(8,128)(2,1)S(1)} %shard_map.102.grad_ref.left_ref, bf16[512,384]{1,0:T(8,128)(2,1)S(1)} %collective-permute-done.32.refs_0_, ...), custom_call_target="tpu_custom_call", output_to_operand_aliasing={{}: (10, {})} | custom-call | flops 1179648 | bytes 3456 | tf_op jit(solution)/shard_map/pallas_call | solution.py:178
  (127 shorter events, 40.8 us)
Async XLA Ops:
  0.6 12.4 %collective-permute-start.1 = (bf16[512,384]{1,0:T(8,128)(2,1)}, bf16[512,384]{1,0:T(8,128)(2,1)S(1)}, u32[]{:S(2)}, u32[]{:S(2)}) collective-permute-start(bf16[512,384]{1,0:T(8,128)(2,1)} %refs_0_.4), channel_id=1, source_target_pairs={{0,2},{1,3},{4,0},{5,1},{8,4},{9,5},{12,8},{13,9},{14,12},{15,13},... | collective-permute-start | bytes 1179656 | tf_op jit(solution)/shard_map/ppermute | solution.py:310
  3.8 13.3 %collective-permute-start.4 = (bf16[512,384]{1,0:T(8,128)(2,1)}, bf16[512,384]{1,0:T(8,128)(2,1)S(1)}, u32[]{:S(2)}, u32[]{:S(2)}) collective-permute-start(bf16[512,384]{1,0:T(8,128)(2,1)} %refs_0_.4), channel_id=1, source_target_pairs={{0,1},{1,0},{2,3},{3,2},{4,5},{5,4},{6,7},{7,6},{8,9},{9,8},{10,11... | collective-permute-start | bytes 1179656 | tf_op jit(solution)/shard_map/ppermute | solution.py:322
  15.1 11.3 %collective-permute-start.2 = (bf16[512,384]{1,0:T(8,128)(2,1)}, bf16[512,384]{1,0:T(8,128)(2,1)}, u32[]{:S(2)}, u32[]{:S(2)}) collective-permute-start(bf16[512,384]{1,0:T(8,128)(2,1)} %collective-permute-done.refs_2_), channel_id=1, source_target_pairs={{2,0},{3,1},{0,4},{1,5},{4,8},{5,9},{8,12},{9,13},{12,14},{13,15},... | collective-permute-start | bytes 1179656 | tf_op jit(solution)/shard_map/ppermute | solution.py:310
  15.5 10.9 %collective-permute-start.3 = (bf16[512,384]{1,0:T(8,128)(2,1)S(1)}, bf16[512,384]{1,0:T(8,128)(2,1)}, u32[]{:S(2)}, u32[]{:S(2)}) collective-permute-start(bf16[512,384]{1,0:T(8,128)(2,1)S(1)} %collective-permute-done.1.refs_3_), channel_id=1, source_target_pairs={{0,2},{1,3},{4,0},{5,1},{8,4},{9,5},{12,8},{13,9},{14,12},{15,13},... | collective-permute-start | bytes 1179656 | tf_op jit(solution)/shard_map/ppermute | solution.py:310
  26.9 11.2 %collective-permute-start.7 = (bf16[512,384]{1,0:T(8,128)(2,1)}, bf16[512,384]{1,0:T(8,128)(2,1)S(1)}, u32[]{:S(2)}, u32[]{:S(2)}) collective-permute-start(bf16[512,384]{1,0:T(8,128)(2,1)} %collective-permute-done.2.refs_0_), channel_id=1, source_target_pairs={{2,0},{3,1},{0,4},{1,5},{4,8},{5,9},{8,12},{9,13},{12,14},{13,15},... | collective-permute-start | bytes 1179656 | tf_op jit(solution)/shard_map/ppermute | solution.py:310
  28.5 11.0 %collective-permute-start.8 = (bf16[512,384]{1,0:T(8,128)(2,1)}, bf16[512,384]{1,0:T(8,128)(2,1)S(1)}, u32[]{:S(2)}, u32[]{:S(2)}) collective-permute-start(bf16[512,384]{1,0:T(8,128)(2,1)} %collective-permute-done.3.refs_1_), channel_id=1, source_target_pairs={{0,2},{1,3},{4,0},{5,1},{8,4},{9,5},{12,8},{13,9},{14,12},{15,13},... | collective-permute-start | bytes 1179656 | tf_op jit(solution)/shard_map/ppermute | solution.py:310
  40.0 10.9 %collective-permute-start.11 = (bf16[512,384]{1,0:T(8,128)(2,1)S(1)}, bf16[512,384]{1,0:T(8,128)(2,1)S(1)}, u32[]{:S(2)}, u32[]{:S(2)}) collective-permute-start(bf16[512,384]{1,0:T(8,128)(2,1)S(1)} %broadcast_select_fusion), channel_id=1, source_target_pairs={{2,0},{0,4},{4,8},{8,12},{12,14},{14,10},{10,6},{6,2},{1,3},{5,1},... | collective-permute-start | bytes 1179656 | tf_op jit(solution)/shard_map/ppermute | solution.py:313
  52.1 12.5 %collective-permute-start.17 = (bf16[512,384]{1,0:T(8,128)(2,1)S(1)}, bf16[512,384]{1,0:T(8,128)(2,1)S(1)}, u32[]{:S(2)}, u32[]{:S(2)}) collective-permute-start(bf16[512,384]{1,0:T(8,128)(2,1)S(1)} %copy-done.16), channel_id=1, source_target_pairs={{0,2},{4,0},{8,4},{12,8},{14,12},{10,14},{6,10},{2,6},{3,1},{1,5},... | collective-permute-start | bytes 1179656 | tf_op jit(solution)/shard_map/ppermute | solution.py:319
  52.5 12.1 %collective-permute-start.18 = (bf16[512,384]{1,0:T(8,128)(2,1)S(1)}, bf16[512,384]{1,0:T(8,128)(2,1)S(1)}, u32[]{:S(2)}, u32[]{:S(2)}) collective-permute-start(bf16[512,384]{1,0:T(8,128)(2,1)S(1)} %copy-done.16), channel_id=1, source_target_pairs={{0,1},{1,0},{2,3},{3,2},{4,5},{5,4},{6,7},{7,6},{8,9},{9,8},{10,11... | collective-permute-start | bytes 1179656 | tf_op jit(solution)/shard_map/ppermute | solution.py:322
  55.5 19.1 %collective-permute-start.22 = (bf16[512,384]{1,0:T(8,128)(2,1)S(1)}, bf16[512,384]{1,0:T(8,128)(2,1)S(1)}, u32[]{:S(2)}, u32[]{:S(2)}) collective-permute-start(bf16[512,384]{1,0:T(8,128)(2,1)S(1)} %collective-permute-done.12.refs_2_), channel_id=1, source_target_pairs={{0,1},{1,0},{2,3},{3,2},{4,5},{5,4},{6,7},{7,6},{8,9},{9,8},{10,11... | collective-permute-start | bytes 1179656 | tf_op jit(solution)/shard_map/ppermute | solution.py:322
  65.1 11.4 %collective-permute-start.20 = (bf16[512,384]{1,0:T(8,128)(2,1)}, bf16[512,384]{1,0:T(8,128)(2,1)S(1)}, u32[]{:S(2)}, u32[]{:S(2)}) collective-permute-start(bf16[512,384]{1,0:T(8,128)(2,1)} %collective-permute-done.16.refs_6_), channel_id=1, source_target_pairs={{2,0},{0,4},{4,8},{8,12},{12,14},{14,10},{10,6},{6,2},{1,3},{5,1},... | collective-permute-start | bytes 1179656 | tf_op jit(solution)/shard_map/ppermute | solution.py:316
  76.6 16.1 %collective-permute-start.24 = (bf16[2,512,384]{2,1,0:T(8,128)(2,1)S(1)}, bf16[2,512,384]{2,1,0:T(8,128)(2,1)S(1)}, u32[]{:S(2)}, u32[]{:S(2)}) collective-permute-start(bf16[2,512,384]{2,1,0:T(8,128)(2,1)S(1)} %get-tuple-element.119), channel_id=1, source_target_pairs={{0,1},{1,0},{2,3},{3,2},{4,5},{5,4},{6,7},{7,6},{8,9},{9,8},{10,11... | collective-permute-start | bytes 2359304 | tf_op jit(solution)/shard_map/ppermute | solution.py:322
  77.2 15.5 %collective-permute-start.27 = (bf16[512,384]{1,0:T(8,128)(2,1)S(1)}, bf16[512,384]{1,0:T(8,128)(2,1)S(1)}, u32[]{:S(2)}, u32[]{:S(2)}) collective-permute-start(bf16[512,384]{1,0:T(8,128)(2,1)S(1)} %collective-permute-done.20.refs_2_), channel_id=1, source_target_pairs={{2,0},{0,4},{4,8},{8,12},{12,14},{14,10},{10,6},{6,2},{1,3},{5,1},... | collective-permute-start | bytes 1179656 | tf_op jit(solution)/shard_map/ppermute | solution.py:316
  78.8 13.9 %collective-permute-start.28 = (bf16[512,384]{1,0:T(8,128)(2,1)S(1)}, bf16[512,384]{1,0:T(8,128)(2,1)S(1)}, u32[]{:S(2)}, u32[]{:S(2)}) collective-permute-start(bf16[512,384]{1,0:T(8,128)(2,1)S(1)} %collective-permute-done.21.refs_7_), channel_id=1, source_target_pairs={{0,2},{4,0},{8,4},{12,8},{14,12},{10,14},{6,10},{2,6},{3,1},{1,5},... | collective-permute-start | bytes 1179656 | tf_op jit(solution)/shard_map/ppermute | solution.py:319
  79.3 13.4 %collective-permute-start.26 = (bf16[256,384]{1,0:T(8,128)(2,1)S(1)}, bf16[256,384]{1,0:T(8,128)(2,1)S(1)}, u32[]{:S(2)}, u32[]{:S(2)}) collective-permute-start(bf16[256,384]{1,0:T(8,128)(2,1)S(1)} %get-tuple-element.163), channel_id=1, source_target_pairs={{0,2},{1,3},{4,0},{5,1},{8,4},{9,5},{12,8},{13,9},{14,12},{15,13},... | collective-permute-start | bytes 589832 | tf_op jit(solution)/shard_map/ppermute | solution.py:310
  79.8 12.9 %collective-permute-start.25 = (bf16[256,384]{1,0:T(8,128)(2,1)S(1)}, bf16[256,384]{1,0:T(8,128)(2,1)S(1)}, u32[]{:S(2)}, u32[]{:S(2)}) collective-permute-start(bf16[256,384]{1,0:T(8,128)(2,1)S(1)} %get-tuple-element.164), channel_id=1, source_target_pairs={{2,0},{3,1},{0,4},{1,5},{4,8},{5,9},{8,12},{9,13},{12,14},{13,15},... | collective-permute-start | bytes 589832 | tf_op jit(solution)/shard_map/ppermute | solution.py:310
  92.7 12.9 %collective-permute-start.29 = (bf16[2,512,384]{2,1,0:T(8,128)(2,1)S(1)}, bf16[2,512,384]{2,1,0:T(8,128)(2,1)S(1)}, u32[]{:S(2)}, u32[]{:S(2)}) collective-permute-start(bf16[2,512,384]{2,1,0:T(8,128)(2,1)S(1)} %get-tuple-element.127), channel_id=1, source_target_pairs={{0,1},{1,0},{2,3},{3,2},{4,5},{5,4},{6,7},{7,6},{8,9},{9,8},{10,11... | collective-permute-start | bytes 2359304 | tf_op jit(solution)/shard_map/ppermute | solution.py:322
  93.6 11.5 %collective-permute-start.31 = (bf16[512,384]{1,0:T(8,128)(2,1)S(1)}, bf16[512,384]{1,0:T(8,128)(2,1)S(1)}, u32[]{:S(2)}, u32[]{:S(2)}) collective-permute-start(bf16[512,384]{1,0:T(8,128)(2,1)S(1)} %get-tuple-element.161), channel_id=1, source_target_pairs={{0,2},{1,3},{4,0},{5,1},{8,4},{9,5},{12,8},{13,9},{14,12},{15,13},... | collective-permute-start | bytes 1179656 | tf_op jit(solution)/shard_map/ppermute | solution.py:310
  94.5 11.1 %collective-permute-start.30 = (bf16[512,384]{1,0:T(8,128)(2,1)S(1)}, bf16[512,384]{1,0:T(8,128)(2,1)S(1)}, u32[]{:S(2)}, u32[]{:S(2)}) collective-permute-start(bf16[512,384]{1,0:T(8,128)(2,1)S(1)} %get-tuple-element.162), channel_id=1, source_target_pairs={{2,0},{3,1},{0,4},{1,5},{4,8},{5,9},{8,12},{9,13},{12,14},{13,15},... | collective-permute-start | bytes 1179656 | tf_op jit(solution)/shard_map/ppermute | solution.py:310
  105.6 14.6 %collective-permute-start.34 = (bf16[3,512,384]{2,1,0:T(8,128)(2,1)S(1)}, bf16[3,512,384]{2,1,0:T(8,128)(2,1)S(1)}, u32[]{:S(2)}, u32[]{:S(2)}) collective-permute-start(bf16[3,512,384]{2,1,0:T(8,128)(2,1)S(1)} %get-tuple-element.135), channel_id=1, source_target_pairs={{0,1},{1,0},{2,3},{3,2},{4,5},{5,4},{6,7},{7,6},{8,9},{9,8},{10,11... | collective-permute-start | bytes 3538952 | tf_op jit(solution)/shard_map/ppermute | solution.py:322
  106.1 12.2 %collective-permute-start.38 = (bf16[512,384]{1,0:T(8,128)(2,1)S(1)}, bf16[512,384]{1,0:T(8,128)(2,1)S(1)}, u32[]{:S(2)}, u32[]{:S(2)}) collective-permute-start(bf16[512,384]{1,0:T(8,128)(2,1)S(1)} %collective-permute-done.27.refs_6_), channel_id=1, source_target_pairs={{0,1},{1,0},{2,3},{3,2},{4,5},{5,4},{6,7},{7,6},{8,9},{9,8},{10,11... | collective-permute-start | bytes 1179656 | tf_op jit(solution)/shard_map/ppermute | solution.py:322
  106.1 12.2 %collective-permute-start.39 = (bf16[512,384]{1,0:T(8,128)(2,1)S(1)}, bf16[512,384]{1,0:T(8,128)(2,1)S(1)}, u32[]{:S(2)}, u32[]{:S(2)}) collective-permute-start(bf16[512,384]{1,0:T(8,128)(2,1)S(1)} %collective-permute-done.28.refs_3_), channel_id=1, source_target_pairs={{0,1},{1,0},{2,3},{3,2},{4,5},{5,4},{6,7},{7,6},{8,9},{9,8},{10,11... | collective-permute-start | bytes 1179656 | tf_op jit(solution)/shard_map/ppermute | solution.py:322
  107.0 11.4 %collective-permute-start.36 = (bf16[512,384]{1,0:T(8,128)(2,1)S(1)}, bf16[512,384]{1,0:T(8,128)(2,1)S(1)}, u32[]{:S(2)}, u32[]{:S(2)}) collective-permute-start(bf16[512,384]{1,0:T(8,128)(2,1)S(1)} %get-tuple-element.159), channel_id=1, source_target_pairs={{0,2},{1,3},{4,0},{5,1},{8,4},{9,5},{12,8},{13,9},{14,12},{15,13},... | collective-permute-start | bytes 1179656 | tf_op jit(solution)/shard_map/ppermute | solution.py:310
  109.0 11.2 %collective-permute-start.35 = (bf16[512,384]{1,0:T(8,128)(2,1)S(1)}, bf16[512,384]{1,0:T(8,128)(2,1)S(1)}, u32[]{:S(2)}, u32[]{:S(2)}) collective-permute-start(bf16[512,384]{1,0:T(8,128)(2,1)S(1)} %get-tuple-element.160), channel_id=1, source_target_pairs={{2,0},{3,1},{0,4},{1,5},{4,8},{5,9},{8,12},{9,13},{12,14},{13,15},... | collective-permute-start | bytes 1179656 | tf_op jit(solution)/shard_map/ppermute | solution.py:310
  (39 other events, 261.3 us)

commit v12 on v10

--- a/solution.py
+++ b/solution.py
@@ -375,25 +375,26 @@
     grad_h = grad_out_heads(plan, g3, grad_h)
 
     x4, i1, grad_h, out, plan = together(x4, i1, grad_h, out, plan)
-    x4x, other = swapped(x4, inputs)
+    x4x = swapped(x4)
     i2, j1 = first_chain(i1), second_chain(inputs)
-    f0 = in_blocks(0, inputs, other)
     g4 = blocks(4, x4, x4x)
     grad_h = grad_out_heads(plan, g4, grad_h, last=True)
     grad = attend_back(qkv, attn, attended, grad_h)
 
-    grad, plan = together(grad, plan)
+    grad, inputs, plan = together(grad, inputs, plan)
+    other = swapped(inputs)
+    f0 = in_blocks(0, inputs, other)
     out = grad_out(plan, g3, out)
 
     out, i2, j1, other, plan = together(out, i2, j1, other, plan)
     i3, j2 = first_chain(i2), second_chain(j1)
-    i1x, j1x = swapped(i1, j1)
+    i1x, j1x, i2x = swapped(i1, j1, i2)
     theirs3, mine3 = terms(plan, 17, 3, grad, w, part)
 
     theirs3, mine3, i3, j2, i1x, j1x, plan = together(theirs3, mine3, i3, j2, i1x, j1x, plan)
     theirs3 = swapped(theirs3)
     i4, j3 = first_chain(i3), second_chain(j2)
-    i2x, j2x = swapped(i2, j2)
+    j2x = swapped(j2)
     out = grad_out(plan, g4, out)
 
     out, theirs3, plan = together(out, theirs3, plan)

time: 129 us -> 128 us (level)
  transfers between devices with their start and end apart: 41 -> 41, of which waited for: 15 -> 17; matrix products, arithmetic and copies ran while one was open for 1% -> 1% of each run, Pallas kernels for 54% -> 54%
where the time goes in v12:
time: 128 us
  Pallas kernels  68.8 us (54%)
  starting transfers between devices  29.7 us (23%)
  waiting for transfers between devices  23.9 us (19%)
  local copies, waits for them, and re-layouts  2.3 us (2%)
  other arithmetic  1.97 us (2%)
    pallas_call x7, Pallas kernels, weight_grad(): pl.pallas_call(functools.partial(weight_kernel, [place for place, _ in bl...  29.1 us
    pallas_call x3, Pallas kernels, terms(): pl.pallas_call(terms_kernel, grid_spec=pltpu.PrefetchScalarGridSpec(num_s...  19.3 us
    ppermute x14, waiting for transfers between devices, both_ways(): return (lax.ppermute(right, 'gx', ahead), lax.ppermute(left, 'gx', back))  18.7 us
    ppermute x14, starting transfers between devices, both_ways(): return (lax.ppermute(right, 'gx', ahead), lax.ppermute(left, 'gx', back))  15.5 us
    pallas_call x4, Pallas kernels, grad_heads(): pl.pallas_call(functools.partial(grad_heads_kernel, count, first, last),...  9.95 us
    pallas_call x1, Pallas kernels, attend(): pl.pallas_call(attend_kernel, grid=(heads,), in_specs=[pl.BlockSpec((1, s...  6.57 us
    ppermute x4, waiting for transfers between devices, first_chain(): return lax.ppermute(x, 'gx', apart)  4.59 us
    ppermute x19, starting transfers between devices, swapped(): found = [lax.ppermute(x, 'gx', swap) for x in arrays]  4.39 us
  transfers between devices with their start and end apart: 41, of which 17 were waited for; matrix products, arithmetic and copies ran while one was open for 1% of the time, Pallas kernels for 54%

profile of v12, /device:TPU:0, one launch (start us, length us, event | category | flops | bytes accessed | tf_op | source)
XLA Modules:
  0.0 127.7 jit_solution(1527815752901541398)
XLA Ops:
  0.6 3.0 %collective-permute-start.1 = (bf16[512,384]{1,0:T(8,128)(2,1)}, bf16[512,384]{1,0:T(8,128)(2,1)}, u32[]{:S(2)}, u32[]{:S(2)}) collective-permute-start(bf16[512,384]{1,0:T(8,128)(2,1)} %refs_0_.3), channel_id=1, source_target_pairs={{0,2},{1,3},{4,0},{5,1},{8,4},{9,5},{12,8},{13,9},{14,12},{15,13},... | collective-permute-start | bytes 1179656 | tf_op jit(solution)/shard_map/ppermute | solution.py:310
  3.8 6.6 %shard_map.94 = (bf16[4,512,512]{2,1,0:T(8,128)(2,1)}, bf16[512,512]{1,0:T(8,128)(2,1)}, bf16[512,512]{1,0:T(8,128)(2,1)}) custom-call(s32[1,512]{1,0:T(1,128)} %bitcast.58, bf16[3,512,512]{2,1,0:T(8,128)(2,1)} %bitcast.52), custom_call_target="tpu_custom_call" | custom-call | flops 131072 | bytes 1280 | tf_op jit(solution)/shard_map/pallas_call | solution.py:51
  11.1 2.0 %collective-permute-done.1.refs_3_.refs_1_ = bf16[512,384]{1,0:T(8,128)(2,1)} collective-permute-done((bf16[512,384]{1,0:T(8,128)(2,1)}, bf16[512,384]{1,0:T(8,128)(2,1)}, u32[]{:S(2)}, u32[]{:S(2)}) %collective-permute-start.1) | collective-permute-done | bytes 393248 | tf_op jit(solution)/shard_map/ppermute | solution.py:310
  18.3 2.0 %shard_map.95.refs_4_ = bf16[512,6144]{1,0:T(8,128)(2,1)} custom-call(s32[41]{0:T(128)S(1)} %dynamic_slice.3.plan_ref, bf16[512,512]{1,0:T(8,128)(2,1)S(1)} %copy-done, bf16[512,384]{1,0:T(8,128)(2,1)S(1)} %copy-done.3, bf16[512,384]{1,0:T(8,128)(2,1)S(1)} %collective-permute-done.4.refs_1_), custom_call_target="tpu_custom_call" | custom-call | flops 98304 | bytes 288 | tf_op jit(solution)/shard_map/pallas_call | solution.py:178
  20.3 4.2 %collective-permute-done.2.refs_0_ = bf16[512,384]{1,0:T(8,128)(2,1)} collective-permute-done((bf16[512,384]{1,0:T(8,128)(2,1)}, bf16[512,384]{1,0:T(8,128)(2,1)}, u32[]{:S(2)}, u32[]{:S(2)}) %collective-permute-start.2) | collective-permute-done | bytes 393248 | tf_op jit(solution)/shard_map/ppermute | solution.py:310
  27.6 3.7 %shard_map.97.refs_4_ = bf16[512,6144]{1,0:T(8,128)(2,1)} custom-call(s32[41]{0:T(128)S(1)} %dynamic_slice.3.plan_ref, bf16[512,512]{1,0:T(8,128)(2,1)S(1)} %copy-done.1, bf16[512,384]{1,0:T(8,128)(2,1)} %collective-permute-done.refs_2_.refs_0_, bf16[512,384]{1,0:T(8,128)(2,1)} %collective-permute-done.1.refs_3_.refs_1_, ...), custom_call_target="tpu_custom_call", output_to_operand_aliasing={{}: (6, {})} | custom-call | flops 196608 | bytes 576 | tf_op jit(solution)/shard_map/pallas_call | solution.py:178
  31.3 3.7 %shard_map.96.refs_8_ = f32[512,512]{1,0:T(8,128)S(1)} custom-call(s32[41]{0:T(128)S(1)} %dynamic_slice.3.plan_ref, bf16[512,384]{1,0:T(8,128)(2,1)S(1)} %copy-done.4, bf16[512,384]{1,0:T(8,128)(2,1)S(1)} %copy-done.6, bf16[512,384]{1,0:T(8,128)(2,1)} %collective-permute-done.refs_2_.refs_0_, bf16[512,384]{1,0:T(8,128)(2,1)} %collective-permute-done.1.refs_3_.refs_1_, ...), custom_call_target="tpu_custom_call" | custom-call | flops 294912 | bytes 1536 | tf_op jit(solution)/shard_map/pallas_call | solution.py:126
  38.9 3.0 %shard_map.98.refs_8_ = f32[512,512]{1,0:T(8,128)S(1)} custom-call(s32[41]{0:T(128)S(1)} %dynamic_slice.3.plan_ref, bf16[512,384]{1,0:T(8,128)(2,1)} %collective-permute-done.2.refs_0_, bf16[512,384]{1,0:T(8,128)(2,1)} %collective-permute-done.3.refs_1_, bf16[512,384]{1,0:T(8,128)(2,1)} %collective-permute-done.11.refs_2_, ...), custom_call_target="tpu_custom_call" | custom-call | flops 196608 | bytes 1024 | tf_op jit(solution)/shard_map/pallas_call | solution.py:126
  41.9 3.3 %shard_map.100.refs_4_ = bf16[512,6144]{1,0:T(8,128)(2,1)} custom-call(s32[41]{0:T(128)S(1)} %dynamic_slice.3.plan_ref, bf16[512,512]{1,0:T(8,128)(2,1)S(1)} %copy-done.1, bf16[512,384]{1,0:T(8,128)(2,1)} %collective-permute-done.2.refs_0_, bf16[512,384]{1,0:T(8,128)(2,1)} %collective-permute-done.3.refs_1_, ...), custom_call_target="tpu_custom_call", output_to_operand_aliasing={{}: (6, {})} | custom-call | flops 196608 | bytes 576 | tf_op jit(solution)/shard_map/pallas_call | solution.py:178
  45.2 1.9 %shard_map.99.refs_4_ = f32[512,512]{1,0:T(8,128)S(1)} custom-call(s32[41]{0:T(128)S(1)} %dynamic_slice.3.plan_ref, bf16[512,384]{1,0:T(8,128)(2,1)S(1)} %collective-permute-done.5.refs_0_, bf16[512,384]{1,0:T(8,128)(2,1)S(1)} %collective-permute-done.6.refs_1_, bf16[512,384]{1,0:T(8,128)(2,1)S(1)} %collective-permute-done.13.refs_2_, ...), custom_call_target="tpu_custom_call" | custom-call | flops 196608 | bytes 1024 | tf_op jit(solution)/shard_map/pallas_call | solution.py:126
  51.4 4.0 %shard_map.102.grad_ref.left_ref = bf16[3,512,512]{2,1,0:T(8,128)(2,1)S(1)} custom-call(bf16[3,512,512]{2,1,0:T(8,128)(2,1)S(1)} %bitcast.53, bf16[4,512,512]{2,1,0:T(8,128)(2,1)S(1)} %copy-done.2, bf16[512,512]{1,0:T(8,128)(2,1)S(1)} %copy-done.8, bf16[512,512]{1,0:T(8,128)(2,1)S(1)} %shard_map.101.grad_ref), custom_call_target="tpu_custom_call" | custom-call | flops 262144 | bytes 1536 | tf_op jit(solution)/shard_map/pallas_call | solution.py:91
  55.9 2.6 %shard_map.103.refs_2_ = bf16[512,6144]{1,0:T(8,128)(2,1)} custom-call(s32[41]{0:T(128)S(1)} %dynamic_slice.3.plan_ref, bf16[512,512]{1,0:T(8,128)(2,1)S(1)} %copy-done.1, bf16[512,384]{1,0:T(8,128)(2,1)S(1)} %collective-permute-done.5.refs_0_, bf16[512,384]{1,0:T(8,128)(2,1)S(1)} %collective-permute-done.6.refs_1_, ...), custom_call_target="tpu_custom_call", output_to_operand_aliasing={{}: (6, {})} | custom-call | flops 196608 | bytes 576 | tf_op jit(solution)/shard_map/pallas_call | solution.py:178
  62.0 7.0 %shard_map.104 = (bf16[3,512,384]{2,1,0:T(8,128)(2,1)S(1)}, bf16[3,512,384]{2,1,0:T(8,128)(2,1)S(1)}) custom-call(s32[41]{0:T(128)S(1)} %dynamic_slice.3.plan_ref, bf16[3,512,512]{2,1,0:T(8,128)(2,1)S(1)} %shard_map.102.grad_ref.left_ref, bf16[3,6144,512]{2,1,0:T(8,128)(2,1)} %bitcast.54), custom_call_target="tpu_custom_call" | custom-call | flops 884736 | bytes 3840 | tf_op jit(solution)/shard_map/pallas_call | solution.py:217
  69.0 1.8 %collective-permute-done.19.refs_2_ = bf16[512,384]{1,0:T(8,128)(2,1)S(1)} collective-permute-done((bf16[512,384]{1,0:T(8,128)(2,1)}, bf16[512,384]{1,0:T(8,128)(2,1)S(1)}, u32[]{:S(2)}, u32[]{:S(2)}) %collective-permute-start.19) | collective-permute-done | bytes 393248 | tf_op jit(solution)/shard_map/ppermute | solution.py:316
  74.0 2.0 %shard_map.105 = bf16[512,6144]{1,0:T(8,128)(2,1)} custom-call(s32[41]{0:T(128)S(1)} %dynamic_slice.3.plan_ref, bf16[512,512]{1,0:T(8,128)(2,1)S(1)} %copy-done.1, bf16[512,384]{1,0:T(8,128)(2,1)S(1)} %collective-permute-done.9.refs_0_, bf16[512,384]{1,0:T(8,128)(2,1)S(1)} %collective-permute-done.15.refs_1_, ...), custom_call_target="tpu_custom_call", output_to_operand_aliasing={{}: (4, {})} | custom-call | flops 98304 | bytes 288 | tf_op jit(solution)/shard_map/pallas_call | solution.py:178
  76.2 1.7 %collective-permute-start.25 = (bf16[256,384]{1,0:T(8,128)(2,1)S(1)}, bf16[256,384]{1,0:T(8,128)(2,1)S(1)}, u32[]{:S(2)}, u32[]{:S(2)}) collective-permute-start(bf16[256,384]{1,0:T(8,128)(2,1)S(1)} %get-tuple-element.155), channel_id=1, source_target_pairs={{0,2},{1,3},{4,0},{5,1},{8,4},{9,5},{12,8},{13,9},{14,12},{15,13},... | collective-permute-start | bytes 589832 | tf_op jit(solution)/shard_map/ppermute | solution.py:310
  78.3 5.3 %shard_map.106 = (bf16[2,512,384]{2,1,0:T(8,128)(2,1)S(1)}, bf16[2,512,384]{2,1,0:T(8,128)(2,1)S(1)}) custom-call(s32[41]{0:T(128)S(1)} %dynamic_slice.3.plan_ref, bf16[3,512,512]{2,1,0:T(8,128)(2,1)S(1)} %shard_map.102.grad_ref.left_ref, bf16[3,6144,512]{2,1,0:T(8,128)(2,1)} %bitcast.55), custom_call_target="tpu_custom_call" | custom-call | flops 589824 | bytes 2560 | tf_op jit(solution)/shard_map/pallas_call | solution.py:217
  83.6 1.8 %collective-permute-done.26.refs_6_ = bf16[512,384]{1,0:T(8,128)(2,1)S(1)} collective-permute-done((bf16[512,384]{1,0:T(8,128)(2,1)S(1)}, bf16[512,384]{1,0:T(8,128)(2,1)S(1)}, u32[]{:S(2)}, u32[]{:S(2)}) %collective-permute-start.26) | collective-permute-done | bytes 393248 | tf_op jit(solution)/shard_map/ppermute | solution.py:316
  85.4 2.4 %collective-permute-done.25 = bf16[256,384]{1,0:T(8,128)(2,1)S(1)} collective-permute-done((bf16[256,384]{1,0:T(8,128)(2,1)S(1)}, bf16[256,384]{1,0:T(8,128)(2,1)S(1)}, u32[]{:S(2)}, u32[]{:S(2)}) %collective-permute-start.25) | collective-permute-done | bytes 196640 | tf_op jit(solution)/shard_map/ppermute | solution.py:310
  90.7 7.0 %shard_map.107 = (bf16[3,512,384]{2,1,0:T(8,128)(2,1)S(1)}, bf16[3,512,384]{2,1,0:T(8,128)(2,1)S(1)}) custom-call(s32[41]{0:T(128)S(1)} %dynamic_slice.3.plan_ref, bf16[3,512,512]{2,1,0:T(8,128)(2,1)S(1)} %shard_map.102.grad_ref.left_ref, bf16[3,6144,512]{2,1,0:T(8,128)(2,1)} %bitcast.56), custom_call_target="tpu_custom_call" | custom-call | flops 884736 | bytes 3840 | tf_op jit(solution)/shard_map/pallas_call | solution.py:217
  97.7 2.1 %collective-permute-done.32 = bf16[512,384]{1,0:T(8,128)(2,1)S(1)} collective-permute-done((bf16[512,384]{1,0:T(8,128)(2,1)S(1)}, bf16[512,384]{1,0:T(8,128)(2,1)S(1)}, u32[]{:S(2)}, u32[]{:S(2)}) %collective-permute-start.32) | collective-permute-done | bytes 393248 | tf_op jit(solution)/shard_map/ppermute | solution.py:310
  101.8 1.8 %collective-permute-start.36 = (bf16[512,384]{1,0:T(8,128)(2,1)S(1)}, bf16[512,384]{1,0:T(8,128)(2,1)S(1)}, u32[]{:S(2)}, u32[]{:S(2)}) collective-permute-start(bf16[512,384]{1,0:T(8,128)(2,1)S(1)} %get-tuple-element.153), channel_id=1, source_target_pairs={{0,2},{1,3},{4,0},{5,1},{8,4},{9,5},{12,8},{13,9},{14,12},{15,13},... | collective-permute-start | bytes 1179656 | tf_op jit(solution)/shard_map/ppermute | solution.py:310
  103.9 7.9 %shard_map.108.refs_8_ = bf16[3,6144,512]{2,1,0:T(8,128)(2,1)} custom-call(s32[41]{0:T(128)S(1)} %dynamic_slice.3.plan_ref, bf16[3,512,512]{2,1,0:T(8,128)(2,1)S(1)} %shard_map.102.grad_ref.left_ref, bf16[512,384]{1,0:T(8,128)(2,1)S(1)} %copy-done.10, bf16[512,384]{1,0:T(8,128)(2,1)S(1)} %collective-permute-done.18.refs_1_, bf16[512,384]{1,0:T(8,128)(2,1)S(1)} %copy-done.12, ...), custom_call_target="tpu_custom_call" | custom-call | flops 1179648 | bytes 3456 | tf_op jit(solution)/shard_map/pallas_call | solution.py:178
  117.2 7.5 %shard_map.109 = bf16[3,6144,512]{2,1,0:T(8,128)(2,1)} custom-call(s32[41]{0:T(128)S(1)} %dynamic_slice.3.plan_ref, bf16[3,512,512]{2,1,0:T(8,128)(2,1)S(1)} %shard_map.102.grad_ref.left_ref, bf16[512,384]{1,0:T(8,128)(2,1)S(1)} %collective-permute-done.28.refs_0_, ...), custom_call_target="tpu_custom_call", output_to_operand_aliasing={{}: (10, {})} | custom-call | flops 1179648 | bytes 3456 | tf_op jit(solution)/shard_map/pallas_call | solution.py:178
  (117 shorter events, 38.2 us)
Async XLA Ops:
  0.6 12.5 %collective-permute-start.1 = (bf16[512,384]{1,0:T(8,128)(2,1)}, bf16[512,384]{1,0:T(8,128)(2,1)}, u32[]{:S(2)}, u32[]{:S(2)}) collective-permute-start(bf16[512,384]{1,0:T(8,128)(2,1)} %refs_0_.3), channel_id=1, source_target_pairs={{0,2},{1,3},{4,0},{5,1},{8,4},{9,5},{12,8},{13,9},{14,12},{15,13},... | collective-permute-start | bytes 1179656 | tf_op jit(solution)/shard_map/ppermute | solution.py:310
  3.7 10.9 %collective-permute-start = (bf16[512,384]{1,0:T(8,128)(2,1)}, bf16[512,384]{1,0:T(8,128)(2,1)}, u32[]{:S(2)}, u32[]{:S(2)}) collective-permute-start(bf16[512,384]{1,0:T(8,128)(2,1)} %refs_0_.3), channel_id=1, source_target_pairs={{2,0},{3,1},{0,4},{1,5},{4,8},{5,9},{8,12},{9,13},{12,14},{13,15},... | collective-permute-start | bytes 1179656 | tf_op jit(solution)/shard_map/ppermute | solution.py:310
  3.8 13.3 %collective-permute-start.4 = (bf16[512,384]{1,0:T(8,128)(2,1)}, bf16[512,384]{1,0:T(8,128)(2,1)S(1)}, u32[]{:S(2)}, u32[]{:S(2)}) collective-permute-start(bf16[512,384]{1,0:T(8,128)(2,1)} %refs_0_.3), channel_id=1, source_target_pairs={{0,1},{1,0},{2,3},{3,2},{4,5},{5,4},{6,7},{7,6},{8,9},{9,8},{10,11... | collective-permute-start | bytes 1179656 | tf_op jit(solution)/shard_map/ppermute | solution.py:322
  16.6 10.4 %collective-permute-start.7 = (bf16[512,384]{1,0:T(8,128)(2,1)}, bf16[512,384]{1,0:T(8,128)(2,1)}, u32[]{:S(2)}, u32[]{:S(2)}) collective-permute-start(bf16[512,384]{1,0:T(8,128)(2,1)} %collective-permute-done.refs_2_.refs_0_), channel_id=1, source_target_pairs={{0,1},{1,0},{2,3},{3,2},{4,5},{5,4},{6,7},{7,6},{8,9},{9,8},{10,11... | collective-permute-start | bytes 1179656 | tf_op jit(solution)/shard_map/ppermute | solution.py:322
  16.6 11.0 %collective-permute-start.8 = (bf16[512,384]{1,0:T(8,128)(2,1)}, bf16[512,384]{1,0:T(8,128)(2,1)}, u32[]{:S(2)}, u32[]{:S(2)}) collective-permute-start(bf16[512,384]{1,0:T(8,128)(2,1)} %collective-permute-done.1.refs_3_.refs_1_), channel_id=1, source_target_pairs={{0,1},{1,0},{2,3},{3,2},{4,5},{5,4},{6,7},{7,6},{8,9},{9,8},{10,11... | collective-permute-start | bytes 1179656 | tf_op jit(solution)/shard_map/ppermute | solution.py:322
  27.0 11.8 %collective-permute-start.12 = (bf16[512,384]{1,0:T(8,128)(2,1)}, bf16[512,384]{1,0:T(8,128)(2,1)S(1)}, u32[]{:S(2)}, u32[]{:S(2)}) collective-permute-start(bf16[512,384]{1,0:T(8,128)(2,1)} %collective-permute-done.3.refs_1_), channel_id=1, source_target_pairs={{0,1},{1,0},{2,3},{3,2},{4,5},{5,4},{6,7},{7,6},{8,9},{9,8},{10,11... | collective-permute-start | bytes 1179656 | tf_op jit(solution)/shard_map/ppermute | solution.py:322
  35.7 11.4 %collective-permute-start.9 = (bf16[512,384]{1,0:T(8,128)(2,1)S(1)}, bf16[512,384]{1,0:T(8,128)(2,1)S(1)}, u32[]{:S(2)}, u32[]{:S(2)}) collective-permute-start(bf16[512,384]{1,0:T(8,128)(2,1)S(1)} %broadcast_select_fusion), channel_id=1, source_target_pairs={{2,0},{0,4},{4,8},{8,12},{12,14},{14,10},{10,6},{6,2},{1,3},{5,1},... | collective-permute-start | bytes 1179656 | tf_op jit(solution)/shard_map/ppermute | solution.py:313
  37.3 10.5 %collective-permute-start.10 = (bf16[512,384]{1,0:T(8,128)(2,1)S(1)}, bf16[512,384]{1,0:T(8,128)(2,1)S(1)}, u32[]{:S(2)}, u32[]{:S(2)}) collective-permute-start(bf16[512,384]{1,0:T(8,128)(2,1)S(1)} %copy-done.9), channel_id=1, source_target_pairs={{2,0},{0,4},{4,8},{8,12},{12,14},{14,10},{10,6},{6,2},{1,3},{5,1},... | collective-permute-start | bytes 1179656 | tf_op jit(solution)/shard_map/ppermute | solution.py:316
  47.8 11.3 %collective-permute-start.17 = (bf16[512,384]{1,0:T(8,128)(2,1)S(1)}, bf16[512,384]{1,0:T(8,128)(2,1)S(1)}, u32[]{:S(2)}, u32[]{:S(2)}) collective-permute-start(bf16[512,384]{1,0:T(8,128)(2,1)S(1)} %copy-done.9), channel_id=1, source_target_pairs={{0,2},{4,0},{8,4},{12,8},{14,12},{10,14},{6,10},{2,6},{3,1},{1,5},... | collective-permute-start | bytes 1179656 | tf_op jit(solution)/shard_map/ppermute | solution.py:319
  55.4 13.5 %collective-permute-start.21 = (bf16[512,384]{1,0:T(8,128)(2,1)S(1)}, bf16[512,384]{1,0:T(8,128)(2,1)S(1)}, u32[]{:S(2)}, u32[]{:S(2)}) collective-permute-start(bf16[512,384]{1,0:T(8,128)(2,1)S(1)} %collective-permute-done.10.refs_2_), channel_id=1, source_target_pairs={{0,1},{1,0},{2,3},{3,2},{4,5},{5,4},{6,7},{7,6},{8,9},{9,8},{10,11... | collective-permute-start | bytes 1179656 | tf_op jit(solution)/shard_map/ppermute | solution.py:322
  59.4 11.4 %collective-permute-start.19 = (bf16[512,384]{1,0:T(8,128)(2,1)}, bf16[512,384]{1,0:T(8,128)(2,1)S(1)}, u32[]{:S(2)}, u32[]{:S(2)}) collective-permute-start(bf16[512,384]{1,0:T(8,128)(2,1)} %collective-permute-done.16.refs_6_), channel_id=1, source_target_pairs={{2,0},{0,4},{4,8},{8,12},{12,14},{14,10},{10,6},{6,2},{1,3},{5,1},... | collective-permute-start | bytes 1179656 | tf_op jit(solution)/shard_map/ppermute | solution.py:316
  71.4 14.0 %collective-permute-start.29 = (bf16[512,384]{1,0:T(8,128)(2,1)S(1)}, bf16[512,384]{1,0:T(8,128)(2,1)S(1)}, u32[]{:S(2)}, u32[]{:S(2)}) collective-permute-start(bf16[512,384]{1,0:T(8,128)(2,1)S(1)} %collective-permute-done.20.refs_7_), channel_id=1, source_target_pairs={{0,1},{1,0},{2,3},{3,2},{4,5},{5,4},{6,7},{7,6},{8,9},{9,8},{10,11... | collective-permute-start | bytes 1179656 | tf_op jit(solution)/shard_map/ppermute | solution.py:322
  71.9 13.5 %collective-permute-start.27 = (bf16[512,384]{1,0:T(8,128)(2,1)S(1)}, bf16[512,384]{1,0:T(8,128)(2,1)S(1)}, u32[]{:S(2)}, u32[]{:S(2)}) collective-permute-start(bf16[512,384]{1,0:T(8,128)(2,1)S(1)} %collective-permute-done.20.refs_7_), channel_id=1, source_target_pairs={{0,2},{4,0},{8,4},{12,8},{14,12},{10,14},{6,10},{2,6},{3,1},{1,5},... | collective-permute-start | bytes 1179656 | tf_op jit(solution)/shard_map/ppermute | solution.py:319
  73.6 11.8 %collective-permute-start.26 = (bf16[512,384]{1,0:T(8,128)(2,1)S(1)}, bf16[512,384]{1,0:T(8,128)(2,1)S(1)}, u32[]{:S(2)}, u32[]{:S(2)}) collective-permute-start(bf16[512,384]{1,0:T(8,128)(2,1)S(1)} %collective-permute-done.19.refs_2_), channel_id=1, source_target_pairs={{2,0},{0,4},{4,8},{8,12},{12,14},{14,10},{10,6},{6,2},{1,3},{5,1},... | collective-permute-start | bytes 1179656 | tf_op jit(solution)/shard_map/ppermute | solution.py:316
  76.2 11.7 %collective-permute-start.25 = (bf16[256,384]{1,0:T(8,128)(2,1)S(1)}, bf16[256,384]{1,0:T(8,128)(2,1)S(1)}, u32[]{:S(2)}, u32[]{:S(2)}) collective-permute-start(bf16[256,384]{1,0:T(8,128)(2,1)S(1)} %get-tuple-element.155), channel_id=1, source_target_pairs={{0,2},{1,3},{4,0},{5,1},{8,4},{9,5},{12,8},{13,9},{14,12},{15,13},... | collective-permute-start | bytes 589832 | tf_op jit(solution)/shard_map/ppermute | solution.py:310
  87.9 13.0 %collective-permute-start.30 = (bf16[2,512,384]{2,1,0:T(8,128)(2,1)S(1)}, bf16[2,512,384]{2,1,0:T(8,128)(2,1)S(1)}, u32[]{:S(2)}, u32[]{:S(2)}) collective-permute-start(bf16[2,512,384]{2,1,0:T(8,128)(2,1)S(1)} %get-tuple-element.121), channel_id=1, source_target_pairs={{0,1},{1,0},{2,3},{3,2},{4,5},{5,4},{6,7},{7,6},{8,9},{9,8},{10,11... | collective-permute-start | bytes 2359304 | tf_op jit(solution)/shard_map/ppermute | solution.py:322
  88.6 11.2 %collective-permute-start.32 = (bf16[512,384]{1,0:T(8,128)(2,1)S(1)}, bf16[512,384]{1,0:T(8,128)(2,1)S(1)}, u32[]{:S(2)}, u32[]{:S(2)}) collective-permute-start(bf16[512,384]{1,0:T(8,128)(2,1)S(1)} %get-tuple-element.151), channel_id=1, source_target_pairs={{0,2},{1,3},{4,0},{5,1},{8,4},{9,5},{12,8},{13,9},{14,12},{15,13},... | collective-permute-start | bytes 1179656 | tf_op jit(solution)/shard_map/ppermute | solution.py:310
  90.1 10.7 %collective-permute-start.31 = (bf16[512,384]{1,0:T(8,128)(2,1)S(1)}, bf16[512,384]{1,0:T(8,128)(2,1)S(1)}, u32[]{:S(2)}, u32[]{:S(2)}) collective-permute-start(bf16[512,384]{1,0:T(8,128)(2,1)S(1)} %get-tuple-element.152), channel_id=1, source_target_pairs={{2,0},{3,1},{0,4},{1,5},{4,8},{5,9},{8,12},{9,13},{12,14},{13,15},... | collective-permute-start | bytes 1179656 | tf_op jit(solution)/shard_map/ppermute | solution.py:310
  100.9 14.0 %collective-permute-start.34 = (bf16[3,512,384]{2,1,0:T(8,128)(2,1)S(1)}, bf16[3,512,384]{2,1,0:T(8,128)(2,1)S(1)}, u32[]{:S(2)}, u32[]{:S(2)}) collective-permute-start(bf16[3,512,384]{2,1,0:T(8,128)(2,1)S(1)} %get-tuple-element.127), channel_id=1, source_target_pairs={{0,1},{1,0},{2,3},{3,2},{4,5},{5,4},{6,7},{7,6},{8,9},{9,8},{10,11... | collective-permute-start | bytes 3538952 | tf_op jit(solution)/shard_map/ppermute | solution.py:322
  100.9 10.9 %collective-permute-start.37 = (bf16[512,384]{1,0:T(8,128)(2,1)S(1)}, bf16[512,384]{1,0:T(8,128)(2,1)S(1)}, u32[]{:S(2)}, u32[]{:S(2)}) collective-permute-start(bf16[512,384]{1,0:T(8,128)(2,1)S(1)} %collective-permute-done.26.refs_6_), channel_id=1, source_target_pairs={{0,1},{1,0},{2,3},{3,2},{4,5},{5,4},{6,7},{7,6},{8,9},{9,8},{10,11... | collective-permute-start | bytes 1179656 | tf_op jit(solution)/shard_map/ppermute | solution.py:322
  101.4 10.4 %collective-permute-start.38 = (bf16[512,384]{1,0:T(8,128)(2,1)S(1)}, bf16[512,384]{1,0:T(8,128)(2,1)S(1)}, u32[]{:S(2)}, u32[]{:S(2)}) collective-permute-start(bf16[512,384]{1,0:T(8,128)(2,1)S(1)} %collective-permute-done.27.refs_3_), channel_id=1, source_target_pairs={{0,1},{1,0},{2,3},{3,2},{4,5},{5,4},{6,7},{7,6},{8,9},{9,8},{10,11... | collective-permute-start | bytes 1179656 | tf_op jit(solution)/shard_map/ppermute | solution.py:322
  101.8 11.5 %collective-permute-start.36 = (bf16[512,384]{1,0:T(8,128)(2,1)S(1)}, bf16[512,384]{1,0:T(8,128)(2,1)S(1)}, u32[]{:S(2)}, u32[]{:S(2)}) collective-permute-start(bf16[512,384]{1,0:T(8,128)(2,1)S(1)} %get-tuple-element.153), channel_id=1, source_target_pairs={{0,2},{1,3},{4,0},{5,1},{8,4},{9,5},{12,8},{13,9},{14,12},{15,13},... | collective-permute-start | bytes 1179656 | tf_op jit(solution)/shard_map/ppermute | solution.py:310
  103.6 11.2 %collective-permute-start.35 = (bf16[512,384]{1,0:T(8,128)(2,1)S(1)}, bf16[512,384]{1,0:T(8,128)(2,1)S(1)}, u32[]{:S(2)}, u32[]{:S(2)}) collective-permute-start(bf16[512,384]{1,0:T(8,128)(2,1)S(1)} %get-tuple-element.154), channel_id=1, source_target_pairs={{2,0},{3,1},{0,4},{1,5},{4,8},{5,9},{8,12},{9,13},{12,14},{13,15},... | collective-permute-start | bytes 1179656 | tf_op jit(solution)/shard_map/ppermute | solution.py:310
  115.1 10.4 %collective-permute-start.40 = (bf16[512,384]{1,0:T(8,128)(2,1)S(1)}, bf16[512,384]{1,0:T(8,128)(2,1)S(1)}, u32[]{:S(2)}, u32[]{:S(2)}) collective-permute-start(bf16[512,384]{1,0:T(8,128)(2,1)S(1)} %get-tuple-element.149), channel_id=1, source_target_pairs={{0,2},{1,3},{4,0},{5,1},{8,4},{9,5},{12,8},{13,9},{14,12},{15,13},... | collective-permute-start | bytes 1179656 | tf_op jit(solution)/shard_map/ppermute | solution.py:310
  (34 other events, 234.9 us)
